TPU v7x, 256 devices: a whole 4x4x8 slice. The times are simulated.
256 devices in a mesh: head: 8 (over y_hi, x), ctx: 32 (over z, y_lo, core).
Axes of the slice: x: 4, y: 4 (y_hi: 2, y_lo: 2; y = y_hi * 2 + y_lo), z: 8, core: 2. Of those that a mesh axis runs over, the one named last changes fastest.
Arguments:
- main_queries: bfloat16 [64, 4096, 576], P('head', 'ctx')
- latent_keys: bfloat16 [5120, 576], P('ctx'), may hold values from -6 to 6
- index_queries: bfloat16 [4096, 64, 128], P('ctx'), may hold values from -6 to 6
- index_weights: float32 [4096, 64], P('ctx')
- index_keys: bfloat16 [5120, 128], P('ctx'), may hold values from -6 to 6
- tile_order: int32 [128], P('ctx'), may hold values from 0 to 127, each once
- offset: int32 [1], replicated, may hold values from 864 to 1024
Outputs:
- divergence: float32 [4096], P('ctx')
- weight_grad: float32 [4096, 64], P('ctx')
- key_grad: float32 [5120, 128], P('ctx')
All inputs are finite; a program needn't handle non-finite values.
Results may differ from a plain program's by a relative error of at most 0.0075.
Values may be sent and summed in bfloat16 or wider, within the bound.
No kernel may reach another device: no remote copies, remote signals or barrier semaphores. Data moves between devices by JAX's collectives and lax.ppermute only.
A program may use at most 64 MiB of HBM per device.

v0:
```python
import math

import jax
import jax.numpy as jnp
from jax import lax
from jax.sharding import PartitionSpec as P

H = 64
TILE = 32


score_scale = 192.0 ** (-0.5)


def head_total(query_set, keys_all, visible_rows):

    def head_step(head_id, total):
        queries = lax.dynamic_index_in_dim(query_set, head_id, 0, keepdims=False)
        scores = (
            lax.dot_general(
                queries, keys_all, (((1,), (1,)), ((), ())), preferred_element_type=jnp.float32
            )
            * score_scale
        )
        scores = jnp.where(visible_rows, scores, -jnp.inf)
        return total + jax.nn.softmax(scores, axis=1)

    start = jnp.zeros((query_set.shape[1], keys_all.shape[0]), jnp.float32)
    return lax.fori_loop(0, query_set.shape[0], head_step, start)


def body(main_queries, latent_keys, index_queries, index_weights, index_keys, tile_order, offset):
    local_heads, local_rows, latent_size = main_queries.shape
    n_heads_axis = lax.axis_size("head")
    head_pos = lax.axis_index("head")
    keys_all, ikeys_all = (
        lax.all_gather(latent_keys, "ctx", axis=0, tiled=True),
        lax.all_gather(index_keys, "ctx", axis=0, tiled=True),
    )
    total_keys = keys_all.shape[0]
    index_size = ikeys_all.shape[1]
    index_scale = index_size ** (-0.5)
    row_ids = jnp.arange(local_rows, dtype=jnp.int32)
    positions = (
        offset[0]
        + jnp.repeat(tile_order, TILE, total_repeat_length=local_rows) * TILE
        + row_ids % TILE
    )
    visible_int = jnp.where(
        jnp.arange(total_keys, dtype=jnp.int32)[None, :] <= positions[:, None], 1, 0
    ).astype(jnp.int32)
    visible_all = visible_int > 0
    row_share = local_rows // n_heads_axis
    visible = lax.dynamic_slice_in_dim(visible_all, head_pos * row_share, row_share, 0)
    partial_sum = head_total(main_queries, keys_all, visible_all)
    everything = lax.psum(partial_sum, "head")
    summed = lax.dynamic_slice_in_dim(everything, head_pos * row_share, row_share, 0)
    target = summed / H
    row_queries = lax.dynamic_slice_in_dim(index_queries, head_pos * row_share, row_share, 0)
    row_weights = lax.dynamic_slice_in_dim(index_weights, head_pos * row_share, row_share, 0)
    block = math.gcd(total_keys, 1536)
    blocks = total_keys // block
    key_blocks = ikeys_all.reshape(blocks, block, index_size)

    def logits_block(key_block):
        inner = jnp.einsum(
            "tjd,sd->tjs", row_queries, key_block, preferred_element_type=jnp.float32
        )
        return jnp.sum(row_weights[:, :, None] * jax.nn.relu(inner), axis=1) * index_scale

    logits = lax.map(logits_block, key_blocks).transpose(1, 0, 2).reshape(row_share, total_keys)
    masked = jnp.where(visible, logits, -jnp.inf)
    log_probs = masked - jax.scipy.special.logsumexp(masked, axis=1, keepdims=True)
    index_probs = jnp.where(visible, jnp.exp(log_probs), 0.0)
    live = visible & (target > 0)
    safe_target = jnp.where(target > 0, target, 1.0)
    divergence = jnp.sum(jnp.where(live, target * (jnp.log(safe_target) - log_probs), 0.0), axis=1)
    grad_logit = jnp.where(visible, index_probs - target, 0.0)
    grad_blocks = grad_logit.reshape(row_share, blocks, block).transpose(1, 0, 2)

    def grad_block(items):
        key_block, grad_piece = items
        inner = jnp.einsum(
            "tjd,sd->tjs", row_queries, key_block, preferred_element_type=jnp.float32
        )
        weight_part = jnp.sum(grad_piece[:, None, :] * jax.nn.relu(inner), axis=2) * index_scale
        coeff = (
            grad_piece[:, None, :] * row_weights[:, :, None] * index_scale * (inner > 0)
        ).astype(jnp.bfloat16)
        key_part = jnp.einsum("tjs,tjd->sd", coeff, row_queries, preferred_element_type=jnp.float32)
        return (weight_part, key_part)

    weight_parts, key_parts = lax.map(grad_block, (key_blocks, grad_blocks))
    weight_grad = jnp.sum(weight_parts, axis=0)
    key_terms = key_parts.reshape(total_keys, index_size)
    owner_terms = lax.psum_scatter(key_terms, "ctx", scatter_dimension=0, tiled=True)
    key_grad = lax.psum(owner_terms, "head")
    weight_all, divergence_all = (
        lax.all_gather(weight_grad, "head", axis=0, tiled=True),
        lax.all_gather(divergence, "head", axis=0, tiled=True),
    )
    return (divergence_all, weight_all, key_grad)


def solution(mesh):
    in_specs = (
        P("head", "ctx", None),
        P("ctx", None),
        P("ctx", None, None),
        P("ctx", None),
        P("ctx", None),
        P("ctx"),
        P(),
    )
    out_specs = (P("ctx"), P("ctx", None), P("ctx", None))
    return jax.shard_map(body, mesh=mesh, in_specs=in_specs, out_specs=out_specs, check_vma=False)
```

profile of v0, /device:TPU:2, one launch (start us, length us, event | category | flops | bytes accessed | tf_op | source)
XLA Modules:
  0.0 521.1 jit_solution(15352166601625122679)
XLA Ops:
  15.1 68.3 %all-gather.3.cloned.1.call-done = bf16[5120,576]{1,0:T(8,128)(2,1)} async-done(((bf16[160,576]{1,0:T(8,128)(2,1)}), bf16[5120,576]{1,0:T(8,128)(2,1)}) %all-gather.3.cloned.1.call-update) | async-done | bytes 5898256 | tf_op jit(solution)/shard_map/all_gather | solution.py:37
  83.4 95.7 %while.39 = (s32[]{:T(128)}, f32[128,5120]{1,0:T(8,128)}, bf16[8,128,576]{1,2,0:T(8,128)(2,1)}, bf16[5120,576]{1,0:T(8,128)(2,1)}, s32[128]{0:T(128)S(1)}, /*index=5*/s32[]{:T(128)}, s32[]{:T(128)}) while((s32[]{:T(128)}, f32[128,5120]{1,0:T(8,128)}, bf16[8,128,576]{1,2,0:T(8,128)(2,1)}, bf16[5120,576]{1,0:T(8,128)(2,1)}, ...), condition=%wide.region_3.4_spmd.clone, body=%wide.region_0.3_spmd.clone.sunk | while | flops 762838784 | bytes 30297212 | solution.py:29
  83.4 5.3 %fusion.53 = (f32[128]{0:T(128)S(1)}, f32[128,5120]{1,0:T(8,128)S(1)}) fusion(bf16[5120,576]{1,0:T(8,128)(2,1)} %get-tuple-element.390, bf16[8,128,576]{1,2,0:T(8,128)(2,1)} %get-tuple-element.389, s32[]{:T(128)S(6)} %copy.32, s32[128]{0:T(128)S(1)} %get-tuple-element.391), kind=kOutput, calls=%fused_computation.56.clone.1 | convolution fusion | flops 758906752 | bytes 9323524 | tf_op jit(solution)/shard_map/while/body/eval_jaxpr/dot_general | solution.py:20
  94.6 5.4 %fusion.53 = (f32[128]{0:T(128)S(1)}, f32[128,5120]{1,0:T(8,128)S(1)}) fusion(bf16[5120,576]{1,0:T(8,128)(2,1)} %get-tuple-element.390, bf16[8,128,576]{1,2,0:T(8,128)(2,1)} %get-tuple-element.389, s32[]{:T(128)S(6)} %copy.32, s32[128]{0:T(128)S(1)} %get-tuple-element.391), kind=kOutput, calls=%fused_computation.56.clone.1 | convolution fusion | flops 758906752 | bytes 9323524 | tf_op jit(solution)/shard_map/while/body/eval_jaxpr/dot_general | solution.py:20
  102.1 4.6 select_add_fusion.2
  106.7 5.4 %fusion.53 = (f32[128]{0:T(128)S(1)}, f32[128,5120]{1,0:T(8,128)S(1)}) fusion(bf16[5120,576]{1,0:T(8,128)(2,1)} %get-tuple-element.390, bf16[8,128,576]{1,2,0:T(8,128)(2,1)} %get-tuple-element.389, s32[]{:T(128)S(6)} %copy.32, s32[128]{0:T(128)S(1)} %get-tuple-element.391), kind=kOutput, calls=%fused_computation.56.clone.1 | convolution fusion | flops 758906752 | bytes 9323524 | tf_op jit(solution)/shard_map/while/body/eval_jaxpr/dot_general | solution.py:20
  114.2 4.6 select_add_fusion.2
  118.8 5.3 %fusion.53 = (f32[128]{0:T(128)S(1)}, f32[128,5120]{1,0:T(8,128)S(1)}) fusion(bf16[5120,576]{1,0:T(8,128)(2,1)} %get-tuple-element.390, bf16[8,128,576]{1,2,0:T(8,128)(2,1)} %get-tuple-element.389, s32[]{:T(128)S(6)} %copy.32, s32[128]{0:T(128)S(1)} %get-tuple-element.391), kind=kOutput, calls=%fused_computation.56.clone.1 | convolution fusion | flops 758906752 | bytes 9323524 | tf_op jit(solution)/shard_map/while/body/eval_jaxpr/dot_general | solution.py:20
  126.3 4.6 select_add_fusion.2
  130.9 5.4 %fusion.53 = (f32[128]{0:T(128)S(1)}, f32[128,5120]{1,0:T(8,128)S(1)}) fusion(bf16[5120,576]{1,0:T(8,128)(2,1)} %get-tuple-element.390, bf16[8,128,576]{1,2,0:T(8,128)(2,1)} %get-tuple-element.389, s32[]{:T(128)S(6)} %copy.32, s32[128]{0:T(128)S(1)} %get-tuple-element.391), kind=kOutput, calls=%fused_computation.56.clone.1 | convolution fusion | flops 758906752 | bytes 9323524 | tf_op jit(solution)/shard_map/while/body/eval_jaxpr/dot_general | solution.py:20
  138.3 4.6 select_add_fusion.2
  142.9 5.4 %fusion.53 = (f32[128]{0:T(128)S(1)}, f32[128,5120]{1,0:T(8,128)S(1)}) fusion(bf16[5120,576]{1,0:T(8,128)(2,1)} %get-tuple-element.390, bf16[8,128,576]{1,2,0:T(8,128)(2,1)} %get-tuple-element.389, s32[]{:T(128)S(6)} %copy.32, s32[128]{0:T(128)S(1)} %get-tuple-element.391), kind=kOutput, calls=%fused_computation.56.clone.1 | convolution fusion | flops 758906752 | bytes 9323524 | tf_op jit(solution)/shard_map/while/body/eval_jaxpr/dot_general | solution.py:20
  150.4 4.6 select_add_fusion.2
  155.0 5.3 %fusion.53 = (f32[128]{0:T(128)S(1)}, f32[128,5120]{1,0:T(8,128)S(1)}) fusion(bf16[5120,576]{1,0:T(8,128)(2,1)} %get-tuple-element.390, bf16[8,128,576]{1,2,0:T(8,128)(2,1)} %get-tuple-element.389, s32[]{:T(128)S(6)} %copy.32, s32[128]{0:T(128)S(1)} %get-tuple-element.391), kind=kOutput, calls=%fused_computation.56.clone.1 | convolution fusion | flops 758906752 | bytes 9323524 | tf_op jit(solution)/shard_map/while/body/eval_jaxpr/dot_general | solution.py:20
  162.4 4.6 select_add_fusion.2
  167.0 5.3 %fusion.53 = (f32[128]{0:T(128)S(1)}, f32[128,5120]{1,0:T(8,128)S(1)}) fusion(bf16[5120,576]{1,0:T(8,128)(2,1)} %get-tuple-element.390, bf16[8,128,576]{1,2,0:T(8,128)(2,1)} %get-tuple-element.389, s32[]{:T(128)S(6)} %copy.32, s32[128]{0:T(128)S(1)} %get-tuple-element.391), kind=kOutput, calls=%fused_computation.56.clone.1 | convolution fusion | flops 758906752 | bytes 9323524 | tf_op jit(solution)/shard_map/while/body/eval_jaxpr/dot_general | solution.py:20
  174.5 4.6 select_add_fusion.2
  179.2 13.9 %while.37 = (s32[]{:T(128)}, f32[10,16,512]{2,1,0:T(8,128)S(1)}, f32[16,64]{1,0:T(8,128)S(1)}, bf16[10,512,128]{2,1,0:T(8,128)(2,1)}, bf16[16,64,128]{2,1,0:T(8,128)(2,1)S(1)}, /*index=5*/s32[]{:T(128)}) while((s32[]{:T(128)}, f32[10,16,512]{2,1,0:T(8,128)S(1)}, f32[16,64]{1,0:T(8,128)S(1)}, bf16[10,512,128]{2,1,0:T(8,128)(2,1)}, ...), condition=%wide.region_7.8_spmd, body=%wide.region_5.7_spmd.sunk | while | flops 135790592 | bytes 495701 | solution.py:71
  193.7 84.2 %all-reduce.4.cloned.1.call-done = f32[128,5120]{1,0:T(8,128)} async-done(((f32[128,5120]{1,0:T(8,128)}), f32[128,5120]{1,0:T(8,128)}) %all-reduce.4.cloned.1.call-update) | async-done | bytes 2621456 | tf_op jit(solution)/shard_map/psum | solution.py:56
  279.3 29.2 %while.38 = (s32[]{:T(128)}, f32[10,16,64]{2,1,0:T(8,128)S(1)}, f32[10,512,128]{2,1,0:T(8,128)}, f32[10,16,512]{2,0,1:T(8,128)S(1)}, bf16[10,512,128]{2,1,0:T(8,...) while((s32[]{:T(128)}, f32[10,16,64]{2,1,0:T(8,128)S(1)}, ...), condition=%wide.region_13.14_spmd, body=%wide.region_11.13_spmd.sunk | while | flops 272629760 | bytes 5333101 | solution.py:93
  308.6 121.4 %reduce-scatter.2.cloned.1.call-done = f32[160,128]{1,0:T(8,128)} async-done(((f32[5120,128]{1,0:T(8,128)}), f32[160,128]{1,0:T(8,128)}) %reduce-scatter.2.cloned.1.call-update) | async-done | bytes 81936 | tf_op jit(solution)/shard_map/reduce_scatter | solution.py:96
  431.3 33.8 %all_gather.15 = f32[128,64]{1,0:T(8,128)S(1)} all-gather(f32[16,64]{1,0:T(8,128)S(1)} %reduce_sum.60), channel_id=1, replica_groups=mesh['head'=8,'ctx'=32] {'head'}, dimensions={0}, use_global_device_ids=true | all-gather | bytes 36864 | tf_op jit(solution)/shard_map/all_gather | solution.py:99
  466.0 20.4 %all-reduce = f32[128]{0:T(128)} all-reduce(f32[128]{0:T(128)S(1)} %dynamic-update-slice.3), channel_id=1, replica_groups=mesh['head'=8,'ctx'=32] {'head'}, use_global_device_ids=true, to_apply=%add | all-reduce | flops 128 | bytes 1024
  486.4 26.6 %all-reduce.6.cloned.1.call-done = f32[160,128]{1,0:T(8,128)} async-done(((f32[160,128]{1,0:T(8,128)}), f32[160,128]{1,0:T(8,128)}) %all-reduce.6.cloned.1.call-update) | async-done | bytes 81936 | tf_op jit(solution)/shard_map/psum | solution.py:97
  (133 shorter events, 75.4 us)
Async XLA Ops:
  7.2 7.9 %copy-start = (bf16[128,64,128]{2,1,0:T(8,128)(2,1)S(1)}, bf16[128,64,128]{2,1,0:T(8,128)(2,1)}, u32[]{:S(2)}) copy-start(bf16[128,64,128]{2,1,0:T(8,128)(2,1)} %param.17) | copy-start | bytes 6291460
  7.2 76.2 %all-gather.3.cloned.1.call-start = ((), (), s32[]{:S(2)}) async-start(), calls=%async_computation.1 | async-start | bytes 6758400 | tf_op jit(solution)/shard_map/all_gather | solution.py:37
  7.9 171.2 %all-gather.5.cloned.1.call-start = ((), (), s32[]{:S(2)}) async-start(), calls=%async_computation.3 | async-start | bytes 1351680 | tf_op jit(solution)/shard_map/all_gather | solution.py:38
  8.7 269.2 %all-reduce.4.cloned.1.call-start = ((), (), s32[]{:S(2)}) async-start(), calls=%async_computation.2 | async-start | bytes 5242880 | tf_op jit(solution)/shard_map/psum | solution.py:56
  88.7 1.6 copy-start.1
  100.0 1.6 copy-start.1
  112.1 1.6 copy-start.1
  124.2 1.6 copy-start.1
  136.2 1.6 copy-start.1
  148.3 1.6 copy-start.1
  160.3 1.6 copy-start.1
  172.4 1.6 copy-start.1
  179.1 250.9 %reduce-scatter.2.cloned.1.call-start = ((), (), s32[]{:S(2)}) async-start(), calls=%async_computation.4 | async-start | bytes 2703360 | tf_op jit(solution)/shard_map/reduce_scatter | solution.py:96
  308.5 121.5 %copy-start.2 = (u32[256]{0:T(256)S(1)}, u32[256]{0:T(256)}, u32[]{:S(2)}) copy-start(u32[256]{0:T(256)} %constant.214) | copy-start | bytes 3076
  308.5 204.5 %all-reduce.6.cloned.1.call-start = ((), (), s32[]{:S(2)}) async-start(), calls=%async_computation.5 | async-start | bytes 163840 | tf_op jit(solution)/shard_map/psum | solution.py:97
Sparse Core Ops, SparseCore 0:
  9.9 73.4 all-gather.2
  85.2 63.9 all-gather.4
  179.2 98.6 all-reduce.3
  308.7 121.3 reduce-scatter.1
  432.5 80.4 all-reduce.5
where the time goes:
time: 522 us; the launch traced here: 521 us
  waiting for transfers between devices  302 us (58%)
  matrix products  84.9 us (16%)
  blocking collectives  54.2 us (10%)
  other arithmetic  45.4 us (9%)
  local copies, waits for them, and re-layouts  18.5 us (4%)
  between operations  15.2 us (3%)
    reduce_scatter x1, waiting for transfers between devices, body(): lax.psum_scatter(key_terms, 'ctx', scatter_dimension=0, tiled=True)  121 us
    psum x1, waiting for transfers between devices, body(): everything = lax.psum(partial_sum, 'head')  84.2 us
    all_gather x1, waiting for transfers between devices, body(): lax.all_gather(latent_keys, 'ctx', axis=0, tiled=True)  68.3 us
    dot_general x8, matrix products, head_step(): lax.dot_general(queries, keys_all, (((1,), (1,)), ((), ())), preferred_el...  42.8 us
    add x8, other arithmetic, head_step(): return total + jax.nn.softmax(scores, axis=1)  36.1 us
    all_gather x1, blocking collectives, body(): lax.all_gather(weight_grad, 'head', axis=0, tiled=True)  33.8 us
    psum x1, waiting for transfers between devices, body(): key_grad = lax.psum(owner_terms, 'head')  26.6 us
    unnamed x1, blocking collectives  20.4 us
  transfers between devices with their start and end apart: 5, of which 4 were waited for; matrix products, arithmetic and copies ran while one was open for 20% of the time, Pallas kernels for 0%

commit v1 on v0

v1 whole, which is shorter than its diff:
```python
import math

import jax
import jax.numpy as jnp
import numpy as np
from jax import lax
from jax.experimental import pallas as pl
from jax.experimental.pallas import tpu as pltpu
from jax.sharding import Mesh
from jax.sharding import PartitionSpec as P

TILE = 32
DQ = 576
DI = 128
NI = 64
HALF = 80
UNIT = 16
BLOCKS = 16
ROWS = 320
SCORE2 = 192.0 ** (-0.5) * math.log2(math.e)
INDEX_SCALE = DI ** (-0.5)
ALL = ("yhi", "xh", "xp", "z", "ylo", "core")
NEG = -jnp.inf


def flat(x, y, z, c):
    return ((y // 2) * 4 + x) * 32 + (z * 2 + (y % 2)) * 2 + c


def shift(value, dx=0, dy=0, dz=0, flip=0):
    pairs = [
        (flat(x, y, z, c), flat((x + dx) % 4, (y + dy) % 4, (z + dz) % 8, c ^ flip))
        for x in range(4)
        for y in range(4)
        for z in range(8)
        for c in range(2)
    ]
    return lax.ppermute(value, ALL, pairs)


def swap_core(value):
    return shift(value, flip=1)


def score_kernel(n, meta, *refs):
    blocks, (qa, qb, wa, wb) = refs[:n], refs[n : n + 4]
    e_ref, m_ref, l_ref, keys, bias, raw = refs[n + 4 :]

    @pl.when(pl.program_id(0) == 0)
    def _():
        place = jnp.concatenate([wa[NI : NI + 1, :], wb[NI : NI + 1, :]], axis=1)
        rows = lax.broadcasted_iota(jnp.int32, (HALF, 256), 0).astype(jnp.float32)
        for i in range(n):
            keys[i * HALF : (i + 1) * HALF, :] = blocks[i][:, DI : DI + DQ]
            base = meta[i].astype(jnp.float32)
            bias[i * HALF : (i + 1) * HALF, :] = jnp.where(rows + base <= place, 0.0, NEG)

    queries = jnp.concatenate([qa[0], qb[0]], axis=1)
    scores = jnp.dot(keys[...], queries, preferred_element_type=jnp.float32) + bias[...]
    raw[...] = scores
    top = jnp.max(scores, axis=0, keepdims=True)
    safe = jnp.where(top == NEG, 0.0, top)
    exps = jnp.exp2((raw[...] - safe) * SCORE2)
    e_ref[0] = exps.astype(jnp.bfloat16)
    m_ref[0] = top
    l_ref[0] = jnp.sum(exps, axis=0, keepdims=True)


def score_call(meta, blocks, qa, qb, wa, wb):
    n = len(blocks)
    heads = qa.shape[0]
    whole = lambda shape: pl.BlockSpec(shape, lambda h, meta: (0,) * len(shape))
    per_head = lambda shape: pl.BlockSpec((1,) + shape, lambda h, meta: (h, 0, 0))
    return pl.pallas_call(
        lambda *refs: score_kernel(n, *refs),
        grid_spec=pltpu.PrefetchScalarGridSpec(
            num_scalar_prefetch=1,
            grid=(heads,),
            in_specs=[whole((HALF, DI + DQ))] * n
            + [per_head((DQ, 128))] * 2
            + [whole((72, 128))] * 2,
            out_specs=[per_head((n * HALF, 256)), per_head((1, 256)), per_head((1, 256))],
            scratch_shapes=[
                pltpu.VMEM((n * HALF, DQ), jnp.bfloat16),
                pltpu.VMEM((n * HALF, 256), jnp.float32),
                pltpu.VMEM((n * HALF, 256), jnp.float32),
            ],
        ),
        out_shape=[
            jax.ShapeDtypeStruct((heads, n * HALF, 256), jnp.bfloat16),
            jax.ShapeDtypeStruct((heads, 1, 256), jnp.float32),
            jax.ShapeDtypeStruct((heads, 1, 256), jnp.float32),
        ],
        cost_estimate=pl.CostEstimate(
            flops=2 * heads * n * HALF * 256 * DQ,
            bytes_accessed=heads * n * HALF * 512,
            transcendentals=heads * n * HALF * 256,
        ),
        compiler_params=pltpu.CompilerParams(vmem_limit_bytes=40 << 20),
        name="scores",
    )(meta, *blocks, qa, qb, wa, wb)


def head_sum_kernel(meta, e0, e1, r0, r1, out):
    i = pl.program_id(0)
    total = jnp.zeros((HALF, 256), jnp.float32)
    for e_ref, r_ref in ((e0, r0), (e1, r1)):
        for h in range(8):
            total = total + e_ref[h].astype(jnp.float32) * r_ref[h]
    total = total.astype(jnp.bfloat16)
    slot = meta[BLOCKS + i]
    for q in range(4):
        out[q, pl.ds(pl.multiple_of(slot * UNIT, UNIT), UNIT), :] = total[q * UNIT : (q + 1) * UNIT]
    extra = pl.multiple_of(256 + (slot >> 2) * UNIT, UNIT)
    out[slot & 3, pl.ds(extra, UNIT), :] = total[4 * UNIT :]


def head_sum_call(meta, e0, e1, r0, r1):
    piece = pl.BlockSpec((8, HALF, 256), lambda i, meta: (0, i, 0))
    ratio = pl.BlockSpec((8, 1, 256), lambda i, meta: (0, 0, 0))
    return pl.pallas_call(
        head_sum_kernel,
        grid_spec=pltpu.PrefetchScalarGridSpec(
            num_scalar_prefetch=1,
            grid=(BLOCKS,),
            in_specs=[piece, piece, ratio, ratio],
            out_specs=pl.BlockSpec((4, ROWS, 256), lambda i, meta: (0, 0, 0)),
        ),
        out_shape=jax.ShapeDtypeStruct((4, ROWS, 256), jnp.bfloat16),
        cost_estimate=pl.CostEstimate(flops=0, bytes_accessed=11 << 20, transcendentals=0),
        compiler_params=pltpu.CompilerParams(vmem_limit_bytes=40 << 20),
        name="head_sum",
    )(meta, e0, e1, r0, r1)


def key_places(meta):
    core, half, quarter = meta[32], meta[33], meta[34]
    rows = lax.broadcasted_iota(jnp.int32, (UNIT, 256), 0)
    out = []
    for u in range(16):
        out.append(rows + ((u // 2 * 4 + (u % 2) * 2 + core) * 160 + half * HALF + quarter * UNIT))
    for e in range(4):
        z, ylo = 2 * e + (quarter >> 1), quarter & 1
        out.append(rows + ((z * 4 + ylo * 2 + core) * 160 + half * HALF + 4 * UNIT))
    return out


def inner_of(keys, ia, ib, j):
    queries = jnp.concatenate([ia[j], ib[j]], axis=0)
    return lax.dot_general(
        keys[...], queries, (((1,), (1,)), ((), ())), preferred_element_type=jnp.float32
    ), queries


JSTEP = 8


def forward_kernel(meta, *refs):
    blocks = refs[:BLOCKS]
    ia, ib, wa, wb, wja, wjb, keys, logits, stats = refs[BLOCKS:]
    step = pl.program_id(0)

    @pl.when(step == 0)
    def _():
        quarter = meta[34]
        for i in range(BLOCKS):
            slot = meta[BLOCKS + i]
            mine = pl.ds(pl.multiple_of(quarter * UNIT, UNIT), UNIT)
            keys[pl.ds(pl.multiple_of(slot * UNIT, UNIT), UNIT), :] = blocks[i][mine, 0:DI]

            @pl.when((slot & 3) == quarter)
            def _():
                extra = pl.multiple_of(256 + (slot >> 2) * UNIT, UNIT)
                keys[pl.ds(extra, UNIT), :] = blocks[i][4 * UNIT :, 0:DI]

        logits[...] = jnp.zeros_like(logits)

    total = logits[...]
    for j in range(JSTEP):
        inner, _ = inner_of(keys, ia, ib, j)
        weight = jnp.concatenate([wja[j : j + 1, :], wjb[j : j + 1, :]], axis=1)
        total = total + weight * jnp.maximum(inner, 0.0)
    logits[...] = total

    @pl.when(step == NI // JSTEP - 1)
    def _():
        place = jnp.concatenate([wa[NI : NI + 1, :], wb[NI : NI + 1, :]], axis=1)
        places = key_places(meta)
        top = jnp.full((1, 256), NEG, jnp.float32)
        for u in range(20):
            cut = slice(u * UNIT, (u + 1) * UNIT)
            value = logits[cut, :] * INDEX_SCALE
            value = jnp.where(places[u].astype(jnp.float32) <= place, value, NEG)
            logits[cut, :] = value
            top = jnp.maximum(top, jnp.max(value, axis=0, keepdims=True))
        safe = jnp.where(top == NEG, 0.0, top)
        total = jnp.sum(jnp.exp(logits[...] - safe), axis=0, keepdims=True)
        stats[...] = jnp.zeros_like(stats)
        stats[0:1, :] = top
        stats[1:2, :] = total


def j_specs():
    whole = lambda shape: pl.BlockSpec(shape, lambda s, meta: (0,) * len(shape))
    queries = pl.BlockSpec((JSTEP, 128, DI), lambda s, meta: (s, 0, 0))
    weights = pl.BlockSpec((JSTEP, 128), lambda s, meta: (s, 0))
    return whole, [queries, queries, whole((72, 128)), whole((72, 128)), weights, weights]


def forward_call(meta, blocks, ia, ib, wa, wb):
    whole, specs = j_specs()
    return pl.pallas_call(
        forward_kernel,
        grid_spec=pltpu.PrefetchScalarGridSpec(
            num_scalar_prefetch=1,
            grid=(NI // JSTEP,),
            in_specs=[whole((HALF, DI + DQ))] * BLOCKS + specs,
            out_specs=[whole((ROWS, DI)), whole((ROWS, 256)), whole((8, 256))],
        ),
        out_shape=[
            jax.ShapeDtypeStruct((ROWS, DI), jnp.bfloat16),
            jax.ShapeDtypeStruct((ROWS, 256), jnp.float32),
            jax.ShapeDtypeStruct((8, 256), jnp.float32),
        ],
        cost_estimate=pl.CostEstimate(
            flops=2 * NI * ROWS * 256 * DI, bytes_accessed=5 << 20, transcendentals=0
        ),
        compiler_params=pltpu.CompilerParams(vmem_limit_bytes=40 << 20),
        name="index_forward",
    )(meta, *blocks, ia, ib, wa, wb, wa, wb)


def backward_kernel(meta, keys, logits, stats, target, ia, ib, wa, wb, wja, wjb, wg, div, kg, grad, acc):
    step = pl.program_id(0)

    @pl.when(step == 0)
    def _():
        tops = [stats[d, 0:1, :] for d in range(8)]
        top = tops[0]
        for d in range(1, 8):
            top = jnp.maximum(top, tops[d])
        total = jnp.zeros((1, 256), jnp.float32)
        for d in range(8):
            total = total + stats[d, 1:2, :] * jnp.exp(tops[d] - top)
        norm = top + jnp.log(total)
        goal = jnp.zeros((ROWS, 256), jnp.float32)
        for d in range(4):
            goal = goal + target[d].astype(jnp.float32)
        goal = goal * (1.0 / 64.0)
        value = logits[...]
        seen = value != NEG
        logp = value - norm
        live = seen & (goal > 0)
        safe = jnp.where(goal > 0, goal, 1.0)
        part = jnp.where(live, goal * (jnp.log(safe) - logp), 0.0)
        div[...] = jnp.zeros_like(div)
        div[0:1, :] = jnp.sum(part, axis=0, keepdims=True)
        grad[...] = jnp.where(seen, jnp.exp(logp) - goal, 0.0) * INDEX_SCALE
        acc[...] = jnp.zeros_like(acc)

    total = acc[...]
    slope = grad[...]
    for j in range(JSTEP):
        inner, queries = inner_of(keys, ia, ib, j)
        weight = jnp.concatenate([wja[j : j + 1, :], wjb[j : j + 1, :]], axis=1)
        wg[j : j + 1, :] = jnp.sum(slope * jnp.maximum(inner, 0.0), axis=0, keepdims=True)
        coeff = jnp.where(inner > 0, slope * weight, 0.0).astype(jnp.bfloat16)
        total = total + jnp.dot(coeff, queries, preferred_element_type=jnp.float32)
    acc[...] = total

    @pl.when(step == NI // JSTEP - 1)
    def _():
        quarter = meta[34]
        for b in range(BLOCKS):
            kg[b, 0:UNIT, :] = acc[b * UNIT : (b + 1) * UNIT, :]
            at = 256 + (b // 4) * UNIT
            kg[b, UNIT:, :] = jnp.where(quarter == b % 4, acc[at : at + UNIT, :], 0.0)


def backward_call(meta, keys, logits, stats, target, ia, ib, wa, wb):
    whole, specs = j_specs()
    return pl.pallas_call(
        backward_kernel,
        grid_spec=pltpu.PrefetchScalarGridSpec(
            num_scalar_prefetch=1,
            grid=(NI // JSTEP,),
            in_specs=[
                whole((ROWS, DI)),
                whole((ROWS, 256)),
                whole((8, 8, 256)),
                whole((4, ROWS, 256)),
            ]
            + specs,
            out_specs=[
                pl.BlockSpec((JSTEP, 256), lambda s, meta: (s, 0)),
                whole((8, 256)),
                whole((BLOCKS, 2 * UNIT, DI)),
            ],
            scratch_shapes=[
                pltpu.VMEM((ROWS, 256), jnp.float32),
                pltpu.VMEM((ROWS, DI), jnp.float32),
            ],
        ),
        out_shape=[
            jax.ShapeDtypeStruct((NI, 256), jnp.float32),
            jax.ShapeDtypeStruct((8, 256), jnp.float32),
            jax.ShapeDtypeStruct((BLOCKS, 2 * UNIT, DI), jnp.float32),
        ],
        cost_estimate=pl.CostEstimate(
            flops=4 * NI * ROWS * 256 * DI, bytes_accessed=6 << 20, transcendentals=0
        ),
        compiler_params=pltpu.CompilerParams(vmem_limit_bytes=40 << 20),
        name="index_backward",
    )(meta, keys, logits, stats, target, ia, ib, wa, wb, wa, wb)


def merge(m0, l0, m1, l1):
    top = jnp.maximum(m0, m1)
    return top, l0 * jnp.exp2((m0 - top) * SCORE2) + l1 * jnp.exp2((m1 - top) * SCORE2)


def swap_halves(value):
    return jnp.concatenate([value[..., 128:], value[..., :128]], axis=-1)


def gather_head(value):
    wide = jnp.broadcast_to(value[None], (8,) + value.shape)
    return lax.all_to_all(wide, ("yhi", "xh", "xp"), 0, 0, tiled=True)


def body(main_queries, latent_keys, index_queries, index_weights, index_keys, tile_order, offset):
    z, ylo, core = lax.axis_index("z"), lax.axis_index("ylo"), lax.axis_index("core")
    half = lax.axis_index("xp")
    quarter = lax.axis_index("yhi") * 2 + lax.axis_index("xh")

    rows = jnp.arange(128, dtype=jnp.int32)
    place = offset[0] + jnp.repeat(tile_order, TILE, total_repeat_length=128) * TILE + rows % TILE
    wa = jnp.concatenate(
        [index_weights.T, place.astype(jnp.float32)[None], jnp.zeros((7, 128), jnp.float32)], axis=0
    )
    own = jnp.concatenate([index_keys, latent_keys], axis=1)
    own = lax.dynamic_slice_in_dim(own, half * HALF, HALF, 0)

    queries = main_queries.transpose(0, 2, 1)
    column = [(0, own)]
    forward = back = own
    for s in range(1, 5):
        forward = shift(forward, dz=1)
        column.append((-s, forward))
        if s < 4:
            back = shift(back, dz=7)
            column.append((s, back))
    other = [(dz, shift(block, dy=1 if dz <= 0 else 3)) for dz, block in column]
    blocks = [block for _, block in column + other]
    spots = [(dz, 0) for dz, _ in column] + [(dz, 1) for dz, _ in other]

    near = jnp.concatenate([shift(queries[:4], dx=1), shift(queries[4:], dx=3)], axis=0)
    wb = swap_core(wa)
    queries_b = swap_core(queries)
    near_b = swap_core(near)
    ia = index_queries.transpose(1, 0, 2)
    ib = swap_core(ia)

    zs = jnp.stack([(z + dz) % 8 for dz, _ in spots])
    ys = jnp.stack([ylo ^ dy for _, dy in spots])
    bases = (zs * 4 + ys * 2 + core) * 160 + half * HALF
    meta = jnp.concatenate(
        [bases, zs * 2 + ys, jnp.stack([core, half, quarter])]
    ).astype(jnp.int32)

    e0, m0, l0 = score_call(meta, blocks, queries, queries_b, wa, wb)
    e1, m1, l1 = score_call(meta, blocks, near, near_b, wa, wb)
    keys, logits, stats = forward_call(meta, blocks, ia, ib, wa, wb)

    m = jnp.concatenate([m0, m1], axis=0)[:, 0]
    l = jnp.concatenate([l0, l1], axis=0)[:, 0]
    away = swap_core(swap_halves(jnp.stack([m, l])))
    m2, l2 = merge(m, l, away[0], away[1])
    part = lambda a, b: jnp.stack(
        [jnp.concatenate([v[4 * a : 4 * a + 4], v[4 * b : 4 * b + 4]]) for v in (m2, l2)]
    )
    left = shift(part(0, 3), dx=1)
    right = shift(part(1, 2), dx=3)
    peer = jnp.concatenate([right[:, 4:], left[:, 4:], left[:, :4], right[:, :4]], axis=1)
    top, total = merge(m2, l2, peer[0], peer[1])
    ratio = (jnp.exp2((m - top) * SCORE2) / total)[:, None, :]
    sums = head_sum_call(meta, e0, e1, ratio[:8], ratio[8:])
    target = lax.all_to_all(sums, ("yhi", "xh"), 0, 0, tiled=True)

    far = swap_core(swap_halves(stats))
    itop = jnp.maximum(stats[0], far[0])
    isum = stats[1] * jnp.exp(stats[0] - itop) + far[1] * jnp.exp(far[0] - itop)
    istats = jnp.concatenate([itop[None], isum[None], jnp.zeros((6, 256), jnp.float32)], axis=0)
    istats = gather_head(istats)

    wg, div, kg = backward_call(meta, keys, logits, istats, target, ia, ib, wa, wb)
    rows_out = jnp.concatenate([wg, div], axis=0)
    rows_out = rows_out[:, :128] + swap_core(rows_out[:, 128:])
    kg = jnp.sum(lax.all_to_all(kg, ("z", "ylo"), 0, 0, tiled=True), axis=0)
    last = gather_head(jnp.concatenate([kg, rows_out], axis=0))
    rows_sum = jnp.sum(last[:, 2 * UNIT :], axis=0)
    pieces = last[:, : 2 * UNIT].reshape(4, 2, 2 * UNIT, DI)
    main = pieces[:, :, :UNIT].transpose(1, 0, 2, 3).reshape(2, 4 * UNIT, DI)
    extra = jnp.sum(pieces[:, :, UNIT:], axis=0)
    key_grad = jnp.concatenate([main, extra], axis=1).reshape(160, DI)
    return rows_sum[NI], rows_sum[:NI].T, key_grad


def solution(mesh):
    fine = Mesh(np.asarray(mesh.devices).reshape(2, 2, 2, 8, 2, 2), ALL)
    head, ctx = ("yhi", "xh", "xp"), ("z", "ylo", "core")
    in_specs = (
        P(head, ctx, None),
        P(ctx, None),
        P(ctx, None, None),
        P(ctx, None),
        P(ctx, None),
        P(ctx),
        P(),
    )
    out_specs = (P(ctx), P(ctx, None), P(ctx, None))
    return jax.shard_map(body, mesh=fine, in_specs=in_specs, out_specs=out_specs, check_vma=False)
```

time: 522 us -> 172 us (0.33)
  waiting for transfers between devices: 302 us -> 37 us
  matrix products: 84.9 us -> 0 us
  other arithmetic: 45.4 us -> 3.62 us
  starting transfers between devices: 0.2 us -> 38.8 us
  Pallas kernels: 0 us -> 38.4 us
  blocking collectives: 54.2 us -> 31.1 us
  between operations: 15.2 us -> 1.87 us
    reduce_scatter x1 -> x0, waiting for transfers between devices: 121 us -> none  [body(): lax.psum_scatter(key_terms, 'ctx', scatter_dimension=0, tiled=True)]
    psum x2 -> x0, waiting for transfers between devices: 111 us -> none  [the longest x1 84.2 us: body(): everything = lax.psum(partial_sum, 'head')]
    dot_general x38 -> x0, matrix products: 84.9 us -> none  [the longest x8 42.8 us: head_step(): lax.dot_general(queries, keys_all, (((1,), (1,)), ((), ())), preferred_el...]
    all_gather x2 -> x0, waiting for transfers between devices: 68.3 us -> none  [the longest x1 68.3 us: body(): lax.all_gather(latent_keys, 'ctx', axis=0, tiled=True)]
    add x10 -> x3, other arithmetic: 39.3 us -> 0.03 us  [the longest x1 0.01 us: body(): isum = stats[1] * jnp.exp(stats[0] - itop) + far[1] * jnp.exp(far[0] - itop)]
    pallas_call x0 -> x5, Pallas kernels: none -> 38.4 us  [the longest x2 20.3 us: score_call(): pl.pallas_call(lambda *refs: score_kernel(n, *refs), grid_spec=pltpu.Pref...]
    all_gather x1 -> x0, blocking collectives: 33.8 us -> none  [body(): lax.all_gather(weight_grad, 'head', axis=0, tiled=True)]
    all_to_all x0 -> x2, blocking collectives: none -> 31.1 us  [the longest x1 18.4 us: body(): target = lax.all_to_all(sums, ('yhi', 'xh'), 0, 0, tiled=True)]
  transfers between devices with their start and end apart: 5 -> 28, of which waited for: 4 -> 14; matrix products, arithmetic and copies ran while one was open for 20% -> 4% of each run, Pallas kernels for 0% -> 8%
where the time goes in v1:
time: 172 us; the launch traced here: 171 us
  starting transfers between devices  38.8 us (23%)
  Pallas kernels  38.4 us (22%)
  waiting for transfers between devices  37 us (22%)
  blocking collectives  31.1 us (18%)
  local copies, waits for them, and re-layouts  20.4 us (12%)
  other arithmetic  3.62 us (2%)
  between operations  1.87 us (1%)
    ppermute x26, starting transfers between devices, shift(): return lax.ppermute(value, ALL, pairs)  27.8 us
    ppermute x26, waiting for transfers between devices, shift(): return lax.ppermute(value, ALL, pairs)  27.6 us
    pallas_call x2, Pallas kernels, score_call(): pl.pallas_call(lambda *refs: score_kernel(n, *refs), grid_spec=pltpu.Pref...  20.3 us
    all_to_all x1, blocking collectives, body(): target = lax.all_to_all(sums, ('yhi', 'xh'), 0, 0, tiled=True)  18.4 us
    unnamed x62, local copies, waits for them, and re-layouts  14.3 us
    all_to_all x1, blocking collectives, gather_head(): return lax.all_to_all(wide, ('yhi', 'xh', 'xp'), 0, 0, tiled=True)  12.7 us
    pallas_call x1, Pallas kernels, backward_call(): pl.pallas_call(backward_kernel, grid_spec=pltpu.PrefetchScalarGridSpec(nu...  9.41 us
    all_to_all x1, waiting for transfers between devices, body(): kg = jnp.sum(lax.all_to_all(kg, ('z', 'ylo'), 0, 0, tiled=True), axis=0)  9.41 us
  transfers between devices with their start and end apart: 28, of which 14 were waited for; matrix products, arithmetic and copies ran while one was open for 4% of the time, Pallas kernels for 8%

profile of v1, /device:TPU:2, one launch (start us, length us, event | category | flops | bytes accessed | tf_op | source)
XLA Modules:
  0.0 171.2 jit_solution(15622985188778611118)
XLA Ops:
  6.5 4.0 %collective-permute-start.1 = (bf16[80,704]{1,0:T(8,128)(2,1)S(1)}, bf16[80,704]{1,0:T(8,128)(2,1)S(1)}, u32[]{:S(2)}, u32[]{:S(2)}) collective-permute-start(bf16[80,704]{1,0:T(8,128)(2,1)S(1)} %fusion.refs_0_.refs_1_), channel_id=1, source_target_pairs={{0,28},{1,29},{4,0},{5,1},{8,4},{9,5},{12,8},{13,9},{16,12},{17,13... | collective-permute-start | bytes 337928 | tf_op jit(solution)/shard_map/ppermute | solution.py:38
  12.4 2.6 %fusion.18 = f32[1,128]{1,0:T(1,128)S(1)} fusion(pred[128]{0:T(512)(128)(4,1)S(1)} %copy-done.26, pred[128]{0:T(512)(128)(4,1)S(1)} %copy-done.27, pred[128]{0:T(512)(128)(4,1)S(1)} %copy-done.28, s32[]{:T(128)} %bitcast.19, s32[]{:T(128)} %bitcast.16, s32[]{:T(128)} %bitcast.17, s32[]{:T(128)} %bitcast.18, s32[]{:T(128)} %bitcast.100), kind=kLoop, calls=%fused_computation.64 | loop fusion | flops 1664 | bytes 916 | tf_op jit(solution)/shard_map/convert_element_type | solution.py:339
  15.2 3.1 %collective-permute-done.19 = bf16[4,576,128]{2,1,0:T(8,128)(2,1)S(1)} collective-permute-done((bf16[4,576,128]{2,1,0:T(8,128)(2,1)}, bf16[4,576,128]{2,1,0:T(8,128)(2,1)S(1)}, u32[]{:S(2)}, u32[]{:S(2)}) %collective-permute-start.19) | collective-permute-done | bytes 589856 | tf_op jit(solution)/shard_map/ppermute | solution.py:38
  20.7 5.6 %collective-permute-done.20 = bf16[4,576,128]{2,1,0:T(8,128)(2,1)S(1)} collective-permute-done((bf16[4,576,128]{2,1,0:T(8,128)(2,1)S(1)}, bf16[4,576,128]{2,1,0:T(8,128)(2,1)S(1)}, u32[]{:S(2)}, u32[]{:S(2)}) %collective-permute-start.20) | collective-permute-done | bytes 589856 | tf_op jit(solution)/shard_map/ppermute | solution.py:38
  27.7 3.2 %collective-permute-start.3 = (bf16[80,704]{1,0:T(8,128)(2,1)S(1)}, bf16[80,704]{1,0:T(8,128)(2,1)S(1)}, u32[]{:S(2)}, u32[]{:S(2)}) collective-permute-start(bf16[80,704]{1,0:T(8,128)(2,1)S(1)} %collective-permute-done.1.refs_2_.refs_3_), channel_id=1, source_target_pairs={{0,28},{1,29},{4,0},{5,1},{8,4},{9,5},{12,8},{13,9},{16,12},{17,13... | collective-permute-start | bytes 337928 | tf_op jit(solution)/shard_map/ppermute | solution.py:38
  34.4 3.0 %collective-permute-start.9 = (bf16[80,704]{1,0:T(8,128)(2,1)S(1)}, bf16[80,704]{1,0:T(8,128)(2,1)S(1)}, u32[]{:S(2)}, u32[]{:S(2)}) collective-permute-start(bf16[80,704]{1,0:T(8,128)(2,1)S(1)} %collective-permute-done.1.refs_2_.refs_3_), channel_id=1, source_target_pairs={{0,130},{1,131},{4,134},{5,135},{8,138},{9,139},{12,142},{13,143},... | collective-permute-start | bytes 337928 | tf_op jit(solution)/shard_map/ppermute | solution.py:38
  37.5 3.2 %collective-permute-start.5 = (bf16[80,704]{1,0:T(8,128)(2,1)S(1)}, bf16[80,704]{1,0:T(8,128)(2,1)S(1)}, u32[]{:S(2)}, u32[]{:S(2)}) collective-permute-start(bf16[80,704]{1,0:T(8,128)(2,1)S(1)} %collective-permute-done.3.refs_4_.refs_5_), channel_id=1, source_target_pairs={{0,28},{1,29},{4,0},{5,1},{8,4},{9,5},{12,8},{13,9},{16,12},{17,13... | collective-permute-start | bytes 337928 | tf_op jit(solution)/shard_map/ppermute | solution.py:38
  40.9 2.7 %collective-permute-done.4.refs_5_.refs_6_ = bf16[80,704]{1,0:T(8,128)(2,1)S(1)} collective-permute-done((bf16[80,704]{1,0:T(8,128)(2,1)S(1)}, bf16[80,704]{1,0:T(8,128)(2,1)S(1)}, u32[]{:S(2)}, u32[]{:S(2)}) %collective-permute-start.4) | collective-permute-done | bytes 112672 | tf_op jit(solution)/shard_map/ppermute | solution.py:38
  44.5 2.3 %collective-permute-done.10.refs_11_.refs_12_ = bf16[80,704]{1,0:T(8,128)(2,1)S(1)} collective-permute-done((bf16[80,704]{1,0:T(8,128)(2,1)S(1)}, bf16[80,704]{1,0:T(8,128)(2,1)S(1)}, u32[]{:S(2)}, u32[]{:S(2)}) %collective-permute-start.10) | collective-permute-done | bytes 112672 | tf_op jit(solution)/shard_map/ppermute | solution.py:38
  53.8 2.7 %collective-permute-done.14.refs_15_.refs_16_ = bf16[80,704]{1,0:T(8,128)(2,1)S(1)} collective-permute-done((bf16[80,704]{1,0:T(8,128)(2,1)S(1)}, bf16[80,704]{1,0:T(8,128)(2,1)S(1)}, u32[]{:S(2)}, u32[]{:S(2)}) %collective-permute-start.14) | collective-permute-done | bytes 112672 | tf_op jit(solution)/shard_map/ppermute | solution.py:38
  56.5 10.1 %scores.2 = (bf16[8,1280,256]{2,1,0:T(8,128)(2,1)S(1)}, f32[8,1,256]{2,1,0:T(1,128)S(1)}, f32[8,1,256]{2,1,0:T(1,128)S(1)}) custom-call(s32[35]{0:T(128)S(1)} %concatenate.55.meta.refs_0_, bf16[80,704]{1,0:T(8,128)(2,1)S(1)} %fusion.refs_0_.refs_1_, bf16[80,704]{1,0:T(8,128)(2,1)S(1)} %collective-permute-done.refs_1_.refs_2_, ...), custom_call_target="tpu_custom_call" | custom-call | flops 3019898880 | bytes 5242880 | tf_op jit(solution)/shard_map/scores/pallas_call | solution.py:74
  66.5 2.3 %copy-done = bf16[8,1280,256]{2,1,0:T(8,128)(2,1)} copy-done((bf16[8,1280,256]{2,1,0:T(8,128)(2,1)}, bf16[8,1280,256]{2,1,0:T(8,128)(2,1)S(1)}, u32[]{:S(2)}) %copy-start) | copy-done | bytes 5242904
  68.9 10.2 %scores.3 = (bf16[8,1280,256]{2,1,0:T(8,128)(2,1)S(1)}, f32[8,1,256]{2,1,0:T(1,128)S(1)}, f32[8,1,256]{2,1,0:T(1,128)S(1)}) custom-call(s32[35]{0:T(128)S(1)} %concatenate.55.meta.refs_0_, bf16[80,704]{1,0:T(8,128)(2,1)S(1)} %fusion.refs_0_.refs_1_, bf16[80,704]{1,0:T(8,128)(2,1)S(1)} %collective-permute-done.refs_1_.refs_2_, ...), custom_call_target="tpu_custom_call" | custom-call | flops 3019898880 | bytes 5242880 | tf_op jit(solution)/shard_map/scores/pallas_call | solution.py:74
  79.2 2.4 %copy-done.2 = bf16[8,1280,256]{2,1,0:T(8,128)(2,1)} copy-done((bf16[8,1280,256]{2,1,0:T(8,128)(2,1)}, bf16[8,1280,256]{2,1,0:T(8,128)(2,1)S(1)}, u32[]{:S(2)}) %copy-start.2) | copy-done | bytes 5242904
  89.1 5.1 %index_forward.1 = (bf16[320,128]{1,0:T(8,128)(2,1)S(1)}, f32[320,256]{1,0:T(8,128)S(1)}, f32[8,256]{1,0:T(8,128)S(1)}) custom-call(s32[35]{0:T(128)S(1)} %concatenate.55.meta.refs_0_, bf16[80,704]{1,0:T(8,128)(2,1)S(1)} %fusion.refs_0_.refs_1_, bf16[80,704]{1,0:T(8,128)(2,1)S(1)} %collective-permute-done.refs_1_.refs_2_, ...), custom_call_target="tpu_custom_call" | custom-call | flops 1342177280 | bytes 5242880 | tf_op jit(solution)/shard_map/index_forward/pallas_call | solution.py:212
  96.8 5.1 %all-to-all-start = ((f32[8,8,256]{2,1,0:T(8,128)}), f32[8,8,256]{2,1,0:T(8,128)S(1)}, u32[]{:S(2)}, u32[]{:S(2)}) async-start(f32[8,8,256]{2,1,0:T(8,128)} %broadcast_in_dim.17), calls=%async_computation | async-start | bytes 131072 | tf_op jit(solution)/shard_map/all_to_all | solution.py:328
  101.9 2.5 %copy-done.1 = bf16[8,1280,256]{2,1,0:T(8,128)(2,1)S(1)} copy-done((bf16[8,1280,256]{2,1,0:T(8,128)(2,1)S(1)}, bf16[8,1280,256]{2,1,0:T(8,128)(2,1)}, u32[]{:S(2)}) %copy-start.1) | copy-done | bytes 5242904
  104.4 2.5 %copy-done.3 = bf16[8,1280,256]{2,1,0:T(8,128)(2,1)S(1)} copy-done((bf16[8,1280,256]{2,1,0:T(8,128)(2,1)S(1)}, bf16[8,1280,256]{2,1,0:T(8,128)(2,1)}, u32[]{:S(2)}) %copy-start.3) | copy-done | bytes 5242904
  106.9 3.7 %head_sum.1 = bf16[4,320,256]{2,1,0:T(8,128)(2,1)S(1)} custom-call(s32[35]{0:T(128)S(1)} %concatenate.55.meta.refs_0_, bf16[8,1280,256]{2,1,0:T(8,128)(2,1)S(1)} %copy-done.1, bf16[8,1280,256]{2,1,0:T(8,128)(2,1)S(1)} %copy-done.3, f32[8,1,256]{2,1,0:T(1,128)S(1)} %copy.27.r0, f32[8,1,256]{2,1,0:T(1,128)S(1)} %slice.148.r1), custom_call_target="tpu_custom_call" | custom-call | bytes 11534336 | tf_op jit(solution)/shard_map/head_sum/pallas_call | solution.py:121
  110.6 18.4 %all_to_all.20.target = bf16[4,320,256]{2,1,0:T(8,128)(2,1)S(1)} all-to-all(bf16[4,320,256]{2,1,0:T(8,128)(2,1)S(1)} %head_sum.1), channel_id=1, replica_groups=mesh['yhi'=2,'xh'=2,'xp'=2,'z'=8,'ylo'=2,'core'=2] {'yhi','xh'}, dimensions={0} | all-to-all | bytes 1310720 | tf_op jit(solution)/shard_map/all_to_all | solution.py:388
  130.5 9.4 %index_backward.1 = (f32[64,256]{1,0:T(8,128)S(1)}, f32[8,256]{1,0:T(8,128)S(1)}, f32[16,32,128]{2,1,0:T(8,128)}) custom-call(s32[35]{0:T(128)S(1)} %concatenate.55.meta.refs_0_, bf16[320,128]{1,0:T(8,128)(2,1)S(1)} %get-tuple-element.27.keys, f32[320,256]{1,0:T(8,128)S(1)} %copy-done.20, f32[8,8,256]{2,1,0:T(8,128)S(1)} %all-to-all-done.stats, ...), custom_call_target="tpu_custom_call" | custom-call | flops 2684354560 | bytes 6291456 | tf_op jit(solution)/shard_map/index_backward/pallas_call | solution.py:282
  140.0 5.9 %all-to-all-start.2 = ((f32[16,32,128]{2,1,0:T(8,128)}), f32[16,32,128]{2,1,0:T(8,128)S(1)}, u32[]{:S(2)}, u32[]{:S(2)}) async-start(f32[16,32,128]{2,1,0:T(8,128)} %get-tuple-element.36), calls=%async_computation.2 | async-start | bytes 524288 | tf_op jit(solution)/shard_map/all_to_all | solution.py:399
  147.2 9.4 %all-to-all-done.2 = f32[16,32,128]{2,1,0:T(8,128)S(1)} async-done(((f32[16,32,128]{2,1,0:T(8,128)}), f32[16,32,128]{2,1,0:T(8,128)S(1)}, u32[]{:S(2)}, u32[]{:S(2)}) %all-to-all-start.2) | async-done | bytes 262176 | tf_op jit(solution)/shard_map/all_to_all | solution.py:399
  156.7 12.7 %all_to_all.21 = f32[8,104,128]{2,1,0:T(8,128)S(1)} all-to-all(f32[8,104,128]{2,1,0:T(8,128)S(1)} %broadcast_in_dim.18), channel_id=1, replica_groups=mesh['yhi'=2,'xh'=2,'xp'=2,'z'=8,'ylo'=2,'core'=2] {'yhi','xh','xp'}, dimensions={0} | all-to-all | bytes 851968 | tf_op jit(solution)/shard_map/all_to_all | solution.py:328
  (153 shorter events, 37.4 us)
Async XLA Ops:
  3.0 15.3 %collective-permute-start.19 = (bf16[4,576,128]{2,1,0:T(8,128)(2,1)}, bf16[4,576,128]{2,1,0:T(8,128)(2,1)S(1)}, u32[]{:S(2)}, u32[]{:S(2)}) collective-permute-start(bf16[4,576,128]{2,1,0:T(8,128)(2,1)} %get-tuple-element.42), channel_id=1, source_target_pairs={{0,32},{1,33},{4,36},{5,37},{8,40},{9,41},{12,44},{13,45},{16,48},... | collective-permute-start | bytes 1769480 | tf_op jit(solution)/shard_map/ppermute | solution.py:38
  4.5 23.2 %collective-permute-start = (bf16[80,704]{1,0:T(8,128)(2,1)S(1)}, bf16[80,704]{1,0:T(8,128)(2,1)S(1)}, u32[]{:S(2)}, u32[]{:S(2)}) collective-permute-start(bf16[80,704]{1,0:T(8,128)(2,1)S(1)} %fusion.refs_0_.refs_1_), channel_id=1, source_target_pairs={{0,4},{1,5},{4,8},{5,9},{8,12},{9,13},{12,16},{13,17},{16,20},{17,... | collective-permute-start | bytes 337928 | tf_op jit(solution)/shard_map/ppermute | solution.py:38
  6.5 21.2 %collective-permute-start.1 = (bf16[80,704]{1,0:T(8,128)(2,1)S(1)}, bf16[80,704]{1,0:T(8,128)(2,1)S(1)}, u32[]{:S(2)}, u32[]{:S(2)}) collective-permute-start(bf16[80,704]{1,0:T(8,128)(2,1)S(1)} %fusion.refs_0_.refs_1_), channel_id=1, source_target_pairs={{0,28},{1,29},{4,0},{5,1},{8,4},{9,5},{12,8},{13,9},{16,12},{17,13... | collective-permute-start | bytes 337928 | tf_op jit(solution)/shard_map/ppermute | solution.py:38
  10.5 46.0 %collective-permute-start.18 = (bf16[8,576,128]{2,1,0:T(8,128)(2,1)S(1)}, bf16[8,576,128]{2,1,0:T(8,128)(2,1)}, u32[]{:S(2)}, u32[]{:S(2)}) collective-permute-start(bf16[8,576,128]{2,1,0:T(8,128)(2,1)S(1)} %bitcast.105), channel_id=1, source_target_pairs={{0,1},{1,0},{4,5},{5,4},{8,9},{9,8},{12,13},{13,12},{16,17},{17,16... | collective-permute-start | bytes 3538952 | tf_op jit(solution)/shard_map/ppermute | solution.py:38
  10.5 15.7 %collective-permute-start.20 = (bf16[4,576,128]{2,1,0:T(8,128)(2,1)S(1)}, bf16[4,576,128]{2,1,0:T(8,128)(2,1)S(1)}, u32[]{:S(2)}, u32[]{:S(2)}) collective-permute-start(bf16[4,576,128]{2,1,0:T(8,128)(2,1)S(1)} %get-tuple-element.41), channel_id=1, source_target_pairs={{0,96},{1,97},{4,100},{5,101},{8,104},{9,105},{12,108},{13,109},{1... | collective-permute-start | bytes 1769480 | tf_op jit(solution)/shard_map/ppermute | solution.py:38
  18.2 12.7 %collective-permute-start.7 = (bf16[80,704]{1,0:T(8,128)(2,1)S(1)}, bf16[80,704]{1,0:T(8,128)(2,1)S(1)}, u32[]{:S(2)}, u32[]{:S(2)}) collective-permute-start(bf16[80,704]{1,0:T(8,128)(2,1)S(1)} %fusion.refs_0_.refs_1_), channel_id=1, source_target_pairs={{0,2},{1,3},{4,6},{5,7},{8,10},{9,11},{12,14},{13,15},{16,18},{17,... | collective-permute-start | bytes 337928 | tf_op jit(solution)/shard_map/ppermute | solution.py:38
  27.5 41.4 %collective-permute-start.21 = (bf16[8,576,128]{2,1,0:T(8,128)(2,1)}, bf16[8,576,128]{2,1,0:T(8,128)(2,1)}, u32[]{:S(2)}, u32[]{:S(2)}) collective-permute-start(bf16[8,576,128]{2,1,0:T(8,128)(2,1)} %constant_dynamic-update-slice_fusion.refs_17_), channel_id=1, source_target_pairs={{0,1},{1,0},{4,5},{5,4},{8,9},{9,8},{12,13},{13,12},{16,17},{17,16... | collective-permute-start | bytes 3538952 | tf_op jit(solution)/shard_map/ppermute | solution.py:38
  27.7 6.7 %collective-permute-start.2 = (bf16[80,704]{1,0:T(8,128)(2,1)S(1)}, bf16[80,704]{1,0:T(8,128)(2,1)S(1)}, u32[]{:S(2)}, u32[]{:S(2)}) collective-permute-start(bf16[80,704]{1,0:T(8,128)(2,1)S(1)} %collective-permute-done.refs_1_.refs_2_), channel_id=1, source_target_pairs={{0,4},{1,5},{4,8},{5,9},{8,12},{9,13},{12,16},{13,17},{16,20},{17,... | collective-permute-start | bytes 337928 | tf_op jit(solution)/shard_map/ppermute | solution.py:38
  27.7 9.8 %collective-permute-start.3 = (bf16[80,704]{1,0:T(8,128)(2,1)S(1)}, bf16[80,704]{1,0:T(8,128)(2,1)S(1)}, u32[]{:S(2)}, u32[]{:S(2)}) collective-permute-start(bf16[80,704]{1,0:T(8,128)(2,1)S(1)} %collective-permute-done.1.refs_2_.refs_3_), channel_id=1, source_target_pairs={{0,28},{1,29},{4,0},{5,1},{8,4},{9,5},{12,8},{13,9},{16,12},{17,13... | collective-permute-start | bytes 337928 | tf_op jit(solution)/shard_map/ppermute | solution.py:38
  30.9 6.5 %collective-permute-start.8 = (bf16[80,704]{1,0:T(8,128)(2,1)S(1)}, bf16[80,704]{1,0:T(8,128)(2,1)S(1)}, u32[]{:S(2)}, u32[]{:S(2)}) collective-permute-start(bf16[80,704]{1,0:T(8,128)(2,1)S(1)} %collective-permute-done.refs_1_.refs_2_), channel_id=1, source_target_pairs={{0,2},{1,3},{4,6},{5,7},{8,10},{9,11},{12,14},{13,15},{16,18},{17,... | collective-permute-start | bytes 337928 | tf_op jit(solution)/shard_map/ppermute | solution.py:38
  34.4 6.3 %collective-permute-start.9 = (bf16[80,704]{1,0:T(8,128)(2,1)S(1)}, bf16[80,704]{1,0:T(8,128)(2,1)S(1)}, u32[]{:S(2)}, u32[]{:S(2)}) collective-permute-start(bf16[80,704]{1,0:T(8,128)(2,1)S(1)} %collective-permute-done.1.refs_2_.refs_3_), channel_id=1, source_target_pairs={{0,130},{1,131},{4,134},{5,135},{8,138},{9,139},{12,142},{13,143},... | collective-permute-start | bytes 337928 | tf_op jit(solution)/shard_map/ppermute | solution.py:38
  37.4 6.1 %collective-permute-start.4 = (bf16[80,704]{1,0:T(8,128)(2,1)S(1)}, bf16[80,704]{1,0:T(8,128)(2,1)S(1)}, u32[]{:S(2)}, u32[]{:S(2)}) collective-permute-start(bf16[80,704]{1,0:T(8,128)(2,1)S(1)} %collective-permute-done.2.refs_3_.refs_4_), channel_id=1, source_target_pairs={{0,4},{1,5},{4,8},{5,9},{8,12},{9,13},{12,16},{13,17},{16,20},{17,... | collective-permute-start | bytes 337928 | tf_op jit(solution)/shard_map/ppermute | solution.py:38
  37.5 6.8 %collective-permute-start.5 = (bf16[80,704]{1,0:T(8,128)(2,1)S(1)}, bf16[80,704]{1,0:T(8,128)(2,1)S(1)}, u32[]{:S(2)}, u32[]{:S(2)}) collective-permute-start(bf16[80,704]{1,0:T(8,128)(2,1)S(1)} %collective-permute-done.3.refs_4_.refs_5_), channel_id=1, source_target_pairs={{0,28},{1,29},{4,0},{5,1},{8,4},{9,5},{12,8},{13,9},{16,12},{17,13... | collective-permute-start | bytes 337928 | tf_op jit(solution)/shard_map/ppermute | solution.py:38
  40.7 6.1 %collective-permute-start.10 = (bf16[80,704]{1,0:T(8,128)(2,1)S(1)}, bf16[80,704]{1,0:T(8,128)(2,1)S(1)}, u32[]{:S(2)}, u32[]{:S(2)}) collective-permute-start(bf16[80,704]{1,0:T(8,128)(2,1)S(1)} %collective-permute-done.2.refs_3_.refs_4_), channel_id=1, source_target_pairs={{0,2},{1,3},{4,6},{5,7},{8,10},{9,11},{12,14},{13,15},{16,18},{17,... | collective-permute-start | bytes 337928 | tf_op jit(solution)/shard_map/ppermute | solution.py:38
  43.5 5.0 %collective-permute-start.11 = (bf16[80,704]{1,0:T(8,128)(2,1)S(1)}, bf16[80,704]{1,0:T(8,128)(2,1)S(1)}, u32[]{:S(2)}, u32[]{:S(2)}) collective-permute-start(bf16[80,704]{1,0:T(8,128)(2,1)S(1)} %collective-permute-done.3.refs_4_.refs_5_), channel_id=1, source_target_pairs={{0,130},{1,131},{4,134},{5,135},{8,138},{9,139},{12,142},{13,143},... | collective-permute-start | bytes 337928 | tf_op jit(solution)/shard_map/ppermute | solution.py:38
  44.3 6.1 %collective-permute-start.6 = (bf16[80,704]{1,0:T(8,128)(2,1)S(1)}, bf16[80,704]{1,0:T(8,128)(2,1)S(1)}, u32[]{:S(2)}, u32[]{:S(2)}) collective-permute-start(bf16[80,704]{1,0:T(8,128)(2,1)S(1)} %collective-permute-done.4.refs_5_.refs_6_), channel_id=1, source_target_pairs={{0,4},{1,5},{4,8},{5,9},{8,12},{9,13},{12,16},{13,17},{16,20},{17,... | collective-permute-start | bytes 337928 | tf_op jit(solution)/shard_map/ppermute | solution.py:38
  46.8 7.0 %collective-permute-start.12 = (bf16[80,704]{1,0:T(8,128)(2,1)S(1)}, bf16[80,704]{1,0:T(8,128)(2,1)S(1)}, u32[]{:S(2)}, u32[]{:S(2)}) collective-permute-start(bf16[80,704]{1,0:T(8,128)(2,1)S(1)} %collective-permute-done.4.refs_5_.refs_6_), channel_id=1, source_target_pairs={{0,2},{1,3},{4,6},{5,7},{8,10},{9,11},{12,14},{13,15},{16,18},{17,... | collective-permute-start | bytes 337928 | tf_op jit(solution)/shard_map/ppermute | solution.py:38
  48.6 5.2 %collective-permute-start.13 = (bf16[80,704]{1,0:T(8,128)(2,1)S(1)}, bf16[80,704]{1,0:T(8,128)(2,1)S(1)}, u32[]{:S(2)}, u32[]{:S(2)}) collective-permute-start(bf16[80,704]{1,0:T(8,128)(2,1)S(1)} %collective-permute-done.5.refs_6_.refs_7_), channel_id=1, source_target_pairs={{0,130},{1,131},{4,134},{5,135},{8,138},{9,139},{12,142},{13,143},... | collective-permute-start | bytes 337928 | tf_op jit(solution)/shard_map/ppermute | solution.py:38
  50.4 6.1 %collective-permute-start.14 = (bf16[80,704]{1,0:T(8,128)(2,1)S(1)}, bf16[80,704]{1,0:T(8,128)(2,1)S(1)}, u32[]{:S(2)}, u32[]{:S(2)}) collective-permute-start(bf16[80,704]{1,0:T(8,128)(2,1)S(1)} %collective-permute-done.6.refs_7_.refs_8_), channel_id=1, source_target_pairs={{0,2},{1,3},{4,6},{5,7},{8,10},{9,11},{12,14},{13,15},{16,18},{17,... | collective-permute-start | bytes 337928 | tf_op jit(solution)/shard_map/ppermute | solution.py:38
  83.1 5.9 %collective-permute-start.15 = (bf16[64,128,128]{2,1,0:T(8,128)(2,1)S(1)}, bf16[64,128,128]{2,1,0:T(8,128)(2,1)S(1)}, u32[]{:S(2)}, u32[]{:S(2)}) collective-permute-start(bf16[64,128,128]{2,1,0:T(8,128)(2,1)S(1)} %bitcast.101), channel_id=1, source_target_pairs={{0,1},{1,0},{4,5},{5,4},{8,9},{9,8},{12,13},{13,12},{16,17},{17,16... | collective-permute-start | bytes 6291464 | tf_op jit(solution)/shard_map/ppermute | solution.py:38
  83.8 3.8 %collective-permute-start.24 = (f32[2,8,256]{2,1,0:T(8,128)S(1)}, f32[2,8,256]{2,1,0:T(8,128)S(1)}, u32[]{:S(2)}, u32[]{:S(2)}) collective-permute-start(f32[2,8,256]{2,1,0:T(8,128)S(1)} %pad_maximum_fusion.5), channel_id=1, source_target_pairs={{0,32},{1,33},{4,36},{5,37},{8,40},{9,41},{12,44},{13,45},{16,48},... | collective-permute-start | bytes 49160 | tf_op jit(solution)/shard_map/ppermute | solution.py:38
  85.1 3.8 %collective-permute-start.23 = (f32[2,8,256]{2,1,0:T(8,128)S(1)}, f32[2,8,256]{2,1,0:T(8,128)S(1)}, u32[]{:S(2)}, u32[]{:S(2)}) collective-permute-start(f32[2,8,256]{2,1,0:T(8,128)S(1)} %pad_maximum_fusion.4), channel_id=1, source_target_pairs={{0,96},{1,97},{4,100},{5,101},{8,104},{9,105},{12,108},{13,109},{1... | collective-permute-start | bytes 49160 | tf_op jit(solution)/shard_map/ppermute | solution.py:38
  96.8 13.7 %all-to-all-start = ((f32[8,8,256]{2,1,0:T(8,128)}), f32[8,8,256]{2,1,0:T(8,128)S(1)}, u32[]{:S(2)}, u32[]{:S(2)}) async-start(f32[8,8,256]{2,1,0:T(8,128)} %broadcast_in_dim.17), calls=%async_computation | async-start | bytes 131072 | tf_op jit(solution)/shard_map/all_to_all | solution.py:328
  140.0 16.6 %all-to-all-start.2 = ((f32[16,32,128]{2,1,0:T(8,128)}), f32[16,32,128]{2,1,0:T(8,128)S(1)}, u32[]{:S(2)}, u32[]{:S(2)}) async-start(f32[16,32,128]{2,1,0:T(8,128)} %get-tuple-element.36), calls=%async_computation.2 | async-start | bytes 524288 | tf_op jit(solution)/shard_map/all_to_all | solution.py:399
  (33 other events, 279.7 us)

commit v2 on v1

v2 whole, which is shorter than its diff:
```python
import math

import jax
import jax.numpy as jnp
import numpy as np
from jax import lax
from jax.experimental import pallas as pl
from jax.experimental.pallas import tpu as pltpu
from jax.sharding import Mesh
from jax.sharding import PartitionSpec as P

TILE = 32
DQ = 576
DI = 128
NI = 64
HALF = 80
UNIT = 16
BLOCKS = 16
ROWS = 320
SCORE2 = 192.0 ** (-0.5) * math.log2(math.e)
INDEX_SCALE = DI ** (-0.5)
ALL = ("yhi", "xh", "xp", "z", "ylo", "core")
NEG = -jnp.inf
VMEM = 18 << 20


def flat(x, y, z, c):
    return ((y // 2) * 4 + x) * 32 + (z * 2 + (y % 2)) * 2 + c


def shift(value, dx=0, dy=0, dz=0, flip=0):
    pairs = [
        (flat(x, y, z, c), flat((x + dx) % 4, (y + dy) % 4, (z + dz) % 8, c ^ flip))
        for x in range(4)
        for y in range(4)
        for z in range(8)
        for c in range(2)
    ]
    return lax.ppermute(value, ALL, pairs)


def swap_core(value):
    return shift(value, flip=1)


def score_kernel(spans, first, meta, *refs):
    n = len(spans)
    blocks, (qa, qb, na, nb, wa, wb) = refs[:n], refs[n : n + 6]
    e_ref, m_ref, l_ref, keys, bias, raw, tops = refs[n + 6 :]
    step = pl.program_id(0)
    rows = keys.shape[0]
    cut = 320

    @pl.when(step == 0)
    def _():
        at = 0
        for block, span in zip(blocks, spans):
            keys[at : at + span, :] = block[:, DI : DI + DQ]
            at += span
        place = jnp.concatenate([wa[NI : NI + 1, :], wb[NI : NI + 1, :]], axis=1)
        offsets = lax.broadcasted_iota(jnp.int32, (HALF, 256), 0).astype(jnp.float32)
        for i in range(rows // HALF):
            base = meta[first + i].astype(jnp.float32)
            bias[i * HALF : (i + 1) * HALF, :] = jnp.where(offsets + base <= place, 0.0, NEG)
        tops[...] = jnp.zeros_like(tops)

    def work(now, last):
        own = jnp.concatenate([qa[0], qb[0]], axis=1)
        near = jnp.concatenate([na[0], nb[0]], axis=1)
        queries = jnp.where(step < 4, own, near)
        top = jnp.max(tops[last], axis=0, keepdims=True)
        safe = jnp.where(top == NEG, 0.0, top)
        new = jnp.full((8, 256), NEG, jnp.float32)
        total = jnp.zeros((8, 256), jnp.float32)
        for t in range(0, rows, cut):
            piece = slice(t, t + cut)
            scores = jnp.dot(keys[piece, :], queries, preferred_element_type=jnp.float32)
            scores = scores + bias[piece, :]
            raw[now, piece, :] = scores
            new = jnp.maximum(new, jnp.max(scores.reshape(cut // 8, 8, 256), axis=0))
            exps = jnp.exp2((raw[last, piece, :] - safe) * SCORE2)
            e_ref[0, piece, :] = exps.astype(jnp.bfloat16)
            total = total + jnp.sum(exps.reshape(cut // 8, 8, 256), axis=0)
        tops[now] = new
        m_ref[0] = top
        l_ref[0] = jnp.sum(total, axis=0, keepdims=True)

    @pl.when(step % 2 == 0)
    def _():
        work(0, 1)

    @pl.when(step % 2 == 1)
    def _():
        work(1, 0)


def score_call(meta, first, blocks, group, qa, qb, na, nb, wa, wb):
    spans = [block.shape[0] for block in blocks]
    rows = sum(spans)
    whole = lambda shape: pl.BlockSpec(shape, lambda h, meta: (0,) * len(shape))
    own = pl.BlockSpec((1, DQ, 128), lambda h, meta: (jnp.minimum(h, 3) + 4 * group, 0, 0))
    near = pl.BlockSpec((1, DQ, 128), lambda h, meta: (jnp.clip(h - 4, 0, 3), 0, 0))
    lag = lambda shape: pl.BlockSpec((1,) + shape, lambda h, meta: (jnp.maximum(h - 1, 0), 0, 0))
    return pl.pallas_call(
        lambda *refs: score_kernel(spans, first, *refs),
        grid_spec=pltpu.PrefetchScalarGridSpec(
            num_scalar_prefetch=1,
            grid=(9,),
            in_specs=[whole(block.shape) for block in blocks]
            + [own, own, near, near]
            + [whole((72, 128))] * 2,
            out_specs=[lag((rows, 256)), lag((1, 256)), lag((1, 256))],
            scratch_shapes=[
                pltpu.VMEM((rows, DQ), jnp.bfloat16),
                pltpu.VMEM((rows, 256), jnp.float32),
                pltpu.VMEM((2, rows, 256), jnp.float32),
                pltpu.VMEM((2, 8, 256), jnp.float32),
            ],
        ),
        out_shape=[
            jax.ShapeDtypeStruct((8, rows, 256), jnp.bfloat16),
            jax.ShapeDtypeStruct((8, 1, 256), jnp.float32),
            jax.ShapeDtypeStruct((8, 1, 256), jnp.float32),
        ],
        cost_estimate=pl.CostEstimate(
            flops=24 * rows * 256 * DQ, bytes_accessed=8 * rows * 512, transcendentals=8 * rows * 256
        ),
        compiler_params=pltpu.CompilerParams(vmem_limit_bytes=VMEM),
        name="scores",
    )(meta, *blocks, qa, qb, na, nb, wa, wb)


def head_sum_kernel(meta, ea0, ea1, eb0, eb1, ra, rb, o0, o1, o2, o3, total_ref):
    i = pl.program_id(0)

    def add(parts, chunk):
        total = jnp.zeros((HALF, 256), jnp.float32)
        for e_ref, r_ref in parts:
            for h in range(8):
                total = total + e_ref[h].astype(jnp.float32) * r_ref[chunk, h]
        total_ref[...] = total

    @pl.when(i < 8)
    def _():
        add(((ea0, ra), (eb0, rb)), 0)

    @pl.when(i >= 8)
    def _():
        add(((ea1, ra), (eb1, rb)), 1)

    slot = meta[BLOCKS + i]
    quarter = meta[34]
    at = pl.ds(pl.multiple_of(slot * UNIT, UNIT), UNIT)
    extra = pl.ds(pl.multiple_of(256 + (slot >> 2) * UNIT, UNIT), UNIT)
    for k, out in enumerate((o0, o1, o2, o3)):
        unit = pl.multiple_of((quarter ^ k) * UNIT, UNIT)
        out[at, :] = total_ref[pl.ds(unit, UNIT), :].astype(jnp.bfloat16)

        @pl.when((slot & 3) == (quarter ^ k))
        def _():
            out[extra, :] = total_ref[4 * UNIT :, :].astype(jnp.bfloat16)


def head_sum_call(meta, ea, eb, ra, rb):
    early = pl.BlockSpec((8, HALF, 256), lambda i, meta: (0, jnp.minimum(i, 7), 0))
    late = pl.BlockSpec((8, HALF, 256), lambda i, meta: (0, jnp.maximum(i - 8, 0), 0))
    ratio = pl.BlockSpec((2, 8, 1, 256), lambda i, meta: (0, 0, 0, 0))
    out = pl.BlockSpec((ROWS, 256), lambda i, meta: (0, 0))
    return pl.pallas_call(
        head_sum_kernel,
        grid_spec=pltpu.PrefetchScalarGridSpec(
            num_scalar_prefetch=1,
            grid=(BLOCKS,),
            in_specs=[early, late, early, late, ratio, ratio],
            out_specs=[out] * 4,
            scratch_shapes=[pltpu.VMEM((HALF, 256), jnp.float32)],
        ),
        out_shape=[jax.ShapeDtypeStruct((ROWS, 256), jnp.bfloat16)] * 4,
        cost_estimate=pl.CostEstimate(flops=0, bytes_accessed=11 << 20, transcendentals=0),
        compiler_params=pltpu.CompilerParams(vmem_limit_bytes=VMEM),
        name="head_sum",
    )(meta, *ea, *eb, ra, rb)


def key_places(meta):
    core, half, quarter = meta[32], meta[33], meta[34]
    rows = lax.broadcasted_iota(jnp.int32, (UNIT, 256), 0)
    out = []
    for u in range(16):
        out.append(rows + ((u // 2 * 4 + (u % 2) * 2 + core) * 160 + half * HALF + quarter * UNIT))
    for e in range(4):
        z, ylo = 2 * e + (quarter >> 1), quarter & 1
        out.append(rows + ((z * 4 + ylo * 2 + core) * 160 + half * HALF + 4 * UNIT))
    return out


def inner_of(keys, ia, ib, j):
    queries = jnp.concatenate([ia[j], ib[j]], axis=0)
    return lax.dot_general(
        keys[...], queries, (((1,), (1,)), ((), ())), preferred_element_type=jnp.float32
    ), queries


JSTEP = 8


def forward_kernel(spans, meta, *refs):
    n = len(spans)
    ia, ib, wa, wb, wja, wjb, keys, logits, stats = refs[n:]
    blocks = [ref.at[at : at + HALF, 0:DI] for ref, span in zip(refs, spans) for at in range(0, span, HALF)]
    step = pl.program_id(0)

    @pl.when(step == 0)
    def _():
        quarter = meta[34]
        for i in range(BLOCKS):
            slot = meta[BLOCKS + i]
            mine = pl.ds(pl.multiple_of(quarter * UNIT, UNIT), UNIT)
            keys[pl.ds(pl.multiple_of(slot * UNIT, UNIT), UNIT), :] = blocks[i][mine, :]

            @pl.when((slot & 3) == quarter)
            def _():
                extra = pl.multiple_of(256 + (slot >> 2) * UNIT, UNIT)
                keys[pl.ds(extra, UNIT), :] = blocks[i][4 * UNIT :, :]

        logits[...] = jnp.zeros_like(logits)

    total = logits[...]
    for j in range(JSTEP):
        inner, _ = inner_of(keys, ia, ib, j)
        weight = jnp.concatenate([wja[j : j + 1, :], wjb[j : j + 1, :]], axis=1)
        total = total + weight * jnp.maximum(inner, 0.0)
    logits[...] = total

    @pl.when(step == NI // JSTEP - 1)
    def _():
        place = jnp.concatenate([wa[NI : NI + 1, :], wb[NI : NI + 1, :]], axis=1)
        places = key_places(meta)
        top = jnp.full((1, 256), NEG, jnp.float32)
        for u in range(20):
            cut = slice(u * UNIT, (u + 1) * UNIT)
            value = logits[cut, :] * INDEX_SCALE
            value = jnp.where(places[u].astype(jnp.float32) <= place, value, NEG)
            logits[cut, :] = value
            top = jnp.maximum(top, jnp.max(value, axis=0, keepdims=True))
        safe = jnp.where(top == NEG, 0.0, top)
        total = jnp.sum(jnp.exp(logits[...] - safe), axis=0, keepdims=True)
        stats[...] = jnp.zeros_like(stats)
        stats[0:1, :] = top
        stats[1:2, :] = total


def j_specs():
    whole = lambda shape: pl.BlockSpec(shape, lambda s, meta: (0,) * len(shape))
    queries = pl.BlockSpec((JSTEP, 128, DI), lambda s, meta: (s, 0, 0))
    weights = pl.BlockSpec((JSTEP, 128), lambda s, meta: (s, 0))
    return whole, [queries, queries, whole((72, 128)), whole((72, 128)), weights, weights]


def forward_call(meta, blocks, ia, ib, wa, wb):
    whole, specs = j_specs()
    spans = [block.shape[0] for block in blocks]
    return pl.pallas_call(
        lambda *refs: forward_kernel(spans, *refs),
        grid_spec=pltpu.PrefetchScalarGridSpec(
            num_scalar_prefetch=1,
            grid=(NI // JSTEP,),
            in_specs=[whole(block.shape) for block in blocks] + specs,
            out_specs=[whole((ROWS, DI)), whole((ROWS, 256)), whole((8, 256))],
        ),
        out_shape=[
            jax.ShapeDtypeStruct((ROWS, DI), jnp.bfloat16),
            jax.ShapeDtypeStruct((ROWS, 256), jnp.float32),
            jax.ShapeDtypeStruct((8, 256), jnp.float32),
        ],
        cost_estimate=pl.CostEstimate(
            flops=2 * NI * ROWS * 256 * DI, bytes_accessed=5 << 20, transcendentals=0
        ),
        compiler_params=pltpu.CompilerParams(vmem_limit_bytes=VMEM),
        name="index_forward",
    )(meta, *blocks, ia, ib, wa, wb, wa, wb)


def backward_kernel(meta, keys, logits, stats, t0, t1, t2, t3, ia, ib, wa, wb, wja, wjb, wg, div, kg, grad, acc):
    step = pl.program_id(0)

    @pl.when(step == 0)
    def _():
        tops = [stats[d, 0:1, :] for d in range(8)]
        top = tops[0]
        for d in range(1, 8):
            top = jnp.maximum(top, tops[d])
        total = jnp.zeros((1, 256), jnp.float32)
        for d in range(8):
            total = total + stats[d, 1:2, :] * jnp.exp(tops[d] - top)
        norm = top + jnp.log(total)
        goal = jnp.zeros((ROWS, 256), jnp.float32)
        for part in (t0, t1, t2, t3):
            goal = goal + part[...].astype(jnp.float32)
        goal = goal * (1.0 / 64.0)
        value = logits[...]
        seen = value != NEG
        logp = value - norm
        live = seen & (goal > 0)
        safe = jnp.where(goal > 0, goal, 1.0)
        part = jnp.where(live, goal * (jnp.log(safe) - logp), 0.0)
        div[...] = jnp.zeros_like(div)
        div[0:1, :] = jnp.sum(part, axis=0, keepdims=True)
        grad[...] = jnp.where(seen, jnp.exp(logp) - goal, 0.0) * INDEX_SCALE
        acc[...] = jnp.zeros_like(acc)

    total = acc[...]
    slope = grad[...]
    for j in range(JSTEP):
        inner, queries = inner_of(keys, ia, ib, j)
        weight = jnp.concatenate([wja[j : j + 1, :], wjb[j : j + 1, :]], axis=1)
        wg[j : j + 1, :] = jnp.sum(slope * jnp.maximum(inner, 0.0), axis=0, keepdims=True)
        coeff = jnp.where(inner > 0, slope * weight, 0.0).astype(jnp.bfloat16)
        total = total + jnp.dot(coeff, queries, preferred_element_type=jnp.float32)
    acc[...] = total

    @pl.when(step == NI // JSTEP - 1)
    def _():
        quarter = meta[34]
        for b in range(BLOCKS):
            kg[b, 0:UNIT, :] = acc[b * UNIT : (b + 1) * UNIT, :].astype(jnp.bfloat16)
            at = 256 + (b // 4) * UNIT
            extra = jnp.where(quarter == b % 4, acc[at : at + UNIT, :], 0.0)
            kg[b, UNIT:, :] = extra.astype(jnp.bfloat16)


def backward_call(meta, keys, logits, stats, target, ia, ib, wa, wb):
    whole, specs = j_specs()
    return pl.pallas_call(
        backward_kernel,
        grid_spec=pltpu.PrefetchScalarGridSpec(
            num_scalar_prefetch=1,
            grid=(NI // JSTEP,),
            in_specs=[
                whole((ROWS, DI)),
                whole((ROWS, 256)),
                whole((8, 8, 256)),
            ]
            + [whole((ROWS, 256))] * 4
            + specs,
            out_specs=[
                pl.BlockSpec((JSTEP, 256), lambda s, meta: (s, 0)),
                whole((8, 256)),
                whole((BLOCKS, 2 * UNIT, DI)),
            ],
            scratch_shapes=[
                pltpu.VMEM((ROWS, 256), jnp.float32),
                pltpu.VMEM((ROWS, DI), jnp.float32),
            ],
        ),
        out_shape=[
            jax.ShapeDtypeStruct((NI, 256), jnp.float32),
            jax.ShapeDtypeStruct((8, 256), jnp.float32),
            jax.ShapeDtypeStruct((BLOCKS, 2 * UNIT, DI), jnp.bfloat16),
        ],
        cost_estimate=pl.CostEstimate(
            flops=4 * NI * ROWS * 256 * DI, bytes_accessed=6 << 20, transcendentals=0
        ),
        compiler_params=pltpu.CompilerParams(vmem_limit_bytes=VMEM),
        name="index_backward",
    )(meta, keys, logits, stats, *target, ia, ib, wa, wb, wa, wb)


def merge(m0, l0, m1, l1):
    top = jnp.maximum(m0, m1)
    return top, l0 * jnp.exp2((m0 - top) * SCORE2) + l1 * jnp.exp2((m1 - top) * SCORE2)


def swap_halves(value):
    return jnp.concatenate([value[..., 128:], value[..., :128]], axis=-1)


def gather_head(value):
    wide = jnp.broadcast_to(value[None], (8,) + value.shape)
    return lax.all_to_all(wide, ("yhi", "xh", "xp"), 0, 0, tiled=True)


def after(value, *others):
    return lax.optimization_barrier((value,) + others)[0]


def body(main_queries, latent_keys, index_queries, index_weights, index_keys, tile_order, offset):
    z, ylo, core = lax.axis_index("z"), lax.axis_index("ylo"), lax.axis_index("core")
    half = lax.axis_index("xp")
    quarter = lax.axis_index("yhi") * 2 + lax.axis_index("xh")

    rows = jnp.arange(TILE, dtype=jnp.int32)
    place = (offset + (tile_order[:, None] * TILE + rows[None, :])).reshape(1, 128)
    wa = jnp.concatenate(
        [index_weights.T, place.astype(jnp.float32), jnp.zeros((7, 128), jnp.float32)], axis=0
    )
    own = jnp.concatenate([index_keys, latent_keys], axis=1)
    own = lax.dynamic_slice_in_dim(own, half * HALF, HALF, 0)

    queries = main_queries.transpose(0, 2, 1)
    f1, b1 = shift(own, dz=1), shift(own, dz=7)
    near_a, near_b = shift(queries[:4], dx=1), shift(queries[4:], dx=3)
    wb = swap_core(wa)
    queries_far = swap_core(queries)
    y0 = shift(own, dy=1)
    f2, b2 = shift(f1, dz=1), shift(b1, dz=7)
    y1 = shift(jnp.concatenate([f1, b1]), dy=3)
    f2, b2 = lax.optimization_barrier((f2, b2, y0))[:2]
    f3, b3 = shift(f2, dz=1), shift(b2, dz=7)
    y2 = shift(jnp.concatenate([f2, b2]), dy=1)
    near_a, near_b = lax.optimization_barrier((near_a, near_b, f2))[:2]
    near_a_far, near_b_far = swap_core(near_a), swap_core(near_b)
    f3, b3 = lax.optimization_barrier((f3, b3, y1))[:2]
    f4 = shift(f3, dz=1)
    y3 = shift(jnp.concatenate([f3, b3]), dy=3)
    y4 = shift(f4, dy=1)
    ia = after(index_queries, f4).transpose(1, 0, 2)
    ib = swap_core(ia)
    column = [(0, own), (-1, f1), (1, b1), (-2, f2), (2, b2), (-3, f3), (3, b3), (-4, f4)]
    blocks = [[block for _, block in column], [y0, y1, y2, y3, y4]]

    steps = jnp.asarray([dz for dz, _ in column] * 2, dtype=jnp.int32)
    zs = (z + 8 + steps) % 8
    ys = ylo ^ jnp.asarray([0] * 8 + [1] * 8, dtype=jnp.int32)
    bases = (zs * 4 + ys * 2 + core) * 160 + half * HALF
    meta = jnp.concatenate(
        [bases, zs * 2 + ys, jnp.stack([core, half, quarter])]
    ).astype(jnp.int32)

    near = [(near_a, near_a_far), (near_b, near_b_far)]

    def score(c, g, weights):
        return score_call(
            meta, 8 * c, blocks[c], g, queries, queries_far, *near[g], weights, wb
        )

    early = [score(0, g, wa) for g in range(2)]
    late = [score(1, 0, wa)]
    keys, logits, stats = forward_call(meta, blocks[0] + blocks[1], ia, ib, after(wa, late[0][1]), wb)
    late.append(score(1, 1, after(wa, stats)))

    ratios = []
    for g in range(2):
        (_, m0, l0), (_, m1, l1) = early[g], late[g]
        m, l = merge(m0[:, 0], l0[:, 0], m1[:, 0], l1[:, 0])
        away = swap_core(swap_halves(jnp.stack([m, l])))
        m, l = merge(m, l, away[0], away[1])
        ours = jnp.stack([m, l])
        out, back = (1, 3) if g == 0 else (3, 1)
        theirs = jnp.concatenate([shift(ours[:, 4:], dx=back), shift(ours[:, :4], dx=out)], axis=1)
        top, total = merge(m, l, theirs[0], theirs[1])
        ratios.append(jnp.stack([jnp.exp2((v - top[:, None]) * SCORE2) / total[:, None] for v in (m0, m1)]))
    sums = head_sum_call(meta, [early[0][0], late[0][0]], [early[1][0], late[1][0]], *ratios)
    target = [sums[0], shift(sums[1], dx=2), shift(sums[2], dy=2), shift(sums[3], dx=2, dy=2)]

    far = swap_core(swap_halves(stats))
    itop = jnp.maximum(stats[0], far[0])
    isum = stats[1] * jnp.exp(stats[0] - itop) + far[1] * jnp.exp(far[0] - itop)
    istats = jnp.concatenate([itop[None], isum[None], jnp.zeros((6, 256), jnp.float32)], axis=0)
    istats = gather_head(istats)

    wg, div, kg = backward_call(meta, keys, logits, istats, target, ia, ib, wa, wb)
    rows_out = jnp.concatenate([wg, div], axis=0)
    rows_out = rows_out[:, :128] + swap_core(rows_out[:, 128:])
    rows_sum = jnp.sum(gather_head(rows_out), axis=0)
    kg = lax.all_to_all(kg, ("z", "ylo"), 0, 0, tiled=True)
    kg = jnp.sum(kg.astype(jnp.float32), axis=0).astype(jnp.bfloat16)
    pieces = gather_head(kg).astype(jnp.float32).reshape(4, 2, 2 * UNIT, DI)
    main = pieces[:, :, :UNIT].transpose(1, 0, 2, 3).reshape(2, 4 * UNIT, DI)
    extra = jnp.sum(pieces[:, :, UNIT:], axis=0)
    key_grad = jnp.concatenate([main, extra], axis=1).reshape(160, DI)
    return rows_sum[NI], rows_sum[:NI].T, key_grad


def solution(mesh):
    fine = Mesh(np.asarray(mesh.devices).reshape(2, 2, 2, 8, 2, 2), ALL)
    head, ctx = ("yhi", "xh", "xp"), ("z", "ylo", "core")
    in_specs = (
        P(head, ctx, None),
        P(ctx, None),
        P(ctx, None, None),
        P(ctx, None),
        P(ctx, None),
        P(ctx),
        P(),
    )
    out_specs = (P(ctx), P(ctx, None), P(ctx, None))
    return jax.shard_map(body, mesh=fine, in_specs=in_specs, out_specs=out_specs, check_vma=False)
```

time: 172 us -> 174 us (1.012)
  blocking collectives: 31.1 us -> 14.5 us
  local copies, waits for them, and re-layouts: 20.4 us -> 7.26 us
  starting transfers between devices: 38.8 us -> 51.6 us
  waiting for transfers between devices: 37 us -> 47.1 us
  Pallas kernels: 38.4 us -> 47 us
    all_to_all x1 -> x0, blocking collectives: 18.4 us -> none  [body(): target = lax.all_to_all(sums, ('yhi', 'xh'), 0, 0, tiled=True)]
    unnamed x62 -> x13, local copies, waits for them, and re-layouts: 14.3 us -> 0.03 us
    all_to_all x1 -> x2, waiting for transfers between devices: 0.01 us -> 13.3 us  [gather_head(): return lax.all_to_all(wide, ('yhi', 'xh', 'xp'), 0, 0, tiled=True)]
    ppermute x26 -> x30, starting transfers between devices: 27.8 us -> 36.4 us  [shift(): return lax.ppermute(value, ALL, pairs)]
    pallas_call x3 -> x5, Pallas kernels: 25.4 us -> 33.1 us  [the longest x4 27.9 us: score_call(): pl.pallas_call(lambda *refs: score_kernel(spans, first, *refs), grid_spec...]
    ppermute x26 -> x30, waiting for transfers between devices: 27.6 us -> 23.6 us  [shift(): return lax.ppermute(value, ALL, pairs)]
    all_to_all x1 -> x2, starting transfers between devices: 5.06 us -> 9.03 us  [gather_head(): return lax.all_to_all(wide, ('yhi', 'xh', 'xp'), 0, 0, tiled=True)]
    optimization_barrier x0 -> x1, local copies, waits for them, and re-layouts: none -> 3.04 us  [after(): return lax.optimization_barrier((value,) + others)[0]]
  transfers between devices with their start and end apart: 28 -> 33, of which waited for: 14 -> 14; matrix products, arithmetic and copies ran while one was open for 4% -> 5% of each run, Pallas kernels for 8% -> 12%
where the time goes in v2:
time: 174 us; the launch traced here: 173 us
  starting transfers between devices  51.6 us (30%)
  waiting for transfers between devices  47.1 us (27%)
  Pallas kernels  47 us (27%)
  blocking collectives  14.5 us (8%)
  local copies, waits for them, and re-layouts  7.26 us (4%)
  other arithmetic  3.96 us (2%)
    ppermute x30, starting transfers between devices, shift(): return lax.ppermute(value, ALL, pairs)  36.4 us
    pallas_call x4, Pallas kernels, score_call(): pl.pallas_call(lambda *refs: score_kernel(spans, first, *refs), grid_spec...  27.9 us
    ppermute x30, waiting for transfers between devices, shift(): return lax.ppermute(value, ALL, pairs)  23.6 us
    all_to_all x1, blocking collectives, gather_head(): return lax.all_to_all(wide, ('yhi', 'xh', 'xp'), 0, 0, tiled=True)  14.5 us
    all_to_all x2, waiting for transfers between devices, gather_head(): return lax.all_to_all(wide, ('yhi', 'xh', 'xp'), 0, 0, tiled=True)  13.3 us
    all_to_all x1, waiting for transfers between devices, body(): kg = lax.all_to_all(kg, ('z', 'ylo'), 0, 0, tiled=True)  10.2 us
    pallas_call x1, Pallas kernels, backward_call(): pl.pallas_call(backward_kernel, grid_spec=pltpu.PrefetchScalarGridSpec(nu...  9.49 us
    all_to_all x2, starting transfers between devices, gather_head(): return lax.all_to_all(wide, ('yhi', 'xh', 'xp'), 0, 0, tiled=True)  9.03 us
  transfers between devices with their start and end apart: 33, of which 14 were waited for; matrix products, arithmetic and copies ran while one was open for 5% of the time, Pallas kernels for 12%

profile of v2, /device:TPU:2, one launch (start us, length us, event | category | flops | bytes accessed | tf_op | source)
XLA Modules:
  0.0 173.1 jit_solution(577519454912151741)
XLA Ops:
  3.6 4.0 %collective-permute-start.1 = (bf16[80,704]{1,0:T(8,128)(2,1)S(1)}, bf16[80,704]{1,0:T(8,128)(2,1)S(1)}, u32[]{:S(2)}, u32[]{:S(2)}) collective-permute-start(bf16[80,704]{1,0:T(8,128)(2,1)S(1)} %fusion.refs_1_), channel_id=1, source_target_pairs={{0,28},{1,29},{4,0},{5,1},{8,4},{9,5},{12,8},{13,9},{16,12},{17,13... | collective-permute-start | bytes 337928 | tf_op jit(solution)/shard_map/ppermute | solution.py:39
  13.8 4.7 %collective-permute-done.4.refs_1_.refs_9_ = bf16[80,704]{1,0:T(8,128)(2,1)S(1)} collective-permute-done((bf16[80,704]{1,0:T(8,128)(2,1)S(1)}, bf16[80,704]{1,0:T(8,128)(2,1)S(1)}, u32[]{:S(2)}, u32[]{:S(2)}) %collective-permute-start.4) | collective-permute-done | bytes 112672 | tf_op jit(solution)/shard_map/ppermute | solution.py:39
  26.2 3.2 %collective-permute-start.6 = (bf16[80,704]{1,0:T(8,128)(2,1)S(1)}, bf16[80,704]{1,0:T(8,128)(2,1)S(1)}, u32[]{:S(2)}, u32[]{:S(2)}) collective-permute-start(bf16[80,704]{1,0:T(8,128)(2,1)S(1)} %collective-permute-done.3.refs_5_), channel_id=1, source_target_pairs={{0,28},{1,29},{4,0},{5,1},{8,4},{9,5},{12,8},{13,9},{16,12},{17,13... | collective-permute-start | bytes 337928 | tf_op jit(solution)/shard_map/ppermute | solution.py:39
  29.5 3.7 %collective-permute-done.5.refs_6_ = bf16[80,704]{1,0:T(8,128)(2,1)S(1)} collective-permute-done((bf16[80,704]{1,0:T(8,128)(2,1)S(1)}, bf16[80,704]{1,0:T(8,128)(2,1)S(1)}, u32[]{:S(2)}, u32[]{:S(2)}) %collective-permute-start.5) | collective-permute-done | bytes 112672 | tf_op jit(solution)/shard_map/ppermute | solution.py:39
  35.5 5.9 %collective-permute-done.8.refs_8_ = bf16[80,704]{1,0:T(8,128)(2,1)S(1)} collective-permute-done((bf16[80,704]{1,0:T(8,128)(2,1)S(1)}, bf16[80,704]{1,0:T(8,128)(2,1)S(1)}, u32[]{:S(2)}, u32[]{:S(2)}) %collective-permute-start.8) | collective-permute-done | bytes 112672 | tf_op jit(solution)/shard_map/ppermute | solution.py:39
  43.3 3.0 %copy.19 = bf16[128,64,128]{2,0,1:T(8,128)(2,1)S(1)} copy(bf16[128,64,128]{2,1,0:T(8,128)(2,1)} %param.11) | data formatting | bytes 4194304 | tf_op jit(solution)/shard_map/optimization_barrier | solution.py:384
  47.1 7.1 %scores.5 = (bf16[8,640,256]{2,1,0:T(8,128)(2,1)S(1)}, f32[8,1,256]{2,1,0:T(1,128)S(1)}, f32[8,1,256]{2,1,0:T(1,128)S(1)}) custom-call(s32[35]{0:T(128)S(1)} %concatenate.42.refs_0_.meta, bf16[80,704]{1,0:T(8,128)(2,1)S(1)} %fusion.refs_1_, bf16[80,704]{1,0:T(8,128)(2,1)S(1)} %collective-permute-done.refs_2_, ...), custom_call_target="tpu_custom_call" | custom-call | flops 2264924160 | bytes 2621440 | tf_op jit(solution)/shard_map/scores/pallas_call | solution.py:104
  54.2 7.1 %scores.4 = (bf16[8,640,256]{2,1,0:T(8,128)(2,1)S(1)}, f32[8,1,256]{2,1,0:T(1,128)S(1)}, f32[8,1,256]{2,1,0:T(1,128)S(1)}) custom-call(s32[35]{0:T(128)S(1)} %concatenate.42.refs_0_.meta, bf16[80,704]{1,0:T(8,128)(2,1)S(1)} %collective-permute-done.4.refs_1_.refs_9_, bf16[160,704]{1,0:T(8,128)(2,1)S(1)} %collective-permute-done.7.refs_2_.refs_10_, ...), custom_call_target="tpu_custom_call" | custom-call | flops 2264924160 | bytes 2621440 | tf_op jit(solution)/shard_map/scores/pallas_call | solution.py:104
  63.3 6.9 %scores.6 = (bf16[8,640,256]{2,1,0:T(8,128)(2,1)S(1)}, f32[8,1,256]{2,1,0:T(1,128)S(1)}, f32[8,1,256]{2,1,0:T(1,128)S(1)}) custom-call(s32[35]{0:T(128)S(1)} %concatenate.42.refs_0_.meta, bf16[80,704]{1,0:T(8,128)(2,1)S(1)} %fusion.refs_1_, bf16[80,704]{1,0:T(8,128)(2,1)S(1)} %collective-permute-done.refs_2_, ...), custom_call_target="tpu_custom_call" | custom-call | flops 2264924160 | bytes 2621440 | tf_op jit(solution)/shard_map/scores/pallas_call | solution.py:104
  71.8 3.1 %collective-permute-done.22 = f32[2,4,256]{2,0,1:T(2,128)S(1)} collective-permute-done((f32[2,4,256]{2,0,1:T(2,128)S(1)}, f32[2,4,256]{2,0,1:T(2,128)S(1)}, u32[]{:S(2)}, u32[]{:S(2)}) %collective-permute-start.22) | collective-permute-done | bytes 8224 | tf_op jit(solution)/shard_map/ppermute | solution.py:39
  75.0 5.2 %index_forward.1 = (bf16[320,128]{1,0:T(8,128)(2,1)S(1)}, f32[320,256]{1,0:T(8,128)S(1)}, f32[8,256]{1,0:T(8,128)S(1)}) custom-call(s32[35]{0:T(128)S(1)} %concatenate.42.refs_0_.meta, bf16[80,704]{1,0:T(8,128)(2,1)S(1)} %fusion.refs_1_, bf16[80,704]{1,0:T(8,128)(2,1)S(1)} %collective-permute-done.refs_2_, ...), custom_call_target="tpu_custom_call" | custom-call | flops 1342177280 | bytes 5242880 | tf_op jit(solution)/shard_map/index_forward/pallas_call | solution.py:263
  80.2 6.9 %scores.7 = (bf16[8,640,256]{2,1,0:T(8,128)(2,1)S(1)}, f32[8,1,256]{2,1,0:T(1,128)S(1)}, f32[8,1,256]{2,1,0:T(1,128)S(1)}) custom-call(s32[35]{0:T(128)S(1)} %concatenate.42.refs_0_.meta, bf16[80,704]{1,0:T(8,128)(2,1)S(1)} %collective-permute-done.4.refs_1_.refs_9_, bf16[160,704]{1,0:T(8,128)(2,1)S(1)} %collective-permute-done.7.refs_2_.refs_10_, ...), custom_call_target="tpu_custom_call" | custom-call | flops 2264924160 | bytes 2621440 | tf_op jit(solution)/shard_map/scores/pallas_call | solution.py:104
  89.2 3.0 %collective-permute-start.25 = (f32[2,4,256]{2,0,1:T(2,128)S(1)}, f32[2,4,256]{2,0,1:T(2,128)S(1)}, u32[]{:S(2)}, u32[]{:S(2)}) collective-permute-start(f32[2,4,256]{2,0,1:T(2,128)S(1)} %get-tuple-element.87), channel_id=1, source_target_pairs={{0,96},{1,97},{4,100},{5,101},{8,104},{9,105},{12,108},{13,109},{1... | collective-permute-start | bytes 24584 | tf_op jit(solution)/shard_map/ppermute | solution.py:39
  93.7 4.5 %head_sum.1 = (bf16[320,256]{1,0:T(8,128)(2,1)S(1)}, bf16[320,256]{1,0:T(8,128)(2,1)S(1)}, bf16[320,256]{1,0:T(8,128)(2,1)S(1)}, bf16[320,256]{1,0:T(8,128)(2,1)S(1)}) custom-call(s32[35]{0:T(128)S(1)} %concatenate.42.refs_0_.meta, bf16[8,640,256]{2,1,0:T(8,128)(2,1)S(1)} %get-tuple-element.45.ea0, bf16[8,640,256]{2,1,0:T(8,128)(2,1)S(1)} %get-tuple-element.46.ea1, ...), custom_call_target="tpu_custom_call" | custom-call | bytes 11534336 | tf_op jit(solution)/shard_map/head_sum/pallas_call | solution.py:169
  98.2 5.6 %collective-permute-start.26 = (bf16[320,256]{1,0:T(8,128)(2,1)S(1)}, bf16[320,256]{1,0:T(8,128)(2,1)S(1)}, u32[]{:S(2)}, u32[]{:S(2)}) collective-permute-start(bf16[320,256]{1,0:T(8,128)(2,1)S(1)} %get-tuple-element.59), channel_id=1, source_target_pairs={{0,64},{1,65},{4,68},{5,69},{8,72},{9,73},{12,76},{13,77},{16,80},... | collective-permute-start | bytes 491528 | tf_op jit(solution)/shard_map/ppermute | solution.py:39
  103.8 2.8 %collective-permute-start.27 = (bf16[320,256]{1,0:T(8,128)(2,1)S(1)}, bf16[320,256]{1,0:T(8,128)(2,1)S(1)}, u32[]{:S(2)}, u32[]{:S(2)}) collective-permute-start(bf16[320,256]{1,0:T(8,128)(2,1)S(1)} %get-tuple-element.60), channel_id=1, source_target_pairs={{0,128},{1,129},{4,132},{5,133},{8,136},{9,137},{12,140},{13,141},... | collective-permute-start | bytes 491528 | tf_op jit(solution)/shard_map/ppermute | solution.py:39
  107.0 14.5 %all_to_all.20.stats = f32[8,8,256]{2,1,0:T(8,128)S(1)} all-to-all(f32[8,8,256]{2,1,0:T(8,128)S(1)} %broadcast_in_dim.12), channel_id=1, replica_groups=mesh['yhi'=2,'xh'=2,'xp'=2,'z'=8,'ylo'=2,'core'=2] {'yhi','xh','xp'}, dimensions={0} | all-to-all | bytes 131072 | tf_op jit(solution)/shard_map/all_to_all | solution.py:380
  121.4 9.5 %index_backward.1 = (f32[64,256]{1,0:T(8,128)S(1)}, f32[8,256]{1,0:T(8,128)S(1)}, bf16[16,32,128]{2,1,0:T(8,128)(2,1)}) custom-call(s32[35]{0:T(128)S(1)} %concatenate.42.refs_0_.meta, bf16[320,128]{1,0:T(8,128)(2,1)S(1)} %get-tuple-element.42.keys, f32[320,256]{1,0:T(8,128)S(1)} %get-tuple-element.43.logits, f32[8,8,256]{2,1,0:T(8,128)S(1)} %all_to_all.20.stats, ...), custom_call_target="tpu_custom_call" | custom-call | flops 2684354560 | bytes 6291456 | tf_op jit(solution)/shard_map/index_backward/pallas_call | solution.py:334
  131.1 6.2 %all-to-all-start.2 = ((bf16[16,32,128]{2,1,0:T(8,128)(2,1)}), bf16[16,32,128]{2,1,0:T(8,128)(2,1)S(1)}, u32[]{:S(2)}, u32[]{:S(2)}) async-start(bf16[16,32,128]{2,1,0:T(8,128)(2,1)} %get-tuple-element.64), calls=%async_computation.2 | async-start | bytes 262144 | tf_op jit(solution)/shard_map/all_to_all | solution.py:466
  137.3 10.2 %all-to-all-done.2 = bf16[16,32,128]{2,1,0:T(8,128)(2,1)S(1)} async-done(((bf16[16,32,128]{2,1,0:T(8,128)(2,1)}), bf16[16,32,128]{2,1,0:T(8,128)(2,1)S(1)}, u32[]{:S(2)}, u32[]{:S(2)}) %all-to-all-start.2) | async-done | bytes 131104 | tf_op jit(solution)/shard_map/all_to_all | solution.py:466
  148.3 4.6 %all-to-all-start.1 = ((f32[8,72,128]{2,1,0:T(8,128)}), f32[8,72,128]{2,1,0:T(8,128)S(1)}, u32[]{:S(2)}, u32[]{:S(2)}) async-start(f32[8,72,128]{2,1,0:T(8,128)} %broadcast_in_dim.13), calls=%async_computation.1 | async-start | bytes 589824 | tf_op jit(solution)/shard_map/all_to_all | solution.py:380
  152.9 7.8 %all-to-all-done.1 = f32[8,72,128]{2,1,0:T(8,128)S(1)} async-done(((f32[8,72,128]{2,1,0:T(8,128)}), f32[8,72,128]{2,1,0:T(8,128)S(1)}, u32[]{:S(2)}, u32[]{:S(2)}) %all-to-all-start.1) | async-done | bytes 294944 | tf_op jit(solution)/shard_map/all_to_all | solution.py:380
  161.4 4.4 %all-to-all-start.3 = ((bf16[8,32,128]{2,1,0:T(8,128)(2,1)}), bf16[8,32,128]{2,1,0:T(8,128)(2,1)S(1)}, u32[]{:S(2)}, u32[]{:S(2)}) async-start(bf16[8,32,128]{2,1,0:T(8,128)(2,1)} %broadcast_in_dim.14), calls=%async_computation.3 | async-start | bytes 131072 | tf_op jit(solution)/shard_map/all_to_all | solution.py:380
  166.9 5.5 %all-to-all-done.3 = bf16[8,32,128]{2,1,0:T(8,128)(2,1)S(1)} async-done(((bf16[8,32,128]{2,1,0:T(8,128)(2,1)}), bf16[8,32,128]{2,1,0:T(8,128)(2,1)S(1)}, u32[]{:S(2)}, u32[]{:S(2)}) %all-to-all-start.3) | async-done | bytes 65568 | tf_op jit(solution)/shard_map/all_to_all | solution.py:380
  (116 shorter events, 32.1 us)
Async XLA Ops:
  1.6 10.4 %collective-permute-start = (bf16[80,704]{1,0:T(8,128)(2,1)S(1)}, bf16[80,704]{1,0:T(8,128)(2,1)S(1)}, u32[]{:S(2)}, u32[]{:S(2)}) collective-permute-start(bf16[80,704]{1,0:T(8,128)(2,1)S(1)} %fusion.refs_1_), channel_id=1, source_target_pairs={{0,4},{1,5},{4,8},{5,9},{8,12},{9,13},{12,16},{13,17},{16,20},{17,... | collective-permute-start | bytes 337928 | tf_op jit(solution)/shard_map/ppermute | solution.py:39
  3.6 10.0 %collective-permute-start.1 = (bf16[80,704]{1,0:T(8,128)(2,1)S(1)}, bf16[80,704]{1,0:T(8,128)(2,1)S(1)}, u32[]{:S(2)}, u32[]{:S(2)}) collective-permute-start(bf16[80,704]{1,0:T(8,128)(2,1)S(1)} %fusion.refs_1_), channel_id=1, source_target_pairs={{0,28},{1,29},{4,0},{5,1},{8,4},{9,5},{12,8},{13,9},{16,12},{17,13... | collective-permute-start | bytes 337928 | tf_op jit(solution)/shard_map/ppermute | solution.py:39
  7.6 39.1 %collective-permute-start.13 = (bf16[8,576,128]{2,1,0:T(8,128)(2,1)}, bf16[8,576,128]{2,1,0:T(8,128)(2,1)S(1)}, u32[]{:S(2)}, u32[]{:S(2)}) collective-permute-start(bf16[8,576,128]{2,1,0:T(8,128)(2,1)} %bitcast.166), channel_id=1, source_target_pairs={{0,1},{1,0},{4,5},{5,4},{8,9},{9,8},{12,13},{13,12},{16,17},{17,16... | collective-permute-start | bytes 3538952 | tf_op jit(solution)/shard_map/ppermute | solution.py:39
  9.0 15.9 %collective-permute-start.14 = (bf16[4,576,128]{2,1,0:T(8,128)(2,1)S(1)}, bf16[4,576,128]{2,1,0:T(8,128)(2,1)}, u32[]{:S(2)}, u32[]{:S(2)}) collective-permute-start(bf16[4,576,128]{2,1,0:T(8,128)(2,1)S(1)} %get-tuple-element.80), channel_id=1, source_target_pairs={{0,32},{1,33},{4,36},{5,37},{8,40},{9,41},{12,44},{13,45},{16,48},... | collective-permute-start | bytes 1769480 | tf_op jit(solution)/shard_map/ppermute | solution.py:39
  10.6 15.6 %collective-permute-start.15 = (bf16[4,576,128]{2,1,0:T(8,128)(2,1)S(1)}, bf16[4,576,128]{2,1,0:T(8,128)(2,1)}, u32[]{:S(2)}, u32[]{:S(2)}) collective-permute-start(bf16[4,576,128]{2,1,0:T(8,128)(2,1)S(1)} %get-tuple-element.79), channel_id=1, source_target_pairs={{0,96},{1,97},{4,100},{5,101},{8,104},{9,105},{12,108},{13,109},{1... | collective-permute-start | bytes 1769480 | tf_op jit(solution)/shard_map/ppermute | solution.py:39
  13.7 7.4 %collective-permute-start.2 = (bf16[80,704]{1,0:T(8,128)(2,1)S(1)}, bf16[80,704]{1,0:T(8,128)(2,1)S(1)}, u32[]{:S(2)}, u32[]{:S(2)}) collective-permute-start(bf16[80,704]{1,0:T(8,128)(2,1)S(1)} %collective-permute-done.refs_2_), channel_id=1, source_target_pairs={{0,4},{1,5},{4,8},{5,9},{8,12},{9,13},{12,16},{13,17},{16,20},{17,... | collective-permute-start | bytes 337928 | tf_op jit(solution)/shard_map/ppermute | solution.py:39
  21.1 13.6 %collective-permute-start.7 = (bf16[160,704]{1,0:T(8,128)(2,1)}, bf16[160,704]{1,0:T(8,128)(2,1)S(1)}, u32[]{:S(2)}, u32[]{:S(2)}) collective-permute-start(bf16[160,704]{1,0:T(8,128)(2,1)} %pad_maximum_fusion), channel_id=1, source_target_pairs={{0,130},{1,131},{4,134},{5,135},{8,138},{9,139},{12,142},{13,143},... | collective-permute-start | bytes 675848 | tf_op jit(solution)/shard_map/ppermute | solution.py:39
  26.1 20.3 %collective-permute-start.16 = (bf16[4,576,128]{2,1,0:T(8,128)(2,1)}, bf16[4,576,128]{2,1,0:T(8,128)(2,1)}, u32[]{:S(2)}, u32[]{:S(2)}) collective-permute-start(bf16[4,576,128]{2,1,0:T(8,128)(2,1)} %collective-permute-done.14.refs_8_.refs_11_), channel_id=1, source_target_pairs={{0,1},{1,0},{4,5},{5,4},{8,9},{9,8},{12,13},{13,12},{16,17},{17,16... | collective-permute-start | bytes 1769480 | tf_op jit(solution)/shard_map/ppermute | solution.py:39
  26.1 7.0 %collective-permute-start.5 = (bf16[80,704]{1,0:T(8,128)(2,1)S(1)}, bf16[80,704]{1,0:T(8,128)(2,1)S(1)}, u32[]{:S(2)}, u32[]{:S(2)}) collective-permute-start(bf16[80,704]{1,0:T(8,128)(2,1)S(1)} %collective-permute-done.2.refs_4_), channel_id=1, source_target_pairs={{0,4},{1,5},{4,8},{5,9},{8,12},{9,13},{12,16},{13,17},{16,20},{17,... | collective-permute-start | bytes 337928 | tf_op jit(solution)/shard_map/ppermute | solution.py:39
  26.2 6.9 %collective-permute-start.6 = (bf16[80,704]{1,0:T(8,128)(2,1)S(1)}, bf16[80,704]{1,0:T(8,128)(2,1)S(1)}, u32[]{:S(2)}, u32[]{:S(2)}) collective-permute-start(bf16[80,704]{1,0:T(8,128)(2,1)S(1)} %collective-permute-done.3.refs_5_), channel_id=1, source_target_pairs={{0,28},{1,29},{4,0},{5,1},{8,4},{9,5},{12,8},{13,9},{16,12},{17,13... | collective-permute-start | bytes 337928 | tf_op jit(solution)/shard_map/ppermute | solution.py:39
  33.2 13.2 %collective-permute-start.17 = (f32[72,128]{1,0:T(8,128)S(1)}, f32[72,128]{1,0:T(8,128)S(1)}, u32[]{:S(2)}, u32[]{:S(2)}) collective-permute-start(f32[72,128]{1,0:T(8,128)S(1)} %maximum_maximum_fusion.refs_10_.refs_16_.refs_18_.refs_13_.wa.wja), channel_id=1, source_target_pairs={{0,1},{1,0},{4,5},{5,4},{8,9},{9,8},{12,13},{13,12},{16,17},{17,16... | collective-permute-start | bytes 110600 | tf_op jit(solution)/shard_map/ppermute | solution.py:39
  33.2 21.0 %collective-permute-start.9 = (bf16[160,704]{1,0:T(8,128)(2,1)S(1)}, bf16[160,704]{1,0:T(8,128)(2,1)S(1)}, u32[]{:S(2)}, u32[]{:S(2)}) collective-permute-start(bf16[160,704]{1,0:T(8,128)(2,1)S(1)} %pad_maximum_fusion.1), channel_id=1, source_target_pairs={{0,2},{1,3},{4,6},{5,7},{8,10},{9,11},{12,14},{13,15},{16,18},{17,... | collective-permute-start | bytes 675848 | tf_op jit(solution)/shard_map/ppermute | solution.py:39
  34.7 6.7 %collective-permute-start.8 = (bf16[80,704]{1,0:T(8,128)(2,1)S(1)}, bf16[80,704]{1,0:T(8,128)(2,1)S(1)}, u32[]{:S(2)}, u32[]{:S(2)}) collective-permute-start(bf16[80,704]{1,0:T(8,128)(2,1)S(1)} %collective-permute-done.5.refs_6_), channel_id=1, source_target_pairs={{0,4},{1,5},{4,8},{5,9},{8,12},{9,13},{12,16},{13,17},{16,20},{17,... | collective-permute-start | bytes 337928 | tf_op jit(solution)/shard_map/ppermute | solution.py:39
  41.4 12.7 %collective-permute-start.10 = (bf16[160,704]{1,0:T(8,128)(2,1)}, bf16[160,704]{1,0:T(8,128)(2,1)S(1)}, u32[]{:S(2)}, u32[]{:S(2)}) collective-permute-start(bf16[160,704]{1,0:T(8,128)(2,1)} %pad_maximum_fusion.2), channel_id=1, source_target_pairs={{0,130},{1,131},{4,134},{5,135},{8,138},{9,139},{12,142},{13,143},... | collective-permute-start | bytes 675848 | tf_op jit(solution)/shard_map/ppermute | solution.py:39
  46.4 28.7 %collective-permute-start.12 = (bf16[64,128,128]{2,1,0:T(8,128)(2,1)S(1)}, bf16[64,128,128]{2,1,0:T(8,128)(2,1)S(1)}, u32[]{:S(2)}, u32[]{:S(2)}) collective-permute-start(bf16[64,128,128]{2,1,0:T(8,128)(2,1)S(1)} %bitcast.163), channel_id=1, source_target_pairs={{0,1},{1,0},{4,5},{5,4},{8,9},{9,8},{12,13},{13,12},{16,17},{17,16... | collective-permute-start | bytes 6291464 | tf_op jit(solution)/shard_map/ppermute | solution.py:39
  46.5 7.7 %collective-permute-start.11 = (bf16[80,704]{1,0:T(8,128)(2,1)S(1)}, bf16[80,704]{1,0:T(8,128)(2,1)S(1)}, u32[]{:S(2)}, u32[]{:S(2)}) collective-permute-start(bf16[80,704]{1,0:T(8,128)(2,1)S(1)} %collective-permute-done.8.refs_8_), channel_id=1, source_target_pairs={{0,2},{1,3},{4,6},{5,7},{8,10},{9,11},{12,14},{13,15},{16,18},{17,... | collective-permute-start | bytes 337928 | tf_op jit(solution)/shard_map/ppermute | solution.py:39
  46.8 16.5 %collective-permute-start.19 = (bf16[4,576,128]{2,1,0:T(8,128)(2,1)}, bf16[4,576,128]{2,1,0:T(8,128)(2,1)S(1)}, u32[]{:S(2)}, u32[]{:S(2)}) collective-permute-start(bf16[4,576,128]{2,1,0:T(8,128)(2,1)} %collective-permute-done.15.refs_11_.refs_8_), channel_id=1, source_target_pairs={{0,1},{1,0},{4,5},{5,4},{8,9},{9,8},{12,13},{13,12},{16,17},{17,16... | collective-permute-start | bytes 1769480 | tf_op jit(solution)/shard_map/ppermute | solution.py:39
  62.7 9.1 %collective-permute-start.21 = (f32[2,4,256]{2,0,1:T(2,128)S(1)}, f32[2,4,256]{2,0,1:T(2,128)S(1)}, u32[]{:S(2)}, u32[]{:S(2)}) collective-permute-start(f32[2,4,256]{2,0,1:T(2,128)S(1)} %get-tuple-element.90), channel_id=1, source_target_pairs={{0,96},{1,97},{4,100},{5,101},{8,104},{9,105},{12,108},{13,109},{1... | collective-permute-start | bytes 24584 | tf_op jit(solution)/shard_map/ppermute | solution.py:39
  98.2 23.2 %collective-permute-start.26 = (bf16[320,256]{1,0:T(8,128)(2,1)S(1)}, bf16[320,256]{1,0:T(8,128)(2,1)S(1)}, u32[]{:S(2)}, u32[]{:S(2)}) collective-permute-start(bf16[320,256]{1,0:T(8,128)(2,1)S(1)} %get-tuple-element.59), channel_id=1, source_target_pairs={{0,64},{1,65},{4,68},{5,69},{8,72},{9,73},{12,76},{13,77},{16,80},... | collective-permute-start | bytes 491528 | tf_op jit(solution)/shard_map/ppermute | solution.py:39
  103.8 17.6 %collective-permute-start.27 = (bf16[320,256]{1,0:T(8,128)(2,1)S(1)}, bf16[320,256]{1,0:T(8,128)(2,1)S(1)}, u32[]{:S(2)}, u32[]{:S(2)}) collective-permute-start(bf16[320,256]{1,0:T(8,128)(2,1)S(1)} %get-tuple-element.60), channel_id=1, source_target_pairs={{0,128},{1,129},{4,132},{5,133},{8,136},{9,137},{12,140},{13,141},... | collective-permute-start | bytes 491528 | tf_op jit(solution)/shard_map/ppermute | solution.py:39
  106.6 14.8 %collective-permute-start.28 = (bf16[320,256]{1,0:T(8,128)(2,1)S(1)}, bf16[320,256]{1,0:T(8,128)(2,1)S(1)}, u32[]{:S(2)}, u32[]{:S(2)}) collective-permute-start(bf16[320,256]{1,0:T(8,128)(2,1)S(1)} %get-tuple-element.61), channel_id=1, source_target_pairs={{0,192},{1,193},{4,196},{5,197},{8,200},{9,201},{12,204},{13,205},... | collective-permute-start | bytes 491528 | tf_op jit(solution)/shard_map/ppermute | solution.py:39
  131.1 16.5 %all-to-all-start.2 = ((bf16[16,32,128]{2,1,0:T(8,128)(2,1)}), bf16[16,32,128]{2,1,0:T(8,128)(2,1)S(1)}, u32[]{:S(2)}, u32[]{:S(2)}) async-start(bf16[16,32,128]{2,1,0:T(8,128)(2,1)} %get-tuple-element.64), calls=%async_computation.2 | async-start | bytes 262144 | tf_op jit(solution)/shard_map/all_to_all | solution.py:466
  148.3 12.4 %all-to-all-start.1 = ((f32[8,72,128]{2,1,0:T(8,128)}), f32[8,72,128]{2,1,0:T(8,128)S(1)}, u32[]{:S(2)}, u32[]{:S(2)}) async-start(f32[8,72,128]{2,1,0:T(8,128)} %broadcast_in_dim.13), calls=%async_computation.1 | async-start | bytes 589824 | tf_op jit(solution)/shard_map/all_to_all | solution.py:380
  161.4 11.0 %all-to-all-start.3 = ((bf16[8,32,128]{2,1,0:T(8,128)(2,1)}), bf16[8,32,128]{2,1,0:T(8,128)(2,1)S(1)}, u32[]{:S(2)}, u32[]{:S(2)}) async-start(bf16[8,32,128]{2,1,0:T(8,128)(2,1)} %broadcast_in_dim.14), calls=%async_computation.3 | async-start | bytes 131072 | tf_op jit(solution)/shard_map/all_to_all | solution.py:380
  (14 other events, 114.2 us)

commit v3 on v2

--- a/solution.py
+++ b/solution.py
@@ -43,38 +43,56 @@
     return shift(value, flip=1)
 
 
-def score_kernel(spans, first, meta, *refs):
+HEADS = 16
+KEYS_HERE = BLOCKS * HALF
+
+
+def score_kernel(spans, meta, *refs):
     n = len(spans)
-    blocks, (qa, qb, na, nb, wa, wb) = refs[:n], refs[n : n + 6]
-    e_ref, m_ref, l_ref, keys, bias, raw, tops = refs[n + 6 :]
+    blocks, (qa, qb, na, nb, ma, mb, wa, wb) = refs[:n], refs[n : n + 8]
+    e_ref, m_ref, l_ref, ik_ref, keys, bias, raw, tops, sems = refs[n + 8 :]
     step = pl.program_id(0)
-    rows = keys.shape[0]
     cut = 320
 
     @pl.when(step == 0)
     def _():
         at = 0
-        for block, span in zip(blocks, spans):
-            keys[at : at + span, :] = block[:, DI : DI + DQ]
+        copies = []
+        for i, (block, span) in enumerate(zip(blocks, spans)):
+            copies.append(pltpu.make_async_copy(block, keys.at[at : at + span, :], sems.at[i]))
+            copies[-1].start()
             at += span
         place = jnp.concatenate([wa[NI : NI + 1, :], wb[NI : NI + 1, :]], axis=1)
         offsets = lax.broadcasted_iota(jnp.int32, (HALF, 256), 0).astype(jnp.float32)
-        for i in range(rows // HALF):
-            base = meta[first + i].astype(jnp.float32)
+        for i in range(BLOCKS):
+            base = meta[i].astype(jnp.float32)
             bias[i * HALF : (i + 1) * HALF, :] = jnp.where(offsets + base <= place, 0.0, NEG)
         tops[...] = jnp.zeros_like(tops)
+        for copy in copies:
+            copy.wait()
+        quarter = meta[34]
+        for i in range(BLOCKS):
+            slot = meta[BLOCKS + i]
+            mine = pl.ds(pl.multiple_of(i * HALF + quarter * UNIT, UNIT), UNIT)
+            ik_ref[pl.ds(pl.multiple_of(slot * UNIT, UNIT), UNIT), :] = keys[mine, 0:DI]
+
+            @pl.when((slot & 3) == quarter)
+            def _():
+                extra = pl.multiple_of(256 + (slot >> 2) * UNIT, UNIT)
+                ik_ref[pl.ds(extra, UNIT), :] = keys[i * HALF + 4 * UNIT : (i + 1) * HALF, 0:DI]
 
     def work(now, last):
         own = jnp.concatenate([qa[0], qb[0]], axis=1)
-        near = jnp.concatenate([na[0], nb[0]], axis=1)
-        queries = jnp.where(step < 4, own, near)
+        left = jnp.concatenate([na[0], nb[0]], axis=1)
+        right = jnp.concatenate([ma[0], mb[0]], axis=1)
+        queries = jnp.where(step < 8, own, jnp.where(step < 12, left, right))
         top = jnp.max(tops[last], axis=0, keepdims=True)
         safe = jnp.where(top == NEG, 0.0, top)
         new = jnp.full((8, 256), NEG, jnp.float32)
         total = jnp.zeros((8, 256), jnp.float32)
-        for t in range(0, rows, cut):
+        for t in range(0, KEYS_HERE, cut):
             piece = slice(t, t + cut)
-            scores = jnp.dot(keys[piece, :], queries, preferred_element_type=jnp.float32)
+            scores = jnp.dot(keys[piece, DI:], queries, preferred_element_type=jnp.float32)
             scores = scores + bias[piece, :]
             raw[now, piece, :] = scores
             new = jnp.maximum(new, jnp.max(scores.reshape(cut // 8, 8, 256), axis=0))
@@ -94,60 +112,55 @@
         work(1, 0)
 
 
-def score_call(meta, first, blocks, group, qa, qb, na, nb, wa, wb):
+def score_call(meta, blocks, qa, qb, na, nb, ma, mb, wa, wb):
     spans = [block.shape[0] for block in blocks]
-    rows = sum(spans)
     whole = lambda shape: pl.BlockSpec(shape, lambda h, meta: (0,) * len(shape))
-    own = pl.BlockSpec((1, DQ, 128), lambda h, meta: (jnp.minimum(h, 3) + 4 * group, 0, 0))
-    near = pl.BlockSpec((1, DQ, 128), lambda h, meta: (jnp.clip(h - 4, 0, 3), 0, 0))
+
+    def heads(first, count):
+        return pl.BlockSpec((1, DQ, 128), lambda h, meta: (jnp.clip(h - first, 0, count - 1), 0, 0))
+
     lag = lambda shape: pl.BlockSpec((1,) + shape, lambda h, meta: (jnp.maximum(h - 1, 0), 0, 0))
     return pl.pallas_call(
-        lambda *refs: score_kernel(spans, first, *refs),
+        lambda *refs: score_kernel(spans, *refs),
         grid_spec=pltpu.PrefetchScalarGridSpec(
             num_scalar_prefetch=1,
-            grid=(9,),
-            in_specs=[whole(block.shape) for block in blocks]
-            + [own, own, near, near]
+            grid=(HEADS + 1,),
+            in_specs=[pl.BlockSpec(memory_space=pl.ANY)] * len(blocks)
+            + [heads(0, 8)] * 2
+            + [heads(8, 4)] * 2
+            + [heads(12, 4)] * 2
             + [whole((72, 128))] * 2,
-            out_specs=[lag((rows, 256)), lag((1, 256)), lag((1, 256))],
+            out_specs=[lag((KEYS_HERE, 256)), lag((1, 256)), lag((1, 256)), whole((ROWS, DI))],
             scratch_shapes=[
-                pltpu.VMEM((rows, DQ), jnp.bfloat16),
-                pltpu.VMEM((rows, 256), jnp.float32),
-                pltpu.VMEM((2, rows, 256), jnp.float32),
+                pltpu.VMEM((KEYS_HERE, DI + DQ), jnp.bfloat16),
+                pltpu.VMEM((KEYS_HERE, 256), jnp.float32),
+                pltpu.VMEM((2, KEYS_HERE, 256), jnp.float32),
                 pltpu.VMEM((2, 8, 256), jnp.float32),
+                pltpu.SemaphoreType.DMA((len(blocks),)),
             ],
         ),
         out_shape=[
-            jax.ShapeDtypeStruct((8, rows, 256), jnp.bfloat16),
-            jax.ShapeDtypeStruct((8, 1, 256), jnp.float32),
-            jax.ShapeDtypeStruct((8, 1, 256), jnp.float32),
+            jax.ShapeDtypeStruct((HEADS, KEYS_HERE, 256), jnp.bfloat16),
+            jax.ShapeDtypeStruct((HEADS, 1, 256), jnp.float32),
+            jax.ShapeDtypeStruct((HEADS, 1, 256), jnp.float32),
+            jax.ShapeDtypeStruct((ROWS, DI), jnp.bfloat16),
         ],
         cost_estimate=pl.CostEstimate(
-            flops=24 * rows * 256 * DQ, bytes_accessed=8 * rows * 512, transcendentals=8 * rows * 256
+            flops=4 * HEADS * KEYS_HERE * 256 * DQ,
+            bytes_accessed=HEADS * KEYS_HERE * 512,
+            transcendentals=HEADS * KEYS_HERE * 256,
         ),
         compiler_params=pltpu.CompilerParams(vmem_limit_bytes=VMEM),
         name="scores",
-    )(meta, *blocks, qa, qb, na, nb, wa, wb)
-
-
-def head_sum_kernel(meta, ea0, ea1, eb0, eb1, ra, rb, o0, o1, o2, o3, total_ref):
+    )(meta, *blocks, qa, qb, na, nb, ma, mb, wa, wb)
+
+
+def head_sum_kernel(meta, e_ref, r_ref, o0, o1, o2, o3, total_ref):
     i = pl.program_id(0)
-
-    def add(parts, chunk):
-        total = jnp.zeros((HALF, 256), jnp.float32)
-        for e_ref, r_ref in parts:
-            for h in range(8):
-                total = total + e_ref[h].astype(jnp.float32) * r_ref[chunk, h]
-        total_ref[...] = total
-
-    @pl.when(i < 8)
-    def _():
-        add(((ea0, ra), (eb0, rb)), 0)
-
-    @pl.when(i >= 8)
-    def _():
-        add(((ea1, ra), (eb1, rb)), 1)
-
+    total = jnp.zeros((HALF, 256), jnp.float32)
+    for h in range(HEADS):
+        total = total + e_ref[h].astype(jnp.float32) * r_ref[h]
+    total_ref[...] = total
     slot = meta[BLOCKS + i]
     quarter = meta[34]
     at = pl.ds(pl.multiple_of(slot * UNIT, UNIT), UNIT)
@@ -161,17 +174,16 @@
             out[extra, :] = total_ref[4 * UNIT :, :].astype(jnp.bfloat16)
 
 
-def head_sum_call(meta, ea, eb, ra, rb):
-    early = pl.BlockSpec((8, HALF, 256), lambda i, meta: (0, jnp.minimum(i, 7), 0))
-    late = pl.BlockSpec((8, HALF, 256), lambda i, meta: (0, jnp.maximum(i - 8, 0), 0))
-    ratio = pl.BlockSpec((2, 8, 1, 256), lambda i, meta: (0, 0, 0, 0))
+def head_sum_call(meta, exps, ratio):
+    piece = pl.BlockSpec((HEADS, HALF, 256), lambda i, meta: (0, i, 0))
+    ratios = pl.BlockSpec((HEADS, 1, 256), lambda i, meta: (0, 0, 0))
     out = pl.BlockSpec((ROWS, 256), lambda i, meta: (0, 0))
     return pl.pallas_call(
         head_sum_kernel,
         grid_spec=pltpu.PrefetchScalarGridSpec(
             num_scalar_prefetch=1,
             grid=(BLOCKS,),
-            in_specs=[early, late, early, late, ratio, ratio],
+            in_specs=[piece, ratios],
             out_specs=[out] * 4,
             scratch_shapes=[pltpu.VMEM((HALF, 256), jnp.float32)],
         ),
@@ -179,7 +191,7 @@
         cost_estimate=pl.CostEstimate(flops=0, bytes_accessed=11 << 20, transcendentals=0),
         compiler_params=pltpu.CompilerParams(vmem_limit_bytes=VMEM),
         name="head_sum",
-    )(meta, *ea, *eb, ra, rb)
+    )(meta, exps, ratio)
 
 
 def key_places(meta):
@@ -204,25 +216,11 @@
 JSTEP = 8
 
 
-def forward_kernel(spans, meta, *refs):
-    n = len(spans)
-    ia, ib, wa, wb, wja, wjb, keys, logits, stats = refs[n:]
-    blocks = [ref.at[at : at + HALF, 0:DI] for ref, span in zip(refs, spans) for at in range(0, span, HALF)]
+def forward_kernel(meta, keys, ia, ib, wa, wb, wja, wjb, logits, stats):
     step = pl.program_id(0)
 
     @pl.when(step == 0)
     def _():
-        quarter = meta[34]
-        for i in range(BLOCKS):
-            slot = meta[BLOCKS + i]
-            mine = pl.ds(pl.multiple_of(quarter * UNIT, UNIT), UNIT)
-            keys[pl.ds(pl.multiple_of(slot * UNIT, UNIT), UNIT), :] = blocks[i][mine, :]
-
-            @pl.when((slot & 3) == quarter)
-            def _():
-                extra = pl.multiple_of(256 + (slot >> 2) * UNIT, UNIT)
-                keys[pl.ds(extra, UNIT), :] = blocks[i][4 * UNIT :, :]
-
         logits[...] = jnp.zeros_like(logits)
 
     total = logits[...]
@@ -257,19 +255,17 @@
     return whole, [queries, queries, whole((72, 128)), whole((72, 128)), weights, weights]
 
 
-def forward_call(meta, blocks, ia, ib, wa, wb):
+def forward_call(meta, keys, ia, ib, wa, wb):
     whole, specs = j_specs()
-    spans = [block.shape[0] for block in blocks]
     return pl.pallas_call(
-        lambda *refs: forward_kernel(spans, *refs),
+        forward_kernel,
         grid_spec=pltpu.PrefetchScalarGridSpec(
             num_scalar_prefetch=1,
             grid=(NI // JSTEP,),
-            in_specs=[whole(block.shape) for block in blocks] + specs,
-            out_specs=[whole((ROWS, DI)), whole((ROWS, 256)), whole((8, 256))],
+            in_specs=[whole((ROWS, DI))] + specs,
+            out_specs=[whole((ROWS, 256)), whole((8, 256))],
         ),
         out_shape=[
-            jax.ShapeDtypeStruct((ROWS, DI), jnp.bfloat16),
             jax.ShapeDtypeStruct((ROWS, 256), jnp.float32),
             jax.ShapeDtypeStruct((8, 256), jnp.float32),
         ],
@@ -278,21 +274,22 @@
         ),
         compiler_params=pltpu.CompilerParams(vmem_limit_bytes=VMEM),
         name="index_forward",
-    )(meta, *blocks, ia, ib, wa, wb, wa, wb)
-
-
-def backward_kernel(meta, keys, logits, stats, t0, t1, t2, t3, ia, ib, wa, wb, wja, wjb, wg, div, kg, grad, acc):
+    )(meta, keys, ia, ib, wa, wb, wa, wb)
+
+
+def backward_kernel(meta, keys, logits, s0, s1, s2, s3, t0, t1, t2, t3, ia, ib, wa, wb, wja, wjb, wg, div, kg, grad, acc):
     step = pl.program_id(0)
 
     @pl.when(step == 0)
     def _():
-        tops = [stats[d, 0:1, :] for d in range(8)]
+        stats = (s0, s1, s2, s3)
+        tops = [part[0:1, :] for part in stats]
         top = tops[0]
-        for d in range(1, 8):
-            top = jnp.maximum(top, tops[d])
+        for other in tops[1:]:
+            top = jnp.maximum(top, other)
         total = jnp.zeros((1, 256), jnp.float32)
-        for d in range(8):
-            total = total + stats[d, 1:2, :] * jnp.exp(tops[d] - top)
+        for part, other in zip(stats, tops):
+            total = total + part[1:2, :] * jnp.exp(other - top)
         norm = top + jnp.log(total)
         goal = jnp.zeros((ROWS, 256), jnp.float32)
         for part in (t0, t1, t2, t3):
@@ -339,8 +336,8 @@
             in_specs=[
                 whole((ROWS, DI)),
                 whole((ROWS, 256)),
-                whole((8, 8, 256)),
             ]
+            + [whole((8, 256))] * 4
             + [whole((ROWS, 256))] * 4
             + specs,
             out_specs=[
@@ -363,12 +360,18 @@
         ),
         compiler_params=pltpu.CompilerParams(vmem_limit_bytes=VMEM),
         name="index_backward",
-    )(meta, keys, logits, stats, *target, ia, ib, wa, wb, wa, wb)
+    )(meta, keys, logits, *stats, *target, ia, ib, wa, wb, wa, wb)
 
 
 def merge(m0, l0, m1, l1):
     top = jnp.maximum(m0, m1)
     return top, l0 * jnp.exp2((m0 - top) * SCORE2) + l1 * jnp.exp2((m1 - top) * SCORE2)
+
+
+def merge_rows(a, b):
+    top = jnp.maximum(a[0:1], b[0:1])
+    total = a[1:2] * jnp.exp(a[0:1] - top) + b[1:2] * jnp.exp(b[0:1] - top)
+    return jnp.concatenate([top, total, jnp.zeros((6, 256), jnp.float32)])
 
 
 def swap_halves(value):
@@ -399,25 +402,23 @@
 
     queries = main_queries.transpose(0, 2, 1)
     f1, b1 = shift(own, dz=1), shift(own, dz=7)
-    near_a, near_b = shift(queries[:4], dx=1), shift(queries[4:], dx=3)
+    left, right = shift(queries[:4], dx=1), shift(queries[4:], dx=3)
     wb = swap_core(wa)
     queries_far = swap_core(queries)
     y0 = shift(own, dy=1)
     f2, b2 = shift(f1, dz=1), shift(b1, dz=7)
     y1 = shift(jnp.concatenate([f1, b1]), dy=3)
-    f2, b2 = lax.optimization_barrier((f2, b2, y0))[:2]
+    ia = after(index_queries, f1).transpose(1, 0, 2)
+    ib = swap_core(ia)
     f3, b3 = shift(f2, dz=1), shift(b2, dz=7)
     y2 = shift(jnp.concatenate([f2, b2]), dy=1)
-    near_a, near_b = lax.optimization_barrier((near_a, near_b, f2))[:2]
-    near_a_far, near_b_far = swap_core(near_a), swap_core(near_b)
-    f3, b3 = lax.optimization_barrier((f3, b3, y1))[:2]
+    left, right = lax.optimization_barrier((left, right, f3))[:2]
+    left_far, right_far = swap_core(left), swap_core(right)
     f4 = shift(f3, dz=1)
     y3 = shift(jnp.concatenate([f3, b3]), dy=3)
     y4 = shift(f4, dy=1)
-    ia = after(index_queries, f4).transpose(1, 0, 2)
-    ib = swap_core(ia)
     column = [(0, own), (-1, f1), (1, b1), (-2, f2), (2, b2), (-3, f3), (3, b3), (-4, f4)]
-    blocks = [[block for _, block in column], [y0, y1, y2, y3, y4]]
+    blocks = [block for _, block in column] + [y0, y1, y2, y3, y4]
 
     steps = jnp.asarray([dz for dz, _ in column] * 2, dtype=jnp.int32)
     zs = (z + 8 + steps) % 8
@@ -427,49 +428,44 @@
         [bases, zs * 2 + ys, jnp.stack([core, half, quarter])]
     ).astype(jnp.int32)
 
-    near = [(near_a, near_a_far), (near_b, near_b_far)]
-
-    def score(c, g, weights):
-        return score_call(
-            meta, 8 * c, blocks[c], g, queries, queries_far, *near[g], weights, wb
-        )
-
-    early = [score(0, g, wa) for g in range(2)]
-    late = [score(1, 0, wa)]
-    keys, logits, stats = forward_call(meta, blocks[0] + blocks[1], ia, ib, after(wa, late[0][1]), wb)
-    late.append(score(1, 1, after(wa, stats)))
-
-    ratios = []
-    for g in range(2):
-        (_, m0, l0), (_, m1, l1) = early[g], late[g]
-        m, l = merge(m0[:, 0], l0[:, 0], m1[:, 0], l1[:, 0])
-        away = swap_core(swap_halves(jnp.stack([m, l])))
-        m, l = merge(m, l, away[0], away[1])
-        ours = jnp.stack([m, l])
-        out, back = (1, 3) if g == 0 else (3, 1)
-        theirs = jnp.concatenate([shift(ours[:, 4:], dx=back), shift(ours[:, :4], dx=out)], axis=1)
-        top, total = merge(m, l, theirs[0], theirs[1])
-        ratios.append(jnp.stack([jnp.exp2((v - top[:, None]) * SCORE2) / total[:, None] for v in (m0, m1)]))
-    sums = head_sum_call(meta, [early[0][0], late[0][0]], [early[1][0], late[1][0]], *ratios)
-    target = [sums[0], shift(sums[1], dx=2), shift(sums[2], dy=2), shift(sums[3], dx=2, dy=2)]
-
-    far = swap_core(swap_halves(stats))
-    itop = jnp.maximum(stats[0], far[0])
-    isum = stats[1] * jnp.exp(stats[0] - itop) + far[1] * jnp.exp(far[0] - itop)
-    istats = jnp.concatenate([itop[None], isum[None], jnp.zeros((6, 256), jnp.float32)], axis=0)
-    istats = gather_head(istats)
+    exps, m0, l0, keys = score_call(
+        meta, blocks, queries, queries_far, left, left_far, right, right_far, wa, wb
+    )
+    m0, l0 = m0[:, 0], l0[:, 0]
+
+    away = swap_core(swap_halves(jnp.stack([m0, l0])))
+    m, l = merge(m0, l0, away[0], away[1])
+    ours = jnp.stack([m, l])
+    up = shift(jnp.concatenate([ours[:, 0:4], ours[:, 12:16]], axis=1), dx=1)
+    down = shift(ours[:, 4:12], dx=3)
+    theirs = jnp.concatenate([down[:, 4:], up[:, 4:], up[:, :4], down[:, :4]], axis=1)
+    top, total = merge(m, l, theirs[0], theirs[1])
+    ratio = (jnp.exp2((m0 - top) * SCORE2) / total)[:, None]
+
+    logits, stats = forward_call(meta, keys, ia, ib, wa, wb)
+    stats = merge_rows(stats, swap_core(swap_halves(stats)))
+    stats = merge_rows(stats, shift(stats, dx=3))
+
+    sums = head_sum_call(meta, exps, ratio)
+    group = (dict(dx=2), dict(dy=2), dict(dx=2, dy=2))
+    target = [sums[0]] + [shift(part, **move) for part, move in zip(sums[1:], group)]
+    istats = [stats] + [shift(stats, **move) for move in group]
 
     wg, div, kg = backward_call(meta, keys, logits, istats, target, ia, ib, wa, wb)
     rows_out = jnp.concatenate([wg, div], axis=0)
     rows_out = rows_out[:, :128] + swap_core(rows_out[:, 128:])
-    rows_sum = jnp.sum(gather_head(rows_out), axis=0)
+    rows_high = lax.reduce_precision(rows_out, 8, 7)
+    tail = rows_high[NI : NI + 1]
+    tail = jnp.concatenate([rows_high, rows_out[NI : NI + 1] - tail, jnp.zeros((7, 128), jnp.float32)])
     kg = lax.all_to_all(kg, ("z", "ylo"), 0, 0, tiled=True)
-    kg = jnp.sum(kg.astype(jnp.float32), axis=0).astype(jnp.bfloat16)
-    pieces = gather_head(kg).astype(jnp.float32).reshape(4, 2, 2 * UNIT, DI)
+    kg = jnp.sum(kg.astype(jnp.float32), axis=0)
+    last = gather_head(jnp.concatenate([kg, tail]).astype(jnp.bfloat16)).astype(jnp.float32)
+    rows_sum = jnp.sum(last[:, 2 * UNIT :], axis=0)
+    pieces = last[:, : 2 * UNIT].reshape(4, 2, 2 * UNIT, DI)
     main = pieces[:, :, :UNIT].transpose(1, 0, 2, 3).reshape(2, 4 * UNIT, DI)
     extra = jnp.sum(pieces[:, :, UNIT:], axis=0)
     key_grad = jnp.concatenate([main, extra], axis=1).reshape(160, DI)
-    return rows_sum[NI], rows_sum[:NI].T, key_grad
+    return rows_sum[NI] + rows_sum[NI + 8], rows_sum[:NI].T, key_grad
 
 
 def solution(mesh):

time: 174 us -> 148 us (0.85)
  Pallas kernels: 47 us -> 36.9 us
  waiting for transfers between devices: 47.1 us -> 38.2 us
  starting transfers between devices: 51.6 us -> 44.5 us
    all_to_all x2 -> x0, waiting for transfers between devices: 13.3 us -> none  [gather_head(): return lax.all_to_all(wide, ('yhi', 'xh', 'xp'), 0, 0, tiled=True)]
    pallas_call x5 -> x2, Pallas kernels: 33.1 us -> 23.5 us  [the longest x1 18.6 us: score_call(): pl.pallas_call(lambda *refs: score_kernel(spans, *refs), grid_spec=pltpu....]
    all_to_all x2 -> x0, starting transfers between devices: 9.03 us -> none  [gather_head(): return lax.all_to_all(wide, ('yhi', 'xh', 'xp'), 0, 0, tiled=True)]
    ppermute x30 -> x31, waiting for transfers between devices: 23.6 us -> 28.1 us  [shift(): return lax.ppermute(value, ALL, pairs)]
    ppermute x30 -> x31, starting transfers between devices: 36.4 us -> 38.4 us  [shift(): return lax.ppermute(value, ALL, pairs)]
  transfers between devices with their start and end apart: 33 -> 32, of which waited for: 14 -> 13; matrix products, arithmetic and copies ran while one was open for 5% -> 6% of each run, Pallas kernels for 12% -> 15%
where the time goes in v3:
time: 148 us
  starting transfers between devices  44.5 us (30%)
  waiting for transfers between devices  38.2 us (26%)
  Pallas kernels  36.9 us (25%)
  blocking collectives  14.7 us (10%)
  local copies, waits for them, and re-layouts  6.53 us (4%)
  other arithmetic  5.12 us (3%)
  between operations  1.67 us (1%)
    ppermute x31, starting transfers between devices, shift(): return lax.ppermute(value, ALL, pairs)  38.4 us
    ppermute x31, waiting for transfers between devices, shift(): return lax.ppermute(value, ALL, pairs)  28.1 us
    pallas_call x1, Pallas kernels, score_call(): pl.pallas_call(lambda *refs: score_kernel(spans, *refs), grid_spec=pltpu....  18.6 us
    all_to_all x1, blocking collectives, gather_head(): return lax.all_to_all(wide, ('yhi', 'xh', 'xp'), 0, 0, tiled=True)  14.7 us
    all_to_all x1, waiting for transfers between devices, body(): kg = lax.all_to_all(kg, ('z', 'ylo'), 0, 0, tiled=True)  10.2 us
    pallas_call x1, Pallas kernels, backward_call(): pl.pallas_call(backward_kernel, grid_spec=pltpu.PrefetchScalarGridSpec(nu...  9.46 us
    all_to_all x1, starting transfers between devices, body(): kg = lax.all_to_all(kg, ('z', 'ylo'), 0, 0, tiled=True)  6.17 us
    pallas_call x1, Pallas kernels, forward_call(): pl.pallas_call(forward_kernel, grid_spec=pltpu.PrefetchScalarGridSpec(num...  4.93 us
  transfers between devices with their start and end apart: 32, of which 13 were waited for; matrix products, arithmetic and copies ran while one was open for 6% of the time, Pallas kernels for 15%

profile of v3, /device:TPU:2, one launch (start us, length us, event | category | flops | bytes accessed | tf_op | source)
XLA Modules:
  0.0 147.7 jit_solution(16579086804196989754)
XLA Ops:
  1.6 2.0 %collective-permute-start = (bf16[80,704]{1,0:T(8,128)(2,1)S(1)}, bf16[80,704]{1,0:T(8,128)(2,1)S(1)}, u32[]{:S(2)}, u32[]{:S(2)}) collective-permute-start(bf16[80,704]{1,0:T(8,128)(2,1)S(1)} %fusion.refs_1_), channel_id=1, source_target_pairs={{0,4},{1,5},{4,8},{5,9},{8,12},{9,13},{12,16},{13,17},{16,20},{17,... | collective-permute-start | bytes 337928 | tf_op jit(solution)/shard_map/ppermute | solution.py:39
  3.6 4.0 %collective-permute-start.1 = (bf16[80,704]{1,0:T(8,128)(2,1)S(1)}, bf16[80,704]{1,0:T(8,128)(2,1)S(1)}, u32[]{:S(2)}, u32[]{:S(2)}) collective-permute-start(bf16[80,704]{1,0:T(8,128)(2,1)S(1)} %fusion.refs_1_), channel_id=1, source_target_pairs={{0,28},{1,29},{4,0},{5,1},{8,4},{9,5},{12,8},{13,9},{16,12},{17,13... | collective-permute-start | bytes 337928 | tf_op jit(solution)/shard_map/ppermute | solution.py:39
  7.7 2.4 %fusion.23 = (bf16[4,576,128]{2,1,0:T(8,128)(2,1)}, bf16[4,576,128]{2,1,0:T(8,128)(2,1)}) fusion(bf16[8,576,128]{2,1,0:T(8,128)(2,1)} %bitcast.65), kind=kLoop, calls=%fused_computation.73 | loop fusion | bytes 2359296 | tf_op jit(solution)/shard_map/slice | solution.py:405
  13.0 3.2 %collective-permute-start.3 = (bf16[80,704]{1,0:T(8,128)(2,1)S(1)}, bf16[80,704]{1,0:T(8,128)(2,1)S(1)}, u32[]{:S(2)}, u32[]{:S(2)}) collective-permute-start(bf16[80,704]{1,0:T(8,128)(2,1)S(1)} %collective-permute-done.1.refs_3_), channel_id=1, source_target_pairs={{0,28},{1,29},{4,0},{5,1},{8,4},{9,5},{12,8},{13,9},{16,12},{17,13... | collective-permute-start | bytes 337928 | tf_op jit(solution)/shard_map/ppermute | solution.py:39
  16.3 2.9 %collective-permute-done.2.refs_4_ = bf16[80,704]{1,0:T(8,128)(2,1)S(1)} collective-permute-done((bf16[80,704]{1,0:T(8,128)(2,1)S(1)}, bf16[80,704]{1,0:T(8,128)(2,1)S(1)}, u32[]{:S(2)}, u32[]{:S(2)}) %collective-permute-start.2) | collective-permute-done | bytes 112672 | tf_op jit(solution)/shard_map/ppermute | solution.py:39
  20.9 4.3 %collective-permute-done.4.refs_6_ = bf16[80,704]{1,0:T(8,128)(2,1)S(1)} collective-permute-done((bf16[80,704]{1,0:T(8,128)(2,1)S(1)}, bf16[80,704]{1,0:T(8,128)(2,1)S(1)}, u32[]{:S(2)}, u32[]{:S(2)}) %collective-permute-start.4) | collective-permute-done | bytes 112672 | tf_op jit(solution)/shard_map/ppermute | solution.py:39
  26.0 3.0 %collective-permute-start.8 = (bf16[160,704]{1,0:T(8,128)(2,1)}, bf16[160,704]{1,0:T(8,128)(2,1)S(1)}, u32[]{:S(2)}, u32[]{:S(2)}) collective-permute-start(bf16[160,704]{1,0:T(8,128)(2,1)} %pad_maximum_fusion), channel_id=1, source_target_pairs={{0,130},{1,131},{4,134},{5,135},{8,138},{9,139},{12,142},{13,143},... | collective-permute-start | bytes 675848 | tf_op jit(solution)/shard_map/ppermute | solution.py:39
  29.0 1.9 %collective-permute-start.5 = (bf16[80,704]{1,0:T(8,128)(2,1)S(1)}, bf16[80,704]{1,0:T(8,128)(2,1)S(1)}, u32[]{:S(2)}, u32[]{:S(2)}) collective-permute-start(bf16[80,704]{1,0:T(8,128)(2,1)S(1)} %collective-permute-done.3.refs_5_), channel_id=1, source_target_pairs={{0,28},{1,29},{4,0},{5,1},{8,4},{9,5},{12,8},{13,9},{16,12},{17,13... | collective-permute-start | bytes 337928 | tf_op jit(solution)/shard_map/ppermute | solution.py:39
  32.1 2.3 %collective-permute-done.5.refs_7_ = bf16[80,704]{1,0:T(8,128)(2,1)S(1)} collective-permute-done((bf16[80,704]{1,0:T(8,128)(2,1)S(1)}, bf16[80,704]{1,0:T(8,128)(2,1)S(1)}, u32[]{:S(2)}, u32[]{:S(2)}) %collective-permute-start.5) | collective-permute-done | bytes 112672 | tf_op jit(solution)/shard_map/ppermute | solution.py:39
  35.9 7.3 %collective-permute-done.9.refs_11_ = bf16[160,704]{1,0:T(8,128)(2,1)} collective-permute-done((bf16[160,704]{1,0:T(8,128)(2,1)}, bf16[160,704]{1,0:T(8,128)(2,1)}, u32[]{:S(2)}, u32[]{:S(2)}) %collective-permute-start.9) | collective-permute-done | bytes 225312 | tf_op jit(solution)/shard_map/ppermute | solution.py:39
  43.2 2.0 %collective-permute-start.11 = (bf16[80,704]{1,0:T(8,128)(2,1)}, bf16[80,704]{1,0:T(8,128)(2,1)}, u32[]{:S(2)}, u32[]{:S(2)}) collective-permute-start(bf16[80,704]{1,0:T(8,128)(2,1)} %collective-permute-done.6.refs_8_), channel_id=1, source_target_pairs={{0,2},{1,3},{4,6},{5,7},{8,10},{9,11},{12,14},{13,15},{16,18},{17,... | collective-permute-start | bytes 337928 | tf_op jit(solution)/shard_map/ppermute | solution.py:39
  45.4 3.0 %copy.17 = bf16[128,64,128]{2,0,1:T(8,128)(2,1)S(1)} copy(bf16[128,64,128]{2,1,0:T(8,128)(2,1)} %param.11) | data formatting | bytes 4194304 | tf_op jit(solution)/shard_map/optimization_barrier | solution.py:387
  50.0 18.6 %scores.1 = (bf16[16,1280,256]{2,1,0:T(8,128)(2,1)S(1)}, f32[16,1,256]{2,1,0:T(1,128)S(1)}, f32[16,1,256]{2,1,0:T(1,128)S(1)}, bf16[320,128]{1,0:T(8,128)(2,1)S(1)}) custom-call(s32[35]{0:T(128)S(1)} %concatenate.50.refs_0_.meta, bf16[80,704]{1,0:T(8,128)(2,1)S(1)} %fusion.refs_1_, bf16[80,704]{1,0:T(8,128)(2,1)S(1)} %collective-permute-done.refs_2_, ...), custom_call_target="tpu_custom_call" | custom-call | flops 12079595520 | bytes 10485760 | tf_op jit(solution)/shard_map/scores/pallas_call | solution.py:123
  74.1 1.9 %collective-permute-done.26 = f32[2,8,256]{2,0,1:T(2,128)S(1)} collective-permute-done((f32[2,8,256]{2,0,1:T(2,128)S(1)}, f32[2,8,256]{2,0,1:T(2,128)S(1)}, u32[]{:S(2)}, u32[]{:S(2)}) %collective-permute-start.26) | collective-permute-done | bytes 16416 | tf_op jit(solution)/shard_map/ppermute | solution.py:39
  75.9 4.9 %index_forward.1 = (f32[320,256]{1,0:T(8,128)S(1)}, f32[8,256]{1,0:T(8,128)S(1)}) custom-call(s32[35]{0:T(128)S(1)} %concatenate.50.refs_0_.meta, bf16[320,128]{1,0:T(8,128)(2,1)S(1)} %get-tuple-element.21.keys, bf16[64,128,128]{2,1,0:T(8,128)(2,1)S(1)} %bitcast.62, bf16[64,128,128]{2,1,0:T(8,128)(2,1)S(1)} %collective-permute-done.18.ib, ...), custom_call_target="tpu_custom_call" | custom-call | flops 1342177280 | bytes 5242880 | tf_op jit(solution)/shard_map/index_forward/pallas_call | solution.py:260
  82.2 2.7 %collective-permute-start.20 = (f32[8,256]{1,0:T(8,128)S(1)}, f32[8,256]{1,0:T(8,128)S(1)}, u32[]{:S(2)}, u32[]{:S(2)}) collective-permute-start(f32[8,256]{1,0:T(8,128)S(1)} %maximum_maximum_fusion.2), channel_id=1, source_target_pairs={{0,96},{1,97},{4,100},{5,101},{8,104},{9,105},{12,108},{13,109},{1... | collective-permute-start | bytes 24584 | tf_op jit(solution)/shard_map/ppermute | solution.py:39
  85.1 3.9 %head_sum.1 = (bf16[320,256]{1,0:T(8,128)(2,1)S(1)}, bf16[320,256]{1,0:T(8,128)(2,1)S(1)}, bf16[320,256]{1,0:T(8,128)(2,1)S(1)}, bf16[320,256]{1,0:T(8,128)(2,1)S(1)}) custom-call(s32[35]{0:T(128)S(1)} %concatenate.50.refs_0_.meta, bf16[16,1280,256]{2,1,0:T(8,128)(2,1)S(1)} %get-tuple-element.25.e_ref, f32[16,1,256]{2,1,0:T(1,128)S(1)} %fusion.6.r_ref), custom_call_target="tpu_custom_call" | custom-call | bytes 11534336 | tf_op jit(solution)/shard_map/head_sum/pallas_call | solution.py:181
  89.7 5.9 %collective-permute-start.29 = (bf16[320,256]{1,0:T(8,128)(2,1)S(1)}, bf16[320,256]{1,0:T(8,128)(2,1)S(1)}, u32[]{:S(2)}, u32[]{:S(2)}) collective-permute-start(bf16[320,256]{1,0:T(8,128)(2,1)S(1)} %get-tuple-element.31), channel_id=1, source_target_pairs={{0,192},{1,193},{4,196},{5,197},{8,200},{9,201},{12,204},{13,205},... | collective-permute-start | bytes 491528 | tf_op jit(solution)/shard_map/ppermute | solution.py:39
  97.3 5.0 %collective-permute-start.23 = (f32[8,256]{1,0:T(8,128)S(1)}, f32[8,256]{1,0:T(8,128)S(1)}, u32[]{:S(2)}, u32[]{:S(2)}) collective-permute-start(f32[8,256]{1,0:T(8,128)S(1)} %maximum_maximum_fusion.3.s0), channel_id=1, source_target_pairs={{0,192},{1,193},{4,196},{5,197},{8,200},{9,201},{12,204},{13,205},... | collective-permute-start | bytes 24584 | tf_op jit(solution)/shard_map/ppermute | solution.py:39
  102.3 2.6 %collective-permute-done.23.s3 = f32[8,256]{1,0:T(8,128)S(1)} collective-permute-done((f32[8,256]{1,0:T(8,128)S(1)}, f32[8,256]{1,0:T(8,128)S(1)}, u32[]{:S(2)}, u32[]{:S(2)}) %collective-permute-start.23) | collective-permute-done | bytes 8224 | tf_op jit(solution)/shard_map/ppermute | solution.py:39
  104.8 9.5 %index_backward.1 = (f32[64,256]{1,0:T(8,128)S(1)}, f32[8,256]{1,0:T(8,128)S(1)}, bf16[16,32,128]{2,1,0:T(8,128)(2,1)}) custom-call(s32[35]{0:T(128)S(1)} %concatenate.50.refs_0_.meta, bf16[320,128]{1,0:T(8,128)(2,1)S(1)} %get-tuple-element.21.keys, f32[320,256]{1,0:T(8,128)S(1)} %get-tuple-element.23.logits, f32[8,256]{1,0:T(8,128)S(1)} %maximum_maximum_fusion.3.s0, ...), custom_call_target="tpu_custom_call" | custom-call | flops 2684354560 | bytes 6291456 | tf_op jit(solution)/shard_map/index_backward/pallas_call | solution.py:331
  114.5 6.2 %all-to-all-start = ((bf16[16,32,128]{2,1,0:T(8,128)(2,1)}), bf16[16,32,128]{2,1,0:T(8,128)(2,1)S(1)}, u32[]{:S(2)}, u32[]{:S(2)}) async-start(bf16[16,32,128]{2,1,0:T(8,128)(2,1)} %get-tuple-element.32), calls=%async_computation | async-start | bytes 262144 | tf_op jit(solution)/shard_map/all_to_all | solution.py:460
  120.7 10.2 %all-to-all-done = bf16[16,32,128]{2,1,0:T(8,128)(2,1)S(1)} async-done(((bf16[16,32,128]{2,1,0:T(8,128)(2,1)}), bf16[16,32,128]{2,1,0:T(8,128)(2,1)S(1)}, u32[]{:S(2)}, u32[]{:S(2)}) %all-to-all-start) | async-done | bytes 131104 | tf_op jit(solution)/shard_map/all_to_all | solution.py:460
  131.1 14.7 %all_to_all.10 = bf16[8,112,128]{2,1,0:T(8,128)(2,1)S(1)} all-to-all(bf16[8,112,128]{2,1,0:T(8,128)(2,1)S(1)} %broadcast_in_dim.2), channel_id=1, replica_groups=mesh['yhi'=2,'xh'=2,'xp'=2,'z'=8,'ylo'=2,'core'=2] {'yhi','xh','xp'}, dimensions={0} | all-to-all | bytes 458752 | tf_op jit(solution)/shard_map/all_to_all | solution.py:383
  (110 shorter events, 21.5 us)
Async XLA Ops:
  1.6 11.1 %collective-permute-start = (bf16[80,704]{1,0:T(8,128)(2,1)S(1)}, bf16[80,704]{1,0:T(8,128)(2,1)S(1)}, u32[]{:S(2)}, u32[]{:S(2)}) collective-permute-start(bf16[80,704]{1,0:T(8,128)(2,1)S(1)} %fusion.refs_1_), channel_id=1, source_target_pairs={{0,4},{1,5},{4,8},{5,9},{8,12},{9,13},{12,16},{13,17},{16,20},{17,... | collective-permute-start | bytes 337928 | tf_op jit(solution)/shard_map/ppermute | solution.py:39
  3.6 9.4 %collective-permute-start.1 = (bf16[80,704]{1,0:T(8,128)(2,1)S(1)}, bf16[80,704]{1,0:T(8,128)(2,1)S(1)}, u32[]{:S(2)}, u32[]{:S(2)}) collective-permute-start(bf16[80,704]{1,0:T(8,128)(2,1)S(1)} %fusion.refs_1_), channel_id=1, source_target_pairs={{0,28},{1,29},{4,0},{5,1},{8,4},{9,5},{12,8},{13,9},{16,12},{17,13... | collective-permute-start | bytes 337928 | tf_op jit(solution)/shard_map/ppermute | solution.py:39
  7.6 42.3 %collective-permute-start.12 = (bf16[8,576,128]{2,1,0:T(8,128)(2,1)}, bf16[8,576,128]{2,1,0:T(8,128)(2,1)S(1)}, u32[]{:S(2)}, u32[]{:S(2)}) collective-permute-start(bf16[8,576,128]{2,1,0:T(8,128)(2,1)} %bitcast.64), channel_id=1, source_target_pairs={{0,1},{1,0},{4,5},{5,4},{8,9},{9,8},{12,13},{13,12},{16,17},{17,16... | collective-permute-start | bytes 3538952 | tf_op jit(solution)/shard_map/ppermute | solution.py:39
  10.0 16.0 %collective-permute-start.13 = (bf16[4,576,128]{2,1,0:T(8,128)(2,1)}, bf16[4,576,128]{2,1,0:T(8,128)(2,1)S(1)}, u32[]{:S(2)}, u32[]{:S(2)}) collective-permute-start(bf16[4,576,128]{2,1,0:T(8,128)(2,1)} %get-tuple-element.42), channel_id=1, source_target_pairs={{0,32},{1,33},{4,36},{5,37},{8,40},{9,41},{12,44},{13,45},{16,48},... | collective-permute-start | bytes 1769480 | tf_op jit(solution)/shard_map/ppermute | solution.py:39
  11.5 17.5 %collective-permute-start.14 = (bf16[4,576,128]{2,1,0:T(8,128)(2,1)}, bf16[4,576,128]{2,1,0:T(8,128)(2,1)S(1)}, u32[]{:S(2)}, u32[]{:S(2)}) collective-permute-start(bf16[4,576,128]{2,1,0:T(8,128)(2,1)} %get-tuple-element.41), channel_id=1, source_target_pairs={{0,96},{1,97},{4,100},{5,101},{8,104},{9,105},{12,108},{13,109},{1... | collective-permute-start | bytes 1769480 | tf_op jit(solution)/shard_map/ppermute | solution.py:39
  12.7 6.5 %collective-permute-start.2 = (bf16[80,704]{1,0:T(8,128)(2,1)S(1)}, bf16[80,704]{1,0:T(8,128)(2,1)S(1)}, u32[]{:S(2)}, u32[]{:S(2)}) collective-permute-start(bf16[80,704]{1,0:T(8,128)(2,1)S(1)} %collective-permute-done.refs_2_), channel_id=1, source_target_pairs={{0,4},{1,5},{4,8},{5,9},{8,12},{9,13},{12,16},{13,17},{16,20},{17,... | collective-permute-start | bytes 337928 | tf_op jit(solution)/shard_map/ppermute | solution.py:39
  19.3 11.7 %collective-permute-start.7 = (bf16[80,704]{1,0:T(8,128)(2,1)S(1)}, bf16[80,704]{1,0:T(8,128)(2,1)S(1)}, u32[]{:S(2)}, u32[]{:S(2)}) collective-permute-start(bf16[80,704]{1,0:T(8,128)(2,1)S(1)} %fusion.refs_1_), channel_id=1, source_target_pairs={{0,2},{1,3},{4,6},{5,7},{8,10},{9,11},{12,14},{13,15},{16,18},{17,... | collective-permute-start | bytes 337928 | tf_op jit(solution)/shard_map/ppermute | solution.py:39
  26.0 9.2 %collective-permute-start.8 = (bf16[160,704]{1,0:T(8,128)(2,1)}, bf16[160,704]{1,0:T(8,128)(2,1)S(1)}, u32[]{:S(2)}, u32[]{:S(2)}) collective-permute-start(bf16[160,704]{1,0:T(8,128)(2,1)} %pad_maximum_fusion), channel_id=1, source_target_pairs={{0,130},{1,131},{4,134},{5,135},{8,138},{9,139},{12,142},{13,143},... | collective-permute-start | bytes 675848 | tf_op jit(solution)/shard_map/ppermute | solution.py:39
  30.9 19.0 %collective-permute-start.15 = (bf16[4,576,128]{2,1,0:T(8,128)(2,1)S(1)}, bf16[4,576,128]{2,1,0:T(8,128)(2,1)}, u32[]{:S(2)}, u32[]{:S(2)}) collective-permute-start(bf16[4,576,128]{2,1,0:T(8,128)(2,1)S(1)} %collective-permute-done.13.refs_16_), channel_id=1, source_target_pairs={{0,1},{1,0},{4,5},{5,4},{8,9},{9,8},{12,13},{13,12},{16,17},{17,16... | collective-permute-start | bytes 1769480 | tf_op jit(solution)/shard_map/ppermute | solution.py:39
  30.9 19.0 %collective-permute-start.16 = (bf16[4,576,128]{2,1,0:T(8,128)(2,1)S(1)}, bf16[4,576,128]{2,1,0:T(8,128)(2,1)}, u32[]{:S(2)}, u32[]{:S(2)}) collective-permute-start(bf16[4,576,128]{2,1,0:T(8,128)(2,1)S(1)} %collective-permute-done.14.refs_18_), channel_id=1, source_target_pairs={{0,1},{1,0},{4,5},{5,4},{8,9},{9,8},{12,13},{13,12},{16,17},{17,16... | collective-permute-start | bytes 1769480 | tf_op jit(solution)/shard_map/ppermute | solution.py:39
  34.4 8.8 %collective-permute-start.9 = (bf16[160,704]{1,0:T(8,128)(2,1)}, bf16[160,704]{1,0:T(8,128)(2,1)}, u32[]{:S(2)}, u32[]{:S(2)}) collective-permute-start(bf16[160,704]{1,0:T(8,128)(2,1)} %pad_maximum_fusion.1), channel_id=1, source_target_pairs={{0,2},{1,3},{4,6},{5,7},{8,10},{9,11},{12,14},{13,15},{16,18},{17,... | collective-permute-start | bytes 675848 | tf_op jit(solution)/shard_map/ppermute | solution.py:39
  35.2 8.1 %collective-permute-start.6 = (bf16[80,704]{1,0:T(8,128)(2,1)S(1)}, bf16[80,704]{1,0:T(8,128)(2,1)}, u32[]{:S(2)}, u32[]{:S(2)}) collective-permute-start(bf16[80,704]{1,0:T(8,128)(2,1)S(1)} %collective-permute-done.4.refs_6_), channel_id=1, source_target_pairs={{0,4},{1,5},{4,8},{5,9},{8,12},{9,13},{12,16},{13,17},{16,20},{17,... | collective-permute-start | bytes 337928 | tf_op jit(solution)/shard_map/ppermute | solution.py:39
  43.2 6.7 %collective-permute-start.10 = (bf16[160,704]{1,0:T(8,128)(2,1)}, bf16[160,704]{1,0:T(8,128)(2,1)}, u32[]{:S(2)}, u32[]{:S(2)}) collective-permute-start(bf16[160,704]{1,0:T(8,128)(2,1)} %pad_maximum_fusion.2), channel_id=1, source_target_pairs={{0,130},{1,131},{4,134},{5,135},{8,138},{9,139},{12,142},{13,143},... | collective-permute-start | bytes 675848 | tf_op jit(solution)/shard_map/ppermute | solution.py:39
  43.2 6.7 %collective-permute-start.11 = (bf16[80,704]{1,0:T(8,128)(2,1)}, bf16[80,704]{1,0:T(8,128)(2,1)}, u32[]{:S(2)}, u32[]{:S(2)}) collective-permute-start(bf16[80,704]{1,0:T(8,128)(2,1)} %collective-permute-done.6.refs_8_), channel_id=1, source_target_pairs={{0,2},{1,3},{4,6},{5,7},{8,10},{9,11},{12,14},{13,15},{16,18},{17,... | collective-permute-start | bytes 337928 | tf_op jit(solution)/shard_map/ppermute | solution.py:39
  49.9 26.0 %collective-permute-start.18 = (bf16[64,128,128]{2,1,0:T(8,128)(2,1)S(1)}, bf16[64,128,128]{2,1,0:T(8,128)(2,1)S(1)}, u32[]{:S(2)}, u32[]{:S(2)}) collective-permute-start(bf16[64,128,128]{2,1,0:T(8,128)(2,1)S(1)} %bitcast.61), channel_id=1, source_target_pairs={{0,1},{1,0},{4,5},{5,4},{8,9},{9,8},{12,13},{13,12},{16,17},{17,16... | collective-permute-start | bytes 6291464 | tf_op jit(solution)/shard_map/ppermute | solution.py:39
  82.2 13.4 %collective-permute-start.20 = (f32[8,256]{1,0:T(8,128)S(1)}, f32[8,256]{1,0:T(8,128)S(1)}, u32[]{:S(2)}, u32[]{:S(2)}) collective-permute-start(f32[8,256]{1,0:T(8,128)S(1)} %maximum_maximum_fusion.2), channel_id=1, source_target_pairs={{0,96},{1,97},{4,100},{5,101},{8,104},{9,105},{12,108},{13,109},{1... | collective-permute-start | bytes 24584 | tf_op jit(solution)/shard_map/ppermute | solution.py:39
  89.0 8.2 %collective-permute-start.27 = (bf16[320,256]{1,0:T(8,128)(2,1)S(1)}, bf16[320,256]{1,0:T(8,128)(2,1)S(1)}, u32[]{:S(2)}, u32[]{:S(2)}) collective-permute-start(bf16[320,256]{1,0:T(8,128)(2,1)S(1)} %get-tuple-element.29), channel_id=1, source_target_pairs={{0,64},{1,65},{4,68},{5,69},{8,72},{9,73},{12,76},{13,77},{16,80},... | collective-permute-start | bytes 491528 | tf_op jit(solution)/shard_map/ppermute | solution.py:39
  89.1 13.1 %collective-permute-start.28 = (bf16[320,256]{1,0:T(8,128)(2,1)S(1)}, bf16[320,256]{1,0:T(8,128)(2,1)S(1)}, u32[]{:S(2)}, u32[]{:S(2)}) collective-permute-start(bf16[320,256]{1,0:T(8,128)(2,1)S(1)} %get-tuple-element.30), channel_id=1, source_target_pairs={{0,128},{1,129},{4,132},{5,133},{8,136},{9,137},{12,140},{13,141},... | collective-permute-start | bytes 491528 | tf_op jit(solution)/shard_map/ppermute | solution.py:39
  89.7 12.6 %collective-permute-start.29 = (bf16[320,256]{1,0:T(8,128)(2,1)S(1)}, bf16[320,256]{1,0:T(8,128)(2,1)S(1)}, u32[]{:S(2)}, u32[]{:S(2)}) collective-permute-start(bf16[320,256]{1,0:T(8,128)(2,1)S(1)} %get-tuple-element.31), channel_id=1, source_target_pairs={{0,192},{1,193},{4,196},{5,197},{8,200},{9,201},{12,204},{13,205},... | collective-permute-start | bytes 491528 | tf_op jit(solution)/shard_map/ppermute | solution.py:39
  95.7 6.5 %collective-permute-start.21 = (f32[8,256]{1,0:T(8,128)S(1)}, f32[8,256]{1,0:T(8,128)S(1)}, u32[]{:S(2)}, u32[]{:S(2)}) collective-permute-start(f32[8,256]{1,0:T(8,128)S(1)} %maximum_maximum_fusion.3.s0), channel_id=1, source_target_pairs={{0,64},{1,65},{4,68},{5,69},{8,72},{9,73},{12,76},{13,77},{16,80},... | collective-permute-start | bytes 24584 | tf_op jit(solution)/shard_map/ppermute | solution.py:39
  95.8 6.4 %collective-permute-start.22 = (f32[8,256]{1,0:T(8,128)S(1)}, f32[8,256]{1,0:T(8,128)S(1)}, u32[]{:S(2)}, u32[]{:S(2)}) collective-permute-start(f32[8,256]{1,0:T(8,128)S(1)} %maximum_maximum_fusion.3.s0), channel_id=1, source_target_pairs={{0,128},{1,129},{4,132},{5,133},{8,136},{9,137},{12,140},{13,141},... | collective-permute-start | bytes 24584 | tf_op jit(solution)/shard_map/ppermute | solution.py:39
  97.3 7.6 %collective-permute-start.23 = (f32[8,256]{1,0:T(8,128)S(1)}, f32[8,256]{1,0:T(8,128)S(1)}, u32[]{:S(2)}, u32[]{:S(2)}) collective-permute-start(f32[8,256]{1,0:T(8,128)S(1)} %maximum_maximum_fusion.3.s0), channel_id=1, source_target_pairs={{0,192},{1,193},{4,196},{5,197},{8,200},{9,201},{12,204},{13,205},... | collective-permute-start | bytes 24584 | tf_op jit(solution)/shard_map/ppermute | solution.py:39
  114.3 6.4 %collective-permute-start.30 = (f32[72,128]{1,0:T(8,128)S(1)}, f32[72,128]{1,0:T(8,128)S(1)}, u32[]{:S(2)}, u32[]{:S(2)}) collective-permute-start(f32[72,128]{1,0:T(8,128)S(1)} %slice.160), channel_id=1, source_target_pairs={{0,1},{1,0},{4,5},{5,4},{8,9},{9,8},{12,13},{13,12},{16,17},{17,16... | collective-permute-start | bytes 110600 | tf_op jit(solution)/shard_map/ppermute | solution.py:39
  114.5 16.4 %all-to-all-start = ((bf16[16,32,128]{2,1,0:T(8,128)(2,1)}), bf16[16,32,128]{2,1,0:T(8,128)(2,1)S(1)}, u32[]{:S(2)}, u32[]{:S(2)}) async-start(bf16[16,32,128]{2,1,0:T(8,128)(2,1)} %get-tuple-element.32), calls=%async_computation | async-start | bytes 262144 | tf_op jit(solution)/shard_map/all_to_all | solution.py:460
  (15 other events, 144.0 us)

commit v4 on v3

v4 whole, which is shorter than its diff:
```python
import math

import jax
import jax.numpy as jnp
import numpy as np
from jax import lax
from jax.experimental import pallas as pl
from jax.experimental.pallas import tpu as pltpu
from jax.sharding import Mesh
from jax.sharding import PartitionSpec as P

TILE = 32
DQ = 576
DI = 128
NI = 64
HALF = 80
UNIT = 16
BLOCKS = 16
ROWS = 320
SCORE2 = 192.0 ** (-0.5) * math.log2(math.e)
INDEX_SCALE = DI ** (-0.5)
ALL = ("yhi", "xh", "xp", "z", "ylo", "core")
NEG = -jnp.inf
VMEM = 18 << 20


def flat(x, y, z, c):
    return ((y // 2) * 4 + x) * 32 + (z * 2 + (y % 2)) * 2 + c


def shift(value, dx=0, dy=0, dz=0, flip=0):
    pairs = [
        (flat(x, y, z, c), flat((x + dx) % 4, (y + dy) % 4, (z + dz) % 8, c ^ flip))
        for x in range(4)
        for y in range(4)
        for z in range(8)
        for c in range(2)
    ]
    return lax.ppermute(value, ALL, pairs)


def swap_core(value):
    return shift(value, flip=1)


LOG2E = math.log2(math.e)


def merge(m0, l0, m1, l1, rate):
    top = jnp.maximum(m0, m1)
    return top, l0 * jnp.exp2((m0 - top) * rate) + l1 * jnp.exp2((m1 - top) * rate)


def swapped(value):
    return jnp.concatenate([value[:, 128:], value[:, :128]], axis=1)


HEADS = 16
CHUNK = 8 * HALF


def score_kernel(first, spans, others, meta, *refs):
    n, e = len(spans), len(others)
    blocks, extras = refs[:n], refs[n : n + e]
    qa, qb, na, nb, ma, mb, wa, wb = refs[n + e : n + e + 8]
    refs = refs[n + e + 8 :]
    if e:
        e_ref, m_ref, l_ref, ik_ref, keys, bias, raw, tops, sems, index, isems = refs
    else:
        e_ref, m_ref, l_ref, keys, bias, raw, tops, sems = refs
    step = pl.program_id(0)
    cut = 320

    @pl.when(step == 0)
    def _():
        copies = []
        at = 0
        for i, (block, span) in enumerate(zip(blocks, spans)):
            copies.append(pltpu.make_async_copy(block, keys.at[at : at + span, :], sems.at[i]))
            copies[-1].start()
            at += span
        at = 0
        for i, (block, span) in enumerate(zip(extras, others)):
            source, rows = block.at[:, 0:DI], index.at[at : at + span, :]
            copies.append(pltpu.make_async_copy(source, rows, isems.at[i]))
            copies[-1].start()
            at += span
        place = jnp.concatenate([wa[NI : NI + 1, :], wb[NI : NI + 1, :]], axis=1)
        offsets = lax.broadcasted_iota(jnp.int32, (HALF, 256), 0).astype(jnp.float32)
        for i in range(8):
            base = meta[first + i].astype(jnp.float32)
            bias[i * HALF : (i + 1) * HALF, :] = jnp.where(offsets + base <= place, 0.0, NEG)
        tops[...] = jnp.zeros_like(tops)
        for copy in copies:
            copy.wait()
        if e:
            quarter = meta[34]
            for i in range(BLOCKS):
                slot = meta[BLOCKS + i]
                held = index if i < 8 else keys
                row = (i % 8) * HALF
                mine = pl.ds(pl.multiple_of(row + quarter * UNIT, UNIT), UNIT)
                ik_ref[pl.ds(pl.multiple_of(slot * UNIT, UNIT), UNIT), :] = held[mine, 0:DI]

                @pl.when((slot & 3) == quarter)
                def _():
                    extra = pl.multiple_of(256 + (slot >> 2) * UNIT, UNIT)
                    ik_ref[pl.ds(extra, UNIT), :] = held[row + 4 * UNIT : row + HALF, 0:DI]

    def work(now, last):
        for k in range(2):
            own = jnp.concatenate([qa[k], qb[k]], axis=1)
            left = jnp.concatenate([na[k], nb[k]], axis=1)
            right = jnp.concatenate([ma[k], mb[k]], axis=1)
            queries = jnp.where(step < 4, own, jnp.where(step < 6, left, right))
            top = jnp.max(tops[last, k], axis=0, keepdims=True)
            safe = jnp.where(top == NEG, 0.0, top)
            new = jnp.full((8, 256), NEG, jnp.float32)
            total = jnp.zeros((8, 256), jnp.float32)
            for t in range(0, CHUNK, cut):
                piece = slice(t, t + cut)
                scores = jnp.dot(keys[piece, DI:], queries, preferred_element_type=jnp.float32)
                scores = scores + bias[piece, :]
                raw[now, k, piece, :] = scores
                new = jnp.maximum(new, jnp.max(scores.reshape(cut // 8, 8, 256), axis=0))
                exps = jnp.exp2((raw[last, k, piece, :] - safe) * SCORE2)
                e_ref[k, piece, :] = exps.astype(jnp.bfloat16)
                total = total + jnp.sum(exps.reshape(cut // 8, 8, 256), axis=0)
            tops[now, k] = new
            head = pl.ds(2 * jnp.maximum(step - 1, 0) + k, 1)
            m_ref[head, :] = top
            l_ref[head, :] = jnp.sum(total, axis=0, keepdims=True)

    @pl.when(step % 2 == 0)
    def _():
        work(0, 1)

    @pl.when(step % 2 == 1)
    def _():
        work(1, 0)


def score_call(meta, first, blocks, extras, qa, qb, na, nb, ma, mb, wa, wb):
    spans, others = [b.shape[0] for b in blocks], [b.shape[0] for b in extras]
    whole = lambda shape: pl.BlockSpec(shape, lambda h, meta: (0,) * len(shape))

    def heads(start, count):
        return pl.BlockSpec((2, DQ, 128), lambda h, meta: (jnp.clip(h - start, 0, count - 1), 0, 0))

    lag = lambda shape: pl.BlockSpec((2,) + shape, lambda h, meta: (jnp.maximum(h - 1, 0), 0, 0))
    out_specs = [lag((CHUNK, 256)), whole((HEADS, 256)), whole((HEADS, 256))]
    out_shape = [
        jax.ShapeDtypeStruct((HEADS, CHUNK, 256), jnp.bfloat16),
        jax.ShapeDtypeStruct((HEADS, 256), jnp.float32),
        jax.ShapeDtypeStruct((HEADS, 256), jnp.float32),
    ]
    scratch = [
        pltpu.VMEM((CHUNK, DI + DQ), jnp.bfloat16),
        pltpu.VMEM((CHUNK, 256), jnp.float32),
        pltpu.VMEM((2, 2, CHUNK, 256), jnp.float32),
        pltpu.VMEM((2, 2, 8, 256), jnp.float32),
        pltpu.SemaphoreType.DMA((len(blocks),)),
    ]
    if extras:
        out_specs.append(whole((ROWS, DI)))
        out_shape.append(jax.ShapeDtypeStruct((ROWS, DI), jnp.bfloat16))
        scratch.append(pltpu.VMEM((CHUNK, DI), jnp.bfloat16))
        scratch.append(pltpu.SemaphoreType.DMA((len(extras),)))
    return pl.pallas_call(
        lambda *refs: score_kernel(first, spans, others, *refs),
        grid_spec=pltpu.PrefetchScalarGridSpec(
            num_scalar_prefetch=1,
            grid=(HEADS // 2 + 1,),
            in_specs=[pl.BlockSpec(memory_space=pl.ANY)] * (len(blocks) + len(extras))
            + [heads(0, 4)] * 2
            + [heads(4, 2)] * 2
            + [heads(6, 2)] * 2
            + [whole((72, 128))] * 2,
            out_specs=out_specs,
            scratch_shapes=scratch,
        ),
        out_shape=out_shape,
        cost_estimate=pl.CostEstimate(
            flops=4 * HEADS * CHUNK * 256 * DQ,
            bytes_accessed=HEADS * CHUNK * 512,
            transcendentals=HEADS * CHUNK * 256,
        ),
        compiler_params=pltpu.CompilerParams(vmem_limit_bytes=VMEM),
        name="scores",
    )(meta, *blocks, *extras, qa, qb, na, nb, ma, mb, wa, wb)


def head_sum_kernel(meta, e0, e1, m0, m1, here, up, down, o0, o1, o2, o3, total_ref, ratio):
    i = pl.program_id(0)

    @pl.when(i == 0)
    def _():
        def side(v):
            heads = [down[v, 4:8, :], up[v, 4:8, :], up[v, 0:4, :], down[v, 0:4, :]]
            return jnp.concatenate(heads, axis=0)

        top, total = merge(here[0, 0:16, :], here[1, 0:16, :], side(0), side(1), SCORE2)
        for c, m in enumerate((m0, m1)):
            ratio[c] = jnp.exp2((m[...] - top) * SCORE2) / total
        index = slice(HEADS, HEADS + 1)
        terms = []
        for left in merge(here[0, index, :], here[1, index, :], down[0, 8:9, :], down[1, 8:9, :], LOG2E):
            for _ in range(3):
                term = left.astype(jnp.bfloat16).astype(jnp.float32)
                terms.append(term)
                left = left - term
        packed = jnp.concatenate(terms + [jnp.zeros((10, 256), jnp.float32)], axis=0)
        for out in (o0, o1, o2, o3):
            out[ROWS:, :] = packed.astype(jnp.bfloat16)

    def add(e_ref, c):
        total = jnp.zeros((HALF, 256), jnp.float32)
        for h in range(HEADS):
            total = total + e_ref[h].astype(jnp.float32) * ratio[c, h : h + 1, :]
        total_ref[...] = total

    @pl.when(i < 8)
    def _():
        add(e0, 0)

    @pl.when(i >= 8)
    def _():
        add(e1, 1)

    slot = meta[BLOCKS + i]
    quarter = meta[34]
    at = pl.ds(pl.multiple_of(slot * UNIT, UNIT), UNIT)
    extra = pl.ds(pl.multiple_of(256 + (slot >> 2) * UNIT, UNIT), UNIT)
    for k, out in enumerate((o0, o1, o2, o3)):
        unit = pl.multiple_of((quarter ^ k) * UNIT, UNIT)
        out[at, :] = total_ref[pl.ds(unit, UNIT), :].astype(jnp.bfloat16)

        @pl.when((slot & 3) == (quarter ^ k))
        def _():
            out[extra, :] = total_ref[4 * UNIT :, :].astype(jnp.bfloat16)


def head_sum_call(meta, e0, e1, *stats):
    early = pl.BlockSpec((HEADS, HALF, 256), lambda i, meta: (0, jnp.minimum(i, 7), 0))
    late = pl.BlockSpec((HEADS, HALF, 256), lambda i, meta: (0, jnp.maximum(i - 8, 0), 0))
    whole = lambda shape: pl.BlockSpec(shape, lambda i, meta: (0,) * len(shape))
    out = pl.BlockSpec((ROWS + UNIT, 256), lambda i, meta: (0, 0))
    return pl.pallas_call(
        head_sum_kernel,
        grid_spec=pltpu.PrefetchScalarGridSpec(
            num_scalar_prefetch=1,
            grid=(BLOCKS,),
            in_specs=[early, late] + [whole(part.shape) for part in stats],
            out_specs=[out] * 4,
            scratch_shapes=[
                pltpu.VMEM((HALF, 256), jnp.float32),
                pltpu.VMEM((2, HEADS, 256), jnp.float32),
            ],
        ),
        out_shape=[jax.ShapeDtypeStruct((ROWS + UNIT, 256), jnp.bfloat16)] * 4,
        cost_estimate=pl.CostEstimate(flops=0, bytes_accessed=11 << 20, transcendentals=0),
        compiler_params=pltpu.CompilerParams(vmem_limit_bytes=VMEM),
        name="head_sum",
    )(meta, e0, e1, *stats)


def key_places(meta):
    core, half, quarter = meta[32], meta[33], meta[34]
    rows = lax.broadcasted_iota(jnp.int32, (UNIT, 256), 0)
    out = []
    for u in range(16):
        out.append(rows + ((u // 2 * 4 + (u % 2) * 2 + core) * 160 + half * HALF + quarter * UNIT))
    for e in range(4):
        z, ylo = 2 * e + (quarter >> 1), quarter & 1
        out.append(rows + ((z * 4 + ylo * 2 + core) * 160 + half * HALF + 4 * UNIT))
    return out


def inner_of(keys, ia, ib, j):
    queries = jnp.concatenate([ia[j], ib[j]], axis=0)
    return lax.dot_general(
        keys[...], queries, (((1,), (1,)), ((), ())), preferred_element_type=jnp.float32
    ), queries


JSTEP = 32


def forward_kernel(meta, keys, m0, l0, m1, l1, ia, ib, wa, wb, wja, wjb, logits, here, sent):
    step = pl.program_id(0)

    @pl.when(step == 0)
    def _():
        logits[...] = jnp.zeros_like(logits)

    total = logits[...]
    for j in range(JSTEP):
        inner, _ = inner_of(keys, ia, ib, j)
        weight = jnp.concatenate([wja[j : j + 1, :], wjb[j : j + 1, :]], axis=1)
        total = total + weight * jnp.maximum(inner, 0.0)
    logits[...] = total

    @pl.when(step == NI // JSTEP - 1)
    def _():
        place = jnp.concatenate([wa[NI : NI + 1, :], wb[NI : NI + 1, :]], axis=1)
        places = key_places(meta)
        top = jnp.full((1, 256), NEG, jnp.float32)
        for u in range(20):
            cut = slice(u * UNIT, (u + 1) * UNIT)
            value = logits[cut, :] * INDEX_SCALE
            value = jnp.where(places[u].astype(jnp.float32) <= place, value, NEG)
            logits[cut, :] = value
            top = jnp.maximum(top, jnp.max(value, axis=0, keepdims=True))
        safe = jnp.where(top == NEG, 0.0, top)
        total = jnp.sum(jnp.exp(logits[...] - safe), axis=0, keepdims=True)
        tops, totals = merge(m0[...], l0[...], m1[...], l1[...], SCORE2)
        for v, (heads, index) in enumerate(((tops, top), (totals, total))):
            rows = jnp.concatenate([heads, index, jnp.zeros((7, 256), jnp.float32)], axis=0)
            here[v] = rows
            sent[v] = swapped(rows)


def pair_kernel(ours, theirs, here, up, down):
    index = slice(HEADS, HEADS + 1)
    heads = slice(0, HEADS)
    tops, totals = merge(ours[0, heads, :], ours[1, heads, :], theirs[0, heads, :], theirs[1, heads, :], SCORE2)
    top, total = merge(ours[0, index, :], ours[1, index, :], theirs[0, index, :], theirs[1, index, :], LOG2E)
    for v, (main, extra) in enumerate(((tops, top), (totals, total))):
        pad = jnp.zeros((7, 256), jnp.float32)
        here[v] = jnp.concatenate([main, extra, pad], axis=0)
        up[v] = jnp.concatenate([main[0:4], main[12:16]], axis=0)
        down[v] = jnp.concatenate([main[4:12], extra, pad], axis=0)


def pair_call(ours, theirs):
    return pl.pallas_call(
        pair_kernel,
        out_shape=[jax.ShapeDtypeStruct((2, rows, 256), jnp.float32) for rows in (24, 8, 16)],
        name="pair_statistics",
    )(ours, theirs)


def j_specs():
    whole = lambda shape: pl.BlockSpec(shape, lambda s, meta: (0,) * len(shape))
    queries = pl.BlockSpec((JSTEP, 128, DI), lambda s, meta: (s, 0, 0))
    weights = pl.BlockSpec((JSTEP, 128), lambda s, meta: (s, 0))
    return whole, [queries, queries, whole((72, 128)), whole((72, 128)), weights, weights]


def forward_call(meta, keys, stats, ia, ib, wa, wb):
    whole, specs = j_specs()
    return pl.pallas_call(
        forward_kernel,
        grid_spec=pltpu.PrefetchScalarGridSpec(
            num_scalar_prefetch=1,
            grid=(NI // JSTEP,),
            in_specs=[whole((ROWS, DI))] + [whole((HEADS, 256))] * 4 + specs,
            out_specs=[whole((ROWS, 256)), whole((2, 24, 256)), whole((2, 24, 256))],
        ),
        out_shape=[
            jax.ShapeDtypeStruct((ROWS, 256), jnp.float32),
            jax.ShapeDtypeStruct((2, 24, 256), jnp.float32),
            jax.ShapeDtypeStruct((2, 24, 256), jnp.float32),
        ],
        cost_estimate=pl.CostEstimate(
            flops=2 * NI * ROWS * 256 * DI, bytes_accessed=5 << 20, transcendentals=0
        ),
        compiler_params=pltpu.CompilerParams(vmem_limit_bytes=VMEM),
        name="index_forward",
    )(meta, keys, *stats, ia, ib, wa, wb, wa, wb)


def backward_kernel(meta, keys, logits, t0, t1, t2, t3, ia, ib, wa, wb, wja, wjb, rows_a, rows_b, kg, grad, acc):
    step = pl.program_id(0)

    @pl.when(step == 0)
    def _():
        parts = (t0, t1, t2, t3)

        def value(part, row):
            terms = part[ROWS:, :].astype(jnp.float32)
            return terms[row : row + 1] + terms[row + 1 : row + 2] + terms[row + 2 : row + 3]

        tops = [value(part, 0) for part in parts]
        top = tops[0]
        for other in tops[1:]:
            top = jnp.maximum(top, other)
        total = jnp.zeros((1, 256), jnp.float32)
        for part, other in zip(parts, tops):
            total = total + value(part, 3) * jnp.exp(other - top)
        norm = top + jnp.log(total)
        goal = jnp.zeros((ROWS, 256), jnp.float32)
        for part in parts:
            goal = goal + part[0:ROWS, :].astype(jnp.float32)
        goal = goal * (1.0 / 64.0)
        held = logits[...]
        seen = held != NEG
        logp = held - norm
        live = seen & (goal > 0)
        safe = jnp.where(goal > 0, goal, 1.0)
        part = jnp.where(live, goal * (jnp.log(safe) - logp), 0.0)
        part = jnp.sum(part, axis=0, keepdims=True)
        part = jnp.concatenate([part, jnp.zeros((15, 256), jnp.float32)], axis=0)
        rows_a[NI:, :] = part[:, :128]
        rows_b[NI:, :] = part[:, 128:]
        grad[...] = jnp.where(seen, jnp.exp(logp) - goal, 0.0) * INDEX_SCALE
        acc[...] = jnp.zeros_like(acc)

    total = acc[...]
    slope = grad[...]
    for j in range(JSTEP):
        inner, queries = inner_of(keys, ia, ib, j)
        weight = jnp.concatenate([wja[j : j + 1, :], wjb[j : j + 1, :]], axis=1)
        share = jnp.sum(slope * jnp.maximum(inner, 0.0), axis=0, keepdims=True)
        rows_a[pl.ds(step * JSTEP + j, 1), :] = share[:, :128]
        rows_b[pl.ds(step * JSTEP + j, 1), :] = share[:, 128:]
        coeff = jnp.where(inner > 0, slope * weight, 0.0).astype(jnp.bfloat16)
        total = total + jnp.dot(coeff, queries, preferred_element_type=jnp.float32)
    acc[...] = total

    @pl.when(step == NI // JSTEP - 1)
    def _():
        quarter = meta[34]
        for b in range(BLOCKS):
            kg[b, 0:UNIT, :] = acc[b * UNIT : (b + 1) * UNIT, :].astype(jnp.bfloat16)
            at = 256 + (b // 4) * UNIT
            extra = jnp.where(quarter == b % 4, acc[at : at + UNIT, :], 0.0)
            kg[b, UNIT:, :] = extra.astype(jnp.bfloat16)


def backward_call(meta, keys, logits, target, ia, ib, wa, wb):
    whole, specs = j_specs()
    return pl.pallas_call(
        backward_kernel,
        grid_spec=pltpu.PrefetchScalarGridSpec(
            num_scalar_prefetch=1,
            grid=(NI // JSTEP,),
            in_specs=[
                whole((ROWS, DI)),
                whole((ROWS, 256)),
            ]
            + [whole((ROWS + UNIT, 256))] * 4
            + specs,
            out_specs=[
                whole((NI + 16, 128)),
                whole((NI + 16, 128)),
                whole((BLOCKS, 2 * UNIT, DI)),
            ],
            scratch_shapes=[
                pltpu.VMEM((ROWS, 256), jnp.float32),
                pltpu.VMEM((ROWS, DI), jnp.float32),
            ],
        ),
        out_shape=[
            jax.ShapeDtypeStruct((NI + 16, 128), jnp.float32),
            jax.ShapeDtypeStruct((NI + 16, 128), jnp.float32),
            jax.ShapeDtypeStruct((BLOCKS, 2 * UNIT, DI), jnp.bfloat16),
        ],
        cost_estimate=pl.CostEstimate(
            flops=4 * NI * ROWS * 256 * DI, bytes_accessed=6 << 20, transcendentals=0
        ),
        compiler_params=pltpu.CompilerParams(vmem_limit_bytes=VMEM),
        name="index_backward",
    )(meta, keys, logits, *target, ia, ib, wa, wb, wa, wb)


def gather_head(value):
    wide = jnp.broadcast_to(value[None], (8,) + value.shape)
    return lax.all_to_all(wide, ("yhi", "xh", "xp"), 0, 0, tiled=True)


def after(value, *others):
    return lax.optimization_barrier((value,) + others)[0]


def body(main_queries, latent_keys, index_queries, index_weights, index_keys, tile_order, offset):
    z, ylo, core = lax.axis_index("z"), lax.axis_index("ylo"), lax.axis_index("core")
    half = lax.axis_index("xp")
    quarter = lax.axis_index("yhi") * 2 + lax.axis_index("xh")

    rows = jnp.arange(TILE, dtype=jnp.int32)
    place = (offset + (tile_order[:, None] * TILE + rows[None, :])).reshape(1, 128)
    wa = jnp.concatenate(
        [index_weights.T, place.astype(jnp.float32), jnp.zeros((7, 128), jnp.float32)], axis=0
    )
    own = jnp.concatenate([index_keys, latent_keys], axis=1)
    own = lax.dynamic_slice_in_dim(own, half * HALF, HALF, 0)

    queries = main_queries.transpose(0, 2, 1)
    f1, b1 = shift(own, dz=1), shift(own, dz=7)
    queries_far = swap_core(queries)
    halves = after(queries, f1)
    left, right = shift(halves[:4], dx=1), shift(halves[4:], dx=3)
    wb = swap_core(wa)
    f1, b1 = lax.optimization_barrier((f1, b1))
    f2, b2 = shift(f1, dz=1), shift(b1, dz=7)
    f2, b2 = lax.optimization_barrier((f2, b2))
    f3, b3 = shift(f2, dz=1), shift(b2, dz=7)
    f3, b3 = lax.optimization_barrier((f3, b3))
    left, right = lax.optimization_barrier((left, right, f3))[:2]
    left_far, right_far = swap_core(left), swap_core(right)
    f4 = shift(f3, dz=1)
    f4, ia = lax.optimization_barrier((f4, index_queries.transpose(1, 0, 2)))
    ib = swap_core(ia)
    y0 = shift(jnp.concatenate([own, f1, b1, f2]), dy=1)
    y1 = shift(jnp.concatenate([b2, f3, b3, f4]), dy=3)
    column = [(0, own), (-1, f1), (1, b1), (-2, f2), (2, b2), (-3, f3), (3, b3), (-4, f4)]

    steps = jnp.asarray([dz for dz, _ in column] * 2, dtype=jnp.int32)
    zs = (z + 8 + steps) % 8
    ys = ylo ^ jnp.asarray([0] * 8 + [1] * 8, dtype=jnp.int32)
    bases = (zs * 4 + ys * 2 + core) * 160 + half * HALF
    meta = jnp.concatenate(
        [bases, zs * 2 + ys, jnp.stack([core, half, quarter])]
    ).astype(jnp.int32)

    held = [block for _, block in column]
    sides = (queries, queries_far, left, left_far, right, right_far, wa, wb)
    e0, m0, l0 = score_call(meta, 0, held, [], *sides)
    e1, m1, l1, keys = score_call(meta, 8, [y0, y1], held, *sides)

    logits, ours, sent = forward_call(meta, keys, (m0, l0, m1, l1), ia, ib, wa, wb)
    here, up, down = pair_call(ours, swap_core(sent))
    up, down = shift(up, dx=1), shift(down, dx=3)
    sums = head_sum_call(meta, e0, e1, m0, m1, here, up, down)
    group = (dict(dx=2), dict(dy=2), dict(dx=2, dy=2))
    target = [sums[0]] + [shift(part, **move) for part, move in zip(sums[1:], group)]

    mine, other, kg = backward_call(meta, keys, logits, target, ia, ib, wa, wb)
    rows_out = mine + swap_core(other)
    rows_high = lax.reduce_precision(rows_out, 8, 7)
    low = jnp.concatenate([jnp.zeros((NI + 8, 128), jnp.float32), (rows_out - rows_high)[NI : NI + 8]])
    tail = rows_high + low
    kg = lax.all_to_all(kg, ("z", "ylo"), 0, 0, tiled=True)
    kg = jnp.sum(kg.astype(jnp.float32), axis=0)
    last = gather_head(jnp.concatenate([kg, tail]).astype(jnp.bfloat16)).astype(jnp.float32)
    rows_sum = jnp.sum(last[:, 2 * UNIT :], axis=0)
    pieces = last[:, : 2 * UNIT].reshape(4, 2, 2 * UNIT, DI)
    main = pieces[:, :, :UNIT].transpose(1, 0, 2, 3).reshape(2, 4 * UNIT, DI)
    extra = jnp.sum(pieces[:, :, UNIT:], axis=0)
    key_grad = jnp.concatenate([main, extra], axis=1).reshape(160, DI)
    return rows_sum[NI] + rows_sum[NI + 8], rows_sum[:NI].T, key_grad


def solution(mesh):
    fine = Mesh(np.asarray(mesh.devices).reshape(2, 2, 2, 8, 2, 2), ALL)
    head, ctx = ("yhi", "xh", "xp"), ("z", "ylo", "core")
    in_specs = (
        P(head, ctx, None),
        P(ctx, None),
        P(ctx, None, None),
        P(ctx, None),
        P(ctx, None),
        P(ctx),
        P(),
    )
    out_specs = (P(ctx), P(ctx, None), P(ctx, None))
    return jax.shard_map(body, mesh=fine, in_specs=in_specs, out_specs=out_specs, check_vma=False)
```

time: 148 us -> 159 us (1.074)
  local copies, waits for them, and re-layouts: 6.53 us -> 24.4 us
  starting transfers between devices: 44.5 us -> 34.8 us
  waiting for transfers between devices: 38.2 us -> 31.9 us
  Pallas kernels: 36.9 us -> 42.6 us
  other arithmetic: 5.12 us -> 7.91 us
    unnamed x15 -> x69, local copies, waits for them, and re-layouts: 0.04 us -> 19.9 us
    ppermute x31 -> x23, starting transfers between devices: 38.4 us -> 29.4 us  [shift(): return lax.ppermute(value, ALL, pairs)]
    ppermute x31 -> x23, waiting for transfers between devices: 28.1 us -> 21.7 us  [shift(): return lax.ppermute(value, ALL, pairs)]
    pallas_call x1 -> x3, Pallas kernels: 18.6 us -> 23.8 us  [the longest x2 22.3 us: score_call(): pl.pallas_call(lambda *refs: score_kernel(first, spans, others, *refs), g...]
    optimization_barrier x1 -> x0, local copies, waits for them, and re-layouts: 3.05 us -> none  [after(): return lax.optimization_barrier((value,) + others)[0]]
  transfers between devices with their start and end apart: 32 -> 24, of which waited for: 13 -> 11; matrix products, arithmetic and copies ran while one was open for 6% -> 7% of each run, Pallas kernels for 15% -> 14%
where the time goes in v4:
time: 159 us; the launch traced here: 158 us
  Pallas kernels  42.6 us (27%)
  starting transfers between devices  34.8 us (22%)
  waiting for transfers between devices  31.9 us (20%)
  local copies, waits for them, and re-layouts  24.4 us (15%)
  blocking collectives  14.4 us (9%)
  other arithmetic  7.91 us (5%)
  between operations  1.8 us (1%)
    ppermute x23, starting transfers between devices, shift(): return lax.ppermute(value, ALL, pairs)  29.4 us
    pallas_call x2, Pallas kernels, score_call(): pl.pallas_call(lambda *refs: score_kernel(first, spans, others, *refs), g...  22.3 us
    ppermute x23, waiting for transfers between devices, shift(): return lax.ppermute(value, ALL, pairs)  21.7 us
    unnamed x69, local copies, waits for them, and re-layouts  19.9 us
    all_to_all x1, blocking collectives, gather_head(): return lax.all_to_all(wide, ('yhi', 'xh', 'xp'), 0, 0, tiled=True)  14.4 us
    all_to_all x1, waiting for transfers between devices, body(): kg = lax.all_to_all(kg, ('z', 'ylo'), 0, 0, tiled=True)  10.2 us
    pallas_call x1, Pallas kernels, backward_call(): pl.pallas_call(backward_kernel, grid_spec=pltpu.PrefetchScalarGridSpec(nu...  9.11 us
    all_to_all x1, starting transfers between devices, body(): kg = lax.all_to_all(kg, ('z', 'ylo'), 0, 0, tiled=True)  5.46 us
  transfers between devices with their start and end apart: 24, of which 11 were waited for; matrix products, arithmetic and copies ran while one was open for 7% of the time, Pallas kernels for 14%

profile of v4, /device:TPU:2, one launch (start us, length us, event | category | flops | bytes accessed | tf_op | source)
XLA Modules:
  0.0 157.8 jit_solution(16185243877189964739)
XLA Ops:
  3.7 4.0 %collective-permute-start.1 = (bf16[80,704]{1,0:T(8,128)(2,1)S(1)}, bf16[80,704]{1,0:T(8,128)(2,1)S(1)}, u32[]{:S(2)}, u32[]{:S(2)}) collective-permute-start(bf16[80,704]{1,0:T(8,128)(2,1)S(1)} %fusion.refs_3_.refs_1_), channel_id=1, source_target_pairs={{0,28},{1,29},{4,0},{5,1},{8,4},{9,5},{12,8},{13,9},{16,12},{17,13... | collective-permute-start | bytes 337928 | tf_op jit(solution)/shard_map/ppermute | solution.py:39
  7.8 3.2 %collective-permute-done.refs_4_.refs_2_ = bf16[80,704]{1,0:T(8,128)(2,1)S(1)} collective-permute-done((bf16[80,704]{1,0:T(8,128)(2,1)S(1)}, bf16[80,704]{1,0:T(8,128)(2,1)S(1)}, u32[]{:S(2)}, u32[]{:S(2)}) %collective-permute-start) | collective-permute-done | bytes 112672 | tf_op jit(solution)/shard_map/ppermute | solution.py:39
  11.0 3.2 %collective-permute-start.3 = (bf16[80,704]{1,0:T(8,128)(2,1)S(1)}, bf16[80,704]{1,0:T(8,128)(2,1)S(1)}, u32[]{:S(2)}, u32[]{:S(2)}) collective-permute-start(bf16[80,704]{1,0:T(8,128)(2,1)S(1)} %collective-permute-done.1.refs_5_.refs_3_), channel_id=1, source_target_pairs={{0,28},{1,29},{4,0},{5,1},{8,4},{9,5},{12,8},{13,9},{16,12},{17,13... | collective-permute-start | bytes 337928 | tf_op jit(solution)/shard_map/ppermute | solution.py:39
  14.2 2.9 %collective-permute-done.2.refs_6_.refs_4_ = bf16[80,704]{1,0:T(8,128)(2,1)S(1)} collective-permute-done((bf16[80,704]{1,0:T(8,128)(2,1)S(1)}, bf16[80,704]{1,0:T(8,128)(2,1)S(1)}, u32[]{:S(2)}, u32[]{:S(2)}) %collective-permute-start.2) | collective-permute-done | bytes 112672 | tf_op jit(solution)/shard_map/ppermute | solution.py:39
  17.1 2.6 %collective-permute-start.5 = (bf16[80,704]{1,0:T(8,128)(2,1)S(1)}, bf16[80,704]{1,0:T(8,128)(2,1)S(1)}, u32[]{:S(2)}, u32[]{:S(2)}) collective-permute-start(bf16[80,704]{1,0:T(8,128)(2,1)S(1)} %collective-permute-done.2.refs_6_.refs_4_), channel_id=1, source_target_pairs={{0,4},{1,5},{4,8},{5,9},{8,12},{9,13},{12,16},{13,17},{16,20},{17,... | collective-permute-start | bytes 337928 | tf_op jit(solution)/shard_map/ppermute | solution.py:39
  20.4 2.4 %fusion.8 = (bf16[4,576,128]{2,1,0:T(8,128)(2,1)}, bf16[4,576,128]{2,1,0:T(8,128)(2,1)}) fusion(bf16[8,576,128]{2,1,0:T(8,128)(2,1)} %bitcast.23), kind=kLoop, calls=%fused_computation.30 | loop fusion | bytes 2359296 | tf_op jit(solution)/shard_map/slice | solution.py:493
  28.7 2.3 %collective-permute-done.7.refs_10_.refs_8_ = bf16[80,704]{1,0:T(8,128)(2,1)S(1)} collective-permute-done((bf16[80,704]{1,0:T(8,128)(2,1)S(1)}, bf16[80,704]{1,0:T(8,128)(2,1)S(1)}, u32[]{:S(2)}, u32[]{:S(2)}) %collective-permute-start.7) | collective-permute-done | bytes 112672 | tf_op jit(solution)/shard_map/ppermute | solution.py:39
  50.3 11.4 %scores.3 = (bf16[16,640,256]{2,1,0:T(8,128)(2,1)S(1)}, f32[16,256]{1,0:T(8,128)S(1)}, f32[16,256]{1,0:T(8,128)S(1)}) custom-call(s32[35]{0:T(128)S(1)} %concatenate.29.refs_0_.meta, bf16[80,704]{1,0:T(8,128)(2,1)S(1)} %fusion.refs_3_.refs_1_, bf16[80,704]{1,0:T(8,128)(2,1)S(1)} %collective-permute-done.refs_4_.refs_2_, bf16[80,704]{1,0:T(8,128)(2,1)S(1)} %copy-done.6, ...), custom_call_target="tpu_custom_call" | custom-call | flops 6039797760 | bytes 5242880 | tf_op jit(solution)/shard_map/scores/pallas_call | solution.py:169
  61.8 2.3 %copy-done = bf16[16,640,256]{2,1,0:T(8,128)(2,1)} copy-done((bf16[16,640,256]{2,1,0:T(8,128)(2,1)}, bf16[16,640,256]{2,1,0:T(8,128)(2,1)S(1)}, u32[]{:S(2)}) %copy-start) | copy-done | bytes 5242904
  64.8 10.9 %scores.2 = (bf16[16,640,256]{2,1,0:T(8,128)(2,1)S(1)}, f32[16,256]{1,0:T(8,128)S(1)}, f32[16,256]{1,0:T(8,128)S(1)}, bf16[320,128]{1,0:T(8,128)(2,1)S(1)}) custom-call(s32[35]{0:T(128)S(1)} %copy-done.26, bf16[320,704]{1,0:T(8,128)(2,1)S(1)} %collective-permute-done.4.refs_1_, bf16[320,704]{1,0:T(8,128)(2,1)S(1)} %collective-permute-done.8.refs_2_, ...), custom_call_target="tpu_custom_call" | custom-call | flops 6039797760 | bytes 5242880 | tf_op jit(solution)/shard_map/scores/pallas_call | solution.py:169
  75.8 2.4 %copy-done.2 = bf16[16,640,256]{2,1,0:T(8,128)(2,1)} copy-done((bf16[16,640,256]{2,1,0:T(8,128)(2,1)}, bf16[16,640,256]{2,1,0:T(8,128)(2,1)S(1)}, u32[]{:S(2)}) %copy-start.2) | copy-done | bytes 5242904
  78.1 5.2 %index_forward.1 = (f32[320,256]{1,0:T(8,128)S(1)}, f32[2,24,256]{2,1,0:T(8,128)S(1)}, f32[2,24,256]{2,1,0:T(8,128)S(1)}) custom-call(s32[35]{0:T(128)S(1)} %copy-done.26, bf16[320,128]{1,0:T(8,128)(2,1)S(1)} %get-tuple-element.44.keys, f32[16,256]{1,0:T(8,128)S(1)} %get-tuple-element.45.m0, f32[16,256]{1,0:T(8,128)S(1)} %get-tuple-element.46.l0, ...), custom_call_target="tpu_custom_call" | custom-call | flops 1342177280 | bytes 5242880 | tf_op jit(solution)/shard_map/index_forward/pallas_call | solution.py:352
  89.4 3.4 %collective-permute-done.17.up = f32[2,8,256]{2,1,0:T(8,128)S(1)} collective-permute-done((f32[2,8,256]{2,1,0:T(8,128)}, f32[2,8,256]{2,1,0:T(8,128)S(1)}, u32[]{:S(2)}, u32[]{:S(2)}) %collective-permute-start.17) | collective-permute-done | bytes 16416 | tf_op jit(solution)/shard_map/ppermute | solution.py:39
  92.8 2.5 %copy-done.1 = bf16[16,640,256]{2,1,0:T(8,128)(2,1)S(1)} copy-done((bf16[16,640,256]{2,1,0:T(8,128)(2,1)S(1)}, bf16[16,640,256]{2,1,0:T(8,128)(2,1)}, u32[]{:S(2)}) %copy-start.1) | copy-done | bytes 5242904
  95.3 2.5 %copy-done.3 = bf16[16,640,256]{2,1,0:T(8,128)(2,1)S(1)} copy-done((bf16[16,640,256]{2,1,0:T(8,128)(2,1)S(1)}, bf16[16,640,256]{2,1,0:T(8,128)(2,1)}, u32[]{:S(2)}) %copy-start.3) | copy-done | bytes 5242904
  98.6 4.5 %head_sum.1 = (bf16[336,256]{1,0:T(8,128)(2,1)S(1)}, bf16[336,256]{1,0:T(8,128)(2,1)S(1)}, bf16[336,256]{1,0:T(8,128)(2,1)S(1)}, bf16[336,256]{1,0:T(8,128)(2,1)S(1)}) custom-call(s32[35]{0:T(128)S(1)} %copy-done.27, bf16[16,640,256]{2,1,0:T(8,128)(2,1)S(1)} %copy-done.1, bf16[16,640,256]{2,1,0:T(8,128)(2,1)S(1)} %copy-done.3, ...), custom_call_target="tpu_custom_call" | custom-call | bytes 11534336 | tf_op jit(solution)/shard_map/head_sum/pallas_call | solution.py:248
  103.0 2.3 %collective-permute-start.19 = (bf16[336,256]{1,0:T(8,128)(2,1)S(1)}, bf16[336,256]{1,0:T(8,128)(2,1)S(1)}, u32[]{:S(2)}, u32[]{:S(2)}) collective-permute-start(bf16[336,256]{1,0:T(8,128)(2,1)S(1)} %get-tuple-element.59), channel_id=1, source_target_pairs={{0,64},{1,65},{4,68},{5,69},{8,72},{9,73},{12,76},{13,77},{16,80},... | collective-permute-start | bytes 516104 | tf_op jit(solution)/shard_map/ppermute | solution.py:39
  107.3 2.3 %collective-permute-start.21 = (bf16[336,256]{1,0:T(8,128)(2,1)S(1)}, bf16[336,256]{1,0:T(8,128)(2,1)S(1)}, u32[]{:S(2)}, u32[]{:S(2)}) collective-permute-start(bf16[336,256]{1,0:T(8,128)(2,1)S(1)} %get-tuple-element.61), channel_id=1, source_target_pairs={{0,192},{1,193},{4,196},{5,197},{8,200},{9,201},{12,204},{13,205},... | collective-permute-start | bytes 516104 | tf_op jit(solution)/shard_map/ppermute | solution.py:39
  110.0 2.2 %collective-permute-done.20.t2 = bf16[336,256]{1,0:T(8,128)(2,1)S(1)} collective-permute-done((bf16[336,256]{1,0:T(8,128)(2,1)S(1)}, bf16[336,256]{1,0:T(8,128)(2,1)S(1)}, u32[]{:S(2)}, u32[]{:S(2)}) %collective-permute-start.20) | collective-permute-done | bytes 172064 | tf_op jit(solution)/shard_map/ppermute | solution.py:39
  112.3 4.4 %collective-permute-done.21.t3 = bf16[336,256]{1,0:T(8,128)(2,1)S(1)} collective-permute-done((bf16[336,256]{1,0:T(8,128)(2,1)S(1)}, bf16[336,256]{1,0:T(8,128)(2,1)S(1)}, u32[]{:S(2)}, u32[]{:S(2)}) %collective-permute-start.21) | collective-permute-done | bytes 172064 | tf_op jit(solution)/shard_map/ppermute | solution.py:39
  116.6 9.1 %index_backward.1 = (f32[80,128]{1,0:T(8,128)S(1)}, f32[80,128]{1,0:T(8,128)S(1)}, bf16[16,32,128]{2,1,0:T(8,128)(2,1)}) custom-call(s32[35]{0:T(128)S(1)} %copy-done.27, bf16[320,128]{1,0:T(8,128)(2,1)S(1)} %copy-done.29, f32[320,256]{1,0:T(8,128)S(1)} %get-tuple-element.50.logits, bf16[336,256]{1,0:T(8,128)(2,1)S(1)} %get-tuple-element.58.t0, ...), custom_call_target="tpu_custom_call" | custom-call | flops 2684354560 | bytes 6291456 | tf_op jit(solution)/shard_map/index_backward/pallas_call | solution.py:433
  125.8 5.5 %all-to-all-start = ((bf16[16,32,128]{2,1,0:T(8,128)(2,1)}), bf16[16,32,128]{2,1,0:T(8,128)(2,1)S(1)}, u32[]{:S(2)}, u32[]{:S(2)}) async-start(bf16[16,32,128]{2,1,0:T(8,128)(2,1)} %get-tuple-element.62), calls=%async_computation | async-start | bytes 262144 | tf_op jit(solution)/shard_map/all_to_all | solution.py:534
  131.3 10.2 %all-to-all-done = bf16[16,32,128]{2,1,0:T(8,128)(2,1)S(1)} async-done(((bf16[16,32,128]{2,1,0:T(8,128)(2,1)}), bf16[16,32,128]{2,1,0:T(8,128)(2,1)S(1)}, u32[]{:S(2)}, u32[]{:S(2)}) %all-to-all-start) | async-done | bytes 131104 | tf_op jit(solution)/shard_map/all_to_all | solution.py:534
  141.5 14.4 %all_to_all.10 = bf16[8,112,128]{2,1,0:T(8,128)(2,1)S(1)} all-to-all(bf16[8,112,128]{2,1,0:T(8,128)(2,1)S(1)} %broadcast_in_dim.5), channel_id=1, replica_groups=mesh['yhi'=2,'xh'=2,'xp'=2,'z'=8,'ylo'=2,'core'=2] {'yhi','xh','xp'}, dimensions={0} | all-to-all | bytes 458752 | tf_op jit(solution)/shard_map/all_to_all | solution.py:469
  (127 shorter events, 39.9 us)
Async XLA Ops:
  1.7 9.3 %collective-permute-start = (bf16[80,704]{1,0:T(8,128)(2,1)S(1)}, bf16[80,704]{1,0:T(8,128)(2,1)S(1)}, u32[]{:S(2)}, u32[]{:S(2)}) collective-permute-start(bf16[80,704]{1,0:T(8,128)(2,1)S(1)} %fusion.refs_3_.refs_1_), channel_id=1, source_target_pairs={{0,4},{1,5},{4,8},{5,9},{8,12},{9,13},{12,16},{13,17},{16,20},{17,... | collective-permute-start | bytes 337928 | tf_op jit(solution)/shard_map/ppermute | solution.py:39
  3.7 7.3 %collective-permute-start.1 = (bf16[80,704]{1,0:T(8,128)(2,1)S(1)}, bf16[80,704]{1,0:T(8,128)(2,1)S(1)}, u32[]{:S(2)}, u32[]{:S(2)}) collective-permute-start(bf16[80,704]{1,0:T(8,128)(2,1)S(1)} %fusion.refs_3_.refs_1_), channel_id=1, source_target_pairs={{0,28},{1,29},{4,0},{5,1},{8,4},{9,5},{12,8},{13,9},{16,12},{17,13... | collective-permute-start | bytes 337928 | tf_op jit(solution)/shard_map/ppermute | solution.py:39
  11.0 6.1 %collective-permute-start.2 = (bf16[80,704]{1,0:T(8,128)(2,1)S(1)}, bf16[80,704]{1,0:T(8,128)(2,1)S(1)}, u32[]{:S(2)}, u32[]{:S(2)}) collective-permute-start(bf16[80,704]{1,0:T(8,128)(2,1)S(1)} %collective-permute-done.refs_4_.refs_2_), channel_id=1, source_target_pairs={{0,4},{1,5},{4,8},{5,9},{8,12},{9,13},{12,16},{13,17},{16,20},{17,... | collective-permute-start | bytes 337928 | tf_op jit(solution)/shard_map/ppermute | solution.py:39
  11.0 6.1 %collective-permute-start.3 = (bf16[80,704]{1,0:T(8,128)(2,1)S(1)}, bf16[80,704]{1,0:T(8,128)(2,1)S(1)}, u32[]{:S(2)}, u32[]{:S(2)}) collective-permute-start(bf16[80,704]{1,0:T(8,128)(2,1)S(1)} %collective-permute-done.1.refs_5_.refs_3_), channel_id=1, source_target_pairs={{0,28},{1,29},{4,0},{5,1},{8,4},{9,5},{12,8},{13,9},{16,12},{17,13... | collective-permute-start | bytes 337928 | tf_op jit(solution)/shard_map/ppermute | solution.py:39
  14.2 29.0 %collective-permute-start.9 = (bf16[8,576,128]{2,1,0:T(8,128)(2,1)}, bf16[8,576,128]{2,1,0:T(8,128)(2,1)}, u32[]{:S(2)}, u32[]{:S(2)}) collective-permute-start(bf16[8,576,128]{2,1,0:T(8,128)(2,1)} %bitcast.22), channel_id=1, source_target_pairs={{0,1},{1,0},{4,5},{5,4},{8,9},{9,8},{12,13},{13,12},{16,17},{17,16... | collective-permute-start | bytes 3538952 | tf_op jit(solution)/shard_map/ppermute | solution.py:39
  17.1 7.8 %collective-permute-start.5 = (bf16[80,704]{1,0:T(8,128)(2,1)S(1)}, bf16[80,704]{1,0:T(8,128)(2,1)S(1)}, u32[]{:S(2)}, u32[]{:S(2)}) collective-permute-start(bf16[80,704]{1,0:T(8,128)(2,1)S(1)} %collective-permute-done.2.refs_6_.refs_4_), channel_id=1, source_target_pairs={{0,4},{1,5},{4,8},{5,9},{8,12},{9,13},{12,16},{13,17},{16,20},{17,... | collective-permute-start | bytes 337928 | tf_op jit(solution)/shard_map/ppermute | solution.py:39
  19.6 5.2 %collective-permute-start.6 = (bf16[80,704]{1,0:T(8,128)(2,1)S(1)}, bf16[80,704]{1,0:T(8,128)(2,1)S(1)}, u32[]{:S(2)}, u32[]{:S(2)}) collective-permute-start(bf16[80,704]{1,0:T(8,128)(2,1)S(1)} %collective-permute-done.3.refs_7_.refs_5_), channel_id=1, source_target_pairs={{0,28},{1,29},{4,0},{5,1},{8,4},{9,5},{12,8},{13,9},{16,12},{17,13... | collective-permute-start | bytes 337928 | tf_op jit(solution)/shard_map/ppermute | solution.py:39
  22.8 13.1 %collective-permute-start.10 = (bf16[4,576,128]{2,1,0:T(8,128)(2,1)}, bf16[4,576,128]{2,1,0:T(8,128)(2,1)}, u32[]{:S(2)}, u32[]{:S(2)}) collective-permute-start(bf16[4,576,128]{2,1,0:T(8,128)(2,1)} %get-tuple-element.70), channel_id=1, source_target_pairs={{0,32},{1,33},{4,36},{5,37},{8,40},{9,41},{12,44},{13,45},{16,48},... | collective-permute-start | bytes 1769480 | tf_op jit(solution)/shard_map/ppermute | solution.py:39
  24.3 12.8 %collective-permute-start.11 = (bf16[4,576,128]{2,1,0:T(8,128)(2,1)}, bf16[4,576,128]{2,1,0:T(8,128)(2,1)}, u32[]{:S(2)}, u32[]{:S(2)}) collective-permute-start(bf16[4,576,128]{2,1,0:T(8,128)(2,1)} %get-tuple-element.69), channel_id=1, source_target_pairs={{0,96},{1,97},{4,100},{5,101},{8,104},{9,105},{12,108},{13,109},{1... | collective-permute-start | bytes 1769480 | tf_op jit(solution)/shard_map/ppermute | solution.py:39
  24.9 6.2 %collective-permute-start.7 = (bf16[80,704]{1,0:T(8,128)(2,1)S(1)}, bf16[80,704]{1,0:T(8,128)(2,1)S(1)}, u32[]{:S(2)}, u32[]{:S(2)}) collective-permute-start(bf16[80,704]{1,0:T(8,128)(2,1)S(1)} %collective-permute-done.5.refs_8_.refs_6_), channel_id=1, source_target_pairs={{0,4},{1,5},{4,8},{5,9},{8,12},{9,13},{12,16},{13,17},{16,20},{17,... | collective-permute-start | bytes 337928 | tf_op jit(solution)/shard_map/ppermute | solution.py:39
  31.7 46.4 %collective-permute-start.15 = (bf16[64,128,128]{2,1,0:T(8,128)(2,1)S(1)}, bf16[64,128,128]{2,1,0:T(8,128)(2,1)}, u32[]{:S(2)}, u32[]{:S(2)}) collective-permute-start(bf16[64,128,128]{2,1,0:T(8,128)(2,1)S(1)} %bitcast.19), channel_id=1, source_target_pairs={{0,1},{1,0},{4,5},{5,4},{8,9},{9,8},{12,13},{13,12},{16,17},{17,16... | collective-permute-start | bytes 6291464 | tf_op jit(solution)/shard_map/ppermute | solution.py:39
  35.1 6.3 %collective-permute-start.14 = (f32[72,128]{1,0:T(8,128)}, f32[72,128]{1,0:T(8,128)}, u32[]{:S(2)}, u32[]{:S(2)}) collective-permute-start(f32[72,128]{1,0:T(8,128)} %maximum_maximum_fusion.refs_17_.refs_15_.wa.wja), channel_id=1, source_target_pairs={{0,1},{1,0},{4,5},{5,4},{8,9},{9,8},{12,13},{13,12},{16,17},{17,16... | collective-permute-start | bytes 110600 | tf_op jit(solution)/shard_map/ppermute | solution.py:39
  37.2 7.7 %collective-permute-start.12 = (bf16[4,576,128]{2,1,0:T(8,128)(2,1)}, bf16[4,576,128]{2,1,0:T(8,128)(2,1)}, u32[]{:S(2)}, u32[]{:S(2)}) collective-permute-start(bf16[4,576,128]{2,1,0:T(8,128)(2,1)} %collective-permute-done.10.refs_13_.refs_11_), channel_id=1, source_target_pairs={{0,1},{1,0},{4,5},{5,4},{8,9},{9,8},{12,13},{13,12},{16,17},{17,16... | collective-permute-start | bytes 1769480 | tf_op jit(solution)/shard_map/ppermute | solution.py:39
  37.2 7.7 %collective-permute-start.13 = (bf16[4,576,128]{2,1,0:T(8,128)(2,1)}, bf16[4,576,128]{2,1,0:T(8,128)(2,1)}, u32[]{:S(2)}, u32[]{:S(2)}) collective-permute-start(bf16[4,576,128]{2,1,0:T(8,128)(2,1)} %collective-permute-done.11.refs_15_.refs_13_), channel_id=1, source_target_pairs={{0,1},{1,0},{4,5},{5,4},{8,9},{9,8},{12,13},{13,12},{16,17},{17,16... | collective-permute-start | bytes 1769480 | tf_op jit(solution)/shard_map/ppermute | solution.py:39
  41.4 22.7 %collective-permute-start.4 = (bf16[320,704]{1,0:T(8,128)(2,1)S(1)}, bf16[320,704]{1,0:T(8,128)(2,1)S(1)}, u32[]{:S(2)}, u32[]{:S(2)}) collective-permute-start(bf16[320,704]{1,0:T(8,128)(2,1)S(1)} %pad_maximum_fusion), channel_id=1, source_target_pairs={{0,2},{1,3},{4,6},{5,7},{8,10},{9,11},{12,14},{13,15},{16,18},{17,... | collective-permute-start | bytes 1351688 | tf_op jit(solution)/shard_map/ppermute | solution.py:39
  43.3 20.9 %collective-permute-start.8 = (bf16[320,704]{1,0:T(8,128)(2,1)S(1)}, bf16[320,704]{1,0:T(8,128)(2,1)S(1)}, u32[]{:S(2)}, u32[]{:S(2)}) collective-permute-start(bf16[320,704]{1,0:T(8,128)(2,1)S(1)} %pad_maximum_fusion.1), channel_id=1, source_target_pairs={{0,130},{1,131},{4,134},{5,135},{8,138},{9,139},{12,142},{13,143},... | collective-permute-start | bytes 1351688 | tf_op jit(solution)/shard_map/ppermute | solution.py:39
  84.0 1.2 collective-permute-start.16
  87.3 5.4 %collective-permute-start.18 = (f32[2,16,256]{2,1,0:T(8,128)}, f32[2,16,256]{2,1,0:T(8,128)S(1)}, u32[]{:S(2)}, u32[]{:S(2)}) collective-permute-start(f32[2,16,256]{2,1,0:T(8,128)} %get-tuple-element.57), channel_id=1, source_target_pairs={{0,96},{1,97},{4,100},{5,101},{8,104},{9,105},{12,108},{13,109},{1... | collective-permute-start | bytes 98312 | tf_op jit(solution)/shard_map/ppermute | solution.py:39
  87.9 4.9 %collective-permute-start.17 = (f32[2,8,256]{2,1,0:T(8,128)}, f32[2,8,256]{2,1,0:T(8,128)S(1)}, u32[]{:S(2)}, u32[]{:S(2)}) collective-permute-start(f32[2,8,256]{2,1,0:T(8,128)} %get-tuple-element.56), channel_id=1, source_target_pairs={{0,32},{1,33},{4,36},{5,37},{8,40},{9,41},{12,44},{13,45},{16,48},... | collective-permute-start | bytes 49160 | tf_op jit(solution)/shard_map/ppermute | solution.py:39
  103.0 7.0 %collective-permute-start.19 = (bf16[336,256]{1,0:T(8,128)(2,1)S(1)}, bf16[336,256]{1,0:T(8,128)(2,1)S(1)}, u32[]{:S(2)}, u32[]{:S(2)}) collective-permute-start(bf16[336,256]{1,0:T(8,128)(2,1)S(1)} %get-tuple-element.59), channel_id=1, source_target_pairs={{0,64},{1,65},{4,68},{5,69},{8,72},{9,73},{12,76},{13,77},{16,80},... | collective-permute-start | bytes 516104 | tf_op jit(solution)/shard_map/ppermute | solution.py:39
  105.3 6.9 %collective-permute-start.20 = (bf16[336,256]{1,0:T(8,128)(2,1)S(1)}, bf16[336,256]{1,0:T(8,128)(2,1)S(1)}, u32[]{:S(2)}, u32[]{:S(2)}) collective-permute-start(bf16[336,256]{1,0:T(8,128)(2,1)S(1)} %get-tuple-element.60), channel_id=1, source_target_pairs={{0,128},{1,129},{4,132},{5,133},{8,136},{9,137},{12,140},{13,141},... | collective-permute-start | bytes 516104 | tf_op jit(solution)/shard_map/ppermute | solution.py:39
  107.3 9.3 %collective-permute-start.21 = (bf16[336,256]{1,0:T(8,128)(2,1)S(1)}, bf16[336,256]{1,0:T(8,128)(2,1)S(1)}, u32[]{:S(2)}, u32[]{:S(2)}) collective-permute-start(bf16[336,256]{1,0:T(8,128)(2,1)S(1)} %get-tuple-element.61), channel_id=1, source_target_pairs={{0,192},{1,193},{4,196},{5,197},{8,200},{9,201},{12,204},{13,205},... | collective-permute-start | bytes 516104 | tf_op jit(solution)/shard_map/ppermute | solution.py:39
  125.8 5.5 %collective-permute-start.22 = (f32[80,128]{1,0:T(8,128)S(1)}, f32[80,128]{1,0:T(8,128)S(1)}, u32[]{:S(2)}, u32[]{:S(2)}) collective-permute-start(f32[80,128]{1,0:T(8,128)S(1)} %get-tuple-element.64), channel_id=1, source_target_pairs={{0,1},{1,0},{4,5},{5,4},{8,9},{9,8},{12,13},{13,12},{16,17},{17,16... | collective-permute-start | bytes 122888 | tf_op jit(solution)/shard_map/ppermute | solution.py:39
  125.8 15.7 %all-to-all-start = ((bf16[16,32,128]{2,1,0:T(8,128)(2,1)}), bf16[16,32,128]{2,1,0:T(8,128)(2,1)S(1)}, u32[]{:S(2)}, u32[]{:S(2)}) async-start(bf16[16,32,128]{2,1,0:T(8,128)(2,1)} %get-tuple-element.62), calls=%async_computation | async-start | bytes 262144 | tf_op jit(solution)/shard_map/all_to_all | solution.py:534
  (34 other events, 338.3 us)

commit v5 on v4

--- a/solution.py
+++ b/solution.py
@@ -46,6 +46,17 @@
 LOG2E = math.log2(math.e)
 
 
+def slot_of(meta, i):
+    k = i & 7
+    reach = (k + 1) >> 1
+    step = reach * (1 - 2 * (k & 1))
+    return ((meta[0] + 8 + step) & 7) * 2 + (meta[1] ^ (i >> 3))
+
+
+def place_of(pa, pb):
+    return jnp.concatenate([pa[...], pb[...]], axis=1)
+
+
 def merge(m0, l0, m1, l1, rate):
     top = jnp.maximum(m0, m1)
     return top, l0 * jnp.exp2((m0 - top) * rate) + l1 * jnp.exp2((m1 - top) * rate)
@@ -59,15 +70,13 @@
 CHUNK = 8 * HALF
 
 
-def score_kernel(first, spans, others, meta, *refs):
-    n, e = len(spans), len(others)
-    blocks, extras = refs[:n], refs[n : n + e]
-    qa, qb, na, nb, ma, mb, wa, wb = refs[n + e : n + e + 8]
-    refs = refs[n + e + 8 :]
-    if e:
-        e_ref, m_ref, l_ref, ik_ref, keys, bias, raw, tops, sems, index, isems = refs
-    else:
-        e_ref, m_ref, l_ref, keys, bias, raw, tops, sems = refs
+def score_kernel(chunk, spans, meta, *refs):
+    n = len(spans)
+    blocks, refs = refs[:n], refs[n:]
+    if chunk:
+        _, ik_before, refs = refs[0], refs[1], refs[2:]
+    qa, qb, na, nb, ma, mb, pa, pb = refs[:8]
+    e_ref, m_ref, l_ref, ik_ref, keys, bias, raw, tops, sems = refs[8:]
     step = pl.program_id(0)
     cut = 320
 
@@ -79,33 +88,26 @@
             copies.append(pltpu.make_async_copy(block, keys.at[at : at + span, :], sems.at[i]))
             copies[-1].start()
             at += span
-        at = 0
-        for i, (block, span) in enumerate(zip(extras, others)):
-            source, rows = block.at[:, 0:DI], index.at[at : at + span, :]
-            copies.append(pltpu.make_async_copy(source, rows, isems.at[i]))
-            copies[-1].start()
-            at += span
-        place = jnp.concatenate([wa[NI : NI + 1, :], wb[NI : NI + 1, :]], axis=1)
+        place = place_of(pa, pb)
         offsets = lax.broadcasted_iota(jnp.int32, (HALF, 256), 0).astype(jnp.float32)
+        slots = [slot_of(meta, 8 * chunk + i) for i in range(8)]
         for i in range(8):
-            base = meta[first + i].astype(jnp.float32)
+            base = ((slots[i] * 2 + meta[2]) * 160 + meta[3] * HALF).astype(jnp.float32)
             bias[i * HALF : (i + 1) * HALF, :] = jnp.where(offsets + base <= place, 0.0, NEG)
         tops[...] = jnp.zeros_like(tops)
+        ik_ref[...] = ik_before[...] if chunk else jnp.zeros_like(ik_ref)
         for copy in copies:
             copy.wait()
-        if e:
-            quarter = meta[34]
-            for i in range(BLOCKS):
-                slot = meta[BLOCKS + i]
-                held = index if i < 8 else keys
-                row = (i % 8) * HALF
-                mine = pl.ds(pl.multiple_of(row + quarter * UNIT, UNIT), UNIT)
-                ik_ref[pl.ds(pl.multiple_of(slot * UNIT, UNIT), UNIT), :] = held[mine, 0:DI]
-
-                @pl.when((slot & 3) == quarter)
-                def _():
-                    extra = pl.multiple_of(256 + (slot >> 2) * UNIT, UNIT)
-                    ik_ref[pl.ds(extra, UNIT), :] = held[row + 4 * UNIT : row + HALF, 0:DI]
+        quarter = meta[4]
+        for i in range(8):
+            slot = slots[i]
+            mine = pl.ds(pl.multiple_of(i * HALF + quarter * UNIT, UNIT), UNIT)
+            ik_ref[pl.ds(pl.multiple_of(slot * UNIT, UNIT), UNIT), :] = keys[mine, 0:DI]
+
+            @pl.when((slot & 3) == quarter)
+            def _():
+                extra = pl.multiple_of(256 + (slot >> 2) * UNIT, UNIT)
+                ik_ref[pl.ds(extra, UNIT), :] = keys[i * HALF + 4 * UNIT : (i + 1) * HALF, 0:DI]
 
     def work(now, last):
         for k in range(2):
@@ -140,46 +142,42 @@
         work(1, 0)
 
 
-def score_call(meta, first, blocks, extras, qa, qb, na, nb, ma, mb, wa, wb):
-    spans, others = [b.shape[0] for b in blocks], [b.shape[0] for b in extras]
+def score_call(meta, chunk, blocks, before, qa, qb, na, nb, ma, mb, pa, pb):
+    spans = [b.shape[0] for b in blocks]
     whole = lambda shape: pl.BlockSpec(shape, lambda h, meta: (0,) * len(shape))
 
     def heads(start, count):
         return pl.BlockSpec((2, DQ, 128), lambda h, meta: (jnp.clip(h - start, 0, count - 1), 0, 0))
 
-    lag = lambda shape: pl.BlockSpec((2,) + shape, lambda h, meta: (jnp.maximum(h - 1, 0), 0, 0))
-    out_specs = [lag((CHUNK, 256)), whole((HEADS, 256)), whole((HEADS, 256))]
-    out_shape = [
-        jax.ShapeDtypeStruct((HEADS, CHUNK, 256), jnp.bfloat16),
-        jax.ShapeDtypeStruct((HEADS, 256), jnp.float32),
-        jax.ShapeDtypeStruct((HEADS, 256), jnp.float32),
-    ]
-    scratch = [
-        pltpu.VMEM((CHUNK, DI + DQ), jnp.bfloat16),
-        pltpu.VMEM((CHUNK, 256), jnp.float32),
-        pltpu.VMEM((2, 2, CHUNK, 256), jnp.float32),
-        pltpu.VMEM((2, 2, 8, 256), jnp.float32),
-        pltpu.SemaphoreType.DMA((len(blocks),)),
-    ]
-    if extras:
-        out_specs.append(whole((ROWS, DI)))
-        out_shape.append(jax.ShapeDtypeStruct((ROWS, DI), jnp.bfloat16))
-        scratch.append(pltpu.VMEM((CHUNK, DI), jnp.bfloat16))
-        scratch.append(pltpu.SemaphoreType.DMA((len(extras),)))
+    anywhere = pl.BlockSpec(memory_space=pl.ANY)
+    exps = pl.BlockSpec((2, CHUNK, 256), lambda h, meta: (jnp.maximum(h - 1, 0), chunk, 0))
     return pl.pallas_call(
-        lambda *refs: score_kernel(first, spans, others, *refs),
+        lambda *refs: score_kernel(chunk, spans, *refs),
         grid_spec=pltpu.PrefetchScalarGridSpec(
             num_scalar_prefetch=1,
             grid=(HEADS // 2 + 1,),
-            in_specs=[pl.BlockSpec(memory_space=pl.ANY)] * (len(blocks) + len(extras))
+            in_specs=[anywhere] * len(blocks)
+            + ([anywhere, whole((ROWS, DI))] if chunk else [])
             + [heads(0, 4)] * 2
             + [heads(4, 2)] * 2
             + [heads(6, 2)] * 2
-            + [whole((72, 128))] * 2,
-            out_specs=out_specs,
-            scratch_shapes=scratch,
-        ),
-        out_shape=out_shape,
+            + [whole((1, 128))] * 2,
+            out_specs=[exps, whole((HEADS, 256)), whole((HEADS, 256)), whole((ROWS, DI))],
+            scratch_shapes=[
+                pltpu.VMEM((CHUNK, DI + DQ), jnp.bfloat16),
+                pltpu.VMEM((CHUNK, 256), jnp.float32),
+                pltpu.VMEM((2, 2, CHUNK, 256), jnp.float32),
+                pltpu.VMEM((2, 2, 8, 256), jnp.float32),
+                pltpu.SemaphoreType.DMA((len(blocks),)),
+            ],
+        ),
+        out_shape=[
+            jax.ShapeDtypeStruct((HEADS, 2 * CHUNK, 256), jnp.bfloat16),
+            jax.ShapeDtypeStruct((HEADS, 256), jnp.float32),
+            jax.ShapeDtypeStruct((HEADS, 256), jnp.float32),
+            jax.ShapeDtypeStruct((ROWS, DI), jnp.bfloat16),
+        ],
+        input_output_aliases={1 + len(blocks): 0} if chunk else {},
         cost_estimate=pl.CostEstimate(
             flops=4 * HEADS * CHUNK * 256 * DQ,
             bytes_accessed=HEADS * CHUNK * 512,
@@ -187,10 +185,10 @@
         ),
         compiler_params=pltpu.CompilerParams(vmem_limit_bytes=VMEM),
         name="scores",
-    )(meta, *blocks, *extras, qa, qb, na, nb, ma, mb, wa, wb)
-
-
-def head_sum_kernel(meta, e0, e1, m0, m1, here, up, down, o0, o1, o2, o3, total_ref, ratio):
+    )(meta, *blocks, *before, qa, qb, na, nb, ma, mb, pa, pb)
+
+
+def head_sum_kernel(meta, e_ref, m0, m1, here, up, down, o0, o1, o2, o3, total_ref, ratio):
     i = pl.program_id(0)
 
     @pl.when(i == 0)
@@ -213,22 +211,13 @@
         for out in (o0, o1, o2, o3):
             out[ROWS:, :] = packed.astype(jnp.bfloat16)
 
-    def add(e_ref, c):
-        total = jnp.zeros((HALF, 256), jnp.float32)
-        for h in range(HEADS):
-            total = total + e_ref[h].astype(jnp.float32) * ratio[c, h : h + 1, :]
-        total_ref[...] = total
-
-    @pl.when(i < 8)
-    def _():
-        add(e0, 0)
-
-    @pl.when(i >= 8)
-    def _():
-        add(e1, 1)
-
-    slot = meta[BLOCKS + i]
-    quarter = meta[34]
+    chunk = i // 8
+    total = jnp.zeros((HALF, 256), jnp.float32)
+    for h in range(HEADS):
+        total = total + e_ref[h].astype(jnp.float32) * ratio[chunk, h : h + 1, :]
+    total_ref[...] = total
+    slot = slot_of(meta, i)
+    quarter = meta[4]
     at = pl.ds(pl.multiple_of(slot * UNIT, UNIT), UNIT)
     extra = pl.ds(pl.multiple_of(256 + (slot >> 2) * UNIT, UNIT), UNIT)
     for k, out in enumerate((o0, o1, o2, o3)):
@@ -240,9 +229,8 @@
             out[extra, :] = total_ref[4 * UNIT :, :].astype(jnp.bfloat16)
 
 
-def head_sum_call(meta, e0, e1, *stats):
-    early = pl.BlockSpec((HEADS, HALF, 256), lambda i, meta: (0, jnp.minimum(i, 7), 0))
-    late = pl.BlockSpec((HEADS, HALF, 256), lambda i, meta: (0, jnp.maximum(i - 8, 0), 0))
+def head_sum_call(meta, exps, *stats):
+    piece = pl.BlockSpec((HEADS, HALF, 256), lambda i, meta: (0, i, 0))
     whole = lambda shape: pl.BlockSpec(shape, lambda i, meta: (0,) * len(shape))
     out = pl.BlockSpec((ROWS + UNIT, 256), lambda i, meta: (0, 0))
     return pl.pallas_call(
@@ -250,7 +238,7 @@
         grid_spec=pltpu.PrefetchScalarGridSpec(
             num_scalar_prefetch=1,
             grid=(BLOCKS,),
-            in_specs=[early, late] + [whole(part.shape) for part in stats],
+            in_specs=[piece] + [whole(part.shape) for part in stats],
             out_specs=[out] * 4,
             scratch_shapes=[
                 pltpu.VMEM((HALF, 256), jnp.float32),
@@ -261,11 +249,11 @@
         cost_estimate=pl.CostEstimate(flops=0, bytes_accessed=11 << 20, transcendentals=0),
         compiler_params=pltpu.CompilerParams(vmem_limit_bytes=VMEM),
         name="head_sum",
-    )(meta, e0, e1, *stats)
+    )(meta, exps, *stats)
 
 
 def key_places(meta):
-    core, half, quarter = meta[32], meta[33], meta[34]
+    core, half, quarter = meta[2], meta[3], meta[4]
     rows = lax.broadcasted_iota(jnp.int32, (UNIT, 256), 0)
     out = []
     for u in range(16):
@@ -286,7 +274,7 @@
 JSTEP = 32
 
 
-def forward_kernel(meta, keys, m0, l0, m1, l1, ia, ib, wa, wb, wja, wjb, logits, here, sent):
+def forward_kernel(meta, keys, m0, l0, m1, l1, ia, ib, pa, pb, wja, wjb, logits, here, sent):
     step = pl.program_id(0)
 
     @pl.when(step == 0)
@@ -302,7 +290,7 @@
 
     @pl.when(step == NI // JSTEP - 1)
     def _():
-        place = jnp.concatenate([wa[NI : NI + 1, :], wb[NI : NI + 1, :]], axis=1)
+        place = place_of(pa, pb)
         places = key_places(meta)
         top = jnp.full((1, 256), NEG, jnp.float32)
         for u in range(20):
@@ -344,17 +332,17 @@
     whole = lambda shape: pl.BlockSpec(shape, lambda s, meta: (0,) * len(shape))
     queries = pl.BlockSpec((JSTEP, 128, DI), lambda s, meta: (s, 0, 0))
     weights = pl.BlockSpec((JSTEP, 128), lambda s, meta: (s, 0))
-    return whole, [queries, queries, whole((72, 128)), whole((72, 128)), weights, weights]
-
-
-def forward_call(meta, keys, stats, ia, ib, wa, wb):
-    whole, specs = j_specs()
+    return whole, [queries, queries], [weights, weights]
+
+
+def forward_call(meta, keys, stats, ia, ib, pa, pb, wa, wb):
+    whole, queries, weights = j_specs()
     return pl.pallas_call(
         forward_kernel,
         grid_spec=pltpu.PrefetchScalarGridSpec(
             num_scalar_prefetch=1,
             grid=(NI // JSTEP,),
-            in_specs=[whole((ROWS, DI))] + [whole((HEADS, 256))] * 4 + specs,
+            in_specs=[whole((ROWS, DI))] + [whole((HEADS, 256))] * 4 + queries + [whole((1, 128))] * 2 + weights,
             out_specs=[whole((ROWS, 256)), whole((2, 24, 256)), whole((2, 24, 256))],
         ),
         out_shape=[
@@ -367,10 +355,10 @@
         ),
         compiler_params=pltpu.CompilerParams(vmem_limit_bytes=VMEM),
         name="index_forward",
-    )(meta, keys, *stats, ia, ib, wa, wb, wa, wb)
-
-
-def backward_kernel(meta, keys, logits, t0, t1, t2, t3, ia, ib, wa, wb, wja, wjb, rows_a, rows_b, kg, grad, acc):
+    )(meta, keys, *stats, ia, ib, pa, pb, wa, wb)
+
+
+def backward_kernel(meta, keys, logits, t0, t1, t2, t3, ia, ib, wja, wjb, rows_a, rows_b, kg, grad, acc):
     step = pl.program_id(0)
 
     @pl.when(step == 0)
@@ -420,7 +408,7 @@
 
     @pl.when(step == NI // JSTEP - 1)
     def _():
-        quarter = meta[34]
+        quarter = meta[4]
         for b in range(BLOCKS):
             kg[b, 0:UNIT, :] = acc[b * UNIT : (b + 1) * UNIT, :].astype(jnp.bfloat16)
             at = 256 + (b // 4) * UNIT
@@ -429,7 +417,7 @@
 
 
 def backward_call(meta, keys, logits, target, ia, ib, wa, wb):
-    whole, specs = j_specs()
+    whole, queries, weights = j_specs()
     return pl.pallas_call(
         backward_kernel,
         grid_spec=pltpu.PrefetchScalarGridSpec(
@@ -440,7 +428,8 @@
                 whole((ROWS, 256)),
             ]
             + [whole((ROWS + UNIT, 256))] * 4
-            + specs,
+            + queries
+            + weights,
             out_specs=[
                 whole((NI + 16, 128)),
                 whole((NI + 16, 128)),
@@ -461,7 +450,7 @@
         ),
         compiler_params=pltpu.CompilerParams(vmem_limit_bytes=VMEM),
         name="index_backward",
-    )(meta, keys, logits, *target, ia, ib, wa, wb, wa, wb)
+    )(meta, keys, logits, *target, ia, ib, wa, wb)
 
 
 def gather_head(value):
@@ -480,49 +469,39 @@
 
     rows = jnp.arange(TILE, dtype=jnp.int32)
     place = (offset + (tile_order[:, None] * TILE + rows[None, :])).reshape(1, 128)
-    wa = jnp.concatenate(
-        [index_weights.T, place.astype(jnp.float32), jnp.zeros((7, 128), jnp.float32)], axis=0
-    )
+    pa, wa = place.astype(jnp.float32), index_weights.T
     own = jnp.concatenate([index_keys, latent_keys], axis=1)
     own = lax.dynamic_slice_in_dim(own, half * HALF, HALF, 0)
 
     queries = main_queries.transpose(0, 2, 1)
     f1, b1 = shift(own, dz=1), shift(own, dz=7)
     queries_far = swap_core(queries)
-    halves = after(queries, f1)
-    left, right = shift(halves[:4], dx=1), shift(halves[4:], dx=3)
-    wb = swap_core(wa)
+    left, right = shift(queries[:4], dx=1), shift(queries[4:], dx=3)
     f1, b1 = lax.optimization_barrier((f1, b1))
     f2, b2 = shift(f1, dz=1), shift(b1, dz=7)
     f2, b2 = lax.optimization_barrier((f2, b2))
     f3, b3 = shift(f2, dz=1), shift(b2, dz=7)
     f3, b3 = lax.optimization_barrier((f3, b3))
-    left, right = lax.optimization_barrier((left, right, f3))[:2]
+    f4 = shift(f3, dz=1)
+    ia = index_queries.transpose(1, 0, 2)
+    pb = swap_core(pa)
+    f4, ia, pb, left, right = lax.optimization_barrier((f4, ia, pb, left, right))
+    y0, y1 = jnp.concatenate([own, f1, b1, f2]), jnp.concatenate([b2, f3, b3, f4])
+    y0, y1, left, right = lax.optimization_barrier((y0, y1, left, right))
+    y0, y1 = shift(y0, dy=1), shift(y1, dy=3)
     left_far, right_far = swap_core(left), swap_core(right)
-    f4 = shift(f3, dz=1)
-    f4, ia = lax.optimization_barrier((f4, index_queries.transpose(1, 0, 2)))
-    ib = swap_core(ia)
-    y0 = shift(jnp.concatenate([own, f1, b1, f2]), dy=1)
-    y1 = shift(jnp.concatenate([b2, f3, b3, f4]), dy=3)
-    column = [(0, own), (-1, f1), (1, b1), (-2, f2), (2, b2), (-3, f3), (3, b3), (-4, f4)]
-
-    steps = jnp.asarray([dz for dz, _ in column] * 2, dtype=jnp.int32)
-    zs = (z + 8 + steps) % 8
-    ys = ylo ^ jnp.asarray([0] * 8 + [1] * 8, dtype=jnp.int32)
-    bases = (zs * 4 + ys * 2 + core) * 160 + half * HALF
-    meta = jnp.concatenate(
-        [bases, zs * 2 + ys, jnp.stack([core, half, quarter])]
-    ).astype(jnp.int32)
-
-    held = [block for _, block in column]
-    sides = (queries, queries_far, left, left_far, right, right_far, wa, wb)
-    e0, m0, l0 = score_call(meta, 0, held, [], *sides)
-    e1, m1, l1, keys = score_call(meta, 8, [y0, y1], held, *sides)
-
-    logits, ours, sent = forward_call(meta, keys, (m0, l0, m1, l1), ia, ib, wa, wb)
+    ia, wa = lax.optimization_barrier((ia, wa, left_far, right_far))[:2]
+    ib, wb = swap_core(ia), swap_core(wa)
+    meta = jnp.stack([z, ylo, core, half, quarter]).astype(jnp.int32)
+
+    sides = (queries, queries_far, left, left_far, right, right_far, pa, pb)
+    exps, m0, l0, keys = score_call(meta, 0, [own, f1, b1, f2, b2, f3, b3, f4], [], *sides)
+    exps, m1, l1, keys = score_call(meta, 1, [y0, y1], [exps, keys], *sides)
+
+    logits, ours, sent = forward_call(meta, keys, (m0, l0, m1, l1), ia, ib, pa, pb, wa, wb)
     here, up, down = pair_call(ours, swap_core(sent))
     up, down = shift(up, dx=1), shift(down, dx=3)
-    sums = head_sum_call(meta, e0, e1, m0, m1, here, up, down)
+    sums = head_sum_call(meta, exps, m0, m1, here, up, down)
     group = (dict(dx=2), dict(dy=2), dict(dx=2, dy=2))
     target = [sums[0]] + [shift(part, **move) for part, move in zip(sums[1:], group)]
 

time: 159 us -> 153 us (0.962)
  waiting for transfers between devices: 31.9 us -> 29.4 us
  other arithmetic: 7.91 us -> 5.91 us
  starting transfers between devices: 34.8 us -> 36.7 us
  local copies, waits for them, and re-layouts: 24.4 us -> 22.6 us
    ppermute x23 -> x24, waiting for transfers between devices: 21.7 us -> 19.2 us  [shift(): return lax.ppermute(value, ALL, pairs)]
    ppermute x23 -> x24, starting transfers between devices: 29.4 us -> 30.7 us  [shift(): return lax.ppermute(value, ALL, pairs)]
    unnamed x69 -> x51, local copies, waits for them, and re-layouts: 19.9 us -> 19.4 us
    concatenate x3 -> x2, other arithmetic: 3.56 us -> 3.63 us  [the longest x1 1.89 us: body(): jnp.concatenate([b2, f3, b3, f4])]
  transfers between devices with their start and end apart: 24 -> 25, of which waited for: 11 -> 10; matrix products, arithmetic and copies ran while one was open for 7% -> 5% of each run, Pallas kernels for 14% -> 14%
where the time goes in v5:
time: 153 us; the launch traced here: 152 us
  Pallas kernels  41.5 us (27%)
  starting transfers between devices  36.7 us (24%)
  waiting for transfers between devices  29.4 us (19%)
  local copies, waits for them, and re-layouts  22.6 us (15%)
  blocking collectives  14.4 us (9%)
  other arithmetic  5.91 us (4%)
  between operations  1.61 us (1%)
    ppermute x24, starting transfers between devices, shift(): return lax.ppermute(value, ALL, pairs)  30.7 us
    pallas_call x2, Pallas kernels, score_call(): pl.pallas_call(lambda *refs: score_kernel(chunk, spans, *refs), grid_spec...  22 us
    unnamed x51, local copies, waits for them, and re-layouts  19.4 us
    ppermute x24, waiting for transfers between devices, shift(): return lax.ppermute(value, ALL, pairs)  19.2 us
    all_to_all x1, blocking collectives, gather_head(): return lax.all_to_all(wide, ('yhi', 'xh', 'xp'), 0, 0, tiled=True)  14.4 us
    all_to_all x1, waiting for transfers between devices, body(): kg = lax.all_to_all(kg, ('z', 'ylo'), 0, 0, tiled=True)  10.2 us
    pallas_call x1, Pallas kernels, backward_call(): pl.pallas_call(backward_kernel, grid_spec=pltpu.PrefetchScalarGridSpec(nu...  8.91 us
    all_to_all x1, starting transfers between devices, body(): kg = lax.all_to_all(kg, ('z', 'ylo'), 0, 0, tiled=True)  6.02 us
  transfers between devices with their start and end apart: 25, of which 10 were waited for; matrix products, arithmetic and copies ran while one was open for 5% of the time, Pallas kernels for 14%

profile of v5, /device:TPU:2, one launch (start us, length us, event | category | flops | bytes accessed | tf_op | source)
XLA Modules:
  0.0 152.1 jit_solution(200889619024566945)
XLA Ops:
  1.6 2.0 %collective-permute-start = (bf16[80,704]{1,0:T(8,128)(2,1)S(1)}, bf16[80,704]{1,0:T(8,128)(2,1)S(1)}, u32[]{:S(2)}, u32[]{:S(2)}) collective-permute-start(bf16[80,704]{1,0:T(8,128)(2,1)S(1)} %fusion.refs_1_), channel_id=1, source_target_pairs={{0,4},{1,5},{4,8},{5,9},{8,12},{9,13},{12,16},{13,17},{16,20},{17,... | collective-permute-start | bytes 337928 | tf_op jit(solution)/shard_map/ppermute | solution.py:39
  3.6 4.0 %collective-permute-start.1 = (bf16[80,704]{1,0:T(8,128)(2,1)S(1)}, bf16[80,704]{1,0:T(8,128)(2,1)S(1)}, u32[]{:S(2)}, u32[]{:S(2)}) collective-permute-start(bf16[80,704]{1,0:T(8,128)(2,1)S(1)} %fusion.refs_1_), channel_id=1, source_target_pairs={{0,28},{1,29},{4,0},{5,1},{8,4},{9,5},{12,8},{13,9},{16,12},{17,13... | collective-permute-start | bytes 337928 | tf_op jit(solution)/shard_map/ppermute | solution.py:39
  7.6 2.4 %fusion.3 = (bf16[4,576,128]{2,1,0:T(8,128)(2,1)}, bf16[4,576,128]{2,1,0:T(8,128)(2,1)}) fusion(bf16[8,576,128]{2,1,0:T(8,128)(2,1)} %bitcast.24), kind=kLoop, calls=%fused_computation.19 | loop fusion | bytes 2359296 | tf_op jit(solution)/shard_map/slice | solution.py:479
  12.8 3.2 %collective-permute-start.3 = (bf16[80,704]{1,0:T(8,128)(2,1)S(1)}, bf16[80,704]{1,0:T(8,128)(2,1)}, u32[]{:S(2)}, u32[]{:S(2)}) collective-permute-start(bf16[80,704]{1,0:T(8,128)(2,1)S(1)} %collective-permute-done.1.refs_3_), channel_id=1, source_target_pairs={{0,28},{1,29},{4,0},{5,1},{8,4},{9,5},{12,8},{13,9},{16,12},{17,13... | collective-permute-start | bytes 337928 | tf_op jit(solution)/shard_map/ppermute | solution.py:39
  16.0 3.0 %collective-permute-done.2.refs_4_ = bf16[80,704]{1,0:T(8,128)(2,1)} collective-permute-done((bf16[80,704]{1,0:T(8,128)(2,1)S(1)}, bf16[80,704]{1,0:T(8,128)(2,1)}, u32[]{:S(2)}, u32[]{:S(2)}) %collective-permute-start.2) | collective-permute-done | bytes 112672 | tf_op jit(solution)/shard_map/ppermute | solution.py:39
  19.6 2.6 %collective-permute-start.5 = (bf16[80,704]{1,0:T(8,128)(2,1)}, bf16[80,704]{1,0:T(8,128)(2,1)}, u32[]{:S(2)}, u32[]{:S(2)}) collective-permute-start(bf16[80,704]{1,0:T(8,128)(2,1)} %collective-permute-done.3.refs_5_), channel_id=1, source_target_pairs={{0,28},{1,29},{4,0},{5,1},{8,4},{9,5},{12,8},{13,9},{16,12},{17,13... | collective-permute-start | bytes 337928 | tf_op jit(solution)/shard_map/ppermute | solution.py:39
  22.4 3.0 %copy.16 = bf16[128,64,128]{2,0,1:T(8,128)(2,1)S(1)} copy(bf16[128,64,128]{2,1,0:T(8,128)(2,1)} %param.9) | data formatting | bytes 4194304 | tf_op args[2]
  25.5 2.8 %collective-permute-start.6 = (bf16[80,704]{1,0:T(8,128)(2,1)}, bf16[80,704]{1,0:T(8,128)(2,1)S(1)}, u32[]{:S(2)}, u32[]{:S(2)}) collective-permute-start(bf16[80,704]{1,0:T(8,128)(2,1)} %collective-permute-done.4.refs_6_), channel_id=1, source_target_pairs={{0,4},{1,5},{4,8},{5,9},{8,12},{9,13},{12,16},{13,17},{16,20},{17,... | collective-permute-start | bytes 337928 | tf_op jit(solution)/shard_map/ppermute | solution.py:39
  30.1 2.6 %collective-permute-done.6.refs_8_ = bf16[80,704]{1,0:T(8,128)(2,1)S(1)} collective-permute-done((bf16[80,704]{1,0:T(8,128)(2,1)}, bf16[80,704]{1,0:T(8,128)(2,1)S(1)}, u32[]{:S(2)}, u32[]{:S(2)}) %collective-permute-start.6) | collective-permute-done | bytes 112672 | tf_op jit(solution)/shard_map/ppermute | solution.py:39
  32.7 1.9 %pad_maximum_fusion.1 = bf16[320,704]{1,0:T(8,128)(2,1)} fusion(bf16[80,704]{1,0:T(8,128)(2,1)S(1)} %collective-permute-done.6.refs_8_, bf16[80,704]{1,0:T(8,128)(2,1)} %collective-permute-done.5.refs_7_, bf16[80,704]{1,0:T(8,128)(2,1)} %collective-permute-done.4.refs_6_, bf16[80,704]{1,0:T(8,128)(2,1)} %collective-permute-done.3.refs_5_), kind=kLoop, calls=%fused_computation.2 | loop fusion | flops 1802240 | bytes 901120 | tf_op jit(solution)/shard_map/concatenate | solution.py:489
  46.9 11.4 %scores.2 = (bf16[16,1280,256]{2,1,0:T(8,128)(2,1)S(1)}, f32[16,256]{1,0:T(8,128)S(1)}, f32[16,256]{1,0:T(8,128)S(1)}, bf16[320,128]{1,0:T(8,128)(2,1)S(1)}) custom-call(s32[5]{0:T(128)S(1)} %stack.23.refs_0_.meta, bf16[80,704]{1,0:T(8,128)(2,1)S(1)} %fusion.refs_1_, bf16[80,704]{1,0:T(8,128)(2,1)S(1)} %collective-permute-done.refs_2_, ...), custom_call_target="tpu_custom_call" | custom-call | flops 6039797760 | bytes 5242880 | tf_op jit(solution)/shard_map/scores/pallas_call | solution.py:154
  58.4 10.6 %scores.3 = (bf16[16,1280,256]{2,1,0:T(8,128)(2,1)S(1)}, f32[16,256]{1,0:T(8,128)S(1)}, f32[16,256]{1,0:T(8,128)S(1)}, bf16[320,128]{1,0:T(8,128)(2,1)S(1)}) custom-call(s32[5]{0:T(128)S(1)} %stack.23.refs_0_.meta, bf16[320,704]{1,0:T(8,128)(2,1)S(1)} %collective-permute-done.10.refs_1_, ...), custom_call_target="tpu_custom_call", output_to_operand_aliasing={{0}: (3, {})} | custom-call | flops 6039797760 | bytes 5242880 | tf_op jit(solution)/shard_map/scores/pallas_call | solution.py:154
  69.0 4.0 %copy-done = bf16[16,1280,256]{2,1,0:T(8,128)(2,1)} copy-done((bf16[16,1280,256]{2,1,0:T(8,128)(2,1)}, bf16[16,1280,256]{2,1,0:T(8,128)(2,1)S(1)}, u32[]{:S(2)}) %copy-start) | copy-done | bytes 10485784
  73.0 5.1 %index_forward.1 = (f32[320,256]{1,0:T(8,128)S(1)}, f32[2,24,256]{2,1,0:T(8,128)S(1)}, f32[2,24,256]{2,1,0:T(8,128)S(1)}) custom-call(s32[5]{0:T(128)S(1)} %stack.23.refs_0_.meta, bf16[320,128]{1,0:T(8,128)(2,1)S(1)} %get-tuple-element.57.keys, f32[16,256]{1,0:T(8,128)S(1)} %get-tuple-element.58.m0, f32[16,256]{1,0:T(8,128)S(1)} %get-tuple-element.59.l0, ...), custom_call_target="tpu_custom_call" | custom-call | flops 1342177280 | bytes 5242880 | tf_op jit(solution)/shard_map/index_forward/pallas_call | solution.py:340
  85.0 3.7 %collective-permute-done.18.up = f32[2,8,256]{2,1,0:T(8,128)S(1)} collective-permute-done((f32[2,8,256]{2,1,0:T(8,128)}, f32[2,8,256]{2,1,0:T(8,128)S(1)}, u32[]{:S(2)}, u32[]{:S(2)}) %collective-permute-start.18) | collective-permute-done | bytes 16416 | tf_op jit(solution)/shard_map/ppermute | solution.py:39
  88.7 4.0 %copy-done.1 = bf16[16,1280,256]{2,1,0:T(8,128)(2,1)S(1)} copy-done((bf16[16,1280,256]{2,1,0:T(8,128)(2,1)S(1)}, bf16[16,1280,256]{2,1,0:T(8,128)(2,1)}, u32[]{:S(2)}) %copy-start.1) | copy-done | bytes 10485784
  93.5 4.0 %head_sum.1 = (bf16[336,256]{1,0:T(8,128)(2,1)S(1)}, bf16[336,256]{1,0:T(8,128)(2,1)S(1)}, bf16[336,256]{1,0:T(8,128)(2,1)S(1)}, bf16[336,256]{1,0:T(8,128)(2,1)S(1)}) custom-call(s32[5]{0:T(128)S(1)} %stack.23.refs_0_.meta, bf16[16,1280,256]{2,1,0:T(8,128)(2,1)S(1)} %copy-done.1, f32[16,256]{1,0:T(8,128)S(1)} %get-tuple-element.58.m0, ...), custom_call_target="tpu_custom_call" | custom-call | bytes 11534336 | tf_op jit(solution)/shard_map/head_sum/pallas_call | solution.py:236
  99.3 2.0 %collective-permute-start.21 = (bf16[336,256]{1,0:T(8,128)(2,1)S(1)}, bf16[336,256]{1,0:T(8,128)(2,1)S(1)}, u32[]{:S(2)}, u32[]{:S(2)}) collective-permute-start(bf16[336,256]{1,0:T(8,128)(2,1)S(1)} %get-tuple-element.74), channel_id=1, source_target_pairs={{0,128},{1,129},{4,132},{5,133},{8,136},{9,137},{12,140},{13,141},... | collective-permute-start | bytes 516104 | tf_op jit(solution)/shard_map/ppermute | solution.py:39
  101.3 2.8 %collective-permute-start.22 = (bf16[336,256]{1,0:T(8,128)(2,1)S(1)}, bf16[336,256]{1,0:T(8,128)(2,1)S(1)}, u32[]{:S(2)}, u32[]{:S(2)}) collective-permute-start(bf16[336,256]{1,0:T(8,128)(2,1)S(1)} %get-tuple-element.75), channel_id=1, source_target_pairs={{0,192},{1,193},{4,196},{5,197},{8,200},{9,201},{12,204},{13,205},... | collective-permute-start | bytes 516104 | tf_op jit(solution)/shard_map/ppermute | solution.py:39
  106.2 4.4 %collective-permute-done.22.t3 = bf16[336,256]{1,0:T(8,128)(2,1)S(1)} collective-permute-done((bf16[336,256]{1,0:T(8,128)(2,1)S(1)}, bf16[336,256]{1,0:T(8,128)(2,1)S(1)}, u32[]{:S(2)}, u32[]{:S(2)}) %collective-permute-start.22) | collective-permute-done | bytes 172064 | tf_op jit(solution)/shard_map/ppermute | solution.py:39
  110.6 8.9 %index_backward.1 = (f32[80,128]{1,0:T(8,128)S(1)}, f32[80,128]{1,0:T(8,128)S(1)}, bf16[16,32,128]{2,1,0:T(8,128)(2,1)}) custom-call(s32[5]{0:T(128)S(1)} %stack.23.refs_0_.meta, bf16[320,128]{1,0:T(8,128)(2,1)S(1)} %copy-done.22, f32[320,256]{1,0:T(8,128)S(1)} %copy-done.20, bf16[336,256]{1,0:T(8,128)(2,1)S(1)} %get-tuple-element.72.t0, ...), custom_call_target="tpu_custom_call" | custom-call | flops 2684354560 | bytes 6291456 | tf_op jit(solution)/shard_map/index_backward/pallas_call | solution.py:421
  119.6 6.0 %all-to-all-start = ((bf16[16,32,128]{2,1,0:T(8,128)(2,1)}), bf16[16,32,128]{2,1,0:T(8,128)(2,1)S(1)}, u32[]{:S(2)}, u32[]{:S(2)}) async-start(bf16[16,32,128]{2,1,0:T(8,128)(2,1)} %get-tuple-element.76), calls=%async_computation | async-start | bytes 262144 | tf_op jit(solution)/shard_map/all_to_all | solution.py:513
  125.6 10.2 %all-to-all-done = bf16[16,32,128]{2,1,0:T(8,128)(2,1)S(1)} async-done(((bf16[16,32,128]{2,1,0:T(8,128)(2,1)}), bf16[16,32,128]{2,1,0:T(8,128)(2,1)S(1)}, u32[]{:S(2)}, u32[]{:S(2)}) %all-to-all-start) | async-done | bytes 131104 | tf_op jit(solution)/shard_map/all_to_all | solution.py:513
  135.9 14.4 %all_to_all.10 = bf16[8,112,128]{2,1,0:T(8,128)(2,1)S(1)} all-to-all(bf16[8,112,128]{2,1,0:T(8,128)(2,1)S(1)} %broadcast_in_dim.2), channel_id=1, replica_groups=mesh['yhi'=2,'xh'=2,'xp'=2,'z'=8,'ylo'=2,'core'=2] {'yhi','xh','xp'}, dimensions={0} | all-to-all | bytes 458752 | tf_op jit(solution)/shard_map/all_to_all | solution.py:458
  (106 shorter events, 31.5 us)
Async XLA Ops:
  1.6 11.1 %collective-permute-start = (bf16[80,704]{1,0:T(8,128)(2,1)S(1)}, bf16[80,704]{1,0:T(8,128)(2,1)S(1)}, u32[]{:S(2)}, u32[]{:S(2)}) collective-permute-start(bf16[80,704]{1,0:T(8,128)(2,1)S(1)} %fusion.refs_1_), channel_id=1, source_target_pairs={{0,4},{1,5},{4,8},{5,9},{8,12},{9,13},{12,16},{13,17},{16,20},{17,... | collective-permute-start | bytes 337928 | tf_op jit(solution)/shard_map/ppermute | solution.py:39
  3.6 9.1 %collective-permute-start.1 = (bf16[80,704]{1,0:T(8,128)(2,1)S(1)}, bf16[80,704]{1,0:T(8,128)(2,1)S(1)}, u32[]{:S(2)}, u32[]{:S(2)}) collective-permute-start(bf16[80,704]{1,0:T(8,128)(2,1)S(1)} %fusion.refs_1_), channel_id=1, source_target_pairs={{0,28},{1,29},{4,0},{5,1},{8,4},{9,5},{12,8},{13,9},{16,12},{17,13... | collective-permute-start | bytes 337928 | tf_op jit(solution)/shard_map/ppermute | solution.py:39
  10.0 22.7 %collective-permute-start.8 = (bf16[4,576,128]{2,1,0:T(8,128)(2,1)}, bf16[4,576,128]{2,1,0:T(8,128)(2,1)}, u32[]{:S(2)}, u32[]{:S(2)}) collective-permute-start(bf16[4,576,128]{2,1,0:T(8,128)(2,1)} %get-tuple-element.82), channel_id=1, source_target_pairs={{0,32},{1,33},{4,36},{5,37},{8,40},{9,41},{12,44},{13,45},{16,48},... | collective-permute-start | bytes 1769480 | tf_op jit(solution)/shard_map/ppermute | solution.py:39
  11.5 21.2 %collective-permute-start.9 = (bf16[4,576,128]{2,1,0:T(8,128)(2,1)}, bf16[4,576,128]{2,1,0:T(8,128)(2,1)}, u32[]{:S(2)}, u32[]{:S(2)}) collective-permute-start(bf16[4,576,128]{2,1,0:T(8,128)(2,1)} %get-tuple-element.81), channel_id=1, source_target_pairs={{0,96},{1,97},{4,100},{5,101},{8,104},{9,105},{12,108},{13,109},{1... | collective-permute-start | bytes 1769480 | tf_op jit(solution)/shard_map/ppermute | solution.py:39
  12.7 6.3 %collective-permute-start.2 = (bf16[80,704]{1,0:T(8,128)(2,1)S(1)}, bf16[80,704]{1,0:T(8,128)(2,1)}, u32[]{:S(2)}, u32[]{:S(2)}) collective-permute-start(bf16[80,704]{1,0:T(8,128)(2,1)S(1)} %collective-permute-done.refs_2_), channel_id=1, source_target_pairs={{0,4},{1,5},{4,8},{5,9},{8,12},{9,13},{12,16},{13,17},{16,20},{17,... | collective-permute-start | bytes 337928 | tf_op jit(solution)/shard_map/ppermute | solution.py:39
  12.8 6.2 %collective-permute-start.3 = (bf16[80,704]{1,0:T(8,128)(2,1)S(1)}, bf16[80,704]{1,0:T(8,128)(2,1)}, u32[]{:S(2)}, u32[]{:S(2)}) collective-permute-start(bf16[80,704]{1,0:T(8,128)(2,1)S(1)} %collective-permute-done.1.refs_3_), channel_id=1, source_target_pairs={{0,28},{1,29},{4,0},{5,1},{8,4},{9,5},{12,8},{13,9},{16,12},{17,13... | collective-permute-start | bytes 337928 | tf_op jit(solution)/shard_map/ppermute | solution.py:39
  19.0 6.5 %collective-permute-start.4 = (bf16[80,704]{1,0:T(8,128)(2,1)}, bf16[80,704]{1,0:T(8,128)(2,1)}, u32[]{:S(2)}, u32[]{:S(2)}) collective-permute-start(bf16[80,704]{1,0:T(8,128)(2,1)} %collective-permute-done.2.refs_4_), channel_id=1, source_target_pairs={{0,4},{1,5},{4,8},{5,9},{8,12},{9,13},{12,16},{13,17},{16,20},{17,... | collective-permute-start | bytes 337928 | tf_op jit(solution)/shard_map/ppermute | solution.py:39
  19.6 5.9 %collective-permute-start.5 = (bf16[80,704]{1,0:T(8,128)(2,1)}, bf16[80,704]{1,0:T(8,128)(2,1)}, u32[]{:S(2)}, u32[]{:S(2)}) collective-permute-start(bf16[80,704]{1,0:T(8,128)(2,1)} %collective-permute-done.3.refs_5_), channel_id=1, source_target_pairs={{0,28},{1,29},{4,0},{5,1},{8,4},{9,5},{12,8},{13,9},{16,12},{17,13... | collective-permute-start | bytes 337928 | tf_op jit(solution)/shard_map/ppermute | solution.py:39
  22.4 7.7 %collective-permute-start.7 = (f32[1,128]{1,0:T(1,128)S(1)}, f32[1,128]{1,0:T(1,128)S(1)}, u32[]{:S(2)}, u32[]{:S(2)}) collective-permute-start(f32[1,128]{1,0:T(1,128)S(1)} %convert_element_type.17.refs_15_.refs_11_.pa), channel_id=1, source_target_pairs={{0,1},{1,0},{4,5},{5,4},{8,9},{9,8},{12,13},{13,12},{16,17},{17,16... | collective-permute-start | bytes 1544 | tf_op jit(solution)/shard_map/ppermute | solution.py:39
  25.5 7.2 %collective-permute-start.6 = (bf16[80,704]{1,0:T(8,128)(2,1)}, bf16[80,704]{1,0:T(8,128)(2,1)S(1)}, u32[]{:S(2)}, u32[]{:S(2)}) collective-permute-start(bf16[80,704]{1,0:T(8,128)(2,1)} %collective-permute-done.4.refs_6_), channel_id=1, source_target_pairs={{0,4},{1,5},{4,8},{5,9},{8,12},{9,13},{12,16},{13,17},{16,20},{17,... | collective-permute-start | bytes 337928 | tf_op jit(solution)/shard_map/ppermute | solution.py:39
  34.6 2.2 %collective-permute-start.13 = (bf16[4,576,128]{2,1,0:T(8,128)(2,1)}, bf16[4,576,128]{2,1,0:T(8,128)(2,1)S(1)}, u32[]{:S(2)}, u32[]{:S(2)}) collective-permute-start(bf16[4,576,128]{2,1,0:T(8,128)(2,1)} %collective-permute-done.8.refs_11_.refs_7_), channel_id=1, source_target_pairs={{0,1},{1,0},{4,5},{5,4},{8,9},{9,8},{12,13},{13,12},{16,17},{17,16... | collective-permute-start | bytes 1769480 | tf_op jit(solution)/shard_map/ppermute | solution.py:39
  34.6 3.9 %collective-permute-start.14 = (bf16[4,576,128]{2,1,0:T(8,128)(2,1)}, bf16[4,576,128]{2,1,0:T(8,128)(2,1)S(1)}, u32[]{:S(2)}, u32[]{:S(2)}) collective-permute-start(bf16[4,576,128]{2,1,0:T(8,128)(2,1)} %collective-permute-done.9.refs_13_.refs_9_), channel_id=1, source_target_pairs={{0,1},{1,0},{4,5},{5,4},{8,9},{9,8},{12,13},{13,12},{16,17},{17,16... | collective-permute-start | bytes 1769480 | tf_op jit(solution)/shard_map/ppermute | solution.py:39
  35.1 7.9 %collective-permute-start.12 = (bf16[8,576,128]{2,1,0:T(8,128)(2,1)S(1)}, bf16[8,576,128]{2,1,0:T(8,128)(2,1)}, u32[]{:S(2)}, u32[]{:S(2)}) collective-permute-start(bf16[8,576,128]{2,1,0:T(8,128)(2,1)S(1)} %bitcast.25), channel_id=1, source_target_pairs={{0,1},{1,0},{4,5},{5,4},{8,9},{9,8},{12,13},{13,12},{16,17},{17,16... | collective-permute-start | bytes 3538952 | tf_op jit(solution)/shard_map/ppermute | solution.py:39
  39.3 33.7 %collective-permute-start.15 = (bf16[64,128,128]{2,1,0:T(8,128)(2,1)S(1)}, bf16[64,128,128]{2,1,0:T(8,128)(2,1)}, u32[]{:S(2)}, u32[]{:S(2)}) collective-permute-start(bf16[64,128,128]{2,1,0:T(8,128)(2,1)S(1)} %bitcast.21), channel_id=1, source_target_pairs={{0,1},{1,0},{4,5},{5,4},{8,9},{9,8},{12,13},{13,12},{16,17},{17,16... | collective-permute-start | bytes 6291464 | tf_op jit(solution)/shard_map/ppermute | solution.py:39
  39.5 18.8 %collective-permute-start.10 = (bf16[320,704]{1,0:T(8,128)(2,1)}, bf16[320,704]{1,0:T(8,128)(2,1)S(1)}, u32[]{:S(2)}, u32[]{:S(2)}) collective-permute-start(bf16[320,704]{1,0:T(8,128)(2,1)} %pad_maximum_fusion), channel_id=1, source_target_pairs={{0,2},{1,3},{4,6},{5,7},{8,10},{9,11},{12,14},{13,15},{16,18},{17,... | collective-permute-start | bytes 1351688 | tf_op jit(solution)/shard_map/ppermute | solution.py:39
  41.3 17.0 %collective-permute-start.11 = (bf16[320,704]{1,0:T(8,128)(2,1)}, bf16[320,704]{1,0:T(8,128)(2,1)S(1)}, u32[]{:S(2)}, u32[]{:S(2)}) collective-permute-start(bf16[320,704]{1,0:T(8,128)(2,1)} %pad_maximum_fusion.1), channel_id=1, source_target_pairs={{0,130},{1,131},{4,134},{5,135},{8,138},{9,139},{12,142},{13,143},... | collective-permute-start | bytes 1351688 | tf_op jit(solution)/shard_map/ppermute | solution.py:39
  42.9 30.1 %collective-permute-start.16 = (f32[64,128]{1,0:T(8,128)}, f32[64,128]{1,0:T(8,128)S(1)}, u32[]{:S(2)}, u32[]{:S(2)}) collective-permute-start(f32[64,128]{1,0:T(8,128)} %bitcast.28), channel_id=1, source_target_pairs={{0,1},{1,0},{4,5},{5,4},{8,9},{9,8},{12,13},{13,12},{16,17},{17,16... | collective-permute-start | bytes 98312 | tf_op jit(solution)/shard_map/ppermute | solution.py:39
  83.0 5.7 %collective-permute-start.19 = (f32[2,16,256]{2,1,0:T(8,128)}, f32[2,16,256]{2,1,0:T(8,128)S(1)}, u32[]{:S(2)}, u32[]{:S(2)}) collective-permute-start(f32[2,16,256]{2,1,0:T(8,128)} %get-tuple-element.71), channel_id=1, source_target_pairs={{0,96},{1,97},{4,100},{5,101},{8,104},{9,105},{12,108},{13,109},{1... | collective-permute-start | bytes 98312 | tf_op jit(solution)/shard_map/ppermute | solution.py:39
  84.7 3.9 %collective-permute-start.18 = (f32[2,8,256]{2,1,0:T(8,128)}, f32[2,8,256]{2,1,0:T(8,128)S(1)}, u32[]{:S(2)}, u32[]{:S(2)}) collective-permute-start(f32[2,8,256]{2,1,0:T(8,128)} %get-tuple-element.70), channel_id=1, source_target_pairs={{0,32},{1,33},{4,36},{5,37},{8,40},{9,41},{12,44},{13,45},{16,48},... | collective-permute-start | bytes 49160 | tf_op jit(solution)/shard_map/ppermute | solution.py:39
  97.5 7.0 %collective-permute-start.20 = (bf16[336,256]{1,0:T(8,128)(2,1)S(1)}, bf16[336,256]{1,0:T(8,128)(2,1)S(1)}, u32[]{:S(2)}, u32[]{:S(2)}) collective-permute-start(bf16[336,256]{1,0:T(8,128)(2,1)S(1)} %get-tuple-element.73), channel_id=1, source_target_pairs={{0,64},{1,65},{4,68},{5,69},{8,72},{9,73},{12,76},{13,77},{16,80},... | collective-permute-start | bytes 516104 | tf_op jit(solution)/shard_map/ppermute | solution.py:39
  99.3 6.9 %collective-permute-start.21 = (bf16[336,256]{1,0:T(8,128)(2,1)S(1)}, bf16[336,256]{1,0:T(8,128)(2,1)S(1)}, u32[]{:S(2)}, u32[]{:S(2)}) collective-permute-start(bf16[336,256]{1,0:T(8,128)(2,1)S(1)} %get-tuple-element.74), channel_id=1, source_target_pairs={{0,128},{1,129},{4,132},{5,133},{8,136},{9,137},{12,140},{13,141},... | collective-permute-start | bytes 516104 | tf_op jit(solution)/shard_map/ppermute | solution.py:39
  101.3 9.3 %collective-permute-start.22 = (bf16[336,256]{1,0:T(8,128)(2,1)S(1)}, bf16[336,256]{1,0:T(8,128)(2,1)S(1)}, u32[]{:S(2)}, u32[]{:S(2)}) collective-permute-start(bf16[336,256]{1,0:T(8,128)(2,1)S(1)} %get-tuple-element.75), channel_id=1, source_target_pairs={{0,192},{1,193},{4,196},{5,197},{8,200},{9,201},{12,204},{13,205},... | collective-permute-start | bytes 516104 | tf_op jit(solution)/shard_map/ppermute | solution.py:39
  119.6 6.0 %collective-permute-start.23 = (f32[80,128]{1,0:T(8,128)S(1)}, f32[80,128]{1,0:T(8,128)S(1)}, u32[]{:S(2)}, u32[]{:S(2)}) collective-permute-start(f32[80,128]{1,0:T(8,128)S(1)} %get-tuple-element.78), channel_id=1, source_target_pairs={{0,1},{1,0},{4,5},{5,4},{8,9},{9,8},{12,13},{13,12},{16,17},{17,16... | collective-permute-start | bytes 122888 | tf_op jit(solution)/shard_map/ppermute | solution.py:39
  119.6 16.3 %all-to-all-start = ((bf16[16,32,128]{2,1,0:T(8,128)(2,1)}), bf16[16,32,128]{2,1,0:T(8,128)(2,1)S(1)}, u32[]{:S(2)}, u32[]{:S(2)}) async-start(bf16[16,32,128]{2,1,0:T(8,128)(2,1)} %get-tuple-element.76), calls=%async_computation | async-start | bytes 262144 | tf_op jit(solution)/shard_map/all_to_all | solution.py:513
  (26 other events, 168.9 us)

commit v6 on v5

--- a/solution.py
+++ b/solution.py
@@ -44,6 +44,10 @@
 
 
 LOG2E = math.log2(math.e)
+
+
+def in_vmem(*values):
+    return [pltpu.with_memory_space_constraint(value, pltpu.VMEM) for value in values]
 
 
 def slot_of(meta, i):
@@ -117,21 +121,21 @@
             queries = jnp.where(step < 4, own, jnp.where(step < 6, left, right))
             top = jnp.max(tops[last, k], axis=0, keepdims=True)
             safe = jnp.where(top == NEG, 0.0, top)
+            head = 2 * jnp.maximum(step - 1, 0) + k
             new = jnp.full((8, 256), NEG, jnp.float32)
             total = jnp.zeros((8, 256), jnp.float32)
             for t in range(0, CHUNK, cut):
-                piece = slice(t, t + cut)
+                piece, rows = slice(t, t + cut), slice(chunk * CHUNK + t, chunk * CHUNK + t + cut)
                 scores = jnp.dot(keys[piece, DI:], queries, preferred_element_type=jnp.float32)
                 scores = scores + bias[piece, :]
                 raw[now, k, piece, :] = scores
                 new = jnp.maximum(new, jnp.max(scores.reshape(cut // 8, 8, 256), axis=0))
                 exps = jnp.exp2((raw[last, k, piece, :] - safe) * SCORE2)
-                e_ref[k, piece, :] = exps.astype(jnp.bfloat16)
+                e_ref[head, rows, :] = exps.astype(jnp.bfloat16)
                 total = total + jnp.sum(exps.reshape(cut // 8, 8, 256), axis=0)
             tops[now, k] = new
-            head = pl.ds(2 * jnp.maximum(step - 1, 0) + k, 1)
-            m_ref[head, :] = top
-            l_ref[head, :] = jnp.sum(total, axis=0, keepdims=True)
+            m_ref[pl.ds(head, 1), :] = top
+            l_ref[pl.ds(head, 1), :] = jnp.sum(total, axis=0, keepdims=True)
 
     @pl.when(step % 2 == 0)
     def _():
@@ -150,14 +154,14 @@
         return pl.BlockSpec((2, DQ, 128), lambda h, meta: (jnp.clip(h - start, 0, count - 1), 0, 0))
 
     anywhere = pl.BlockSpec(memory_space=pl.ANY)
-    exps = pl.BlockSpec((2, CHUNK, 256), lambda h, meta: (jnp.maximum(h - 1, 0), chunk, 0))
+    exps = pl.BlockSpec(memory_space=pltpu.VMEM)
     return pl.pallas_call(
         lambda *refs: score_kernel(chunk, spans, *refs),
         grid_spec=pltpu.PrefetchScalarGridSpec(
             num_scalar_prefetch=1,
             grid=(HEADS // 2 + 1,),
             in_specs=[anywhere] * len(blocks)
-            + ([anywhere, whole((ROWS, DI))] if chunk else [])
+            + ([exps, whole((ROWS, DI))] if chunk else [])
             + [heads(0, 4)] * 2
             + [heads(4, 2)] * 2
             + [heads(6, 2)] * 2
@@ -172,10 +176,10 @@
             ],
         ),
         out_shape=[
-            jax.ShapeDtypeStruct((HEADS, 2 * CHUNK, 256), jnp.bfloat16),
-            jax.ShapeDtypeStruct((HEADS, 256), jnp.float32),
-            jax.ShapeDtypeStruct((HEADS, 256), jnp.float32),
-            jax.ShapeDtypeStruct((ROWS, DI), jnp.bfloat16),
+            pltpu.VMEM((HEADS, 2 * CHUNK, 256), jnp.bfloat16),
+            pltpu.VMEM((HEADS, 256), jnp.float32),
+            pltpu.VMEM((HEADS, 256), jnp.float32),
+            pltpu.VMEM((ROWS, DI), jnp.bfloat16),
         ],
         input_output_aliases={1 + len(blocks): 0} if chunk else {},
         cost_estimate=pl.CostEstimate(
@@ -185,7 +189,7 @@
         ),
         compiler_params=pltpu.CompilerParams(vmem_limit_bytes=VMEM),
         name="scores",
-    )(meta, *blocks, *before, qa, qb, na, nb, ma, mb, pa, pb)
+    )(meta, *in_vmem(*blocks), *before, *in_vmem(qa, qb, na, nb, ma, mb, pa, pb))
 
 
 def head_sum_kernel(meta, e_ref, m0, m1, here, up, down, o0, o1, o2, o3, total_ref, ratio):
@@ -214,7 +218,8 @@
     chunk = i // 8
     total = jnp.zeros((HALF, 256), jnp.float32)
     for h in range(HEADS):
-        total = total + e_ref[h].astype(jnp.float32) * ratio[chunk, h : h + 1, :]
+        part = e_ref[h, pl.ds(pl.multiple_of(i * HALF, HALF), HALF), :]
+        total = total + part.astype(jnp.float32) * ratio[chunk, h : h + 1, :]
     total_ref[...] = total
     slot = slot_of(meta, i)
     quarter = meta[4]
@@ -230,7 +235,7 @@
 
 
 def head_sum_call(meta, exps, *stats):
-    piece = pl.BlockSpec((HEADS, HALF, 256), lambda i, meta: (0, i, 0))
+    piece = pl.BlockSpec(memory_space=pltpu.VMEM)
     whole = lambda shape: pl.BlockSpec(shape, lambda i, meta: (0,) * len(shape))
     out = pl.BlockSpec((ROWS + UNIT, 256), lambda i, meta: (0, 0))
     return pl.pallas_call(
@@ -245,11 +250,11 @@
                 pltpu.VMEM((2, HEADS, 256), jnp.float32),
             ],
         ),
-        out_shape=[jax.ShapeDtypeStruct((ROWS + UNIT, 256), jnp.bfloat16)] * 4,
+        out_shape=[pltpu.VMEM((ROWS + UNIT, 256), jnp.bfloat16)] * 4,
         cost_estimate=pl.CostEstimate(flops=0, bytes_accessed=11 << 20, transcendentals=0),
         compiler_params=pltpu.CompilerParams(vmem_limit_bytes=VMEM),
         name="head_sum",
-    )(meta, exps, *stats)
+    )(meta, *in_vmem(exps, *stats))
 
 
 def key_places(meta):
@@ -323,9 +328,9 @@
 def pair_call(ours, theirs):
     return pl.pallas_call(
         pair_kernel,
-        out_shape=[jax.ShapeDtypeStruct((2, rows, 256), jnp.float32) for rows in (24, 8, 16)],
+        out_shape=[pltpu.VMEM((2, rows, 256), jnp.float32) for rows in (24, 8, 16)],
         name="pair_statistics",
-    )(ours, theirs)
+    )(*in_vmem(ours, theirs))
 
 
 def j_specs():
@@ -346,16 +351,16 @@
             out_specs=[whole((ROWS, 256)), whole((2, 24, 256)), whole((2, 24, 256))],
         ),
         out_shape=[
-            jax.ShapeDtypeStruct((ROWS, 256), jnp.float32),
-            jax.ShapeDtypeStruct((2, 24, 256), jnp.float32),
-            jax.ShapeDtypeStruct((2, 24, 256), jnp.float32),
+            pltpu.VMEM((ROWS, 256), jnp.float32),
+            pltpu.VMEM((2, 24, 256), jnp.float32),
+            pltpu.VMEM((2, 24, 256), jnp.float32),
         ],
         cost_estimate=pl.CostEstimate(
             flops=2 * NI * ROWS * 256 * DI, bytes_accessed=5 << 20, transcendentals=0
         ),
         compiler_params=pltpu.CompilerParams(vmem_limit_bytes=VMEM),
         name="index_forward",
-    )(meta, keys, *stats, ia, ib, pa, pb, wa, wb)
+    )(meta, *in_vmem(keys, *stats, ia, ib, pa, pb, wa, wb))
 
 
 def backward_kernel(meta, keys, logits, t0, t1, t2, t3, ia, ib, wja, wjb, rows_a, rows_b, kg, grad, acc):
@@ -441,16 +446,16 @@
             ],
         ),
         out_shape=[
-            jax.ShapeDtypeStruct((NI + 16, 128), jnp.float32),
-            jax.ShapeDtypeStruct((NI + 16, 128), jnp.float32),
-            jax.ShapeDtypeStruct((BLOCKS, 2 * UNIT, DI), jnp.bfloat16),
+            pltpu.VMEM((NI + 16, 128), jnp.float32),
+            pltpu.VMEM((NI + 16, 128), jnp.float32),
+            pltpu.VMEM((BLOCKS, 2 * UNIT, DI), jnp.bfloat16),
         ],
         cost_estimate=pl.CostEstimate(
             flops=4 * NI * ROWS * 256 * DI, bytes_accessed=6 << 20, transcendentals=0
         ),
         compiler_params=pltpu.CompilerParams(vmem_limit_bytes=VMEM),
         name="index_backward",
-    )(meta, keys, logits, *target, ia, ib, wa, wb)
+    )(meta, *in_vmem(keys, logits, *target, ia, ib, wa, wb))
 
 
 def gather_head(value):
@@ -490,13 +495,13 @@
     y0, y1, left, right = lax.optimization_barrier((y0, y1, left, right))
     y0, y1 = shift(y0, dy=1), shift(y1, dy=3)
     left_far, right_far = swap_core(left), swap_core(right)
-    ia, wa = lax.optimization_barrier((ia, wa, left_far, right_far))[:2]
-    ib, wb = swap_core(ia), swap_core(wa)
     meta = jnp.stack([z, ylo, core, half, quarter]).astype(jnp.int32)
 
     sides = (queries, queries_far, left, left_far, right, right_far, pa, pb)
     exps, m0, l0, keys = score_call(meta, 0, [own, f1, b1, f2, b2, f3, b3, f4], [], *sides)
-    exps, m1, l1, keys = score_call(meta, 1, [y0, y1], [exps, keys], *sides)
+    ia, wa = lax.optimization_barrier((ia, wa, m0))[:2]
+    ib, wb = swap_core(ia), swap_core(wa)
+    exps, m1, l1, keys = score_call(meta, 1, [y0, y1], in_vmem(exps, keys), *sides)
 
     logits, ours, sent = forward_call(meta, keys, (m0, l0, m1, l1), ia, ib, pa, pb, wa, wb)
     here, up, down = pair_call(ours, swap_core(sent))

time: 153 us -> 157 us (1.026)
  waiting for transfers between devices: 29.4 us -> 46.3 us
  local copies, waits for them, and re-layouts: 22.6 us -> 17.6 us
  Pallas kernels: 41.5 us -> 36.9 us
  starting transfers between devices: 36.7 us -> 33.1 us
    ppermute x24, waiting for transfers between devices: 19.2 us -> 36.1 us  [shift(): return lax.ppermute(value, ALL, pairs)]
    unnamed x51 -> x43, local copies, waits for them, and re-layouts: 19.4 us -> 14.4 us
    ppermute x24, starting transfers between devices: 30.7 us -> 28.4 us  [shift(): return lax.ppermute(value, ALL, pairs)]
  transfers between devices with their start and end apart: 25 -> 25, of which waited for: 10 -> 12; matrix products, arithmetic and copies ran while one was open for 5% -> 6% of each run, Pallas kernels for 14% -> 7%
where the time goes in v6:
time: 157 us; the launch traced here: 156 us
  waiting for transfers between devices  46.3 us (29%)
  Pallas kernels  36.9 us (24%)
  starting transfers between devices  33.1 us (21%)
  local copies, waits for them, and re-layouts  17.6 us (11%)
  blocking collectives  14.4 us (9%)
  other arithmetic  5.99 us (4%)
    ppermute x24, waiting for transfers between devices, shift(): return lax.ppermute(value, ALL, pairs)  36.1 us
    ppermute x24, starting transfers between devices, shift(): return lax.ppermute(value, ALL, pairs)  28.4 us
    pallas_call x2, Pallas kernels, score_call(): pl.pallas_call(lambda *refs: score_kernel(chunk, spans, *refs), grid_spec...  22.1 us
    unnamed x43, local copies, waits for them, and re-layouts  14.4 us
    all_to_all x1, blocking collectives, gather_head(): return lax.all_to_all(wide, ('yhi', 'xh', 'xp'), 0, 0, tiled=True)  14.4 us
    all_to_all x1, waiting for transfers between devices, body(): kg = lax.all_to_all(kg, ('z', 'ylo'), 0, 0, tiled=True)  10.2 us
    pallas_call x1, Pallas kernels, backward_call(): pl.pallas_call(backward_kernel, grid_spec=pltpu.PrefetchScalarGridSpec(nu...  7.67 us
    all_to_all x1, starting transfers between devices, body(): kg = lax.all_to_all(kg, ('z', 'ylo'), 0, 0, tiled=True)  4.68 us
  transfers between devices with their start and end apart: 25, of which 12 were waited for; matrix products, arithmetic and copies ran while one was open for 6% of the time, Pallas kernels for 7%

profile of v6, /device:TPU:2, one launch (start us, length us, event | category | flops | bytes accessed | tf_op | source)
XLA Modules:
  0.0 155.9 jit_solution(12791804880289480695)
XLA Ops:
  1.7 5.9 %collective-permute-start.1 = (bf16[80,704]{1,0:T(8,128)(2,1)S(1)}, bf16[80,704]{1,0:T(8,128)(2,1)S(1)}, u32[]{:S(2)}, u32[]{:S(2)}) collective-permute-start(bf16[80,704]{1,0:T(8,128)(2,1)S(1)} %fusion.refs_1_), channel_id=1, source_target_pairs={{0,28},{1,29},{4,0},{5,1},{8,4},{9,5},{12,8},{13,9},{16,12},{17,13... | collective-permute-start | bytes 337928 | tf_op jit(solution)/shard_map/ppermute | solution.py:39
  7.6 2.4 %fusion.3 = (bf16[4,576,128]{2,1,0:T(8,128)(2,1)}, bf16[4,576,128]{2,1,0:T(8,128)(2,1)}) fusion(bf16[8,576,128]{2,1,0:T(8,128)(2,1)} %bitcast.24), kind=kLoop, calls=%fused_computation.19 | loop fusion | bytes 2359296 | tf_op jit(solution)/shard_map/slice | solution.py:484
  13.7 3.2 %collective-permute-start.3 = (bf16[80,704]{1,0:T(8,128)(2,1)S(1)}, bf16[80,704]{1,0:T(8,128)(2,1)}, u32[]{:S(2)}, u32[]{:S(2)}) collective-permute-start(bf16[80,704]{1,0:T(8,128)(2,1)S(1)} %collective-permute-done.1.refs_3_), channel_id=1, source_target_pairs={{0,28},{1,29},{4,0},{5,1},{8,4},{9,5},{12,8},{13,9},{16,12},{17,13... | collective-permute-start | bytes 337928 | tf_op jit(solution)/shard_map/ppermute | solution.py:39
  17.0 3.2 %collective-permute-done.2.refs_4_ = bf16[80,704]{1,0:T(8,128)(2,1)} collective-permute-done((bf16[80,704]{1,0:T(8,128)(2,1)S(1)}, bf16[80,704]{1,0:T(8,128)(2,1)}, u32[]{:S(2)}, u32[]{:S(2)}) %collective-permute-start.2) | collective-permute-done | bytes 112672 | tf_op jit(solution)/shard_map/ppermute | solution.py:39
  20.1 3.2 %collective-permute-start.5 = (bf16[80,704]{1,0:T(8,128)(2,1)}, bf16[80,704]{1,0:T(8,128)(2,1)}, u32[]{:S(2)}, u32[]{:S(2)}) collective-permute-start(bf16[80,704]{1,0:T(8,128)(2,1)} %collective-permute-done.3.refs_5_), channel_id=1, source_target_pairs={{0,28},{1,29},{4,0},{5,1},{8,4},{9,5},{12,8},{13,9},{16,12},{17,13... | collective-permute-start | bytes 337928 | tf_op jit(solution)/shard_map/ppermute | solution.py:39
  23.5 3.0 %copy.16 = bf16[128,64,128]{2,0,1:T(8,128)(2,1)S(1)} copy(bf16[128,64,128]{2,1,0:T(8,128)(2,1)} %param.9) | data formatting | bytes 4194304 | tf_op args[2]
  29.5 4.3 %collective-permute-done.6.refs_8_ = bf16[80,704]{1,0:T(8,128)(2,1)S(1)} collective-permute-done((bf16[80,704]{1,0:T(8,128)(2,1)}, bf16[80,704]{1,0:T(8,128)(2,1)S(1)}, u32[]{:S(2)}, u32[]{:S(2)}) %collective-permute-start.6) | collective-permute-done | bytes 112672 | tf_op jit(solution)/shard_map/ppermute | solution.py:39
  33.8 1.9 %pad_maximum_fusion.1 = bf16[320,704]{1,0:T(8,128)(2,1)} fusion(bf16[80,704]{1,0:T(8,128)(2,1)S(1)} %collective-permute-done.6.refs_8_, bf16[80,704]{1,0:T(8,128)(2,1)} %collective-permute-done.5.refs_7_, bf16[80,704]{1,0:T(8,128)(2,1)} %collective-permute-done.4.refs_6_, bf16[80,704]{1,0:T(8,128)(2,1)} %collective-permute-done.3.refs_5_), kind=kLoop, calls=%fused_computation.2 | loop fusion | flops 1802240 | bytes 901120 | tf_op jit(solution)/shard_map/concatenate | solution.py:494
  42.2 11.5 %scores.2 = (bf16[16,1280,256]{2,1,0:T(8,128)(2,1)S(1)}, f32[16,256]{1,0:T(8,128)S(1)}, f32[16,256]{1,0:T(8,128)S(1)}, bf16[320,128]{1,0:T(8,128)(2,1)S(1)}) custom-call(s32[5]{0:T(128)S(1)} %stack.23.refs_0_.meta, bf16[80,704]{1,0:T(8,128)(2,1)S(1)} %fusion.refs_1_, bf16[80,704]{1,0:T(8,128)(2,1)S(1)} %copy-done.8, bf16[80,704]{1,0:T(8,128)(2,1)S(1)} %copy-done.5, ...), custom_call_target="tpu_custom_call" | custom-call | flops 6039797760 | bytes 5242880 | tf_op jit(solution)/shard_map/scores/pallas_call | solution.py:158
  57.2 11.5 %collective-permute-done.10.refs_1_ = bf16[320,704]{1,0:T(8,128)(2,1)S(1)} collective-permute-done((bf16[320,704]{1,0:T(8,128)(2,1)S(1)}, bf16[320,704]{1,0:T(8,128)(2,1)S(1)}, u32[]{:S(2)}, u32[]{:S(2)}) %collective-permute-start.10) | collective-permute-done | bytes 450592 | tf_op jit(solution)/shard_map/ppermute | solution.py:39
  68.7 10.7 %scores.3 = (bf16[16,1280,256]{2,1,0:T(8,128)(2,1)S(1)}, f32[16,256]{1,0:T(8,128)S(1)}, f32[16,256]{1,0:T(8,128)S(1)}, bf16[320,128]{1,0:T(8,128)(2,1)S(1)}) custom-call(s32[5]{0:T(128)S(1)} %stack.23.refs_0_.meta, bf16[320,704]{1,0:T(8,128)(2,1)S(1)} %collective-permute-done.10.refs_1_, ...), custom_call_target="tpu_custom_call", output_to_operand_aliasing={{0}: (3, {})} | custom-call | flops 6039797760 | bytes 5242880 | tf_op jit(solution)/shard_map/scores/pallas_call | solution.py:158
  79.4 4.0 %copy-done = bf16[16,1280,256]{2,1,0:T(8,128)(2,1)} copy-done((bf16[16,1280,256]{2,1,0:T(8,128)(2,1)}, bf16[16,1280,256]{2,1,0:T(8,128)(2,1)S(1)}, u32[]{:S(2)}) %copy-start) | copy-done | bytes 10485784
  83.4 3.8 %index_forward.1 = (f32[320,256]{1,0:T(8,128)S(1)}, f32[2,24,256]{2,1,0:T(8,128)S(1)}, f32[2,24,256]{2,1,0:T(8,128)S(1)}) custom-call(s32[5]{0:T(128)S(1)} %stack.23.refs_0_.meta, bf16[320,128]{1,0:T(8,128)(2,1)S(1)} %get-tuple-element.57.keys, f32[16,256]{1,0:T(8,128)S(1)} %get-tuple-element.58.m0, f32[16,256]{1,0:T(8,128)S(1)} %get-tuple-element.59.l0, ...), custom_call_target="tpu_custom_call" | custom-call | flops 1342177280 | bytes 5242880 | tf_op jit(solution)/shard_map/index_forward/pallas_call | solution.py:345
  90.7 4.4 %collective-permute-done.18.up = f32[2,8,256]{2,1,0:T(8,128)S(1)} collective-permute-done((f32[2,8,256]{2,1,0:T(8,128)S(1)}, f32[2,8,256]{2,1,0:T(8,128)S(1)}, u32[]{:S(2)}, u32[]{:S(2)}) %collective-permute-start.18) | collective-permute-done | bytes 16416 | tf_op jit(solution)/shard_map/ppermute | solution.py:39
  95.1 4.0 %copy-done.1 = bf16[16,1280,256]{2,1,0:T(8,128)(2,1)S(1)} copy-done((bf16[16,1280,256]{2,1,0:T(8,128)(2,1)S(1)}, bf16[16,1280,256]{2,1,0:T(8,128)(2,1)}, u32[]{:S(2)}) %copy-start.1) | copy-done | bytes 10485784
  99.1 3.3 %head_sum.1 = (bf16[336,256]{1,0:T(8,128)(2,1)S(1)}, bf16[336,256]{1,0:T(8,128)(2,1)S(1)}, bf16[336,256]{1,0:T(8,128)(2,1)S(1)}, bf16[336,256]{1,0:T(8,128)(2,1)S(1)}) custom-call(s32[5]{0:T(128)S(1)} %stack.23.refs_0_.meta, bf16[16,1280,256]{2,1,0:T(8,128)(2,1)S(1)} %copy-done.1, f32[16,256]{1,0:T(8,128)S(1)} %get-tuple-element.58.m0, ...), custom_call_target="tpu_custom_call" | custom-call | bytes 11534336 | tf_op jit(solution)/shard_map/head_sum/pallas_call | solution.py:241
  102.4 2.3 %collective-permute-start.20 = (bf16[336,256]{1,0:T(8,128)(2,1)S(1)}, bf16[336,256]{1,0:T(8,128)(2,1)S(1)}, u32[]{:S(2)}, u32[]{:S(2)}) collective-permute-start(bf16[336,256]{1,0:T(8,128)(2,1)S(1)} %get-tuple-element.73), channel_id=1, source_target_pairs={{0,64},{1,65},{4,68},{5,69},{8,72},{9,73},{12,76},{13,77},{16,80},... | collective-permute-start | bytes 516104 | tf_op jit(solution)/shard_map/ppermute | solution.py:39
  104.7 2.9 %collective-permute-start.21 = (bf16[336,256]{1,0:T(8,128)(2,1)S(1)}, bf16[336,256]{1,0:T(8,128)(2,1)S(1)}, u32[]{:S(2)}, u32[]{:S(2)}) collective-permute-start(bf16[336,256]{1,0:T(8,128)(2,1)S(1)} %get-tuple-element.74), channel_id=1, source_target_pairs={{0,128},{1,129},{4,132},{5,133},{8,136},{9,137},{12,140},{13,141},... | collective-permute-start | bytes 516104 | tf_op jit(solution)/shard_map/ppermute | solution.py:39
  109.4 4.9 %collective-permute-done.21.t2 = bf16[336,256]{1,0:T(8,128)(2,1)S(1)} collective-permute-done((bf16[336,256]{1,0:T(8,128)(2,1)S(1)}, bf16[336,256]{1,0:T(8,128)(2,1)S(1)}, u32[]{:S(2)}, u32[]{:S(2)}) %collective-permute-start.21) | collective-permute-done | bytes 172064 | tf_op jit(solution)/shard_map/ppermute | solution.py:39
  114.3 2.7 %collective-permute-done.22.t3 = bf16[336,256]{1,0:T(8,128)(2,1)S(1)} collective-permute-done((bf16[336,256]{1,0:T(8,128)(2,1)S(1)}, bf16[336,256]{1,0:T(8,128)(2,1)S(1)}, u32[]{:S(2)}, u32[]{:S(2)}) %collective-permute-start.22) | collective-permute-done | bytes 172064 | tf_op jit(solution)/shard_map/ppermute | solution.py:39
  116.9 7.7 %index_backward.1 = (f32[80,128]{1,0:T(8,128)S(1)}, f32[80,128]{1,0:T(8,128)S(1)}, bf16[16,32,128]{2,1,0:T(8,128)(2,1)}) custom-call(s32[5]{0:T(128)S(1)} %stack.23.refs_0_.meta, bf16[320,128]{1,0:T(8,128)(2,1)S(1)} %copy-done.17, f32[320,256]{1,0:T(8,128)S(1)} %get-tuple-element.65.logits, bf16[336,256]{1,0:T(8,128)(2,1)S(1)} %get-tuple-element.72.t0, ...), custom_call_target="tpu_custom_call" | custom-call | flops 2684354560 | bytes 6291456 | tf_op jit(solution)/shard_map/index_backward/pallas_call | solution.py:426
  124.6 4.7 %all-to-all-start = ((bf16[16,32,128]{2,1,0:T(8,128)(2,1)}), bf16[16,32,128]{2,1,0:T(8,128)(2,1)S(1)}, u32[]{:S(2)}, u32[]{:S(2)}) async-start(bf16[16,32,128]{2,1,0:T(8,128)(2,1)} %get-tuple-element.76), calls=%async_computation | async-start | bytes 262144 | tf_op jit(solution)/shard_map/all_to_all | solution.py:518
  129.4 10.2 %all-to-all-done = bf16[16,32,128]{2,1,0:T(8,128)(2,1)S(1)} async-done(((bf16[16,32,128]{2,1,0:T(8,128)(2,1)}), bf16[16,32,128]{2,1,0:T(8,128)(2,1)S(1)}, u32[]{:S(2)}, u32[]{:S(2)}) %all-to-all-start) | async-done | bytes 131104 | tf_op jit(solution)/shard_map/all_to_all | solution.py:518
  139.6 14.4 %all_to_all.10 = bf16[8,112,128]{2,1,0:T(8,128)(2,1)S(1)} all-to-all(bf16[8,112,128]{2,1,0:T(8,128)(2,1)S(1)} %broadcast_in_dim.2), channel_id=1, replica_groups=mesh['yhi'=2,'xh'=2,'xp'=2,'z'=8,'ylo'=2,'core'=2] {'yhi','xh','xp'}, dimensions={0} | all-to-all | bytes 458752 | tf_op jit(solution)/shard_map/all_to_all | solution.py:463
  (98 shorter events, 24.5 us)
Async XLA Ops:
  1.7 11.0 %collective-permute-start.1 = (bf16[80,704]{1,0:T(8,128)(2,1)S(1)}, bf16[80,704]{1,0:T(8,128)(2,1)S(1)}, u32[]{:S(2)}, u32[]{:S(2)}) collective-permute-start(bf16[80,704]{1,0:T(8,128)(2,1)S(1)} %fusion.refs_1_), channel_id=1, source_target_pairs={{0,28},{1,29},{4,0},{5,1},{8,4},{9,5},{12,8},{13,9},{16,12},{17,13... | collective-permute-start | bytes 337928 | tf_op jit(solution)/shard_map/ppermute | solution.py:39
  7.6 6.1 %collective-permute-start = (bf16[80,704]{1,0:T(8,128)(2,1)S(1)}, bf16[80,704]{1,0:T(8,128)(2,1)S(1)}, u32[]{:S(2)}, u32[]{:S(2)}) collective-permute-start(bf16[80,704]{1,0:T(8,128)(2,1)S(1)} %fusion.refs_1_), channel_id=1, source_target_pairs={{0,4},{1,5},{4,8},{5,9},{8,12},{9,13},{12,16},{13,17},{16,20},{17,... | collective-permute-start | bytes 337928 | tf_op jit(solution)/shard_map/ppermute | solution.py:39
  10.0 23.8 %collective-permute-start.9 = (bf16[4,576,128]{2,1,0:T(8,128)(2,1)}, bf16[4,576,128]{2,1,0:T(8,128)(2,1)}, u32[]{:S(2)}, u32[]{:S(2)}) collective-permute-start(bf16[4,576,128]{2,1,0:T(8,128)(2,1)} %get-tuple-element.81), channel_id=1, source_target_pairs={{0,96},{1,97},{4,100},{5,101},{8,104},{9,105},{12,108},{13,109},{1... | collective-permute-start | bytes 1769480 | tf_op jit(solution)/shard_map/ppermute | solution.py:39
  10.5 23.3 %collective-permute-start.8 = (bf16[4,576,128]{2,1,0:T(8,128)(2,1)}, bf16[4,576,128]{2,1,0:T(8,128)(2,1)}, u32[]{:S(2)}, u32[]{:S(2)}) collective-permute-start(bf16[4,576,128]{2,1,0:T(8,128)(2,1)} %get-tuple-element.82), channel_id=1, source_target_pairs={{0,32},{1,33},{4,36},{5,37},{8,40},{9,41},{12,44},{13,45},{16,48},... | collective-permute-start | bytes 1769480 | tf_op jit(solution)/shard_map/ppermute | solution.py:39
  12.0 24.9 %collective-permute-start.12 = (bf16[8,576,128]{2,1,0:T(8,128)(2,1)S(1)}, bf16[8,576,128]{2,1,0:T(8,128)(2,1)}, u32[]{:S(2)}, u32[]{:S(2)}) collective-permute-start(bf16[8,576,128]{2,1,0:T(8,128)(2,1)S(1)} %bitcast.25), channel_id=1, source_target_pairs={{0,1},{1,0},{4,5},{5,4},{8,9},{9,8},{12,13},{13,12},{16,17},{17,16... | collective-permute-start | bytes 3538952 | tf_op jit(solution)/shard_map/ppermute | solution.py:39
  13.7 6.4 %collective-permute-start.2 = (bf16[80,704]{1,0:T(8,128)(2,1)S(1)}, bf16[80,704]{1,0:T(8,128)(2,1)}, u32[]{:S(2)}, u32[]{:S(2)}) collective-permute-start(bf16[80,704]{1,0:T(8,128)(2,1)S(1)} %collective-permute-done.refs_2_), channel_id=1, source_target_pairs={{0,4},{1,5},{4,8},{5,9},{8,12},{9,13},{12,16},{13,17},{16,20},{17,... | collective-permute-start | bytes 337928 | tf_op jit(solution)/shard_map/ppermute | solution.py:39
  13.7 6.4 %collective-permute-start.3 = (bf16[80,704]{1,0:T(8,128)(2,1)S(1)}, bf16[80,704]{1,0:T(8,128)(2,1)}, u32[]{:S(2)}, u32[]{:S(2)}) collective-permute-start(bf16[80,704]{1,0:T(8,128)(2,1)S(1)} %collective-permute-done.1.refs_3_), channel_id=1, source_target_pairs={{0,28},{1,29},{4,0},{5,1},{8,4},{9,5},{12,8},{13,9},{16,12},{17,13... | collective-permute-start | bytes 337928 | tf_op jit(solution)/shard_map/ppermute | solution.py:39
  20.1 6.4 %collective-permute-start.4 = (bf16[80,704]{1,0:T(8,128)(2,1)}, bf16[80,704]{1,0:T(8,128)(2,1)}, u32[]{:S(2)}, u32[]{:S(2)}) collective-permute-start(bf16[80,704]{1,0:T(8,128)(2,1)} %collective-permute-done.2.refs_4_), channel_id=1, source_target_pairs={{0,4},{1,5},{4,8},{5,9},{8,12},{9,13},{12,16},{13,17},{16,20},{17,... | collective-permute-start | bytes 337928 | tf_op jit(solution)/shard_map/ppermute | solution.py:39
  20.1 6.5 %collective-permute-start.5 = (bf16[80,704]{1,0:T(8,128)(2,1)}, bf16[80,704]{1,0:T(8,128)(2,1)}, u32[]{:S(2)}, u32[]{:S(2)}) collective-permute-start(bf16[80,704]{1,0:T(8,128)(2,1)} %collective-permute-done.3.refs_5_), channel_id=1, source_target_pairs={{0,28},{1,29},{4,0},{5,1},{8,4},{9,5},{12,8},{13,9},{16,12},{17,13... | collective-permute-start | bytes 337928 | tf_op jit(solution)/shard_map/ppermute | solution.py:39
  26.5 3.0 %collective-permute-start.7 = (f32[1,128]{1,0:T(1,128)S(1)}, f32[1,128]{1,0:T(1,128)S(1)}, u32[]{:S(2)}, u32[]{:S(2)}) collective-permute-start(f32[1,128]{1,0:T(1,128)S(1)} %convert_element_type.17.refs_15_.refs_11_.pa), channel_id=1, source_target_pairs={{0,1},{1,0},{4,5},{5,4},{8,9},{9,8},{12,13},{13,12},{16,17},{17,16... | collective-permute-start | bytes 1544 | tf_op jit(solution)/shard_map/ppermute | solution.py:39
  26.6 7.2 %collective-permute-start.6 = (bf16[80,704]{1,0:T(8,128)(2,1)}, bf16[80,704]{1,0:T(8,128)(2,1)S(1)}, u32[]{:S(2)}, u32[]{:S(2)}) collective-permute-start(bf16[80,704]{1,0:T(8,128)(2,1)} %collective-permute-done.4.refs_6_), channel_id=1, source_target_pairs={{0,4},{1,5},{4,8},{5,9},{8,12},{9,13},{12,16},{13,17},{16,20},{17,... | collective-permute-start | bytes 337928 | tf_op jit(solution)/shard_map/ppermute | solution.py:39
  36.3 2.3 %collective-permute-start.13 = (bf16[4,576,128]{2,1,0:T(8,128)(2,1)}, bf16[4,576,128]{2,1,0:T(8,128)(2,1)}, u32[]{:S(2)}, u32[]{:S(2)}) collective-permute-start(bf16[4,576,128]{2,1,0:T(8,128)(2,1)} %collective-permute-done.8.refs_11_.refs_7_), channel_id=1, source_target_pairs={{0,1},{1,0},{4,5},{5,4},{8,9},{9,8},{12,13},{13,12},{16,17},{17,16... | collective-permute-start | bytes 1769480 | tf_op jit(solution)/shard_map/ppermute | solution.py:39
  36.3 3.2 %collective-permute-start.14 = (bf16[4,576,128]{2,1,0:T(8,128)(2,1)}, bf16[4,576,128]{2,1,0:T(8,128)(2,1)}, u32[]{:S(2)}, u32[]{:S(2)}) collective-permute-start(bf16[4,576,128]{2,1,0:T(8,128)(2,1)} %collective-permute-done.9.refs_13_.refs_9_), channel_id=1, source_target_pairs={{0,1},{1,0},{4,5},{5,4},{8,9},{9,8},{12,13},{13,12},{16,17},{17,16... | collective-permute-start | bytes 1769480 | tf_op jit(solution)/shard_map/ppermute | solution.py:39
  53.7 29.7 %collective-permute-start.15 = (bf16[64,128,128]{2,1,0:T(8,128)(2,1)S(1)}, bf16[64,128,128]{2,1,0:T(8,128)(2,1)S(1)}, u32[]{:S(2)}, u32[]{:S(2)}) collective-permute-start(bf16[64,128,128]{2,1,0:T(8,128)(2,1)S(1)} %bitcast.21), channel_id=1, source_target_pairs={{0,1},{1,0},{4,5},{5,4},{8,9},{9,8},{12,13},{13,12},{16,17},{17,16... | collective-permute-start | bytes 6291464 | tf_op jit(solution)/shard_map/ppermute | solution.py:39
  53.9 14.8 %collective-permute-start.10 = (bf16[320,704]{1,0:T(8,128)(2,1)S(1)}, bf16[320,704]{1,0:T(8,128)(2,1)S(1)}, u32[]{:S(2)}, u32[]{:S(2)}) collective-permute-start(bf16[320,704]{1,0:T(8,128)(2,1)S(1)} %copy-done.18), channel_id=1, source_target_pairs={{0,2},{1,3},{4,6},{5,7},{8,10},{9,11},{12,14},{13,15},{16,18},{17,... | collective-permute-start | bytes 1351688 | tf_op jit(solution)/shard_map/ppermute | solution.py:39
  55.5 13.2 %collective-permute-start.11 = (bf16[320,704]{1,0:T(8,128)(2,1)S(1)}, bf16[320,704]{1,0:T(8,128)(2,1)S(1)}, u32[]{:S(2)}, u32[]{:S(2)}) collective-permute-start(bf16[320,704]{1,0:T(8,128)(2,1)S(1)} %copy-done.19), channel_id=1, source_target_pairs={{0,130},{1,131},{4,134},{5,135},{8,138},{9,139},{12,142},{13,143},... | collective-permute-start | bytes 1351688 | tf_op jit(solution)/shard_map/ppermute | solution.py:39
  57.2 26.2 %collective-permute-start.16 = (f32[64,128]{1,0:T(8,128)S(1)}, f32[64,128]{1,0:T(8,128)S(1)}, u32[]{:S(2)}, u32[]{:S(2)}) collective-permute-start(f32[64,128]{1,0:T(8,128)S(1)} %bitcast.28), channel_id=1, source_target_pairs={{0,1},{1,0},{4,5},{5,4},{8,9},{9,8},{12,13},{13,12},{16,17},{17,16... | collective-permute-start | bytes 98312 | tf_op jit(solution)/shard_map/ppermute | solution.py:39
  88.6 6.5 %collective-permute-start.19 = (f32[2,16,256]{2,1,0:T(8,128)S(1)}, f32[2,16,256]{2,1,0:T(8,128)S(1)}, u32[]{:S(2)}, u32[]{:S(2)}) collective-permute-start(f32[2,16,256]{2,1,0:T(8,128)S(1)} %get-tuple-element.71), channel_id=1, source_target_pairs={{0,96},{1,97},{4,100},{5,101},{8,104},{9,105},{12,108},{13,109},{1... | collective-permute-start | bytes 98312 | tf_op jit(solution)/shard_map/ppermute | solution.py:39
  90.0 5.1 %collective-permute-start.18 = (f32[2,8,256]{2,1,0:T(8,128)S(1)}, f32[2,8,256]{2,1,0:T(8,128)S(1)}, u32[]{:S(2)}, u32[]{:S(2)}) collective-permute-start(f32[2,8,256]{2,1,0:T(8,128)S(1)} %get-tuple-element.70), channel_id=1, source_target_pairs={{0,32},{1,33},{4,36},{5,37},{8,40},{9,41},{12,44},{13,45},{16,48},... | collective-permute-start | bytes 49160 | tf_op jit(solution)/shard_map/ppermute | solution.py:39
  102.4 7.0 %collective-permute-start.20 = (bf16[336,256]{1,0:T(8,128)(2,1)S(1)}, bf16[336,256]{1,0:T(8,128)(2,1)S(1)}, u32[]{:S(2)}, u32[]{:S(2)}) collective-permute-start(bf16[336,256]{1,0:T(8,128)(2,1)S(1)} %get-tuple-element.73), channel_id=1, source_target_pairs={{0,64},{1,65},{4,68},{5,69},{8,72},{9,73},{12,76},{13,77},{16,80},... | collective-permute-start | bytes 516104 | tf_op jit(solution)/shard_map/ppermute | solution.py:39
  104.7 9.6 %collective-permute-start.21 = (bf16[336,256]{1,0:T(8,128)(2,1)S(1)}, bf16[336,256]{1,0:T(8,128)(2,1)S(1)}, u32[]{:S(2)}, u32[]{:S(2)}) collective-permute-start(bf16[336,256]{1,0:T(8,128)(2,1)S(1)} %get-tuple-element.74), channel_id=1, source_target_pairs={{0,128},{1,129},{4,132},{5,133},{8,136},{9,137},{12,140},{13,141},... | collective-permute-start | bytes 516104 | tf_op jit(solution)/shard_map/ppermute | solution.py:39
  107.6 9.3 %collective-permute-start.22 = (bf16[336,256]{1,0:T(8,128)(2,1)S(1)}, bf16[336,256]{1,0:T(8,128)(2,1)S(1)}, u32[]{:S(2)}, u32[]{:S(2)}) collective-permute-start(bf16[336,256]{1,0:T(8,128)(2,1)S(1)} %get-tuple-element.75), channel_id=1, source_target_pairs={{0,192},{1,193},{4,196},{5,197},{8,200},{9,201},{12,204},{13,205},... | collective-permute-start | bytes 516104 | tf_op jit(solution)/shard_map/ppermute | solution.py:39
  124.6 4.7 %collective-permute-start.23 = (f32[80,128]{1,0:T(8,128)S(1)}, f32[80,128]{1,0:T(8,128)S(1)}, u32[]{:S(2)}, u32[]{:S(2)}) collective-permute-start(f32[80,128]{1,0:T(8,128)S(1)} %get-tuple-element.78), channel_id=1, source_target_pairs={{0,1},{1,0},{4,5},{5,4},{8,9},{9,8},{12,13},{13,12},{16,17},{17,16... | collective-permute-start | bytes 122888 | tf_op jit(solution)/shard_map/ppermute | solution.py:39
  124.6 14.9 %all-to-all-start = ((bf16[16,32,128]{2,1,0:T(8,128)(2,1)}), bf16[16,32,128]{2,1,0:T(8,128)(2,1)S(1)}, u32[]{:S(2)}, u32[]{:S(2)}) async-start(bf16[16,32,128]{2,1,0:T(8,128)(2,1)} %get-tuple-element.76), calls=%async_computation | async-start | bytes 262144 | tf_op jit(solution)/shard_map/all_to_all | solution.py:518
  (22 other events, 174.5 us)

commit v7 on v6

--- a/solution.py
+++ b/solution.py
@@ -329,6 +329,7 @@
     return pl.pallas_call(
         pair_kernel,
         out_shape=[pltpu.VMEM((2, rows, 256), jnp.float32) for rows in (24, 8, 16)],
+        compiler_params=pltpu.CompilerParams(vmem_limit_bytes=1 << 20),
         name="pair_statistics",
     )(*in_vmem(ours, theirs))
 
@@ -477,30 +478,30 @@
     pa, wa = place.astype(jnp.float32), index_weights.T
     own = jnp.concatenate([index_keys, latent_keys], axis=1)
     own = lax.dynamic_slice_in_dim(own, half * HALF, HALF, 0)
+    meta = jnp.stack([z, ylo, core, half, quarter]).astype(jnp.int32)
+    own, meta = lax.optimization_barrier((own, meta))
 
     queries = main_queries.transpose(0, 2, 1)
     f1, b1 = shift(own, dz=1), shift(own, dz=7)
     queries_far = swap_core(queries)
-    left, right = shift(queries[:4], dx=1), shift(queries[4:], dx=3)
+    halves = after(queries, own)
+    left, right = shift(halves[:4], dx=1), shift(halves[4:], dx=3)
     f1, b1 = lax.optimization_barrier((f1, b1))
     f2, b2 = shift(f1, dz=1), shift(b1, dz=7)
     f2, b2 = lax.optimization_barrier((f2, b2))
     f3, b3 = shift(f2, dz=1), shift(b2, dz=7)
-    f3, b3 = lax.optimization_barrier((f3, b3))
+    pb = swap_core(pa)
+    ia = index_queries.transpose(1, 0, 2)
+    f3, b3, left, right, ia, pb = lax.optimization_barrier((f3, b3, left, right, ia, pb))
     f4 = shift(f3, dz=1)
-    ia = index_queries.transpose(1, 0, 2)
-    pb = swap_core(pa)
-    f4, ia, pb, left, right = lax.optimization_barrier((f4, ia, pb, left, right))
+    left_far, right_far = swap_core(left), swap_core(right)
     y0, y1 = jnp.concatenate([own, f1, b1, f2]), jnp.concatenate([b2, f3, b3, f4])
-    y0, y1, left, right = lax.optimization_barrier((y0, y1, left, right))
     y0, y1 = shift(y0, dy=1), shift(y1, dy=3)
-    left_far, right_far = swap_core(left), swap_core(right)
-    meta = jnp.stack([z, ylo, core, half, quarter]).astype(jnp.int32)
+    ia, wa = lax.optimization_barrier((ia, wa, f4, left_far, right_far))[:2]
+    ib, wb = swap_core(ia), swap_core(wa)
 
     sides = (queries, queries_far, left, left_far, right, right_far, pa, pb)
     exps, m0, l0, keys = score_call(meta, 0, [own, f1, b1, f2, b2, f3, b3, f4], [], *sides)
-    ia, wa = lax.optimization_barrier((ia, wa, m0))[:2]
-    ib, wb = swap_core(ia), swap_core(wa)
     exps, m1, l1, keys = score_call(meta, 1, [y0, y1], in_vmem(exps, keys), *sides)
 
     logits, ours, sent = forward_call(meta, keys, (m0, l0, m1, l1), ia, ib, pa, pb, wa, wb)

time: 157 us -> 128 us (0.82)
  local copies, waits for them, and re-layouts: 17.6 us -> 5.21 us
  waiting for transfers between devices: 46.3 us -> 35.4 us
  other arithmetic: 5.99 us -> 2.37 us
  Pallas kernels: 36.9 us -> 33.8 us
    unnamed x43 -> x7, local copies, waits for them, and re-layouts: 14.4 us -> 3.04 us
    ppermute x24, waiting for transfers between devices: 36.1 us -> 25.2 us  [shift(): return lax.ppermute(value, ALL, pairs)]
    pallas_call x2, Pallas kernels: 22.1 us -> 18.9 us  [score_call(): pl.pallas_call(lambda *refs: score_kernel(chunk, spans, *refs), grid_spec...]
    concatenate x1, other arithmetic: 1.87 us -> 0.05 us  [body(): jnp.concatenate([b2, f3, b3, f4])]
    concatenate x1, other arithmetic: 1.74 us -> 0.05 us  [body(): jnp.concatenate([own, f1, b1, f2])]
  transfers between devices with their start and end apart: 25 -> 25, of which waited for: 12 -> 12; matrix products, arithmetic and copies ran while one was open for 6% -> 3% of each run, Pallas kernels for 7% -> 15%
where the time goes in v7:
time: 128 us; the launch traced here: 127 us
  waiting for transfers between devices  35.4 us (28%)
  starting transfers between devices  34.5 us (27%)
  Pallas kernels  33.8 us (26%)
  blocking collectives  14.4 us (11%)
  local copies, waits for them, and re-layouts  5.21 us (4%)
  other arithmetic  2.37 us (2%)
  between operations  1.53 us (1%)
    ppermute x24, starting transfers between devices, shift(): return lax.ppermute(value, ALL, pairs)  29.5 us
    ppermute x24, waiting for transfers between devices, shift(): return lax.ppermute(value, ALL, pairs)  25.2 us
    pallas_call x2, Pallas kernels, score_call(): pl.pallas_call(lambda *refs: score_kernel(chunk, spans, *refs), grid_spec...  18.9 us
    all_to_all x1, blocking collectives, gather_head(): return lax.all_to_all(wide, ('yhi', 'xh', 'xp'), 0, 0, tiled=True)  14.4 us
    all_to_all x1, waiting for transfers between devices, body(): kg = lax.all_to_all(kg, ('z', 'ylo'), 0, 0, tiled=True)  10.2 us
    pallas_call x1, Pallas kernels, backward_call(): pl.pallas_call(backward_kernel, grid_spec=pltpu.PrefetchScalarGridSpec(nu...  7.75 us
    all_to_all x1, starting transfers between devices, body(): kg = lax.all_to_all(kg, ('z', 'ylo'), 0, 0, tiled=True)  5 us
    pallas_call x1, Pallas kernels, forward_call(): pl.pallas_call(forward_kernel, grid_spec=pltpu.PrefetchScalarGridSpec(num...  3.85 us
  transfers between devices with their start and end apart: 25, of which 12 were waited for; matrix products, arithmetic and copies ran while one was open for 3% of the time, Pallas kernels for 15%

profile of v7, /device:TPU:2, one launch (start us, length us, event | category | flops | bytes accessed | tf_op | source)
XLA Modules:
  0.0 127.2 jit_solution(3483715706697836262)
XLA Ops:
  7.0 3.9 %collective-permute-start.1 = (bf16[80,704]{1,0:T(8,128)(2,1)S(1)}, bf16[80,704]{1,0:T(8,128)(2,1)S(1)}, u32[]{:S(2)}, u32[]{:S(2)}) collective-permute-start(bf16[80,704]{1,0:T(8,128)(2,1)S(1)} %fusion.refs_1_), channel_id=1, source_target_pairs={{0,28},{1,29},{4,0},{5,1},{8,4},{9,5},{12,8},{13,9},{16,12},{17,13... | collective-permute-start | bytes 337928 | tf_op jit(solution)/shard_map/ppermute | solution.py:39
  11.6 2.2 %collective-permute-done.refs_2_ = bf16[80,704]{1,0:T(8,128)(2,1)S(1)} collective-permute-done((bf16[80,704]{1,0:T(8,128)(2,1)S(1)}, bf16[80,704]{1,0:T(8,128)(2,1)S(1)}, u32[]{:S(2)}, u32[]{:S(2)}) %collective-permute-start) | collective-permute-done | bytes 112672 | tf_op jit(solution)/shard_map/ppermute | solution.py:39
  13.8 3.2 %collective-permute-start.3 = (bf16[80,704]{1,0:T(8,128)(2,1)S(1)}, bf16[80,704]{1,0:T(8,128)(2,1)S(1)}, u32[]{:S(2)}, u32[]{:S(2)}) collective-permute-start(bf16[80,704]{1,0:T(8,128)(2,1)S(1)} %collective-permute-done.1.refs_3_), channel_id=1, source_target_pairs={{0,28},{1,29},{4,0},{5,1},{8,4},{9,5},{12,8},{13,9},{16,12},{17,13... | collective-permute-start | bytes 337928 | tf_op jit(solution)/shard_map/ppermute | solution.py:39
  17.1 2.8 %collective-permute-done.2.refs_4_ = bf16[80,704]{1,0:T(8,128)(2,1)S(1)} collective-permute-done((bf16[80,704]{1,0:T(8,128)(2,1)S(1)}, bf16[80,704]{1,0:T(8,128)(2,1)S(1)}, u32[]{:S(2)}, u32[]{:S(2)}) %collective-permute-start.2) | collective-permute-done | bytes 112672 | tf_op jit(solution)/shard_map/ppermute | solution.py:39
  19.9 3.0 %collective-permute-start.5 = (bf16[80,704]{1,0:T(8,128)(2,1)S(1)}, bf16[80,704]{1,0:T(8,128)(2,1)S(1)}, u32[]{:S(2)}, u32[]{:S(2)}) collective-permute-start(bf16[80,704]{1,0:T(8,128)(2,1)S(1)} %collective-permute-done.2.refs_4_), channel_id=1, source_target_pairs={{0,4},{1,5},{4,8},{5,9},{8,12},{9,13},{12,16},{13,17},{16,20},{17,... | collective-permute-start | bytes 337928 | tf_op jit(solution)/shard_map/ppermute | solution.py:39
  23.4 3.0 %copy.16 = bf16[128,64,128]{2,0,1:T(8,128)(2,1)S(1)} copy(bf16[128,64,128]{2,1,0:T(8,128)(2,1)} %param.9) | data formatting | bytes 4194304 | tf_op args[2]
  28.4 2.0 %collective-permute-start.10 = (bf16[80,704]{1,0:T(8,128)(2,1)S(1)}, bf16[80,704]{1,0:T(8,128)(2,1)S(1)}, u32[]{:S(2)}, u32[]{:S(2)}) collective-permute-start(bf16[80,704]{1,0:T(8,128)(2,1)S(1)} %collective-permute-done.5.refs_6_), channel_id=1, source_target_pairs={{0,4},{1,5},{4,8},{5,9},{8,12},{9,13},{12,16},{13,17},{16,20},{17,... | collective-permute-start | bytes 337928 | tf_op jit(solution)/shard_map/ppermute | solution.py:39
  30.5 4.8 %collective-permute-done.10.refs_8_ = bf16[80,704]{1,0:T(8,128)(2,1)S(1)} collective-permute-done((bf16[80,704]{1,0:T(8,128)(2,1)S(1)}, bf16[80,704]{1,0:T(8,128)(2,1)S(1)}, u32[]{:S(2)}, u32[]{:S(2)}) %collective-permute-start.10) | collective-permute-done | bytes 112672 | tf_op jit(solution)/shard_map/ppermute | solution.py:39
  37.1 1.9 %collective-permute-start.11 = (bf16[320,704]{1,0:T(8,128)(2,1)S(1)}, bf16[320,704]{1,0:T(8,128)(2,1)S(1)}, u32[]{:S(2)}, u32[]{:S(2)}) collective-permute-start(bf16[320,704]{1,0:T(8,128)(2,1)S(1)} %pad_maximum_fusion.1), channel_id=1, source_target_pairs={{0,130},{1,131},{4,134},{5,135},{8,138},{9,139},{12,142},{13,143},... | collective-permute-start | bytes 1351688 | tf_op jit(solution)/shard_map/ppermute | solution.py:39
  39.0 9.9 %scores.2 = (bf16[16,1280,256]{2,1,0:T(8,128)(2,1)S(1)}, f32[16,256]{1,0:T(8,128)S(1)}, f32[16,256]{1,0:T(8,128)S(1)}, bf16[320,128]{1,0:T(8,128)(2,1)S(1)}) custom-call(s32[5]{0:T(128)S(1)} %stack.23.refs_0_.meta, bf16[80,704]{1,0:T(8,128)(2,1)S(1)} %fusion.refs_1_, bf16[80,704]{1,0:T(8,128)(2,1)S(1)} %collective-permute-done.refs_2_, ...), custom_call_target="tpu_custom_call" | custom-call | flops 6039797760 | bytes 5242880 | tf_op jit(solution)/shard_map/scores/pallas_call | solution.py:158
  50.7 9.0 %scores.3 = (bf16[16,1280,256]{2,1,0:T(8,128)(2,1)S(1)}, f32[16,256]{1,0:T(8,128)S(1)}, f32[16,256]{1,0:T(8,128)S(1)}, bf16[320,128]{1,0:T(8,128)(2,1)S(1)}) custom-call(s32[5]{0:T(128)S(1)} %stack.23.refs_0_.meta, bf16[320,704]{1,0:T(8,128)(2,1)S(1)} %collective-permute-done.4.refs_1_, ...), custom_call_target="tpu_custom_call", output_to_operand_aliasing={{0}: (3, {})} | custom-call | flops 6039797760 | bytes 5242880 | tf_op jit(solution)/shard_map/scores/pallas_call | solution.py:158
  59.7 3.9 %index_forward.1 = (f32[320,256]{1,0:T(8,128)S(1)}, f32[2,24,256]{2,1,0:T(8,128)S(1)}, f32[2,24,256]{2,1,0:T(8,128)S(1)}) custom-call(s32[5]{0:T(128)S(1)} %stack.23.refs_0_.meta, bf16[320,128]{1,0:T(8,128)(2,1)S(1)} %get-tuple-element.53.keys, f32[16,256]{1,0:T(8,128)S(1)} %get-tuple-element.54.m0, f32[16,256]{1,0:T(8,128)S(1)} %get-tuple-element.55.l0, ...), custom_call_target="tpu_custom_call" | custom-call | flops 1342177280 | bytes 5242880 | tf_op jit(solution)/shard_map/index_forward/pallas_call | solution.py:346
  65.0 1.8 %collective-permute-start.19 = (f32[2,16,256]{2,1,0:T(8,128)S(1)}, f32[2,16,256]{2,1,0:T(8,128)S(1)}, u32[]{:S(2)}, u32[]{:S(2)}) collective-permute-start(f32[2,16,256]{2,1,0:T(8,128)S(1)} %get-tuple-element.67), channel_id=1, source_target_pairs={{0,96},{1,97},{4,100},{5,101},{8,104},{9,105},{12,108},{13,109},{1... | collective-permute-start | bytes 98312 | tf_op jit(solution)/shard_map/ppermute | solution.py:39
  67.1 3.5 %collective-permute-done.18.up = f32[2,8,256]{2,1,0:T(8,128)S(1)} collective-permute-done((f32[2,8,256]{2,1,0:T(8,128)S(1)}, f32[2,8,256]{2,1,0:T(8,128)S(1)}, u32[]{:S(2)}, u32[]{:S(2)}) %collective-permute-start.18) | collective-permute-done | bytes 16416 | tf_op jit(solution)/shard_map/ppermute | solution.py:39
  70.5 3.3 %head_sum.1 = (bf16[336,256]{1,0:T(8,128)(2,1)S(1)}, bf16[336,256]{1,0:T(8,128)(2,1)S(1)}, bf16[336,256]{1,0:T(8,128)(2,1)S(1)}, bf16[336,256]{1,0:T(8,128)(2,1)S(1)}) custom-call(s32[5]{0:T(128)S(1)} %stack.23.refs_0_.meta, bf16[16,1280,256]{2,1,0:T(8,128)(2,1)S(1)} %get-tuple-element.62.e_ref, f32[16,256]{1,0:T(8,128)S(1)} %get-tuple-element.54.m0, ...), custom_call_target="tpu_custom_call" | custom-call | bytes 11534336 | tf_op jit(solution)/shard_map/head_sum/pallas_call | solution.py:241
  73.8 1.8 %collective-permute-start.20 = (bf16[336,256]{1,0:T(8,128)(2,1)S(1)}, bf16[336,256]{1,0:T(8,128)(2,1)S(1)}, u32[]{:S(2)}, u32[]{:S(2)}) collective-permute-start(bf16[336,256]{1,0:T(8,128)(2,1)S(1)} %get-tuple-element.69), channel_id=1, source_target_pairs={{0,64},{1,65},{4,68},{5,69},{8,72},{9,73},{12,76},{13,77},{16,80},... | collective-permute-start | bytes 516104 | tf_op jit(solution)/shard_map/ppermute | solution.py:39
  75.7 2.9 %collective-permute-start.21 = (bf16[336,256]{1,0:T(8,128)(2,1)S(1)}, bf16[336,256]{1,0:T(8,128)(2,1)S(1)}, u32[]{:S(2)}, u32[]{:S(2)}) collective-permute-start(bf16[336,256]{1,0:T(8,128)(2,1)S(1)} %get-tuple-element.70), channel_id=1, source_target_pairs={{0,128},{1,129},{4,132},{5,133},{8,136},{9,137},{12,140},{13,141},... | collective-permute-start | bytes 516104 | tf_op jit(solution)/shard_map/ppermute | solution.py:39
  78.6 1.8 %collective-permute-start.22 = (bf16[336,256]{1,0:T(8,128)(2,1)S(1)}, bf16[336,256]{1,0:T(8,128)(2,1)S(1)}, u32[]{:S(2)}, u32[]{:S(2)}) collective-permute-start(bf16[336,256]{1,0:T(8,128)(2,1)S(1)} %get-tuple-element.71), channel_id=1, source_target_pairs={{0,192},{1,193},{4,196},{5,197},{8,200},{9,201},{12,204},{13,205},... | collective-permute-start | bytes 516104 | tf_op jit(solution)/shard_map/ppermute | solution.py:39
  80.8 4.4 %collective-permute-done.21.t2 = bf16[336,256]{1,0:T(8,128)(2,1)S(1)} collective-permute-done((bf16[336,256]{1,0:T(8,128)(2,1)S(1)}, bf16[336,256]{1,0:T(8,128)(2,1)S(1)}, u32[]{:S(2)}, u32[]{:S(2)}) %collective-permute-start.21) | collective-permute-done | bytes 172064 | tf_op jit(solution)/shard_map/ppermute | solution.py:39
  85.2 2.7 %collective-permute-done.22.t3 = bf16[336,256]{1,0:T(8,128)(2,1)S(1)} collective-permute-done((bf16[336,256]{1,0:T(8,128)(2,1)S(1)}, bf16[336,256]{1,0:T(8,128)(2,1)S(1)}, u32[]{:S(2)}, u32[]{:S(2)}) %collective-permute-start.22) | collective-permute-done | bytes 172064 | tf_op jit(solution)/shard_map/ppermute | solution.py:39
  87.9 7.8 %index_backward.1 = (f32[80,128]{1,0:T(8,128)S(1)}, f32[80,128]{1,0:T(8,128)S(1)}, bf16[16,32,128]{2,1,0:T(8,128)(2,1)}) custom-call(s32[5]{0:T(128)S(1)} %stack.23.refs_0_.meta, bf16[320,128]{1,0:T(8,128)(2,1)S(1)} %get-tuple-element.53.keys, f32[320,256]{1,0:T(8,128)S(1)} %get-tuple-element.61.logits, bf16[336,256]{1,0:T(8,128)(2,1)S(1)} %get-tuple-element.68.t0, ...), custom_call_target="tpu_custom_call" | custom-call | flops 2684354560 | bytes 6291456 | tf_op jit(solution)/shard_map/index_backward/pallas_call | solution.py:427
  95.6 5.0 %all-to-all-start = ((bf16[16,32,128]{2,1,0:T(8,128)(2,1)}), bf16[16,32,128]{2,1,0:T(8,128)(2,1)S(1)}, u32[]{:S(2)}, u32[]{:S(2)}) async-start(bf16[16,32,128]{2,1,0:T(8,128)(2,1)} %get-tuple-element.72), calls=%async_computation | async-start | bytes 262144 | tf_op jit(solution)/shard_map/all_to_all | solution.py:519
  100.7 10.2 %all-to-all-done = bf16[16,32,128]{2,1,0:T(8,128)(2,1)S(1)} async-done(((bf16[16,32,128]{2,1,0:T(8,128)(2,1)}), bf16[16,32,128]{2,1,0:T(8,128)(2,1)S(1)}, u32[]{:S(2)}, u32[]{:S(2)}) %all-to-all-start) | async-done | bytes 131104 | tf_op jit(solution)/shard_map/all_to_all | solution.py:519
  110.9 14.4 %all_to_all.10 = bf16[8,112,128]{2,1,0:T(8,128)(2,1)S(1)} all-to-all(bf16[8,112,128]{2,1,0:T(8,128)(2,1)S(1)} %broadcast_in_dim.2), channel_id=1, replica_groups=mesh['yhi'=2,'xh'=2,'xp'=2,'z'=8,'ylo'=2,'core'=2] {'yhi','xh','xp'}, dimensions={0} | all-to-all | bytes 458752 | tf_op jit(solution)/shard_map/all_to_all | solution.py:464
  (62 shorter events, 16.3 us)
Async XLA Ops:
  3.0 24.8 %collective-permute-start.7 = (bf16[4,576,128]{2,1,0:T(8,128)(2,1)S(1)}, bf16[4,576,128]{2,1,0:T(8,128)(2,1)S(1)}, u32[]{:S(2)}, u32[]{:S(2)}) collective-permute-start(bf16[4,576,128]{2,1,0:T(8,128)(2,1)S(1)} %get-tuple-element.78), channel_id=1, source_target_pairs={{0,32},{1,33},{4,36},{5,37},{8,40},{9,41},{12,44},{13,45},{16,48},... | collective-permute-start | bytes 1769480 | tf_op jit(solution)/shard_map/ppermute | solution.py:39
  4.6 23.3 %collective-permute-start.8 = (bf16[4,576,128]{2,1,0:T(8,128)(2,1)S(1)}, bf16[4,576,128]{2,1,0:T(8,128)(2,1)S(1)}, u32[]{:S(2)}, u32[]{:S(2)}) collective-permute-start(bf16[4,576,128]{2,1,0:T(8,128)(2,1)S(1)} %get-tuple-element.77), channel_id=1, source_target_pairs={{0,96},{1,97},{4,100},{5,101},{8,104},{9,105},{12,108},{13,109},{1... | collective-permute-start | bytes 1769480 | tf_op jit(solution)/shard_map/ppermute | solution.py:39
  5.4 8.4 %collective-permute-start = (bf16[80,704]{1,0:T(8,128)(2,1)S(1)}, bf16[80,704]{1,0:T(8,128)(2,1)S(1)}, u32[]{:S(2)}, u32[]{:S(2)}) collective-permute-start(bf16[80,704]{1,0:T(8,128)(2,1)S(1)} %fusion.refs_1_), channel_id=1, source_target_pairs={{0,4},{1,5},{4,8},{5,9},{8,12},{9,13},{12,16},{13,17},{16,20},{17,... | collective-permute-start | bytes 337928 | tf_op jit(solution)/shard_map/ppermute | solution.py:39
  7.0 6.8 %collective-permute-start.1 = (bf16[80,704]{1,0:T(8,128)(2,1)S(1)}, bf16[80,704]{1,0:T(8,128)(2,1)S(1)}, u32[]{:S(2)}, u32[]{:S(2)}) collective-permute-start(bf16[80,704]{1,0:T(8,128)(2,1)S(1)} %fusion.refs_1_), channel_id=1, source_target_pairs={{0,28},{1,29},{4,0},{5,1},{8,4},{9,5},{12,8},{13,9},{16,12},{17,13... | collective-permute-start | bytes 337928 | tf_op jit(solution)/shard_map/ppermute | solution.py:39
  13.8 6.1 %collective-permute-start.2 = (bf16[80,704]{1,0:T(8,128)(2,1)S(1)}, bf16[80,704]{1,0:T(8,128)(2,1)S(1)}, u32[]{:S(2)}, u32[]{:S(2)}) collective-permute-start(bf16[80,704]{1,0:T(8,128)(2,1)S(1)} %collective-permute-done.refs_2_), channel_id=1, source_target_pairs={{0,4},{1,5},{4,8},{5,9},{8,12},{9,13},{12,16},{13,17},{16,20},{17,... | collective-permute-start | bytes 337928 | tf_op jit(solution)/shard_map/ppermute | solution.py:39
  13.8 6.1 %collective-permute-start.3 = (bf16[80,704]{1,0:T(8,128)(2,1)S(1)}, bf16[80,704]{1,0:T(8,128)(2,1)S(1)}, u32[]{:S(2)}, u32[]{:S(2)}) collective-permute-start(bf16[80,704]{1,0:T(8,128)(2,1)S(1)} %collective-permute-done.1.refs_3_), channel_id=1, source_target_pairs={{0,28},{1,29},{4,0},{5,1},{8,4},{9,5},{12,8},{13,9},{16,12},{17,13... | collective-permute-start | bytes 337928 | tf_op jit(solution)/shard_map/ppermute | solution.py:39
  19.9 6.5 %collective-permute-start.5 = (bf16[80,704]{1,0:T(8,128)(2,1)S(1)}, bf16[80,704]{1,0:T(8,128)(2,1)S(1)}, u32[]{:S(2)}, u32[]{:S(2)}) collective-permute-start(bf16[80,704]{1,0:T(8,128)(2,1)S(1)} %collective-permute-done.2.refs_4_), channel_id=1, source_target_pairs={{0,4},{1,5},{4,8},{5,9},{8,12},{9,13},{12,16},{13,17},{16,20},{17,... | collective-permute-start | bytes 337928 | tf_op jit(solution)/shard_map/ppermute | solution.py:39
  22.9 4.9 %collective-permute-start.6 = (bf16[80,704]{1,0:T(8,128)(2,1)S(1)}, bf16[80,704]{1,0:T(8,128)(2,1)S(1)}, u32[]{:S(2)}, u32[]{:S(2)}) collective-permute-start(bf16[80,704]{1,0:T(8,128)(2,1)S(1)} %collective-permute-done.3.refs_5_), channel_id=1, source_target_pairs={{0,28},{1,29},{4,0},{5,1},{8,4},{9,5},{12,8},{13,9},{16,12},{17,13... | collective-permute-start | bytes 337928 | tf_op jit(solution)/shard_map/ppermute | solution.py:39
  23.3 3.1 %collective-permute-start.9 = (f32[1,128]{1,0:T(1,128)S(1)}, f32[1,128]{1,0:T(1,128)S(1)}, u32[]{:S(2)}, u32[]{:S(2)}) collective-permute-start(f32[1,128]{1,0:T(1,128)S(1)} %convert_element_type.17.refs_15_.refs_11_.pa), channel_id=1, source_target_pairs={{0,1},{1,0},{4,5},{5,4},{8,9},{9,8},{12,13},{13,12},{16,17},{17,16... | collective-permute-start | bytes 1544 | tf_op jit(solution)/shard_map/ppermute | solution.py:39
  27.8 7.5 %collective-permute-start.13 = (bf16[4,576,128]{2,1,0:T(8,128)(2,1)S(1)}, bf16[4,576,128]{2,1,0:T(8,128)(2,1)S(1)}, u32[]{:S(2)}, u32[]{:S(2)}) collective-permute-start(bf16[4,576,128]{2,1,0:T(8,128)(2,1)S(1)} %collective-permute-done.7.refs_11_.refs_7_), channel_id=1, source_target_pairs={{0,1},{1,0},{4,5},{5,4},{8,9},{9,8},{12,13},{13,12},{16,17},{17,16... | collective-permute-start | bytes 1769480 | tf_op jit(solution)/shard_map/ppermute | solution.py:39
  27.8 7.5 %collective-permute-start.14 = (bf16[4,576,128]{2,1,0:T(8,128)(2,1)S(1)}, bf16[4,576,128]{2,1,0:T(8,128)(2,1)S(1)}, u32[]{:S(2)}, u32[]{:S(2)}) collective-permute-start(bf16[4,576,128]{2,1,0:T(8,128)(2,1)S(1)} %collective-permute-done.8.refs_13_.refs_9_), channel_id=1, source_target_pairs={{0,1},{1,0},{4,5},{5,4},{8,9},{9,8},{12,13},{13,12},{16,17},{17,16... | collective-permute-start | bytes 1769480 | tf_op jit(solution)/shard_map/ppermute | solution.py:39
  28.3 10.7 %collective-permute-start.12 = (bf16[8,576,128]{2,1,0:T(8,128)(2,1)S(1)}, bf16[8,576,128]{2,1,0:T(8,128)(2,1)S(1)}, u32[]{:S(2)}, u32[]{:S(2)}) collective-permute-start(bf16[8,576,128]{2,1,0:T(8,128)(2,1)S(1)} %bitcast.25), channel_id=1, source_target_pairs={{0,1},{1,0},{4,5},{5,4},{8,9},{9,8},{12,13},{13,12},{16,17},{17,16... | collective-permute-start | bytes 3538952 | tf_op jit(solution)/shard_map/ppermute | solution.py:39
  28.4 6.9 %collective-permute-start.10 = (bf16[80,704]{1,0:T(8,128)(2,1)S(1)}, bf16[80,704]{1,0:T(8,128)(2,1)S(1)}, u32[]{:S(2)}, u32[]{:S(2)}) collective-permute-start(bf16[80,704]{1,0:T(8,128)(2,1)S(1)} %collective-permute-done.5.refs_6_), channel_id=1, source_target_pairs={{0,4},{1,5},{4,8},{5,9},{8,12},{9,13},{12,16},{13,17},{16,20},{17,... | collective-permute-start | bytes 337928 | tf_op jit(solution)/shard_map/ppermute | solution.py:39
  35.3 24.4 %collective-permute-start.15 = (bf16[64,128,128]{2,1,0:T(8,128)(2,1)S(1)}, bf16[64,128,128]{2,1,0:T(8,128)(2,1)S(1)}, u32[]{:S(2)}, u32[]{:S(2)}) collective-permute-start(bf16[64,128,128]{2,1,0:T(8,128)(2,1)S(1)} %bitcast.21), channel_id=1, source_target_pairs={{0,1},{1,0},{4,5},{5,4},{8,9},{9,8},{12,13},{13,12},{16,17},{17,16... | collective-permute-start | bytes 6291464 | tf_op jit(solution)/shard_map/ppermute | solution.py:39
  35.4 15.0 %collective-permute-start.4 = (bf16[320,704]{1,0:T(8,128)(2,1)S(1)}, bf16[320,704]{1,0:T(8,128)(2,1)S(1)}, u32[]{:S(2)}, u32[]{:S(2)}) collective-permute-start(bf16[320,704]{1,0:T(8,128)(2,1)S(1)} %pad_maximum_fusion), channel_id=1, source_target_pairs={{0,2},{1,3},{4,6},{5,7},{8,10},{9,11},{12,14},{13,15},{16,18},{17,... | collective-permute-start | bytes 1351688 | tf_op jit(solution)/shard_map/ppermute | solution.py:39
  37.1 13.6 %collective-permute-start.11 = (bf16[320,704]{1,0:T(8,128)(2,1)S(1)}, bf16[320,704]{1,0:T(8,128)(2,1)S(1)}, u32[]{:S(2)}, u32[]{:S(2)}) collective-permute-start(bf16[320,704]{1,0:T(8,128)(2,1)S(1)} %pad_maximum_fusion.1), channel_id=1, source_target_pairs={{0,130},{1,131},{4,134},{5,135},{8,138},{9,139},{12,142},{13,143},... | collective-permute-start | bytes 1351688 | tf_op jit(solution)/shard_map/ppermute | solution.py:39
  39.0 20.7 %collective-permute-start.16 = (f32[64,128]{1,0:T(8,128)S(1)}, f32[64,128]{1,0:T(8,128)S(1)}, u32[]{:S(2)}, u32[]{:S(2)}) collective-permute-start(f32[64,128]{1,0:T(8,128)S(1)} %bitcast.28), channel_id=1, source_target_pairs={{0,1},{1,0},{4,5},{5,4},{8,9},{9,8},{12,13},{13,12},{16,17},{17,16... | collective-permute-start | bytes 98312 | tf_op jit(solution)/shard_map/ppermute | solution.py:39
  65.0 5.6 %collective-permute-start.19 = (f32[2,16,256]{2,1,0:T(8,128)S(1)}, f32[2,16,256]{2,1,0:T(8,128)S(1)}, u32[]{:S(2)}, u32[]{:S(2)}) collective-permute-start(f32[2,16,256]{2,1,0:T(8,128)S(1)} %get-tuple-element.67), channel_id=1, source_target_pairs={{0,96},{1,97},{4,100},{5,101},{8,104},{9,105},{12,108},{13,109},{1... | collective-permute-start | bytes 98312 | tf_op jit(solution)/shard_map/ppermute | solution.py:39
  66.8 3.7 %collective-permute-start.18 = (f32[2,8,256]{2,1,0:T(8,128)S(1)}, f32[2,8,256]{2,1,0:T(8,128)S(1)}, u32[]{:S(2)}, u32[]{:S(2)}) collective-permute-start(f32[2,8,256]{2,1,0:T(8,128)S(1)} %get-tuple-element.66), channel_id=1, source_target_pairs={{0,32},{1,33},{4,36},{5,37},{8,40},{9,41},{12,44},{13,45},{16,48},... | collective-permute-start | bytes 49160 | tf_op jit(solution)/shard_map/ppermute | solution.py:39
  73.8 7.0 %collective-permute-start.20 = (bf16[336,256]{1,0:T(8,128)(2,1)S(1)}, bf16[336,256]{1,0:T(8,128)(2,1)S(1)}, u32[]{:S(2)}, u32[]{:S(2)}) collective-permute-start(bf16[336,256]{1,0:T(8,128)(2,1)S(1)} %get-tuple-element.69), channel_id=1, source_target_pairs={{0,64},{1,65},{4,68},{5,69},{8,72},{9,73},{12,76},{13,77},{16,80},... | collective-permute-start | bytes 516104 | tf_op jit(solution)/shard_map/ppermute | solution.py:39
  75.7 9.5 %collective-permute-start.21 = (bf16[336,256]{1,0:T(8,128)(2,1)S(1)}, bf16[336,256]{1,0:T(8,128)(2,1)S(1)}, u32[]{:S(2)}, u32[]{:S(2)}) collective-permute-start(bf16[336,256]{1,0:T(8,128)(2,1)S(1)} %get-tuple-element.70), channel_id=1, source_target_pairs={{0,128},{1,129},{4,132},{5,133},{8,136},{9,137},{12,140},{13,141},... | collective-permute-start | bytes 516104 | tf_op jit(solution)/shard_map/ppermute | solution.py:39
  78.6 9.3 %collective-permute-start.22 = (bf16[336,256]{1,0:T(8,128)(2,1)S(1)}, bf16[336,256]{1,0:T(8,128)(2,1)S(1)}, u32[]{:S(2)}, u32[]{:S(2)}) collective-permute-start(bf16[336,256]{1,0:T(8,128)(2,1)S(1)} %get-tuple-element.71), channel_id=1, source_target_pairs={{0,192},{1,193},{4,196},{5,197},{8,200},{9,201},{12,204},{13,205},... | collective-permute-start | bytes 516104 | tf_op jit(solution)/shard_map/ppermute | solution.py:39
  95.6 5.0 %collective-permute-start.23 = (f32[80,128]{1,0:T(8,128)S(1)}, f32[80,128]{1,0:T(8,128)S(1)}, u32[]{:S(2)}, u32[]{:S(2)}) collective-permute-start(f32[80,128]{1,0:T(8,128)S(1)} %get-tuple-element.74), channel_id=1, source_target_pairs={{0,1},{1,0},{4,5},{5,4},{8,9},{9,8},{12,13},{13,12},{16,17},{17,16... | collective-permute-start | bytes 122888 | tf_op jit(solution)/shard_map/ppermute | solution.py:39
  95.6 15.2 %all-to-all-start = ((bf16[16,32,128]{2,1,0:T(8,128)(2,1)}), bf16[16,32,128]{2,1,0:T(8,128)(2,1)S(1)}, u32[]{:S(2)}, u32[]{:S(2)}) async-start(bf16[16,32,128]{2,1,0:T(8,128)(2,1)} %get-tuple-element.72), calls=%async_computation | async-start | bytes 262144 | tf_op jit(solution)/shard_map/all_to_all | solution.py:519
  (4 other events, 38.5 us)

commit v8 on v7

--- a/solution.py
+++ b/solution.py
@@ -486,14 +486,14 @@
     queries_far = swap_core(queries)
     halves = after(queries, own)
     left, right = shift(halves[:4], dx=1), shift(halves[4:], dx=3)
+    f4 = shift(own, dz=4)
     f1, b1 = lax.optimization_barrier((f1, b1))
     f2, b2 = shift(f1, dz=1), shift(b1, dz=7)
-    f2, b2 = lax.optimization_barrier((f2, b2))
+    ia = index_queries.transpose(1, 0, 2)
+    pb = swap_core(pa)
+    f2, b2, ia, pb = lax.optimization_barrier((f2, b2, ia, pb))
     f3, b3 = shift(f2, dz=1), shift(b2, dz=7)
-    pb = swap_core(pa)
-    ia = index_queries.transpose(1, 0, 2)
-    f3, b3, left, right, ia, pb = lax.optimization_barrier((f3, b3, left, right, ia, pb))
-    f4 = shift(f3, dz=1)
+    f3, b3, left, right, f4 = lax.optimization_barrier((f3, b3, left, right, f4))
     left_far, right_far = swap_core(left), swap_core(right)
     y0, y1 = jnp.concatenate([own, f1, b1, f2]), jnp.concatenate([b2, f3, b3, f4])
     y0, y1 = shift(y0, dy=1), shift(y1, dy=3)
@@ -509,7 +509,8 @@
     up, down = shift(up, dx=1), shift(down, dx=3)
     sums = head_sum_call(meta, exps, m0, m1, here, up, down)
     group = (dict(dx=2), dict(dy=2), dict(dx=2, dy=2))
-    target = [sums[0]] + [shift(part, **move) for part, move in zip(sums[1:], group)]
+    far = shift(sums[3], **group[2])
+    target = [sums[0]] + [shift(part, **move) for part, move in zip(sums[1:3], group)] + [far]
 
     mine, other, kg = backward_call(meta, keys, logits, target, ia, ib, wa, wb)
     rows_out = mine + swap_core(other)

time: 128 us -> 130 us (1.016)
  starting transfers between devices: 34.5 us -> 36.7 us
    ppermute x24, starting transfers between devices: 29.5 us -> 32.3 us  [shift(): return lax.ppermute(value, ALL, pairs)]
  transfers between devices with their start and end apart: 25 -> 25, of which waited for: 12 -> 13; matrix products, arithmetic and copies ran while one was open for 3% -> 3% of each run, Pallas kernels for 15% -> 14%
where the time goes in v8:
time: 130 us; the launch traced here: 129 us
  starting transfers between devices  36.7 us (28%)
  waiting for transfers between devices  35.6 us (27%)
  Pallas kernels  33.5 us (26%)
  blocking collectives  14.4 us (11%)
  local copies, waits for them, and re-layouts  5.21 us (4%)
  other arithmetic  2.37 us (2%)
  between operations  1.53 us (1%)
    ppermute x24, starting transfers between devices, shift(): return lax.ppermute(value, ALL, pairs)  32.3 us
    ppermute x24, waiting for transfers between devices, shift(): return lax.ppermute(value, ALL, pairs)  25.4 us
    pallas_call x2, Pallas kernels, score_call(): pl.pallas_call(lambda *refs: score_kernel(chunk, spans, *refs), grid_spec...  18.6 us
    all_to_all x1, blocking collectives, gather_head(): return lax.all_to_all(wide, ('yhi', 'xh', 'xp'), 0, 0, tiled=True)  14.4 us
    all_to_all x1, waiting for transfers between devices, body(): kg = lax.all_to_all(kg, ('z', 'ylo'), 0, 0, tiled=True)  10.2 us
    pallas_call x1, Pallas kernels, backward_call(): pl.pallas_call(backward_kernel, grid_spec=pltpu.PrefetchScalarGridSpec(nu...  7.74 us
    all_to_all x1, starting transfers between devices, body(): kg = lax.all_to_all(kg, ('z', 'ylo'), 0, 0, tiled=True)  4.34 us
    pallas_call x1, Pallas kernels, forward_call(): pl.pallas_call(forward_kernel, grid_spec=pltpu.PrefetchScalarGridSpec(num...  3.87 us
  transfers between devices with their start and end apart: 25, of which 13 were waited for; matrix products, arithmetic and copies ran while one was open for 3% of the time, Pallas kernels for 14%

profile of v8, /device:TPU:2, one launch (start us, length us, event | category | flops | bytes accessed | tf_op | source)
XLA Modules:
  0.0 129.3 jit_solution(5654019049997665683)
XLA Ops:
  7.0 3.9 %collective-permute-start.1 = (bf16[80,704]{1,0:T(8,128)(2,1)S(1)}, bf16[80,704]{1,0:T(8,128)(2,1)S(1)}, u32[]{:S(2)}, u32[]{:S(2)}) collective-permute-start(bf16[80,704]{1,0:T(8,128)(2,1)S(1)} %fusion.refs_1_), channel_id=1, source_target_pairs={{0,28},{1,29},{4,0},{5,1},{8,4},{9,5},{12,8},{13,9},{16,12},{17,13... | collective-permute-start | bytes 337928 | tf_op jit(solution)/shard_map/ppermute | solution.py:39
  11.6 2.2 %collective-permute-done.refs_2_ = bf16[80,704]{1,0:T(8,128)(2,1)S(1)} collective-permute-done((bf16[80,704]{1,0:T(8,128)(2,1)S(1)}, bf16[80,704]{1,0:T(8,128)(2,1)S(1)}, u32[]{:S(2)}, u32[]{:S(2)}) %collective-permute-start) | collective-permute-done | bytes 112672 | tf_op jit(solution)/shard_map/ppermute | solution.py:39
  13.8 3.2 %collective-permute-start.3 = (bf16[80,704]{1,0:T(8,128)(2,1)S(1)}, bf16[80,704]{1,0:T(8,128)(2,1)S(1)}, u32[]{:S(2)}, u32[]{:S(2)}) collective-permute-start(bf16[80,704]{1,0:T(8,128)(2,1)S(1)} %collective-permute-done.1.refs_3_), channel_id=1, source_target_pairs={{0,28},{1,29},{4,0},{5,1},{8,4},{9,5},{12,8},{13,9},{16,12},{17,13... | collective-permute-start | bytes 337928 | tf_op jit(solution)/shard_map/ppermute | solution.py:39
  17.3 3.0 %copy.16 = bf16[128,64,128]{2,0,1:T(8,128)(2,1)S(1)} copy(bf16[128,64,128]{2,1,0:T(8,128)(2,1)} %param.9) | data formatting | bytes 4194304 | tf_op args[2]
  20.3 4.7 %collective-permute-start.10 = (bf16[80,704]{1,0:T(8,128)(2,1)S(1)}, bf16[80,704]{1,0:T(8,128)(2,1)S(1)}, u32[]{:S(2)}, u32[]{:S(2)}) collective-permute-start(bf16[80,704]{1,0:T(8,128)(2,1)S(1)} %fusion.refs_1_), channel_id=1, source_target_pairs={{0,16},{1,17},{4,20},{5,21},{8,24},{9,25},{12,28},{13,29},{16,0},{... | collective-permute-start | bytes 337928 | tf_op jit(solution)/shard_map/ppermute | solution.py:39
  25.0 3.2 %collective-permute-start.7 = (bf16[80,704]{1,0:T(8,128)(2,1)S(1)}, bf16[80,704]{1,0:T(8,128)(2,1)S(1)}, u32[]{:S(2)}, u32[]{:S(2)}) collective-permute-start(bf16[80,704]{1,0:T(8,128)(2,1)S(1)} %collective-permute-done.3.refs_5_), channel_id=1, source_target_pairs={{0,28},{1,29},{4,0},{5,1},{8,4},{9,5},{12,8},{13,9},{16,12},{17,13... | collective-permute-start | bytes 337928 | tf_op jit(solution)/shard_map/ppermute | solution.py:39
  28.2 4.5 %collective-permute-done.10.refs_8_ = bf16[80,704]{1,0:T(8,128)(2,1)S(1)} collective-permute-done((bf16[80,704]{1,0:T(8,128)(2,1)S(1)}, bf16[80,704]{1,0:T(8,128)(2,1)S(1)}, u32[]{:S(2)}, u32[]{:S(2)}) %collective-permute-start.10) | collective-permute-done | bytes 112672 | tf_op jit(solution)/shard_map/ppermute | solution.py:39
  32.8 2.5 %collective-permute-done.6.refs_6_ = bf16[80,704]{1,0:T(8,128)(2,1)S(1)} collective-permute-done((bf16[80,704]{1,0:T(8,128)(2,1)S(1)}, bf16[80,704]{1,0:T(8,128)(2,1)S(1)}, u32[]{:S(2)}, u32[]{:S(2)}) %collective-permute-start.6) | collective-permute-done | bytes 112672 | tf_op jit(solution)/shard_map/ppermute | solution.py:39
  40.1 1.9 %collective-permute-start.11 = (bf16[320,704]{1,0:T(8,128)(2,1)S(1)}, bf16[320,704]{1,0:T(8,128)(2,1)S(1)}, u32[]{:S(2)}, u32[]{:S(2)}) collective-permute-start(bf16[320,704]{1,0:T(8,128)(2,1)S(1)} %pad_maximum_fusion.1), channel_id=1, source_target_pairs={{0,130},{1,131},{4,134},{5,135},{8,138},{9,139},{12,142},{13,143},... | collective-permute-start | bytes 1351688 | tf_op jit(solution)/shard_map/ppermute | solution.py:39
  42.0 9.7 %scores.2 = (bf16[16,1280,256]{2,1,0:T(8,128)(2,1)S(1)}, f32[16,256]{1,0:T(8,128)S(1)}, f32[16,256]{1,0:T(8,128)S(1)}, bf16[320,128]{1,0:T(8,128)(2,1)S(1)}) custom-call(s32[5]{0:T(128)S(1)} %stack.23.refs_0_.meta, bf16[80,704]{1,0:T(8,128)(2,1)S(1)} %fusion.refs_1_, bf16[80,704]{1,0:T(8,128)(2,1)S(1)} %collective-permute-done.refs_2_, ...), custom_call_target="tpu_custom_call" | custom-call | flops 6039797760 | bytes 5242880 | tf_op jit(solution)/shard_map/scores/pallas_call | solution.py:158
  53.6 8.9 %scores.3 = (bf16[16,1280,256]{2,1,0:T(8,128)(2,1)S(1)}, f32[16,256]{1,0:T(8,128)S(1)}, f32[16,256]{1,0:T(8,128)S(1)}, bf16[320,128]{1,0:T(8,128)(2,1)S(1)}) custom-call(s32[5]{0:T(128)S(1)} %stack.23.refs_0_.meta, bf16[320,704]{1,0:T(8,128)(2,1)S(1)} %collective-permute-done.5.refs_1_, ...), custom_call_target="tpu_custom_call", output_to_operand_aliasing={{0}: (3, {})} | custom-call | flops 6039797760 | bytes 5242880 | tf_op jit(solution)/shard_map/scores/pallas_call | solution.py:158
  62.5 3.9 %index_forward.1 = (f32[320,256]{1,0:T(8,128)S(1)}, f32[2,24,256]{2,1,0:T(8,128)S(1)}, f32[2,24,256]{2,1,0:T(8,128)S(1)}) custom-call(s32[5]{0:T(128)S(1)} %stack.23.refs_0_.meta, bf16[320,128]{1,0:T(8,128)(2,1)S(1)} %get-tuple-element.55.keys, f32[16,256]{1,0:T(8,128)S(1)} %get-tuple-element.56.m0, f32[16,256]{1,0:T(8,128)S(1)} %get-tuple-element.57.l0, ...), custom_call_target="tpu_custom_call" | custom-call | flops 1342177280 | bytes 5242880 | tf_op jit(solution)/shard_map/index_forward/pallas_call | solution.py:346
  67.7 1.8 %collective-permute-start.19 = (f32[2,16,256]{2,1,0:T(8,128)S(1)}, f32[2,16,256]{2,1,0:T(8,128)S(1)}, u32[]{:S(2)}, u32[]{:S(2)}) collective-permute-start(f32[2,16,256]{2,1,0:T(8,128)S(1)} %get-tuple-element.69), channel_id=1, source_target_pairs={{0,96},{1,97},{4,100},{5,101},{8,104},{9,105},{12,108},{13,109},{1... | collective-permute-start | bytes 98312 | tf_op jit(solution)/shard_map/ppermute | solution.py:39
  69.8 3.5 %collective-permute-done.18.up = f32[2,8,256]{2,1,0:T(8,128)S(1)} collective-permute-done((f32[2,8,256]{2,1,0:T(8,128)S(1)}, f32[2,8,256]{2,1,0:T(8,128)S(1)}, u32[]{:S(2)}, u32[]{:S(2)}) %collective-permute-start.18) | collective-permute-done | bytes 16416 | tf_op jit(solution)/shard_map/ppermute | solution.py:39
  73.3 3.3 %head_sum.1 = (bf16[336,256]{1,0:T(8,128)(2,1)S(1)}, bf16[336,256]{1,0:T(8,128)(2,1)S(1)}, bf16[336,256]{1,0:T(8,128)(2,1)S(1)}, bf16[336,256]{1,0:T(8,128)(2,1)S(1)}) custom-call(s32[5]{0:T(128)S(1)} %stack.23.refs_0_.meta, bf16[16,1280,256]{2,1,0:T(8,128)(2,1)S(1)} %get-tuple-element.64.e_ref, f32[16,256]{1,0:T(8,128)S(1)} %get-tuple-element.56.m0, ...), custom_call_target="tpu_custom_call" | custom-call | bytes 11534336 | tf_op jit(solution)/shard_map/head_sum/pallas_call | solution.py:241
  76.6 1.8 %collective-permute-start.20 = (bf16[336,256]{1,0:T(8,128)(2,1)S(1)}, bf16[336,256]{1,0:T(8,128)(2,1)S(1)}, u32[]{:S(2)}, u32[]{:S(2)}) collective-permute-start(bf16[336,256]{1,0:T(8,128)(2,1)S(1)} %get-tuple-element.71), channel_id=1, source_target_pairs={{0,64},{1,65},{4,68},{5,69},{8,72},{9,73},{12,76},{13,77},{16,80},... | collective-permute-start | bytes 516104 | tf_op jit(solution)/shard_map/ppermute | solution.py:39
  78.4 2.9 %collective-permute-start.21 = (bf16[336,256]{1,0:T(8,128)(2,1)S(1)}, bf16[336,256]{1,0:T(8,128)(2,1)S(1)}, u32[]{:S(2)}, u32[]{:S(2)}) collective-permute-start(bf16[336,256]{1,0:T(8,128)(2,1)S(1)} %get-tuple-element.72), channel_id=1, source_target_pairs={{0,128},{1,129},{4,132},{5,133},{8,136},{9,137},{12,140},{13,141},... | collective-permute-start | bytes 516104 | tf_op jit(solution)/shard_map/ppermute | solution.py:39
  81.3 1.8 %collective-permute-start.22 = (bf16[336,256]{1,0:T(8,128)(2,1)S(1)}, bf16[336,256]{1,0:T(8,128)(2,1)S(1)}, u32[]{:S(2)}, u32[]{:S(2)}) collective-permute-start(bf16[336,256]{1,0:T(8,128)(2,1)S(1)} %get-tuple-element.73), channel_id=1, source_target_pairs={{0,192},{1,193},{4,196},{5,197},{8,200},{9,201},{12,204},{13,205},... | collective-permute-start | bytes 516104 | tf_op jit(solution)/shard_map/ppermute | solution.py:39
  83.6 4.4 %collective-permute-done.21.t2 = bf16[336,256]{1,0:T(8,128)(2,1)S(1)} collective-permute-done((bf16[336,256]{1,0:T(8,128)(2,1)S(1)}, bf16[336,256]{1,0:T(8,128)(2,1)S(1)}, u32[]{:S(2)}, u32[]{:S(2)}) %collective-permute-start.21) | collective-permute-done | bytes 172064 | tf_op jit(solution)/shard_map/ppermute | solution.py:39
  88.0 2.7 %collective-permute-done.22.t3 = bf16[336,256]{1,0:T(8,128)(2,1)S(1)} collective-permute-done((bf16[336,256]{1,0:T(8,128)(2,1)S(1)}, bf16[336,256]{1,0:T(8,128)(2,1)S(1)}, u32[]{:S(2)}, u32[]{:S(2)}) %collective-permute-start.22) | collective-permute-done | bytes 172064 | tf_op jit(solution)/shard_map/ppermute | solution.py:39
  90.6 7.7 %index_backward.1 = (f32[80,128]{1,0:T(8,128)S(1)}, f32[80,128]{1,0:T(8,128)S(1)}, bf16[16,32,128]{2,1,0:T(8,128)(2,1)}) custom-call(s32[5]{0:T(128)S(1)} %stack.23.refs_0_.meta, bf16[320,128]{1,0:T(8,128)(2,1)S(1)} %get-tuple-element.55.keys, f32[320,256]{1,0:T(8,128)S(1)} %get-tuple-element.63.logits, bf16[336,256]{1,0:T(8,128)(2,1)S(1)} %get-tuple-element.70.t0, ...), custom_call_target="tpu_custom_call" | custom-call | flops 2684354560 | bytes 6291456 | tf_op jit(solution)/shard_map/index_backward/pallas_call | solution.py:427
  98.4 4.3 %all-to-all-start = ((bf16[16,32,128]{2,1,0:T(8,128)(2,1)}), bf16[16,32,128]{2,1,0:T(8,128)(2,1)S(1)}, u32[]{:S(2)}, u32[]{:S(2)}) async-start(bf16[16,32,128]{2,1,0:T(8,128)(2,1)} %get-tuple-element.74), calls=%async_computation | async-start | bytes 262144 | tf_op jit(solution)/shard_map/all_to_all | solution.py:520
  102.8 10.2 %all-to-all-done = bf16[16,32,128]{2,1,0:T(8,128)(2,1)S(1)} async-done(((bf16[16,32,128]{2,1,0:T(8,128)(2,1)}), bf16[16,32,128]{2,1,0:T(8,128)(2,1)S(1)}, u32[]{:S(2)}, u32[]{:S(2)}) %all-to-all-start) | async-done | bytes 131104 | tf_op jit(solution)/shard_map/all_to_all | solution.py:520
  113.0 14.4 %all_to_all.10 = bf16[8,112,128]{2,1,0:T(8,128)(2,1)S(1)} all-to-all(bf16[8,112,128]{2,1,0:T(8,128)(2,1)S(1)} %broadcast_in_dim.2), channel_id=1, replica_groups=mesh['yhi'=2,'xh'=2,'xp'=2,'z'=8,'ylo'=2,'core'=2] {'yhi','xh','xp'}, dimensions={0} | all-to-all | bytes 458752 | tf_op jit(solution)/shard_map/all_to_all | solution.py:464
  (62 shorter events, 17.2 us)
Async XLA Ops:
  3.0 32.2 %collective-permute-start.8 = (bf16[4,576,128]{2,1,0:T(8,128)(2,1)S(1)}, bf16[4,576,128]{2,1,0:T(8,128)(2,1)S(1)}, u32[]{:S(2)}, u32[]{:S(2)}) collective-permute-start(bf16[4,576,128]{2,1,0:T(8,128)(2,1)S(1)} %get-tuple-element.80), channel_id=1, source_target_pairs={{0,32},{1,33},{4,36},{5,37},{8,40},{9,41},{12,44},{13,45},{16,48},... | collective-permute-start | bytes 1769480 | tf_op jit(solution)/shard_map/ppermute | solution.py:39
  4.6 30.7 %collective-permute-start.9 = (bf16[4,576,128]{2,1,0:T(8,128)(2,1)S(1)}, bf16[4,576,128]{2,1,0:T(8,128)(2,1)S(1)}, u32[]{:S(2)}, u32[]{:S(2)}) collective-permute-start(bf16[4,576,128]{2,1,0:T(8,128)(2,1)S(1)} %get-tuple-element.79), channel_id=1, source_target_pairs={{0,96},{1,97},{4,100},{5,101},{8,104},{9,105},{12,108},{13,109},{1... | collective-permute-start | bytes 1769480 | tf_op jit(solution)/shard_map/ppermute | solution.py:39
  5.4 8.4 %collective-permute-start = (bf16[80,704]{1,0:T(8,128)(2,1)S(1)}, bf16[80,704]{1,0:T(8,128)(2,1)S(1)}, u32[]{:S(2)}, u32[]{:S(2)}) collective-permute-start(bf16[80,704]{1,0:T(8,128)(2,1)S(1)} %fusion.refs_1_), channel_id=1, source_target_pairs={{0,4},{1,5},{4,8},{5,9},{8,12},{9,13},{12,16},{13,17},{16,20},{17,... | collective-permute-start | bytes 337928 | tf_op jit(solution)/shard_map/ppermute | solution.py:39
  7.0 6.8 %collective-permute-start.1 = (bf16[80,704]{1,0:T(8,128)(2,1)S(1)}, bf16[80,704]{1,0:T(8,128)(2,1)S(1)}, u32[]{:S(2)}, u32[]{:S(2)}) collective-permute-start(bf16[80,704]{1,0:T(8,128)(2,1)S(1)} %fusion.refs_1_), channel_id=1, source_target_pairs={{0,28},{1,29},{4,0},{5,1},{8,4},{9,5},{12,8},{13,9},{16,12},{17,13... | collective-permute-start | bytes 337928 | tf_op jit(solution)/shard_map/ppermute | solution.py:39
  13.8 11.2 %collective-permute-start.2 = (bf16[80,704]{1,0:T(8,128)(2,1)S(1)}, bf16[80,704]{1,0:T(8,128)(2,1)S(1)}, u32[]{:S(2)}, u32[]{:S(2)}) collective-permute-start(bf16[80,704]{1,0:T(8,128)(2,1)S(1)} %collective-permute-done.refs_2_), channel_id=1, source_target_pairs={{0,4},{1,5},{4,8},{5,9},{8,12},{9,13},{12,16},{13,17},{16,20},{17,... | collective-permute-start | bytes 337928 | tf_op jit(solution)/shard_map/ppermute | solution.py:39
  13.8 11.2 %collective-permute-start.3 = (bf16[80,704]{1,0:T(8,128)(2,1)S(1)}, bf16[80,704]{1,0:T(8,128)(2,1)S(1)}, u32[]{:S(2)}, u32[]{:S(2)}) collective-permute-start(bf16[80,704]{1,0:T(8,128)(2,1)S(1)} %collective-permute-done.1.refs_3_), channel_id=1, source_target_pairs={{0,28},{1,29},{4,0},{5,1},{8,4},{9,5},{12,8},{13,9},{16,12},{17,13... | collective-permute-start | bytes 337928 | tf_op jit(solution)/shard_map/ppermute | solution.py:39
  17.2 3.1 %collective-permute-start.4 = (f32[1,128]{1,0:T(1,128)S(1)}, f32[1,128]{1,0:T(1,128)S(1)}, u32[]{:S(2)}, u32[]{:S(2)}) collective-permute-start(f32[1,128]{1,0:T(1,128)S(1)} %convert_element_type.17.refs_15_.refs_11_.pa), channel_id=1, source_target_pairs={{0,1},{1,0},{4,5},{5,4},{8,9},{9,8},{12,13},{13,12},{16,17},{17,16... | collective-permute-start | bytes 1544 | tf_op jit(solution)/shard_map/ppermute | solution.py:39
  20.3 12.4 %collective-permute-start.10 = (bf16[80,704]{1,0:T(8,128)(2,1)S(1)}, bf16[80,704]{1,0:T(8,128)(2,1)S(1)}, u32[]{:S(2)}, u32[]{:S(2)}) collective-permute-start(bf16[80,704]{1,0:T(8,128)(2,1)S(1)} %fusion.refs_1_), channel_id=1, source_target_pairs={{0,16},{1,17},{4,20},{5,21},{8,24},{9,25},{12,28},{13,29},{16,0},{... | collective-permute-start | bytes 337928 | tf_op jit(solution)/shard_map/ppermute | solution.py:39
  25.0 10.3 %collective-permute-start.6 = (bf16[80,704]{1,0:T(8,128)(2,1)S(1)}, bf16[80,704]{1,0:T(8,128)(2,1)S(1)}, u32[]{:S(2)}, u32[]{:S(2)}) collective-permute-start(bf16[80,704]{1,0:T(8,128)(2,1)S(1)} %collective-permute-done.2.refs_4_), channel_id=1, source_target_pairs={{0,4},{1,5},{4,8},{5,9},{8,12},{9,13},{12,16},{13,17},{16,20},{17,... | collective-permute-start | bytes 337928 | tf_op jit(solution)/shard_map/ppermute | solution.py:39
  25.0 10.2 %collective-permute-start.7 = (bf16[80,704]{1,0:T(8,128)(2,1)S(1)}, bf16[80,704]{1,0:T(8,128)(2,1)S(1)}, u32[]{:S(2)}, u32[]{:S(2)}) collective-permute-start(bf16[80,704]{1,0:T(8,128)(2,1)S(1)} %collective-permute-done.3.refs_5_), channel_id=1, source_target_pairs={{0,28},{1,29},{4,0},{5,1},{8,4},{9,5},{12,8},{13,9},{16,12},{17,13... | collective-permute-start | bytes 337928 | tf_op jit(solution)/shard_map/ppermute | solution.py:39
  35.3 2.1 %collective-permute-start.13 = (bf16[4,576,128]{2,1,0:T(8,128)(2,1)S(1)}, bf16[4,576,128]{2,1,0:T(8,128)(2,1)S(1)}, u32[]{:S(2)}, u32[]{:S(2)}) collective-permute-start(bf16[4,576,128]{2,1,0:T(8,128)(2,1)S(1)} %collective-permute-done.8.refs_11_.refs_7_), channel_id=1, source_target_pairs={{0,1},{1,0},{4,5},{5,4},{8,9},{9,8},{12,13},{13,12},{16,17},{17,16... | collective-permute-start | bytes 1769480 | tf_op jit(solution)/shard_map/ppermute | solution.py:39
  35.4 2.8 %collective-permute-start.14 = (bf16[4,576,128]{2,1,0:T(8,128)(2,1)S(1)}, bf16[4,576,128]{2,1,0:T(8,128)(2,1)S(1)}, u32[]{:S(2)}, u32[]{:S(2)}) collective-permute-start(bf16[4,576,128]{2,1,0:T(8,128)(2,1)S(1)} %collective-permute-done.9.refs_13_.refs_9_), channel_id=1, source_target_pairs={{0,1},{1,0},{4,5},{5,4},{8,9},{9,8},{12,13},{13,12},{16,17},{17,16... | collective-permute-start | bytes 1769480 | tf_op jit(solution)/shard_map/ppermute | solution.py:39
  35.9 6.2 %collective-permute-start.12 = (bf16[8,576,128]{2,1,0:T(8,128)(2,1)S(1)}, bf16[8,576,128]{2,1,0:T(8,128)(2,1)S(1)}, u32[]{:S(2)}, u32[]{:S(2)}) collective-permute-start(bf16[8,576,128]{2,1,0:T(8,128)(2,1)S(1)} %bitcast.25), channel_id=1, source_target_pairs={{0,1},{1,0},{4,5},{5,4},{8,9},{9,8},{12,13},{13,12},{16,17},{17,16... | collective-permute-start | bytes 3538952 | tf_op jit(solution)/shard_map/ppermute | solution.py:39
  38.2 24.3 %collective-permute-start.15 = (bf16[64,128,128]{2,1,0:T(8,128)(2,1)S(1)}, bf16[64,128,128]{2,1,0:T(8,128)(2,1)S(1)}, u32[]{:S(2)}, u32[]{:S(2)}) collective-permute-start(bf16[64,128,128]{2,1,0:T(8,128)(2,1)S(1)} %bitcast.21), channel_id=1, source_target_pairs={{0,1},{1,0},{4,5},{5,4},{8,9},{9,8},{12,13},{13,12},{16,17},{17,16... | collective-permute-start | bytes 6291464 | tf_op jit(solution)/shard_map/ppermute | solution.py:39
  38.4 14.9 %collective-permute-start.5 = (bf16[320,704]{1,0:T(8,128)(2,1)S(1)}, bf16[320,704]{1,0:T(8,128)(2,1)S(1)}, u32[]{:S(2)}, u32[]{:S(2)}) collective-permute-start(bf16[320,704]{1,0:T(8,128)(2,1)S(1)} %pad_maximum_fusion), channel_id=1, source_target_pairs={{0,2},{1,3},{4,6},{5,7},{8,10},{9,11},{12,14},{13,15},{16,18},{17,... | collective-permute-start | bytes 1351688 | tf_op jit(solution)/shard_map/ppermute | solution.py:39
  40.1 13.5 %collective-permute-start.11 = (bf16[320,704]{1,0:T(8,128)(2,1)S(1)}, bf16[320,704]{1,0:T(8,128)(2,1)S(1)}, u32[]{:S(2)}, u32[]{:S(2)}) collective-permute-start(bf16[320,704]{1,0:T(8,128)(2,1)S(1)} %pad_maximum_fusion.1), channel_id=1, source_target_pairs={{0,130},{1,131},{4,134},{5,135},{8,138},{9,139},{12,142},{13,143},... | collective-permute-start | bytes 1351688 | tf_op jit(solution)/shard_map/ppermute | solution.py:39
  42.0 20.4 %collective-permute-start.16 = (f32[64,128]{1,0:T(8,128)S(1)}, f32[64,128]{1,0:T(8,128)S(1)}, u32[]{:S(2)}, u32[]{:S(2)}) collective-permute-start(f32[64,128]{1,0:T(8,128)S(1)} %bitcast.28), channel_id=1, source_target_pairs={{0,1},{1,0},{4,5},{5,4},{8,9},{9,8},{12,13},{13,12},{16,17},{17,16... | collective-permute-start | bytes 98312 | tf_op jit(solution)/shard_map/ppermute | solution.py:39
  67.7 5.6 %collective-permute-start.19 = (f32[2,16,256]{2,1,0:T(8,128)S(1)}, f32[2,16,256]{2,1,0:T(8,128)S(1)}, u32[]{:S(2)}, u32[]{:S(2)}) collective-permute-start(f32[2,16,256]{2,1,0:T(8,128)S(1)} %get-tuple-element.69), channel_id=1, source_target_pairs={{0,96},{1,97},{4,100},{5,101},{8,104},{9,105},{12,108},{13,109},{1... | collective-permute-start | bytes 98312 | tf_op jit(solution)/shard_map/ppermute | solution.py:39
  69.5 3.7 %collective-permute-start.18 = (f32[2,8,256]{2,1,0:T(8,128)S(1)}, f32[2,8,256]{2,1,0:T(8,128)S(1)}, u32[]{:S(2)}, u32[]{:S(2)}) collective-permute-start(f32[2,8,256]{2,1,0:T(8,128)S(1)} %get-tuple-element.68), channel_id=1, source_target_pairs={{0,32},{1,33},{4,36},{5,37},{8,40},{9,41},{12,44},{13,45},{16,48},... | collective-permute-start | bytes 49160 | tf_op jit(solution)/shard_map/ppermute | solution.py:39
  76.6 7.0 %collective-permute-start.20 = (bf16[336,256]{1,0:T(8,128)(2,1)S(1)}, bf16[336,256]{1,0:T(8,128)(2,1)S(1)}, u32[]{:S(2)}, u32[]{:S(2)}) collective-permute-start(bf16[336,256]{1,0:T(8,128)(2,1)S(1)} %get-tuple-element.71), channel_id=1, source_target_pairs={{0,64},{1,65},{4,68},{5,69},{8,72},{9,73},{12,76},{13,77},{16,80},... | collective-permute-start | bytes 516104 | tf_op jit(solution)/shard_map/ppermute | solution.py:39
  78.4 9.5 %collective-permute-start.21 = (bf16[336,256]{1,0:T(8,128)(2,1)S(1)}, bf16[336,256]{1,0:T(8,128)(2,1)S(1)}, u32[]{:S(2)}, u32[]{:S(2)}) collective-permute-start(bf16[336,256]{1,0:T(8,128)(2,1)S(1)} %get-tuple-element.72), channel_id=1, source_target_pairs={{0,128},{1,129},{4,132},{5,133},{8,136},{9,137},{12,140},{13,141},... | collective-permute-start | bytes 516104 | tf_op jit(solution)/shard_map/ppermute | solution.py:39
  81.3 9.3 %collective-permute-start.22 = (bf16[336,256]{1,0:T(8,128)(2,1)S(1)}, bf16[336,256]{1,0:T(8,128)(2,1)S(1)}, u32[]{:S(2)}, u32[]{:S(2)}) collective-permute-start(bf16[336,256]{1,0:T(8,128)(2,1)S(1)} %get-tuple-element.73), channel_id=1, source_target_pairs={{0,192},{1,193},{4,196},{5,197},{8,200},{9,201},{12,204},{13,205},... | collective-permute-start | bytes 516104 | tf_op jit(solution)/shard_map/ppermute | solution.py:39
  98.4 4.4 %collective-permute-start.23 = (f32[80,128]{1,0:T(8,128)S(1)}, f32[80,128]{1,0:T(8,128)S(1)}, u32[]{:S(2)}, u32[]{:S(2)}) collective-permute-start(f32[80,128]{1,0:T(8,128)S(1)} %get-tuple-element.76), channel_id=1, source_target_pairs={{0,1},{1,0},{4,5},{5,4},{8,9},{9,8},{12,13},{13,12},{16,17},{17,16... | collective-permute-start | bytes 122888 | tf_op jit(solution)/shard_map/ppermute | solution.py:39
  98.4 14.6 %all-to-all-start = ((bf16[16,32,128]{2,1,0:T(8,128)(2,1)}), bf16[16,32,128]{2,1,0:T(8,128)(2,1)S(1)}, u32[]{:S(2)}, u32[]{:S(2)}) async-start(bf16[16,32,128]{2,1,0:T(8,128)(2,1)} %get-tuple-element.74), calls=%async_computation | async-start | bytes 262144 | tf_op jit(solution)/shard_map/all_to_all | solution.py:520
  (4 other events, 55.7 us)

commit v9 on v8

--- a/solution.py
+++ b/solution.py
@@ -39,6 +39,17 @@
     return lax.ppermute(value, ALL, pairs)
 
 
+def ring(value):
+    pairs = [
+        (flat(x, y, z, c), flat(x, y, (z + (7 if c else 1)) % 8, c))
+        for x in range(4)
+        for y in range(4)
+        for z in range(8)
+        for c in range(2)
+    ]
+    return lax.ppermute(value, ALL, pairs)
+
+
 def swap_core(value):
     return shift(value, flip=1)
 
@@ -53,7 +64,7 @@
 def slot_of(meta, i):
     k = i & 7
     reach = (k + 1) >> 1
-    step = reach * (1 - 2 * (k & 1))
+    step = reach * (1 - 2 * ((k & 1) ^ meta[2]))
     return ((meta[0] + 8 + step) & 7) * 2 + (meta[1] ^ (i >> 3))
 
 
@@ -88,8 +99,9 @@
     def _():
         copies = []
         at = 0
-        for i, (block, span) in enumerate(zip(blocks, spans)):
-            copies.append(pltpu.make_async_copy(block, keys.at[at : at + span, :], sems.at[i]))
+        for i, (block, (row, span)) in enumerate(zip(blocks, spans)):
+            source = block.at[row : row + span, :]
+            copies.append(pltpu.make_async_copy(source, keys.at[at : at + span, :], sems.at[i]))
             copies[-1].start()
             at += span
         place = place_of(pa, pb)
@@ -147,7 +159,7 @@
 
 
 def score_call(meta, chunk, blocks, before, qa, qb, na, nb, ma, mb, pa, pb):
-    spans = [b.shape[0] for b in blocks]
+    spans, blocks = [cut for _, cut in blocks], [block for block, _ in blocks]
     whole = lambda shape: pl.BlockSpec(shape, lambda h, meta: (0,) * len(shape))
 
     def heads(start, count):
@@ -482,27 +494,33 @@
     own, meta = lax.optimization_barrier((own, meta))
 
     queries = main_queries.transpose(0, 2, 1)
-    f1, b1 = shift(own, dz=1), shift(own, dz=7)
+    start = jnp.concatenate([own, swap_core(own)])
+    r1 = ring(start)
     queries_far = swap_core(queries)
-    halves = after(queries, own)
+    halves = after(queries, start)
     left, right = shift(halves[:4], dx=1), shift(halves[4:], dx=3)
-    f4 = shift(own, dz=4)
-    f1, b1 = lax.optimization_barrier((f1, b1))
-    f2, b2 = shift(f1, dz=1), shift(b1, dz=7)
+    r2 = ring(r1)
     ia = index_queries.transpose(1, 0, 2)
     pb = swap_core(pa)
-    f2, b2, ia, pb = lax.optimization_barrier((f2, b2, ia, pb))
-    f3, b3 = shift(f2, dz=1), shift(b2, dz=7)
-    f3, b3, left, right, f4 = lax.optimization_barrier((f3, b3, left, right, f4))
+    r2, ia, pb = lax.optimization_barrier((r2, ia, pb))
+    r3 = ring(r2)
+    x1, x2 = swap_core(r1), swap_core(r2)
+    r3, left, right, x1, x2 = lax.optimization_barrier((r3, left, right, x1, x2))
+    x3 = swap_core(r3)
+    r4 = ring(r3[:HALF])
+    r4, x3 = lax.optimization_barrier((r4, x3))
     left_far, right_far = swap_core(left), swap_core(right)
-    y0, y1 = jnp.concatenate([own, f1, b1, f2]), jnp.concatenate([b2, f3, b3, f4])
+    y0 = jnp.concatenate([own, r1[:HALF], x1[HALF:], r2[:HALF]])
+    y1 = jnp.concatenate([x2[HALF:], r3[:HALF], x3[HALF:], r4])
     y0, y1 = shift(y0, dy=1), shift(y1, dy=3)
-    ia, wa = lax.optimization_barrier((ia, wa, f4, left_far, right_far))[:2]
+    ia, wa = lax.optimization_barrier((ia, wa, r4, left_far, right_far))[:2]
     ib, wb = swap_core(ia), swap_core(wa)
 
     sides = (queries, queries_far, left, left_far, right, right_far, pa, pb)
-    exps, m0, l0, keys = score_call(meta, 0, [own, f1, b1, f2, b2, f3, b3, f4], [], *sides)
-    exps, m1, l1, keys = score_call(meta, 1, [y0, y1], in_vmem(exps, keys), *sides)
+    low, high = (0, HALF), (HALF, HALF)
+    column = [(own, low), (r1, low), (x1, high), (r2, low), (x2, high), (r3, low), (x3, high), (r4, low)]
+    exps, m0, l0, keys = score_call(meta, 0, column, [], *sides)
+    exps, m1, l1, keys = score_call(meta, 1, [(y0, (0, 4 * HALF)), (y1, (0, 4 * HALF))], in_vmem(exps, keys), *sides)
 
     logits, ours, sent = forward_call(meta, keys, (m0, l0, m1, l1), ia, ib, pa, pb, wa, wb)
     here, up, down = pair_call(ours, swap_core(sent))

time: 130 us -> 128 us (0.985)
  starting transfers between devices: 36.7 us -> 26.9 us
  waiting for transfers between devices: 35.6 us -> 44.6 us
    ppermute x0 -> x4, waiting for transfers between devices: none -> 18.7 us  [ring(): return lax.ppermute(value, ALL, pairs)]
    ppermute x24 -> x21, starting transfers between devices: 32.3 us -> 18.6 us  [shift(): return lax.ppermute(value, ALL, pairs)]
    ppermute x24 -> x21, waiting for transfers between devices: 25.4 us -> 15.8 us  [shift(): return lax.ppermute(value, ALL, pairs)]
    ppermute x0 -> x4, starting transfers between devices: none -> 2.08 us  [ring(): return lax.ppermute(value, ALL, pairs)]
    all_to_all x1, starting transfers between devices: 4.34 us -> 6.28 us  [body(): kg = lax.all_to_all(kg, ('z', 'ylo'), 0, 0, tiled=True)]
    unnamed x7 -> x8, local copies, waits for them, and re-layouts: 3.04 us -> 2.97 us
  transfers between devices with their start and end apart: 25 -> 26, of which waited for: 13 -> 14; matrix products, arithmetic and copies ran while one was open for 3% -> 4% of each run, Pallas kernels for 14% -> 14%
where the time goes in v9:
time: 128 us
  waiting for transfers between devices  44.6 us (35%)
  Pallas kernels  33.1 us (26%)
  starting transfers between devices  26.9 us (21%)
  blocking collectives  14.4 us (11%)
  local copies, waits for them, and re-layouts  5.2 us (4%)
  other arithmetic  2.38 us (2%)
  between operations  1.59 us (1%)
    ppermute x4, waiting for transfers between devices, ring(): return lax.ppermute(value, ALL, pairs)  18.7 us
    ppermute x21, starting transfers between devices, shift(): return lax.ppermute(value, ALL, pairs)  18.6 us
    pallas_call x2, Pallas kernels, score_call(): pl.pallas_call(lambda *refs: score_kernel(chunk, spans, *refs), grid_spec...  18.2 us
    ppermute x21, waiting for transfers between devices, shift(): return lax.ppermute(value, ALL, pairs)  15.8 us
    all_to_all x1, blocking collectives, gather_head(): return lax.all_to_all(wide, ('yhi', 'xh', 'xp'), 0, 0, tiled=True)  14.4 us
    all_to_all x1, waiting for transfers between devices, body(): kg = lax.all_to_all(kg, ('z', 'ylo'), 0, 0, tiled=True)  10.2 us
    pallas_call x1, Pallas kernels, backward_call(): pl.pallas_call(backward_kernel, grid_spec=pltpu.PrefetchScalarGridSpec(nu...  7.76 us
    all_to_all x1, starting transfers between devices, body(): kg = lax.all_to_all(kg, ('z', 'ylo'), 0, 0, tiled=True)  6.28 us
  transfers between devices with their start and end apart: 26, of which 14 were waited for; matrix products, arithmetic and copies ran while one was open for 4% of the time, Pallas kernels for 14%

profile of v9, /device:TPU:2, one launch (start us, length us, event | category | flops | bytes accessed | tf_op | source)
XLA Modules:
  0.0 128.2 jit_solution(6746887700244121241)
XLA Ops:
  3.0 2.0 %collective-permute-start.1 = (bf16[160,704]{1,0:T(8,128)(2,1)S(1)}, bf16[160,704]{1,0:T(8,128)(2,1)S(1)}, u32[]{:S(2)}, u32[]{:S(2)}) collective-permute-start(bf16[160,704]{1,0:T(8,128)(2,1)S(1)} %constant_dynamic-update-slice_fusion), channel_id=1, source_target_pairs={{0,4},{1,29},{4,8},{5,1},{8,12},{9,5},{12,16},{13,9},{16,20},{17,1... | collective-permute-start | bytes 675848 | tf_op jit(solution)/shard_map/ppermute | solution.py:50
  6.4 1.6 %collective-permute-start.5 = (bf16[4,576,128]{2,1,0:T(8,128)(2,1)S(1)}, bf16[4,576,128]{2,1,0:T(8,128)(2,1)S(1)}, u32[]{:S(2)}, u32[]{:S(2)}) collective-permute-start(bf16[4,576,128]{2,1,0:T(8,128)(2,1)S(1)} %get-tuple-element.78), channel_id=1, source_target_pairs={{0,32},{1,33},{4,36},{5,37},{8,40},{9,41},{12,44},{13,45},{16,48},... | collective-permute-start | bytes 1769480 | tf_op jit(solution)/shard_map/ppermute | solution.py:39
  8.5 4.7 %collective-permute-done.1.refs_2_ = bf16[160,704]{1,0:T(8,128)(2,1)S(1)} collective-permute-done((bf16[160,704]{1,0:T(8,128)(2,1)S(1)}, bf16[160,704]{1,0:T(8,128)(2,1)S(1)}, u32[]{:S(2)}, u32[]{:S(2)}) %collective-permute-start.1) | collective-permute-done | bytes 225312 | tf_op jit(solution)/shard_map/ppermute | solution.py:50
  14.0 2.0 %collective-permute-start.3 = (f32[1,128]{1,0:T(1,128)S(1)}, f32[1,128]{1,0:T(1,128)S(1)}, u32[]{:S(2)}, u32[]{:S(2)}) collective-permute-start(f32[1,128]{1,0:T(1,128)S(1)} %convert_element_type.17.refs_15_.refs_11_.pa), channel_id=1, source_target_pairs={{0,1},{1,0},{4,5},{5,4},{8,9},{9,8},{12,13},{13,12},{16,17},{17,16... | collective-permute-start | bytes 1544 | tf_op jit(solution)/shard_map/ppermute | solution.py:39
  15.9 2.9 %copy.16 = bf16[128,64,128]{2,0,1:T(8,128)(2,1)S(1)} copy(bf16[128,64,128]{2,1,0:T(8,128)(2,1)} %param.9) | data formatting | bytes 4194304 | tf_op args[2]
  21.5 6.5 %collective-permute-done.4.refs_6_ = bf16[160,704]{1,0:T(8,128)(2,1)S(1)} collective-permute-done((bf16[160,704]{1,0:T(8,128)(2,1)S(1)}, bf16[160,704]{1,0:T(8,128)(2,1)S(1)}, u32[]{:S(2)}, u32[]{:S(2)}) %collective-permute-start.4) | collective-permute-done | bytes 225312 | tf_op jit(solution)/shard_map/ppermute | solution.py:50
  29.1 6.1 %collective-permute-done.10.refs_8_ = bf16[80,704]{1,0:T(8,128)(2,1)S(1)} collective-permute-done((bf16[80,704]{1,0:T(8,128)(2,1)S(1)}, bf16[80,704]{1,0:T(8,128)(2,1)S(1)}, u32[]{:S(2)}, u32[]{:S(2)}) %collective-permute-start.10) | collective-permute-done | bytes 112672 | tf_op jit(solution)/shard_map/ppermute | solution.py:50
  35.4 1.8 %collective-permute-start.9 = (bf16[320,704]{1,0:T(8,128)(2,1)S(1)}, bf16[320,704]{1,0:T(8,128)(2,1)S(1)}, u32[]{:S(2)}, u32[]{:S(2)}) collective-permute-start(bf16[320,704]{1,0:T(8,128)(2,1)S(1)} %pad_maximum_fusion), channel_id=1, source_target_pairs={{0,2},{1,3},{4,6},{5,7},{8,10},{9,11},{12,14},{13,15},{16,18},{17,... | collective-permute-start | bytes 1351688 | tf_op jit(solution)/shard_map/ppermute | solution.py:39
  37.3 1.7 %collective-permute-start.12 = (bf16[320,704]{1,0:T(8,128)(2,1)S(1)}, bf16[320,704]{1,0:T(8,128)(2,1)S(1)}, u32[]{:S(2)}, u32[]{:S(2)}) collective-permute-start(bf16[320,704]{1,0:T(8,128)(2,1)S(1)} %pad_maximum_fusion.1), channel_id=1, source_target_pairs={{0,130},{1,131},{4,134},{5,135},{8,138},{9,139},{12,142},{13,143},... | collective-permute-start | bytes 1351688 | tf_op jit(solution)/shard_map/ppermute | solution.py:39
  39.1 9.5 %scores.2 = (bf16[16,1280,256]{2,1,0:T(8,128)(2,1)S(1)}, f32[16,256]{1,0:T(8,128)S(1)}, f32[16,256]{1,0:T(8,128)S(1)}, bf16[320,128]{1,0:T(8,128)(2,1)S(1)}) custom-call(s32[5]{0:T(128)S(1)} %stack.23.refs_0_.meta, bf16[80,704]{1,0:T(8,128)(2,1)S(1)} %fusion.refs_1_, bf16[160,704]{1,0:T(8,128)(2,1)S(1)} %collective-permute-done.1.refs_2_, ...), custom_call_target="tpu_custom_call" | custom-call | flops 6039797760 | bytes 5242880 | tf_op jit(solution)/shard_map/scores/pallas_call | solution.py:170
  48.6 2.0 %collective-permute-done.9.refs_1_ = bf16[320,704]{1,0:T(8,128)(2,1)S(1)} collective-permute-done((bf16[320,704]{1,0:T(8,128)(2,1)S(1)}, bf16[320,704]{1,0:T(8,128)(2,1)S(1)}, u32[]{:S(2)}, u32[]{:S(2)}) %collective-permute-start.9) | collective-permute-done | bytes 450592 | tf_op jit(solution)/shard_map/ppermute | solution.py:39
  50.7 8.7 %scores.3 = (bf16[16,1280,256]{2,1,0:T(8,128)(2,1)S(1)}, f32[16,256]{1,0:T(8,128)S(1)}, f32[16,256]{1,0:T(8,128)S(1)}, bf16[320,128]{1,0:T(8,128)(2,1)S(1)}) custom-call(s32[5]{0:T(128)S(1)} %stack.23.refs_0_.meta, bf16[320,704]{1,0:T(8,128)(2,1)S(1)} %collective-permute-done.9.refs_1_, ...), custom_call_target="tpu_custom_call", output_to_operand_aliasing={{0}: (3, {})} | custom-call | flops 6039797760 | bytes 5242880 | tf_op jit(solution)/shard_map/scores/pallas_call | solution.py:170
  59.4 3.9 %index_forward.1 = (f32[320,256]{1,0:T(8,128)S(1)}, f32[2,24,256]{2,1,0:T(8,128)S(1)}, f32[2,24,256]{2,1,0:T(8,128)S(1)}) custom-call(s32[5]{0:T(128)S(1)} %stack.23.refs_0_.meta, bf16[320,128]{1,0:T(8,128)(2,1)S(1)} %get-tuple-element.53.keys, f32[16,256]{1,0:T(8,128)S(1)} %get-tuple-element.54.m0, f32[16,256]{1,0:T(8,128)S(1)} %get-tuple-element.55.l0, ...), custom_call_target="tpu_custom_call" | custom-call | flops 1342177280 | bytes 5242880 | tf_op jit(solution)/shard_map/index_forward/pallas_call | solution.py:358
  65.2 1.5 %collective-permute-start.19 = (f32[2,8,256]{2,1,0:T(8,128)S(1)}, f32[2,8,256]{2,1,0:T(8,128)S(1)}, u32[]{:S(2)}, u32[]{:S(2)}) collective-permute-start(f32[2,8,256]{2,1,0:T(8,128)S(1)} %get-tuple-element.66), channel_id=1, source_target_pairs={{0,32},{1,33},{4,36},{5,37},{8,40},{9,41},{12,44},{13,45},{16,48},... | collective-permute-start | bytes 49160 | tf_op jit(solution)/shard_map/ppermute | solution.py:39
  66.7 3.0 %collective-permute-done.19.up = f32[2,8,256]{2,1,0:T(8,128)S(1)} collective-permute-done((f32[2,8,256]{2,1,0:T(8,128)S(1)}, f32[2,8,256]{2,1,0:T(8,128)S(1)}, u32[]{:S(2)}, u32[]{:S(2)}) %collective-permute-start.19) | collective-permute-done | bytes 16416 | tf_op jit(solution)/shard_map/ppermute | solution.py:39
  69.7 3.3 %head_sum.1 = (bf16[336,256]{1,0:T(8,128)(2,1)S(1)}, bf16[336,256]{1,0:T(8,128)(2,1)S(1)}, bf16[336,256]{1,0:T(8,128)(2,1)S(1)}, bf16[336,256]{1,0:T(8,128)(2,1)S(1)}) custom-call(s32[5]{0:T(128)S(1)} %stack.23.refs_0_.meta, bf16[16,1280,256]{2,1,0:T(8,128)(2,1)S(1)} %get-tuple-element.62.e_ref, f32[16,256]{1,0:T(8,128)S(1)} %get-tuple-element.54.m0, ...), custom_call_target="tpu_custom_call" | custom-call | bytes 11534336 | tf_op jit(solution)/shard_map/head_sum/pallas_call | solution.py:253
  73.0 2.3 %collective-permute-start.21 = (bf16[336,256]{1,0:T(8,128)(2,1)S(1)}, bf16[336,256]{1,0:T(8,128)(2,1)S(1)}, u32[]{:S(2)}, u32[]{:S(2)}) collective-permute-start(bf16[336,256]{1,0:T(8,128)(2,1)S(1)} %get-tuple-element.69), channel_id=1, source_target_pairs={{0,64},{1,65},{4,68},{5,69},{8,72},{9,73},{12,76},{13,77},{16,80},... | collective-permute-start | bytes 516104 | tf_op jit(solution)/shard_map/ppermute | solution.py:39
  75.4 2.9 %collective-permute-start.22 = (bf16[336,256]{1,0:T(8,128)(2,1)S(1)}, bf16[336,256]{1,0:T(8,128)(2,1)S(1)}, u32[]{:S(2)}, u32[]{:S(2)}) collective-permute-start(bf16[336,256]{1,0:T(8,128)(2,1)S(1)} %get-tuple-element.70), channel_id=1, source_target_pairs={{0,128},{1,129},{4,132},{5,133},{8,136},{9,137},{12,140},{13,141},... | collective-permute-start | bytes 516104 | tf_op jit(solution)/shard_map/ppermute | solution.py:39
  80.0 4.9 %collective-permute-done.22.t2 = bf16[336,256]{1,0:T(8,128)(2,1)S(1)} collective-permute-done((bf16[336,256]{1,0:T(8,128)(2,1)S(1)}, bf16[336,256]{1,0:T(8,128)(2,1)S(1)}, u32[]{:S(2)}, u32[]{:S(2)}) %collective-permute-start.22) | collective-permute-done | bytes 172064 | tf_op jit(solution)/shard_map/ppermute | solution.py:39
  84.9 2.7 %collective-permute-done.23.t3 = bf16[336,256]{1,0:T(8,128)(2,1)S(1)} collective-permute-done((bf16[336,256]{1,0:T(8,128)(2,1)S(1)}, bf16[336,256]{1,0:T(8,128)(2,1)S(1)}, u32[]{:S(2)}, u32[]{:S(2)}) %collective-permute-start.23) | collective-permute-done | bytes 172064 | tf_op jit(solution)/shard_map/ppermute | solution.py:39
  87.6 7.8 %index_backward.1 = (f32[80,128]{1,0:T(8,128)S(1)}, f32[80,128]{1,0:T(8,128)S(1)}, bf16[16,32,128]{2,1,0:T(8,128)(2,1)}) custom-call(s32[5]{0:T(128)S(1)} %stack.23.refs_0_.meta, bf16[320,128]{1,0:T(8,128)(2,1)S(1)} %get-tuple-element.53.keys, f32[320,256]{1,0:T(8,128)S(1)} %get-tuple-element.61.logits, bf16[336,256]{1,0:T(8,128)(2,1)S(1)} %get-tuple-element.68.t0, ...), custom_call_target="tpu_custom_call" | custom-call | flops 2684354560 | bytes 6291456 | tf_op jit(solution)/shard_map/index_backward/pallas_call | solution.py:439
  95.3 6.3 %all-to-all-start = ((bf16[16,32,128]{2,1,0:T(8,128)(2,1)}), bf16[16,32,128]{2,1,0:T(8,128)(2,1)S(1)}, u32[]{:S(2)}, u32[]{:S(2)}) async-start(bf16[16,32,128]{2,1,0:T(8,128)(2,1)} %get-tuple-element.72), calls=%async_computation | async-start | bytes 262144 | tf_op jit(solution)/shard_map/all_to_all | solution.py:538
  101.7 10.2 %all-to-all-done = bf16[16,32,128]{2,1,0:T(8,128)(2,1)S(1)} async-done(((bf16[16,32,128]{2,1,0:T(8,128)(2,1)}), bf16[16,32,128]{2,1,0:T(8,128)(2,1)S(1)}, u32[]{:S(2)}, u32[]{:S(2)}) %all-to-all-start) | async-done | bytes 131104 | tf_op jit(solution)/shard_map/all_to_all | solution.py:538
  111.9 14.4 %all_to_all.10 = bf16[8,112,128]{2,1,0:T(8,128)(2,1)S(1)} all-to-all(bf16[8,112,128]{2,1,0:T(8,128)(2,1)S(1)} %broadcast_in_dim.2), channel_id=1, replica_groups=mesh['yhi'=2,'xh'=2,'xp'=2,'z'=8,'ylo'=2,'core'=2] {'yhi','xh','xp'}, dimensions={0} | all-to-all | bytes 458752 | tf_op jit(solution)/shard_map/all_to_all | solution.py:476
  (72 shorter events, 14.2 us)
Async XLA Ops:
  3.0 10.1 %collective-permute-start.1 = (bf16[160,704]{1,0:T(8,128)(2,1)S(1)}, bf16[160,704]{1,0:T(8,128)(2,1)S(1)}, u32[]{:S(2)}, u32[]{:S(2)}) collective-permute-start(bf16[160,704]{1,0:T(8,128)(2,1)S(1)} %constant_dynamic-update-slice_fusion), channel_id=1, source_target_pairs={{0,4},{1,29},{4,8},{5,1},{8,12},{9,5},{12,16},{13,9},{16,20},{17,1... | collective-permute-start | bytes 675848 | tf_op jit(solution)/shard_map/ppermute | solution.py:50
  6.4 15.0 %collective-permute-start.5 = (bf16[4,576,128]{2,1,0:T(8,128)(2,1)S(1)}, bf16[4,576,128]{2,1,0:T(8,128)(2,1)S(1)}, u32[]{:S(2)}, u32[]{:S(2)}) collective-permute-start(bf16[4,576,128]{2,1,0:T(8,128)(2,1)S(1)} %get-tuple-element.78), channel_id=1, source_target_pairs={{0,32},{1,33},{4,36},{5,37},{8,40},{9,41},{12,44},{13,45},{16,48},... | collective-permute-start | bytes 1769480 | tf_op jit(solution)/shard_map/ppermute | solution.py:39
  7.9 13.6 %collective-permute-start.6 = (bf16[4,576,128]{2,1,0:T(8,128)(2,1)S(1)}, bf16[4,576,128]{2,1,0:T(8,128)(2,1)S(1)}, u32[]{:S(2)}, u32[]{:S(2)}) collective-permute-start(bf16[4,576,128]{2,1,0:T(8,128)(2,1)S(1)} %get-tuple-element.77), channel_id=1, source_target_pairs={{0,96},{1,97},{4,100},{5,101},{8,104},{9,105},{12,108},{13,109},{1... | collective-permute-start | bytes 1769480 | tf_op jit(solution)/shard_map/ppermute | solution.py:39
  13.2 7.4 %collective-permute-start.2 = (bf16[160,704]{1,0:T(8,128)(2,1)S(1)}, bf16[160,704]{1,0:T(8,128)(2,1)S(1)}, u32[]{:S(2)}, u32[]{:S(2)}) collective-permute-start(bf16[160,704]{1,0:T(8,128)(2,1)S(1)} %collective-permute-done.1.refs_2_), channel_id=1, source_target_pairs={{0,4},{1,29},{4,8},{5,1},{8,12},{9,5},{12,16},{13,9},{16,20},{17,1... | collective-permute-start | bytes 675848 | tf_op jit(solution)/shard_map/ppermute | solution.py:50
  14.0 5.1 %collective-permute-start.3 = (f32[1,128]{1,0:T(1,128)S(1)}, f32[1,128]{1,0:T(1,128)S(1)}, u32[]{:S(2)}, u32[]{:S(2)}) collective-permute-start(f32[1,128]{1,0:T(1,128)S(1)} %convert_element_type.17.refs_15_.refs_11_.pa), channel_id=1, source_target_pairs={{0,1},{1,0},{4,5},{5,4},{8,9},{9,8},{12,13},{13,12},{16,17},{17,16... | collective-permute-start | bytes 1544 | tf_op jit(solution)/shard_map/ppermute | solution.py:39
  18.9 2.5 %collective-permute-start.7 = (bf16[160,704]{1,0:T(8,128)(2,1)S(1)}, bf16[160,704]{1,0:T(8,128)(2,1)S(1)}, u32[]{:S(2)}, u32[]{:S(2)}) collective-permute-start(bf16[160,704]{1,0:T(8,128)(2,1)S(1)} %collective-permute-done.1.refs_2_), channel_id=1, source_target_pairs={{0,1},{1,0},{4,5},{5,4},{8,9},{9,8},{12,13},{13,12},{16,17},{17,16... | collective-permute-start | bytes 675848 | tf_op jit(solution)/shard_map/ppermute | solution.py:39
  20.6 7.4 %collective-permute-start.4 = (bf16[160,704]{1,0:T(8,128)(2,1)S(1)}, bf16[160,704]{1,0:T(8,128)(2,1)S(1)}, u32[]{:S(2)}, u32[]{:S(2)}) collective-permute-start(bf16[160,704]{1,0:T(8,128)(2,1)S(1)} %collective-permute-done.2.refs_4_), channel_id=1, source_target_pairs={{0,4},{1,29},{4,8},{5,1},{8,12},{9,5},{12,16},{13,9},{16,20},{17,1... | collective-permute-start | bytes 675848 | tf_op jit(solution)/shard_map/ppermute | solution.py:50
  20.6 7.4 %collective-permute-start.8 = (bf16[160,704]{1,0:T(8,128)(2,1)S(1)}, bf16[160,704]{1,0:T(8,128)(2,1)S(1)}, u32[]{:S(2)}, u32[]{:S(2)}) collective-permute-start(bf16[160,704]{1,0:T(8,128)(2,1)S(1)} %collective-permute-done.2.refs_4_), channel_id=1, source_target_pairs={{0,1},{1,0},{4,5},{5,4},{8,9},{9,8},{12,13},{13,12},{16,17},{17,16... | collective-permute-start | bytes 675848 | tf_op jit(solution)/shard_map/ppermute | solution.py:39
  28.0 7.2 %collective-permute-start.14 = (bf16[4,576,128]{2,1,0:T(8,128)(2,1)S(1)}, bf16[4,576,128]{2,1,0:T(8,128)(2,1)S(1)}, u32[]{:S(2)}, u32[]{:S(2)}) collective-permute-start(bf16[4,576,128]{2,1,0:T(8,128)(2,1)S(1)} %collective-permute-done.5.refs_11_.refs_7_), channel_id=1, source_target_pairs={{0,1},{1,0},{4,5},{5,4},{8,9},{9,8},{12,13},{13,12},{16,17},{17,16... | collective-permute-start | bytes 1769480 | tf_op jit(solution)/shard_map/ppermute | solution.py:39
  28.0 7.2 %collective-permute-start.15 = (bf16[4,576,128]{2,1,0:T(8,128)(2,1)S(1)}, bf16[4,576,128]{2,1,0:T(8,128)(2,1)S(1)}, u32[]{:S(2)}, u32[]{:S(2)}) collective-permute-start(bf16[4,576,128]{2,1,0:T(8,128)(2,1)S(1)} %collective-permute-done.6.refs_13_.refs_9_), channel_id=1, source_target_pairs={{0,1},{1,0},{4,5},{5,4},{8,9},{9,8},{12,13},{13,12},{16,17},{17,16... | collective-permute-start | bytes 1769480 | tf_op jit(solution)/shard_map/ppermute | solution.py:39
  28.5 6.7 %collective-permute-start.11 = (bf16[160,704]{1,0:T(8,128)(2,1)S(1)}, bf16[160,704]{1,0:T(8,128)(2,1)S(1)}, u32[]{:S(2)}, u32[]{:S(2)}) collective-permute-start(bf16[160,704]{1,0:T(8,128)(2,1)S(1)} %collective-permute-done.4.refs_6_), channel_id=1, source_target_pairs={{0,1},{1,0},{4,5},{5,4},{8,9},{9,8},{12,13},{13,12},{16,17},{17,16... | collective-permute-start | bytes 675848 | tf_op jit(solution)/shard_map/ppermute | solution.py:39
  28.5 10.6 %collective-permute-start.13 = (bf16[8,576,128]{2,1,0:T(8,128)(2,1)S(1)}, bf16[8,576,128]{2,1,0:T(8,128)(2,1)S(1)}, u32[]{:S(2)}, u32[]{:S(2)}) collective-permute-start(bf16[8,576,128]{2,1,0:T(8,128)(2,1)S(1)} %bitcast.25), channel_id=1, source_target_pairs={{0,1},{1,0},{4,5},{5,4},{8,9},{9,8},{12,13},{13,12},{16,17},{17,16... | collective-permute-start | bytes 3538952 | tf_op jit(solution)/shard_map/ppermute | solution.py:39
  29.0 6.2 %collective-permute-start.10 = (bf16[80,704]{1,0:T(8,128)(2,1)S(1)}, bf16[80,704]{1,0:T(8,128)(2,1)S(1)}, u32[]{:S(2)}, u32[]{:S(2)}) collective-permute-start(bf16[80,704]{1,0:T(8,128)(2,1)S(1)} %slice.55), channel_id=1, source_target_pairs={{0,4},{1,29},{4,8},{5,1},{8,12},{9,5},{12,16},{13,9},{16,20},{17,1... | collective-permute-start | bytes 337928 | tf_op jit(solution)/shard_map/ppermute | solution.py:50
  35.2 24.2 %collective-permute-start.16 = (bf16[64,128,128]{2,1,0:T(8,128)(2,1)S(1)}, bf16[64,128,128]{2,1,0:T(8,128)(2,1)S(1)}, u32[]{:S(2)}, u32[]{:S(2)}) collective-permute-start(bf16[64,128,128]{2,1,0:T(8,128)(2,1)S(1)} %bitcast.21), channel_id=1, source_target_pairs={{0,1},{1,0},{4,5},{5,4},{8,9},{9,8},{12,13},{13,12},{16,17},{17,16... | collective-permute-start | bytes 6291464 | tf_op jit(solution)/shard_map/ppermute | solution.py:39
  35.4 15.1 %collective-permute-start.9 = (bf16[320,704]{1,0:T(8,128)(2,1)S(1)}, bf16[320,704]{1,0:T(8,128)(2,1)S(1)}, u32[]{:S(2)}, u32[]{:S(2)}) collective-permute-start(bf16[320,704]{1,0:T(8,128)(2,1)S(1)} %pad_maximum_fusion), channel_id=1, source_target_pairs={{0,2},{1,3},{4,6},{5,7},{8,10},{9,11},{12,14},{13,15},{16,18},{17,... | collective-permute-start | bytes 1351688 | tf_op jit(solution)/shard_map/ppermute | solution.py:39
  37.3 13.4 %collective-permute-start.12 = (bf16[320,704]{1,0:T(8,128)(2,1)S(1)}, bf16[320,704]{1,0:T(8,128)(2,1)S(1)}, u32[]{:S(2)}, u32[]{:S(2)}) collective-permute-start(bf16[320,704]{1,0:T(8,128)(2,1)S(1)} %pad_maximum_fusion.1), channel_id=1, source_target_pairs={{0,130},{1,131},{4,134},{5,135},{8,138},{9,139},{12,142},{13,143},... | collective-permute-start | bytes 1351688 | tf_op jit(solution)/shard_map/ppermute | solution.py:39
  39.1 20.3 %collective-permute-start.17 = (f32[64,128]{1,0:T(8,128)S(1)}, f32[64,128]{1,0:T(8,128)S(1)}, u32[]{:S(2)}, u32[]{:S(2)}) collective-permute-start(f32[64,128]{1,0:T(8,128)S(1)} %bitcast.28), channel_id=1, source_target_pairs={{0,1},{1,0},{4,5},{5,4},{8,9},{9,8},{12,13},{13,12},{16,17},{17,16... | collective-permute-start | bytes 98312 | tf_op jit(solution)/shard_map/ppermute | solution.py:39
  64.6 5.1 %collective-permute-start.20 = (f32[2,16,256]{2,1,0:T(8,128)S(1)}, f32[2,16,256]{2,1,0:T(8,128)S(1)}, u32[]{:S(2)}, u32[]{:S(2)}) collective-permute-start(f32[2,16,256]{2,1,0:T(8,128)S(1)} %get-tuple-element.67), channel_id=1, source_target_pairs={{0,96},{1,97},{4,100},{5,101},{8,104},{9,105},{12,108},{13,109},{1... | collective-permute-start | bytes 98312 | tf_op jit(solution)/shard_map/ppermute | solution.py:39
  65.2 4.5 %collective-permute-start.19 = (f32[2,8,256]{2,1,0:T(8,128)S(1)}, f32[2,8,256]{2,1,0:T(8,128)S(1)}, u32[]{:S(2)}, u32[]{:S(2)}) collective-permute-start(f32[2,8,256]{2,1,0:T(8,128)S(1)} %get-tuple-element.66), channel_id=1, source_target_pairs={{0,32},{1,33},{4,36},{5,37},{8,40},{9,41},{12,44},{13,45},{16,48},... | collective-permute-start | bytes 49160 | tf_op jit(solution)/shard_map/ppermute | solution.py:39
  73.0 7.0 %collective-permute-start.21 = (bf16[336,256]{1,0:T(8,128)(2,1)S(1)}, bf16[336,256]{1,0:T(8,128)(2,1)S(1)}, u32[]{:S(2)}, u32[]{:S(2)}) collective-permute-start(bf16[336,256]{1,0:T(8,128)(2,1)S(1)} %get-tuple-element.69), channel_id=1, source_target_pairs={{0,64},{1,65},{4,68},{5,69},{8,72},{9,73},{12,76},{13,77},{16,80},... | collective-permute-start | bytes 516104 | tf_op jit(solution)/shard_map/ppermute | solution.py:39
  75.4 9.5 %collective-permute-start.22 = (bf16[336,256]{1,0:T(8,128)(2,1)S(1)}, bf16[336,256]{1,0:T(8,128)(2,1)S(1)}, u32[]{:S(2)}, u32[]{:S(2)}) collective-permute-start(bf16[336,256]{1,0:T(8,128)(2,1)S(1)} %get-tuple-element.70), channel_id=1, source_target_pairs={{0,128},{1,129},{4,132},{5,133},{8,136},{9,137},{12,140},{13,141},... | collective-permute-start | bytes 516104 | tf_op jit(solution)/shard_map/ppermute | solution.py:39
  78.3 9.3 %collective-permute-start.23 = (bf16[336,256]{1,0:T(8,128)(2,1)S(1)}, bf16[336,256]{1,0:T(8,128)(2,1)S(1)}, u32[]{:S(2)}, u32[]{:S(2)}) collective-permute-start(bf16[336,256]{1,0:T(8,128)(2,1)S(1)} %get-tuple-element.71), channel_id=1, source_target_pairs={{0,192},{1,193},{4,196},{5,197},{8,200},{9,201},{12,204},{13,205},... | collective-permute-start | bytes 516104 | tf_op jit(solution)/shard_map/ppermute | solution.py:39
  95.3 6.3 %collective-permute-start.24 = (f32[80,128]{1,0:T(8,128)S(1)}, f32[80,128]{1,0:T(8,128)S(1)}, u32[]{:S(2)}, u32[]{:S(2)}) collective-permute-start(f32[80,128]{1,0:T(8,128)S(1)} %get-tuple-element.74), channel_id=1, source_target_pairs={{0,1},{1,0},{4,5},{5,4},{8,9},{9,8},{12,13},{13,12},{16,17},{17,16... | collective-permute-start | bytes 122888 | tf_op jit(solution)/shard_map/ppermute | solution.py:39
  95.3 16.5 %all-to-all-start = ((bf16[16,32,128]{2,1,0:T(8,128)(2,1)}), bf16[16,32,128]{2,1,0:T(8,128)(2,1)S(1)}, u32[]{:S(2)}, u32[]{:S(2)}) async-start(bf16[16,32,128]{2,1,0:T(8,128)(2,1)} %get-tuple-element.72), calls=%async_computation | async-start | bytes 262144 | tf_op jit(solution)/shard_map/all_to_all | solution.py:538
  (5 other events, 49.9 us)

commit v10 on v7

--- a/solution.py
+++ b/solution.py
@@ -21,7 +21,8 @@
 INDEX_SCALE = DI ** (-0.5)
 ALL = ("yhi", "xh", "xp", "z", "ylo", "core")
 NEG = -jnp.inf
-VMEM = 18 << 20
+VMEM = 12 << 20
+HERE = pl.BlockSpec(memory_space=pltpu.VMEM)
 
 
 def flat(x, y, z, c):
@@ -115,9 +116,14 @@
 
     def work(now, last):
         for k in range(2):
-            own = jnp.concatenate([qa[k], qb[k]], axis=1)
-            left = jnp.concatenate([na[k], nb[k]], axis=1)
-            right = jnp.concatenate([ma[k], mb[k]], axis=1)
+            own, left, right = (
+                jnp.concatenate([a[at], b[at]], axis=1)
+                for a, b, at in (
+                    (qa, qb, 2 * jnp.minimum(step, 3) + k),
+                    (na, nb, 2 * jnp.clip(step - 4, 0, 1) + k),
+                    (ma, mb, 2 * jnp.clip(step - 6, 0, 1) + k),
+                )
+            )
             queries = jnp.where(step < 4, own, jnp.where(step < 6, left, right))
             top = jnp.max(tops[last, k], axis=0, keepdims=True)
             safe = jnp.where(top == NEG, 0.0, top)
@@ -148,25 +154,15 @@
 
 def score_call(meta, chunk, blocks, before, qa, qb, na, nb, ma, mb, pa, pb):
     spans = [b.shape[0] for b in blocks]
-    whole = lambda shape: pl.BlockSpec(shape, lambda h, meta: (0,) * len(shape))
-
-    def heads(start, count):
-        return pl.BlockSpec((2, DQ, 128), lambda h, meta: (jnp.clip(h - start, 0, count - 1), 0, 0))
-
     anywhere = pl.BlockSpec(memory_space=pl.ANY)
-    exps = pl.BlockSpec(memory_space=pltpu.VMEM)
     return pl.pallas_call(
         lambda *refs: score_kernel(chunk, spans, *refs),
         grid_spec=pltpu.PrefetchScalarGridSpec(
             num_scalar_prefetch=1,
             grid=(HEADS // 2 + 1,),
             in_specs=[anywhere] * len(blocks)
-            + ([exps, whole((ROWS, DI))] if chunk else [])
-            + [heads(0, 4)] * 2
-            + [heads(4, 2)] * 2
-            + [heads(6, 2)] * 2
-            + [whole((1, 128))] * 2,
-            out_specs=[exps, whole((HEADS, 256)), whole((HEADS, 256)), whole((ROWS, DI))],
+            + [HERE] * (len(before) + 8),
+            out_specs=[HERE] * 4,
             scratch_shapes=[
                 pltpu.VMEM((CHUNK, DI + DQ), jnp.bfloat16),
                 pltpu.VMEM((CHUNK, 256), jnp.float32),
@@ -235,16 +231,13 @@
 
 
 def head_sum_call(meta, exps, *stats):
-    piece = pl.BlockSpec(memory_space=pltpu.VMEM)
-    whole = lambda shape: pl.BlockSpec(shape, lambda i, meta: (0,) * len(shape))
-    out = pl.BlockSpec((ROWS + UNIT, 256), lambda i, meta: (0, 0))
     return pl.pallas_call(
         head_sum_kernel,
         grid_spec=pltpu.PrefetchScalarGridSpec(
             num_scalar_prefetch=1,
             grid=(BLOCKS,),
-            in_specs=[piece] + [whole(part.shape) for part in stats],
-            out_specs=[out] * 4,
+            in_specs=[HERE] * (1 + len(stats)),
+            out_specs=[HERE] * 4,
             scratch_shapes=[
                 pltpu.VMEM((HALF, 256), jnp.float32),
                 pltpu.VMEM((2, HEADS, 256), jnp.float32),
@@ -288,8 +281,9 @@
 
     total = logits[...]
     for j in range(JSTEP):
-        inner, _ = inner_of(keys, ia, ib, j)
-        weight = jnp.concatenate([wja[j : j + 1, :], wjb[j : j + 1, :]], axis=1)
+        at = step * JSTEP + j
+        inner, _ = inner_of(keys, ia, ib, at)
+        weight = jnp.concatenate([wja[pl.ds(at, 1), :], wjb[pl.ds(at, 1), :]], axis=1)
         total = total + weight * jnp.maximum(inner, 0.0)
     logits[...] = total
 
@@ -328,28 +322,22 @@
 def pair_call(ours, theirs):
     return pl.pallas_call(
         pair_kernel,
+        in_specs=[HERE] * 2,
+        out_specs=[HERE] * 3,
         out_shape=[pltpu.VMEM((2, rows, 256), jnp.float32) for rows in (24, 8, 16)],
         compiler_params=pltpu.CompilerParams(vmem_limit_bytes=1 << 20),
         name="pair_statistics",
     )(*in_vmem(ours, theirs))
 
 
-def j_specs():
-    whole = lambda shape: pl.BlockSpec(shape, lambda s, meta: (0,) * len(shape))
-    queries = pl.BlockSpec((JSTEP, 128, DI), lambda s, meta: (s, 0, 0))
-    weights = pl.BlockSpec((JSTEP, 128), lambda s, meta: (s, 0))
-    return whole, [queries, queries], [weights, weights]
-
-
 def forward_call(meta, keys, stats, ia, ib, pa, pb, wa, wb):
-    whole, queries, weights = j_specs()
     return pl.pallas_call(
         forward_kernel,
         grid_spec=pltpu.PrefetchScalarGridSpec(
             num_scalar_prefetch=1,
             grid=(NI // JSTEP,),
-            in_specs=[whole((ROWS, DI))] + [whole((HEADS, 256))] * 4 + queries + [whole((1, 128))] * 2 + weights,
-            out_specs=[whole((ROWS, 256)), whole((2, 24, 256)), whole((2, 24, 256))],
+            in_specs=[HERE] * 11,
+            out_specs=[HERE] * 3,
         ),
         out_shape=[
             pltpu.VMEM((ROWS, 256), jnp.float32),
@@ -403,11 +391,12 @@
     total = acc[...]
     slope = grad[...]
     for j in range(JSTEP):
-        inner, queries = inner_of(keys, ia, ib, j)
-        weight = jnp.concatenate([wja[j : j + 1, :], wjb[j : j + 1, :]], axis=1)
+        at = step * JSTEP + j
+        inner, queries = inner_of(keys, ia, ib, at)
+        weight = jnp.concatenate([wja[pl.ds(at, 1), :], wjb[pl.ds(at, 1), :]], axis=1)
         share = jnp.sum(slope * jnp.maximum(inner, 0.0), axis=0, keepdims=True)
-        rows_a[pl.ds(step * JSTEP + j, 1), :] = share[:, :128]
-        rows_b[pl.ds(step * JSTEP + j, 1), :] = share[:, 128:]
+        rows_a[pl.ds(at, 1), :] = share[:, :128]
+        rows_b[pl.ds(at, 1), :] = share[:, 128:]
         coeff = jnp.where(inner > 0, slope * weight, 0.0).astype(jnp.bfloat16)
         total = total + jnp.dot(coeff, queries, preferred_element_type=jnp.float32)
     acc[...] = total
@@ -423,24 +412,13 @@
 
 
 def backward_call(meta, keys, logits, target, ia, ib, wa, wb):
-    whole, queries, weights = j_specs()
     return pl.pallas_call(
         backward_kernel,
         grid_spec=pltpu.PrefetchScalarGridSpec(
             num_scalar_prefetch=1,
             grid=(NI // JSTEP,),
-            in_specs=[
-                whole((ROWS, DI)),
-                whole((ROWS, 256)),
-            ]
-            + [whole((ROWS + UNIT, 256))] * 4
-            + queries
-            + weights,
-            out_specs=[
-                whole((NI + 16, 128)),
-                whole((NI + 16, 128)),
-                whole((BLOCKS, 2 * UNIT, DI)),
-            ],
+            in_specs=[HERE] * 10,
+            out_specs=[HERE] * 3,
             scratch_shapes=[
                 pltpu.VMEM((ROWS, 256), jnp.float32),
                 pltpu.VMEM((ROWS, DI), jnp.float32),

time: 128 us -> 127 us (level)
  no operation moved by 1% of the time
where the time goes in v10:
time: 127 us
  waiting for transfers between devices  35.6 us (28%)
  starting transfers between devices  34.5 us (27%)
  Pallas kernels  33.4 us (26%)
  blocking collectives  14.4 us (11%)
  local copies, waits for them, and re-layouts  5.21 us (4%)
  other arithmetic  2.38 us (2%)
  between operations  1.53 us (1%)
    ppermute x24, starting transfers between devices, shift(): return lax.ppermute(value, ALL, pairs)  29.5 us
    ppermute x24, waiting for transfers between devices, shift(): return lax.ppermute(value, ALL, pairs)  25.4 us
    pallas_call x2, Pallas kernels, score_call(): pl.pallas_call(lambda *refs: score_kernel(chunk, spans, *refs), grid_spec...  18.5 us
    all_to_all x1, blocking collectives, gather_head(): return lax.all_to_all(wide, ('yhi', 'xh', 'xp'), 0, 0, tiled=True)  14.4 us
    all_to_all x1, waiting for transfers between devices, body(): kg = lax.all_to_all(kg, ('z', 'ylo'), 0, 0, tiled=True)  10.2 us
    pallas_call x1, Pallas kernels, backward_call(): pl.pallas_call(backward_kernel, grid_spec=pltpu.PrefetchScalarGridSpec(nu...  7.74 us
    all_to_all x1, starting transfers between devices, body(): kg = lax.all_to_all(kg, ('z', 'ylo'), 0, 0, tiled=True)  5 us
    pallas_call x1, Pallas kernels, forward_call(): pl.pallas_call(forward_kernel, grid_spec=pltpu.PrefetchScalarGridSpec(num...  3.84 us
  transfers between devices with their start and end apart: 25, of which 12 were waited for; matrix products, arithmetic and copies ran while one was open for 3% of the time, Pallas kernels for 15%

profile of v10, /device:TPU:2, one launch (start us, length us, event | category | flops | bytes accessed | tf_op | source)
XLA Modules:
  0.0 127.0 jit_solution(2307218762006315162)
XLA Ops:
  7.0 3.9 %collective-permute-start.1 = (bf16[80,704]{1,0:T(8,128)(2,1)S(1)}, bf16[80,704]{1,0:T(8,128)(2,1)S(1)}, u32[]{:S(2)}, u32[]{:S(2)}) collective-permute-start(bf16[80,704]{1,0:T(8,128)(2,1)S(1)} %fusion.refs_1_), channel_id=1, source_target_pairs={{0,28},{1,29},{4,0},{5,1},{8,4},{9,5},{12,8},{13,9},{16,12},{17,13... | collective-permute-start | bytes 337928 | tf_op jit(solution)/shard_map/ppermute | solution.py:40
  11.6 2.2 %collective-permute-done.refs_2_ = bf16[80,704]{1,0:T(8,128)(2,1)S(1)} collective-permute-done((bf16[80,704]{1,0:T(8,128)(2,1)S(1)}, bf16[80,704]{1,0:T(8,128)(2,1)S(1)}, u32[]{:S(2)}, u32[]{:S(2)}) %collective-permute-start) | collective-permute-done | bytes 112672 | tf_op jit(solution)/shard_map/ppermute | solution.py:40
  13.8 3.2 %collective-permute-start.3 = (bf16[80,704]{1,0:T(8,128)(2,1)S(1)}, bf16[80,704]{1,0:T(8,128)(2,1)S(1)}, u32[]{:S(2)}, u32[]{:S(2)}) collective-permute-start(bf16[80,704]{1,0:T(8,128)(2,1)S(1)} %collective-permute-done.1.refs_3_), channel_id=1, source_target_pairs={{0,28},{1,29},{4,0},{5,1},{8,4},{9,5},{12,8},{13,9},{16,12},{17,13... | collective-permute-start | bytes 337928 | tf_op jit(solution)/shard_map/ppermute | solution.py:40
  17.1 2.8 %collective-permute-done.2.refs_4_ = bf16[80,704]{1,0:T(8,128)(2,1)S(1)} collective-permute-done((bf16[80,704]{1,0:T(8,128)(2,1)S(1)}, bf16[80,704]{1,0:T(8,128)(2,1)S(1)}, u32[]{:S(2)}, u32[]{:S(2)}) %collective-permute-start.2) | collective-permute-done | bytes 112672 | tf_op jit(solution)/shard_map/ppermute | solution.py:40
  19.9 3.0 %collective-permute-start.5 = (bf16[80,704]{1,0:T(8,128)(2,1)S(1)}, bf16[80,704]{1,0:T(8,128)(2,1)S(1)}, u32[]{:S(2)}, u32[]{:S(2)}) collective-permute-start(bf16[80,704]{1,0:T(8,128)(2,1)S(1)} %collective-permute-done.2.refs_4_), channel_id=1, source_target_pairs={{0,4},{1,5},{4,8},{5,9},{8,12},{9,13},{12,16},{13,17},{16,20},{17,... | collective-permute-start | bytes 337928 | tf_op jit(solution)/shard_map/ppermute | solution.py:40
  23.4 3.0 %copy.16 = bf16[128,64,128]{2,0,1:T(8,128)(2,1)S(1)} copy(bf16[128,64,128]{2,1,0:T(8,128)(2,1)} %param.9) | data formatting | bytes 4194304 | tf_op args[2]
  28.4 2.0 %collective-permute-start.10 = (bf16[80,704]{1,0:T(8,128)(2,1)S(1)}, bf16[80,704]{1,0:T(8,128)(2,1)S(1)}, u32[]{:S(2)}, u32[]{:S(2)}) collective-permute-start(bf16[80,704]{1,0:T(8,128)(2,1)S(1)} %collective-permute-done.5.refs_6_), channel_id=1, source_target_pairs={{0,4},{1,5},{4,8},{5,9},{8,12},{9,13},{12,16},{13,17},{16,20},{17,... | collective-permute-start | bytes 337928 | tf_op jit(solution)/shard_map/ppermute | solution.py:40
  30.5 4.8 %collective-permute-done.10.refs_8_ = bf16[80,704]{1,0:T(8,128)(2,1)S(1)} collective-permute-done((bf16[80,704]{1,0:T(8,128)(2,1)S(1)}, bf16[80,704]{1,0:T(8,128)(2,1)S(1)}, u32[]{:S(2)}, u32[]{:S(2)}) %collective-permute-start.10) | collective-permute-done | bytes 112672 | tf_op jit(solution)/shard_map/ppermute | solution.py:40
  37.1 1.9 %collective-permute-start.11 = (bf16[320,704]{1,0:T(8,128)(2,1)S(1)}, bf16[320,704]{1,0:T(8,128)(2,1)S(1)}, u32[]{:S(2)}, u32[]{:S(2)}) collective-permute-start(bf16[320,704]{1,0:T(8,128)(2,1)S(1)} %pad_maximum_fusion.1), channel_id=1, source_target_pairs={{0,130},{1,131},{4,134},{5,135},{8,138},{9,139},{12,142},{13,143},... | collective-permute-start | bytes 1351688 | tf_op jit(solution)/shard_map/ppermute | solution.py:40
  39.0 9.7 %scores.2 = (bf16[16,1280,256]{2,1,0:T(8,128)(2,1)S(1)}, f32[16,256]{1,0:T(8,128)S(1)}, f32[16,256]{1,0:T(8,128)S(1)}, bf16[320,128]{1,0:T(8,128)(2,1)S(1)}) custom-call(s32[5]{0:T(128)S(1)} %stack.23.refs_0_.meta, bf16[80,704]{1,0:T(8,128)(2,1)S(1)} %fusion.refs_1_, bf16[80,704]{1,0:T(8,128)(2,1)S(1)} %collective-permute-done.refs_2_, ...), custom_call_target="tpu_custom_call" | custom-call | flops 6039797760 | bytes 5242880 | tf_op jit(solution)/shard_map/scores/pallas_call | solution.py:158
  50.7 8.8 %scores.3 = (bf16[16,1280,256]{2,1,0:T(8,128)(2,1)S(1)}, f32[16,256]{1,0:T(8,128)S(1)}, f32[16,256]{1,0:T(8,128)S(1)}, bf16[320,128]{1,0:T(8,128)(2,1)S(1)}) custom-call(s32[5]{0:T(128)S(1)} %stack.23.refs_0_.meta, bf16[320,704]{1,0:T(8,128)(2,1)S(1)} %collective-permute-done.4.refs_1_, ...), custom_call_target="tpu_custom_call", output_to_operand_aliasing={{0}: (3, {})} | custom-call | flops 6039797760 | bytes 5242880 | tf_op jit(solution)/shard_map/scores/pallas_call | solution.py:158
  59.6 3.8 %index_forward.1 = (f32[320,256]{1,0:T(8,128)S(1)}, f32[2,24,256]{2,1,0:T(8,128)S(1)}, f32[2,24,256]{2,1,0:T(8,128)S(1)}) custom-call(s32[5]{0:T(128)S(1)} %stack.23.refs_0_.meta, bf16[320,128]{1,0:T(8,128)(2,1)S(1)} %get-tuple-element.53.keys, f32[16,256]{1,0:T(8,128)S(1)} %get-tuple-element.54.m0, f32[16,256]{1,0:T(8,128)S(1)} %get-tuple-element.55.l0, ...), custom_call_target="tpu_custom_call" | custom-call | flops 1342177280 | bytes 5242880 | tf_op jit(solution)/shard_map/index_forward/pallas_call | solution.py:334
  64.8 1.8 %collective-permute-start.19 = (f32[2,16,256]{2,1,0:T(8,128)S(1)}, f32[2,16,256]{2,1,0:T(8,128)S(1)}, u32[]{:S(2)}, u32[]{:S(2)}) collective-permute-start(f32[2,16,256]{2,1,0:T(8,128)S(1)} %get-tuple-element.67), channel_id=1, source_target_pairs={{0,96},{1,97},{4,100},{5,101},{8,104},{9,105},{12,108},{13,109},{1... | collective-permute-start | bytes 98312 | tf_op jit(solution)/shard_map/ppermute | solution.py:40
  66.9 3.5 %collective-permute-done.18.up = f32[2,8,256]{2,1,0:T(8,128)S(1)} collective-permute-done((f32[2,8,256]{2,1,0:T(8,128)S(1)}, f32[2,8,256]{2,1,0:T(8,128)S(1)}, u32[]{:S(2)}, u32[]{:S(2)}) %collective-permute-start.18) | collective-permute-done | bytes 16416 | tf_op jit(solution)/shard_map/ppermute | solution.py:40
  70.3 3.3 %head_sum.1 = (bf16[336,256]{1,0:T(8,128)(2,1)S(1)}, bf16[336,256]{1,0:T(8,128)(2,1)S(1)}, bf16[336,256]{1,0:T(8,128)(2,1)S(1)}, bf16[336,256]{1,0:T(8,128)(2,1)S(1)}) custom-call(s32[5]{0:T(128)S(1)} %stack.23.refs_0_.meta, bf16[16,1280,256]{2,1,0:T(8,128)(2,1)S(1)} %get-tuple-element.62.e_ref, f32[16,256]{1,0:T(8,128)S(1)} %get-tuple-element.54.m0, ...), custom_call_target="tpu_custom_call" | custom-call | bytes 11534336 | tf_op jit(solution)/shard_map/head_sum/pallas_call | solution.py:234
  73.6 1.8 %collective-permute-start.20 = (bf16[336,256]{1,0:T(8,128)(2,1)S(1)}, bf16[336,256]{1,0:T(8,128)(2,1)S(1)}, u32[]{:S(2)}, u32[]{:S(2)}) collective-permute-start(bf16[336,256]{1,0:T(8,128)(2,1)S(1)} %get-tuple-element.69), channel_id=1, source_target_pairs={{0,64},{1,65},{4,68},{5,69},{8,72},{9,73},{12,76},{13,77},{16,80},... | collective-permute-start | bytes 516104 | tf_op jit(solution)/shard_map/ppermute | solution.py:40
  75.5 2.9 %collective-permute-start.21 = (bf16[336,256]{1,0:T(8,128)(2,1)S(1)}, bf16[336,256]{1,0:T(8,128)(2,1)S(1)}, u32[]{:S(2)}, u32[]{:S(2)}) collective-permute-start(bf16[336,256]{1,0:T(8,128)(2,1)S(1)} %get-tuple-element.70), channel_id=1, source_target_pairs={{0,128},{1,129},{4,132},{5,133},{8,136},{9,137},{12,140},{13,141},... | collective-permute-start | bytes 516104 | tf_op jit(solution)/shard_map/ppermute | solution.py:40
  78.4 1.8 %collective-permute-start.22 = (bf16[336,256]{1,0:T(8,128)(2,1)S(1)}, bf16[336,256]{1,0:T(8,128)(2,1)S(1)}, u32[]{:S(2)}, u32[]{:S(2)}) collective-permute-start(bf16[336,256]{1,0:T(8,128)(2,1)S(1)} %get-tuple-element.71), channel_id=1, source_target_pairs={{0,192},{1,193},{4,196},{5,197},{8,200},{9,201},{12,204},{13,205},... | collective-permute-start | bytes 516104 | tf_op jit(solution)/shard_map/ppermute | solution.py:40
  80.6 4.4 %collective-permute-done.21.t2 = bf16[336,256]{1,0:T(8,128)(2,1)S(1)} collective-permute-done((bf16[336,256]{1,0:T(8,128)(2,1)S(1)}, bf16[336,256]{1,0:T(8,128)(2,1)S(1)}, u32[]{:S(2)}, u32[]{:S(2)}) %collective-permute-start.21) | collective-permute-done | bytes 172064 | tf_op jit(solution)/shard_map/ppermute | solution.py:40
  85.0 2.7 %collective-permute-done.22.t3 = bf16[336,256]{1,0:T(8,128)(2,1)S(1)} collective-permute-done((bf16[336,256]{1,0:T(8,128)(2,1)S(1)}, bf16[336,256]{1,0:T(8,128)(2,1)S(1)}, u32[]{:S(2)}, u32[]{:S(2)}) %collective-permute-start.22) | collective-permute-done | bytes 172064 | tf_op jit(solution)/shard_map/ppermute | solution.py:40
  87.7 7.7 %index_backward.1 = (f32[80,128]{1,0:T(8,128)S(1)}, f32[80,128]{1,0:T(8,128)S(1)}, bf16[16,32,128]{2,1,0:T(8,128)(2,1)}) custom-call(s32[5]{0:T(128)S(1)} %stack.23.refs_0_.meta, bf16[320,128]{1,0:T(8,128)(2,1)S(1)} %get-tuple-element.53.keys, f32[320,256]{1,0:T(8,128)S(1)} %get-tuple-element.61.logits, bf16[336,256]{1,0:T(8,128)(2,1)S(1)} %get-tuple-element.68.t0, ...), custom_call_target="tpu_custom_call" | custom-call | flops 2684354560 | bytes 6291456 | tf_op jit(solution)/shard_map/index_backward/pallas_call | solution.py:415
  95.4 5.0 %all-to-all-start = ((bf16[16,32,128]{2,1,0:T(8,128)(2,1)}), bf16[16,32,128]{2,1,0:T(8,128)(2,1)S(1)}, u32[]{:S(2)}, u32[]{:S(2)}) async-start(bf16[16,32,128]{2,1,0:T(8,128)(2,1)} %get-tuple-element.72), calls=%async_computation | async-start | bytes 262144 | tf_op jit(solution)/shard_map/all_to_all | solution.py:497
  100.5 10.2 %all-to-all-done = bf16[16,32,128]{2,1,0:T(8,128)(2,1)S(1)} async-done(((bf16[16,32,128]{2,1,0:T(8,128)(2,1)}), bf16[16,32,128]{2,1,0:T(8,128)(2,1)S(1)}, u32[]{:S(2)}, u32[]{:S(2)}) %all-to-all-start) | async-done | bytes 131104 | tf_op jit(solution)/shard_map/all_to_all | solution.py:497
  110.7 14.4 %all_to_all.10 = bf16[8,112,128]{2,1,0:T(8,128)(2,1)S(1)} all-to-all(bf16[8,112,128]{2,1,0:T(8,128)(2,1)S(1)} %broadcast_in_dim.2), channel_id=1, replica_groups=mesh['yhi'=2,'xh'=2,'xp'=2,'z'=8,'ylo'=2,'core'=2] {'yhi','xh','xp'}, dimensions={0} | all-to-all | bytes 458752 | tf_op jit(solution)/shard_map/all_to_all | solution.py:442
  (62 shorter events, 16.5 us)
Async XLA Ops:
  3.0 24.8 %collective-permute-start.7 = (bf16[4,576,128]{2,1,0:T(8,128)(2,1)S(1)}, bf16[4,576,128]{2,1,0:T(8,128)(2,1)S(1)}, u32[]{:S(2)}, u32[]{:S(2)}) collective-permute-start(bf16[4,576,128]{2,1,0:T(8,128)(2,1)S(1)} %get-tuple-element.78), channel_id=1, source_target_pairs={{0,32},{1,33},{4,36},{5,37},{8,40},{9,41},{12,44},{13,45},{16,48},... | collective-permute-start | bytes 1769480 | tf_op jit(solution)/shard_map/ppermute | solution.py:40
  4.6 23.3 %collective-permute-start.8 = (bf16[4,576,128]{2,1,0:T(8,128)(2,1)S(1)}, bf16[4,576,128]{2,1,0:T(8,128)(2,1)S(1)}, u32[]{:S(2)}, u32[]{:S(2)}) collective-permute-start(bf16[4,576,128]{2,1,0:T(8,128)(2,1)S(1)} %get-tuple-element.77), channel_id=1, source_target_pairs={{0,96},{1,97},{4,100},{5,101},{8,104},{9,105},{12,108},{13,109},{1... | collective-permute-start | bytes 1769480 | tf_op jit(solution)/shard_map/ppermute | solution.py:40
  5.4 8.4 %collective-permute-start = (bf16[80,704]{1,0:T(8,128)(2,1)S(1)}, bf16[80,704]{1,0:T(8,128)(2,1)S(1)}, u32[]{:S(2)}, u32[]{:S(2)}) collective-permute-start(bf16[80,704]{1,0:T(8,128)(2,1)S(1)} %fusion.refs_1_), channel_id=1, source_target_pairs={{0,4},{1,5},{4,8},{5,9},{8,12},{9,13},{12,16},{13,17},{16,20},{17,... | collective-permute-start | bytes 337928 | tf_op jit(solution)/shard_map/ppermute | solution.py:40
  7.0 6.8 %collective-permute-start.1 = (bf16[80,704]{1,0:T(8,128)(2,1)S(1)}, bf16[80,704]{1,0:T(8,128)(2,1)S(1)}, u32[]{:S(2)}, u32[]{:S(2)}) collective-permute-start(bf16[80,704]{1,0:T(8,128)(2,1)S(1)} %fusion.refs_1_), channel_id=1, source_target_pairs={{0,28},{1,29},{4,0},{5,1},{8,4},{9,5},{12,8},{13,9},{16,12},{17,13... | collective-permute-start | bytes 337928 | tf_op jit(solution)/shard_map/ppermute | solution.py:40
  13.8 6.1 %collective-permute-start.2 = (bf16[80,704]{1,0:T(8,128)(2,1)S(1)}, bf16[80,704]{1,0:T(8,128)(2,1)S(1)}, u32[]{:S(2)}, u32[]{:S(2)}) collective-permute-start(bf16[80,704]{1,0:T(8,128)(2,1)S(1)} %collective-permute-done.refs_2_), channel_id=1, source_target_pairs={{0,4},{1,5},{4,8},{5,9},{8,12},{9,13},{12,16},{13,17},{16,20},{17,... | collective-permute-start | bytes 337928 | tf_op jit(solution)/shard_map/ppermute | solution.py:40
  13.8 6.1 %collective-permute-start.3 = (bf16[80,704]{1,0:T(8,128)(2,1)S(1)}, bf16[80,704]{1,0:T(8,128)(2,1)S(1)}, u32[]{:S(2)}, u32[]{:S(2)}) collective-permute-start(bf16[80,704]{1,0:T(8,128)(2,1)S(1)} %collective-permute-done.1.refs_3_), channel_id=1, source_target_pairs={{0,28},{1,29},{4,0},{5,1},{8,4},{9,5},{12,8},{13,9},{16,12},{17,13... | collective-permute-start | bytes 337928 | tf_op jit(solution)/shard_map/ppermute | solution.py:40
  19.9 6.5 %collective-permute-start.5 = (bf16[80,704]{1,0:T(8,128)(2,1)S(1)}, bf16[80,704]{1,0:T(8,128)(2,1)S(1)}, u32[]{:S(2)}, u32[]{:S(2)}) collective-permute-start(bf16[80,704]{1,0:T(8,128)(2,1)S(1)} %collective-permute-done.2.refs_4_), channel_id=1, source_target_pairs={{0,4},{1,5},{4,8},{5,9},{8,12},{9,13},{12,16},{13,17},{16,20},{17,... | collective-permute-start | bytes 337928 | tf_op jit(solution)/shard_map/ppermute | solution.py:40
  22.9 4.9 %collective-permute-start.6 = (bf16[80,704]{1,0:T(8,128)(2,1)S(1)}, bf16[80,704]{1,0:T(8,128)(2,1)S(1)}, u32[]{:S(2)}, u32[]{:S(2)}) collective-permute-start(bf16[80,704]{1,0:T(8,128)(2,1)S(1)} %collective-permute-done.3.refs_5_), channel_id=1, source_target_pairs={{0,28},{1,29},{4,0},{5,1},{8,4},{9,5},{12,8},{13,9},{16,12},{17,13... | collective-permute-start | bytes 337928 | tf_op jit(solution)/shard_map/ppermute | solution.py:40
  23.3 3.1 %collective-permute-start.9 = (f32[1,128]{1,0:T(1,128)S(1)}, f32[1,128]{1,0:T(1,128)S(1)}, u32[]{:S(2)}, u32[]{:S(2)}) collective-permute-start(f32[1,128]{1,0:T(1,128)S(1)} %convert_element_type.17.refs_15_.refs_11_.pa), channel_id=1, source_target_pairs={{0,1},{1,0},{4,5},{5,4},{8,9},{9,8},{12,13},{13,12},{16,17},{17,16... | collective-permute-start | bytes 1544 | tf_op jit(solution)/shard_map/ppermute | solution.py:40
  27.8 7.5 %collective-permute-start.13 = (bf16[4,576,128]{2,1,0:T(8,128)(2,1)S(1)}, bf16[4,576,128]{2,1,0:T(8,128)(2,1)S(1)}, u32[]{:S(2)}, u32[]{:S(2)}) collective-permute-start(bf16[4,576,128]{2,1,0:T(8,128)(2,1)S(1)} %collective-permute-done.7.refs_11_.refs_7_), channel_id=1, source_target_pairs={{0,1},{1,0},{4,5},{5,4},{8,9},{9,8},{12,13},{13,12},{16,17},{17,16... | collective-permute-start | bytes 1769480 | tf_op jit(solution)/shard_map/ppermute | solution.py:40
  27.8 7.5 %collective-permute-start.14 = (bf16[4,576,128]{2,1,0:T(8,128)(2,1)S(1)}, bf16[4,576,128]{2,1,0:T(8,128)(2,1)S(1)}, u32[]{:S(2)}, u32[]{:S(2)}) collective-permute-start(bf16[4,576,128]{2,1,0:T(8,128)(2,1)S(1)} %collective-permute-done.8.refs_13_.refs_9_), channel_id=1, source_target_pairs={{0,1},{1,0},{4,5},{5,4},{8,9},{9,8},{12,13},{13,12},{16,17},{17,16... | collective-permute-start | bytes 1769480 | tf_op jit(solution)/shard_map/ppermute | solution.py:40
  28.3 10.7 %collective-permute-start.12 = (bf16[8,576,128]{2,1,0:T(8,128)(2,1)S(1)}, bf16[8,576,128]{2,1,0:T(8,128)(2,1)S(1)}, u32[]{:S(2)}, u32[]{:S(2)}) collective-permute-start(bf16[8,576,128]{2,1,0:T(8,128)(2,1)S(1)} %bitcast.25), channel_id=1, source_target_pairs={{0,1},{1,0},{4,5},{5,4},{8,9},{9,8},{12,13},{13,12},{16,17},{17,16... | collective-permute-start | bytes 3538952 | tf_op jit(solution)/shard_map/ppermute | solution.py:40
  28.4 6.9 %collective-permute-start.10 = (bf16[80,704]{1,0:T(8,128)(2,1)S(1)}, bf16[80,704]{1,0:T(8,128)(2,1)S(1)}, u32[]{:S(2)}, u32[]{:S(2)}) collective-permute-start(bf16[80,704]{1,0:T(8,128)(2,1)S(1)} %collective-permute-done.5.refs_6_), channel_id=1, source_target_pairs={{0,4},{1,5},{4,8},{5,9},{8,12},{9,13},{12,16},{13,17},{16,20},{17,... | collective-permute-start | bytes 337928 | tf_op jit(solution)/shard_map/ppermute | solution.py:40
  35.3 24.2 %collective-permute-start.15 = (bf16[64,128,128]{2,1,0:T(8,128)(2,1)S(1)}, bf16[64,128,128]{2,1,0:T(8,128)(2,1)S(1)}, u32[]{:S(2)}, u32[]{:S(2)}) collective-permute-start(bf16[64,128,128]{2,1,0:T(8,128)(2,1)S(1)} %bitcast.21), channel_id=1, source_target_pairs={{0,1},{1,0},{4,5},{5,4},{8,9},{9,8},{12,13},{13,12},{16,17},{17,16... | collective-permute-start | bytes 6291464 | tf_op jit(solution)/shard_map/ppermute | solution.py:40
  35.4 15.0 %collective-permute-start.4 = (bf16[320,704]{1,0:T(8,128)(2,1)S(1)}, bf16[320,704]{1,0:T(8,128)(2,1)S(1)}, u32[]{:S(2)}, u32[]{:S(2)}) collective-permute-start(bf16[320,704]{1,0:T(8,128)(2,1)S(1)} %pad_maximum_fusion), channel_id=1, source_target_pairs={{0,2},{1,3},{4,6},{5,7},{8,10},{9,11},{12,14},{13,15},{16,18},{17,... | collective-permute-start | bytes 1351688 | tf_op jit(solution)/shard_map/ppermute | solution.py:40
  37.1 13.6 %collective-permute-start.11 = (bf16[320,704]{1,0:T(8,128)(2,1)S(1)}, bf16[320,704]{1,0:T(8,128)(2,1)S(1)}, u32[]{:S(2)}, u32[]{:S(2)}) collective-permute-start(bf16[320,704]{1,0:T(8,128)(2,1)S(1)} %pad_maximum_fusion.1), channel_id=1, source_target_pairs={{0,130},{1,131},{4,134},{5,135},{8,138},{9,139},{12,142},{13,143},... | collective-permute-start | bytes 1351688 | tf_op jit(solution)/shard_map/ppermute | solution.py:40
  39.0 20.5 %collective-permute-start.16 = (f32[64,128]{1,0:T(8,128)S(1)}, f32[64,128]{1,0:T(8,128)S(1)}, u32[]{:S(2)}, u32[]{:S(2)}) collective-permute-start(f32[64,128]{1,0:T(8,128)S(1)} %bitcast.28), channel_id=1, source_target_pairs={{0,1},{1,0},{4,5},{5,4},{8,9},{9,8},{12,13},{13,12},{16,17},{17,16... | collective-permute-start | bytes 98312 | tf_op jit(solution)/shard_map/ppermute | solution.py:40
  64.8 5.6 %collective-permute-start.19 = (f32[2,16,256]{2,1,0:T(8,128)S(1)}, f32[2,16,256]{2,1,0:T(8,128)S(1)}, u32[]{:S(2)}, u32[]{:S(2)}) collective-permute-start(f32[2,16,256]{2,1,0:T(8,128)S(1)} %get-tuple-element.67), channel_id=1, source_target_pairs={{0,96},{1,97},{4,100},{5,101},{8,104},{9,105},{12,108},{13,109},{1... | collective-permute-start | bytes 98312 | tf_op jit(solution)/shard_map/ppermute | solution.py:40
  66.6 3.7 %collective-permute-start.18 = (f32[2,8,256]{2,1,0:T(8,128)S(1)}, f32[2,8,256]{2,1,0:T(8,128)S(1)}, u32[]{:S(2)}, u32[]{:S(2)}) collective-permute-start(f32[2,8,256]{2,1,0:T(8,128)S(1)} %get-tuple-element.66), channel_id=1, source_target_pairs={{0,32},{1,33},{4,36},{5,37},{8,40},{9,41},{12,44},{13,45},{16,48},... | collective-permute-start | bytes 49160 | tf_op jit(solution)/shard_map/ppermute | solution.py:40
  73.6 7.0 %collective-permute-start.20 = (bf16[336,256]{1,0:T(8,128)(2,1)S(1)}, bf16[336,256]{1,0:T(8,128)(2,1)S(1)}, u32[]{:S(2)}, u32[]{:S(2)}) collective-permute-start(bf16[336,256]{1,0:T(8,128)(2,1)S(1)} %get-tuple-element.69), channel_id=1, source_target_pairs={{0,64},{1,65},{4,68},{5,69},{8,72},{9,73},{12,76},{13,77},{16,80},... | collective-permute-start | bytes 516104 | tf_op jit(solution)/shard_map/ppermute | solution.py:40
  75.5 9.5 %collective-permute-start.21 = (bf16[336,256]{1,0:T(8,128)(2,1)S(1)}, bf16[336,256]{1,0:T(8,128)(2,1)S(1)}, u32[]{:S(2)}, u32[]{:S(2)}) collective-permute-start(bf16[336,256]{1,0:T(8,128)(2,1)S(1)} %get-tuple-element.70), channel_id=1, source_target_pairs={{0,128},{1,129},{4,132},{5,133},{8,136},{9,137},{12,140},{13,141},... | collective-permute-start | bytes 516104 | tf_op jit(solution)/shard_map/ppermute | solution.py:40
  78.4 9.3 %collective-permute-start.22 = (bf16[336,256]{1,0:T(8,128)(2,1)S(1)}, bf16[336,256]{1,0:T(8,128)(2,1)S(1)}, u32[]{:S(2)}, u32[]{:S(2)}) collective-permute-start(bf16[336,256]{1,0:T(8,128)(2,1)S(1)} %get-tuple-element.71), channel_id=1, source_target_pairs={{0,192},{1,193},{4,196},{5,197},{8,200},{9,201},{12,204},{13,205},... | collective-permute-start | bytes 516104 | tf_op jit(solution)/shard_map/ppermute | solution.py:40
  95.4 5.0 %collective-permute-start.23 = (f32[80,128]{1,0:T(8,128)S(1)}, f32[80,128]{1,0:T(8,128)S(1)}, u32[]{:S(2)}, u32[]{:S(2)}) collective-permute-start(f32[80,128]{1,0:T(8,128)S(1)} %get-tuple-element.74), channel_id=1, source_target_pairs={{0,1},{1,0},{4,5},{5,4},{8,9},{9,8},{12,13},{13,12},{16,17},{17,16... | collective-permute-start | bytes 122888 | tf_op jit(solution)/shard_map/ppermute | solution.py:40
  95.4 15.2 %all-to-all-start = ((bf16[16,32,128]{2,1,0:T(8,128)(2,1)}), bf16[16,32,128]{2,1,0:T(8,128)(2,1)S(1)}, u32[]{:S(2)}, u32[]{:S(2)}) async-start(bf16[16,32,128]{2,1,0:T(8,128)(2,1)} %get-tuple-element.72), calls=%async_computation | async-start | bytes 262144 | tf_op jit(solution)/shard_map/all_to_all | solution.py:497
  (4 other events, 38.5 us)

commit v11 on v10

--- a/solution.py
+++ b/solution.py
@@ -394,10 +394,11 @@
         at = step * JSTEP + j
         inner, queries = inner_of(keys, ia, ib, at)
         weight = jnp.concatenate([wja[pl.ds(at, 1), :], wjb[pl.ds(at, 1), :]], axis=1)
-        share = jnp.sum(slope * jnp.maximum(inner, 0.0), axis=0, keepdims=True)
+        open_slope = jnp.where(inner > 0, slope, 0.0)
+        share = jnp.sum(open_slope * inner, axis=0, keepdims=True)
         rows_a[pl.ds(at, 1), :] = share[:, :128]
         rows_b[pl.ds(at, 1), :] = share[:, 128:]
-        coeff = jnp.where(inner > 0, slope * weight, 0.0).astype(jnp.bfloat16)
+        coeff = (open_slope * weight).astype(jnp.bfloat16)
         total = total + jnp.dot(coeff, queries, preferred_element_type=jnp.float32)
     acc[...] = total
 
@@ -437,9 +438,45 @@
     )(meta, *in_vmem(keys, logits, *target, ia, ib, wa, wb))
 
 
-def gather_head(value):
-    wide = jnp.broadcast_to(value[None], (8,) + value.shape)
-    return lax.all_to_all(wide, ("yhi", "xh", "xp"), 0, 0, tiled=True)
+PART = 7 * UNIT
+
+
+def finish_kernel(meta, p0, p1, p2, p3, div, weight, key, held):
+    quarter = meta[4]
+    for r, pair in enumerate((p0, p1, p2, p3)):
+        held[r] = pair[...]
+    x, yhi = (quarter & 1) * 2 + meta[3], quarter >> 1
+    rows = jnp.zeros((PART - 2 * UNIT, 128), jnp.float32)
+    rest = [jnp.zeros((UNIT, DI), jnp.float32)] * 2
+    for y in range(2):
+        for k in range(4):
+            at = pl.ds(pl.multiple_of((yhi ^ y) * PART, UNIT), PART)
+            part = held[(x - k) & 3, at, :].astype(jnp.float32)
+            rows = rows + part[2 * UNIT :]
+            half = k & 1
+            first = half * HALF + (y * 2 + (k >> 1)) * UNIT
+            key[first : first + UNIT, :] = part[0:UNIT]
+            rest[half] = rest[half] + part[UNIT : 2 * UNIT]
+    for half in range(2):
+        key[half * HALF + 4 * UNIT : (half + 1) * HALF, :] = rest[half]
+    weight[...] = rows[0:NI]
+    div[...] = rows[NI : NI + 1] + rows[NI + 8 : NI + 9]
+
+
+def finish_call(meta, *pairs):
+    return pl.pallas_call(
+        finish_kernel,
+        grid_spec=pltpu.PrefetchScalarGridSpec(
+            num_scalar_prefetch=1,
+            grid=(1,),
+            in_specs=[HERE] * 4,
+            out_specs=[HERE] * 3,
+            scratch_shapes=[pltpu.VMEM((4, 2 * PART, 128), jnp.bfloat16)],
+        ),
+        out_shape=[jax.ShapeDtypeStruct((rows, 128), jnp.float32) for rows in (1, NI, 2 * HALF)],
+        compiler_params=pltpu.CompilerParams(vmem_limit_bytes=2 << 20),
+        name="finish",
+    )(meta, *in_vmem(*pairs))
 
 
 def after(value, *others):
@@ -496,13 +533,10 @@
     tail = rows_high + low
     kg = lax.all_to_all(kg, ("z", "ylo"), 0, 0, tiled=True)
     kg = jnp.sum(kg.astype(jnp.float32), axis=0)
-    last = gather_head(jnp.concatenate([kg, tail]).astype(jnp.bfloat16)).astype(jnp.float32)
-    rows_sum = jnp.sum(last[:, 2 * UNIT :], axis=0)
-    pieces = last[:, : 2 * UNIT].reshape(4, 2, 2 * UNIT, DI)
-    main = pieces[:, :, :UNIT].transpose(1, 0, 2, 3).reshape(2, 4 * UNIT, DI)
-    extra = jnp.sum(pieces[:, :, UNIT:], axis=0)
-    key_grad = jnp.concatenate([main, extra], axis=1).reshape(160, DI)
-    return rows_sum[NI] + rows_sum[NI + 8], rows_sum[:NI].T, key_grad
+    part = jnp.concatenate([kg, tail]).astype(jnp.bfloat16)
+    pair = jnp.concatenate([part, shift(part, dy=2)])
+    div, weight, key_grad = finish_call(meta, pair, *(shift(pair, dx=dx) for dx in (1, 2, 3)))
+    return div.reshape(128), weight.T, key_grad
 
 
 def solution(mesh):

time: 127 us -> 127 us (level)
  blocking collectives: 14.4 us -> 0 us
  waiting for transfers between devices: 35.6 us -> 43 us
  starting transfers between devices: 34.5 us -> 41.1 us
  Pallas kernels: 33.4 us -> 34.9 us
    all_to_all x1 -> x0, blocking collectives: 14.4 us -> none  [gather_head(): return lax.all_to_all(wide, ('yhi', 'xh', 'xp'), 0, 0, tiled=True)]
    ppermute x24 -> x28, waiting for transfers between devices: 25.4 us -> 32.9 us  [shift(): return lax.ppermute(value, ALL, pairs)]
    ppermute x24 -> x28, starting transfers between devices: 29.5 us -> 36.1 us  [shift(): return lax.ppermute(value, ALL, pairs)]
  transfers between devices with their start and end apart: 25 -> 29, of which waited for: 12 -> 15; matrix products, arithmetic and copies ran while one was open for 3% -> 3% of each run, Pallas kernels for 15% -> 15%
where the time goes in v11:
time: 127 us; the launch traced here: 126 us
  waiting for transfers between devices  43 us (34%)
  starting transfers between devices  41.1 us (32%)
  Pallas kernels  34.9 us (27%)
  local copies, waits for them, and re-layouts  4.54 us (4%)
  between operations  1.5 us (1%)
    ppermute x28, starting transfers between devices, shift(): return lax.ppermute(value, ALL, pairs)  36.1 us
    ppermute x28, waiting for transfers between devices, shift(): return lax.ppermute(value, ALL, pairs)  32.9 us
    pallas_call x2, Pallas kernels, score_call(): pl.pallas_call(lambda *refs: score_kernel(chunk, spans, *refs), grid_spec...  18.5 us
    all_to_all x1, waiting for transfers between devices, body(): kg = lax.all_to_all(kg, ('z', 'ylo'), 0, 0, tiled=True)  10.2 us
    pallas_call x1, Pallas kernels, backward_call(): pl.pallas_call(backward_kernel, grid_spec=pltpu.PrefetchScalarGridSpec(nu...  7.95 us
    all_to_all x1, starting transfers between devices, body(): kg = lax.all_to_all(kg, ('z', 'ylo'), 0, 0, tiled=True)  5 us
    pallas_call x1, Pallas kernels, forward_call(): pl.pallas_call(forward_kernel, grid_spec=pltpu.PrefetchScalarGridSpec(num...  3.84 us
    pallas_call x1, Pallas kernels, head_sum_call(): pl.pallas_call(head_sum_kernel, grid_spec=pltpu.PrefetchScalarGridSpec(nu...  3.29 us
  transfers between devices with their start and end apart: 29, of which 15 were waited for; matrix products, arithmetic and copies ran while one was open for 3% of the time, Pallas kernels for 15%

profile of v11, /device:TPU:2, one launch (start us, length us, event | category | flops | bytes accessed | tf_op | source)
XLA Modules:
  0.0 126.2 jit_solution(16350476521125554197)
XLA Ops:
  7.0 3.9 %collective-permute-start.1 = (bf16[80,704]{1,0:T(8,128)(2,1)S(1)}, bf16[80,704]{1,0:T(8,128)(2,1)S(1)}, u32[]{:S(2)}, u32[]{:S(2)}) collective-permute-start(bf16[80,704]{1,0:T(8,128)(2,1)S(1)} %fusion.refs_1_), channel_id=1, source_target_pairs={{0,28},{1,29},{4,0},{5,1},{8,4},{9,5},{12,8},{13,9},{16,12},{17,13... | collective-permute-start | bytes 337928 | tf_op jit(solution)/shard_map/ppermute | solution.py:40
  11.6 2.2 %collective-permute-done.refs_2_ = bf16[80,704]{1,0:T(8,128)(2,1)S(1)} collective-permute-done((bf16[80,704]{1,0:T(8,128)(2,1)S(1)}, bf16[80,704]{1,0:T(8,128)(2,1)S(1)}, u32[]{:S(2)}, u32[]{:S(2)}) %collective-permute-start) | collective-permute-done | bytes 112672 | tf_op jit(solution)/shard_map/ppermute | solution.py:40
  13.8 3.2 %collective-permute-start.3 = (bf16[80,704]{1,0:T(8,128)(2,1)S(1)}, bf16[80,704]{1,0:T(8,128)(2,1)S(1)}, u32[]{:S(2)}, u32[]{:S(2)}) collective-permute-start(bf16[80,704]{1,0:T(8,128)(2,1)S(1)} %collective-permute-done.1.refs_3_), channel_id=1, source_target_pairs={{0,28},{1,29},{4,0},{5,1},{8,4},{9,5},{12,8},{13,9},{16,12},{17,13... | collective-permute-start | bytes 337928 | tf_op jit(solution)/shard_map/ppermute | solution.py:40
  17.1 2.8 %collective-permute-done.2.refs_4_ = bf16[80,704]{1,0:T(8,128)(2,1)S(1)} collective-permute-done((bf16[80,704]{1,0:T(8,128)(2,1)S(1)}, bf16[80,704]{1,0:T(8,128)(2,1)S(1)}, u32[]{:S(2)}, u32[]{:S(2)}) %collective-permute-start.2) | collective-permute-done | bytes 112672 | tf_op jit(solution)/shard_map/ppermute | solution.py:40
  19.9 3.0 %collective-permute-start.5 = (bf16[80,704]{1,0:T(8,128)(2,1)S(1)}, bf16[80,704]{1,0:T(8,128)(2,1)S(1)}, u32[]{:S(2)}, u32[]{:S(2)}) collective-permute-start(bf16[80,704]{1,0:T(8,128)(2,1)S(1)} %collective-permute-done.2.refs_4_), channel_id=1, source_target_pairs={{0,4},{1,5},{4,8},{5,9},{8,12},{9,13},{12,16},{13,17},{16,20},{17,... | collective-permute-start | bytes 337928 | tf_op jit(solution)/shard_map/ppermute | solution.py:40
  23.4 3.0 %copy.13 = bf16[128,64,128]{2,0,1:T(8,128)(2,1)S(1)} copy(bf16[128,64,128]{2,1,0:T(8,128)(2,1)} %param.9) | data formatting | bytes 4194304 | tf_op args[2]
  28.4 2.0 %collective-permute-start.10 = (bf16[80,704]{1,0:T(8,128)(2,1)S(1)}, bf16[80,704]{1,0:T(8,128)(2,1)S(1)}, u32[]{:S(2)}, u32[]{:S(2)}) collective-permute-start(bf16[80,704]{1,0:T(8,128)(2,1)S(1)} %collective-permute-done.5.refs_6_), channel_id=1, source_target_pairs={{0,4},{1,5},{4,8},{5,9},{8,12},{9,13},{12,16},{13,17},{16,20},{17,... | collective-permute-start | bytes 337928 | tf_op jit(solution)/shard_map/ppermute | solution.py:40
  30.5 4.8 %collective-permute-done.10.refs_8_ = bf16[80,704]{1,0:T(8,128)(2,1)S(1)} collective-permute-done((bf16[80,704]{1,0:T(8,128)(2,1)S(1)}, bf16[80,704]{1,0:T(8,128)(2,1)S(1)}, u32[]{:S(2)}, u32[]{:S(2)}) %collective-permute-start.10) | collective-permute-done | bytes 112672 | tf_op jit(solution)/shard_map/ppermute | solution.py:40
  37.1 1.9 %collective-permute-start.11 = (bf16[320,704]{1,0:T(8,128)(2,1)S(1)}, bf16[320,704]{1,0:T(8,128)(2,1)S(1)}, u32[]{:S(2)}, u32[]{:S(2)}) collective-permute-start(bf16[320,704]{1,0:T(8,128)(2,1)S(1)} %pad_maximum_fusion.1), channel_id=1, source_target_pairs={{0,130},{1,131},{4,134},{5,135},{8,138},{9,139},{12,142},{13,143},... | collective-permute-start | bytes 1351688 | tf_op jit(solution)/shard_map/ppermute | solution.py:40
  39.0 9.7 %scores.2 = (bf16[16,1280,256]{2,1,0:T(8,128)(2,1)S(1)}, f32[16,256]{1,0:T(8,128)S(1)}, f32[16,256]{1,0:T(8,128)S(1)}, bf16[320,128]{1,0:T(8,128)(2,1)S(1)}) custom-call(s32[5]{0:T(128)S(1)} %stack.23.refs_0_.meta, bf16[80,704]{1,0:T(8,128)(2,1)S(1)} %fusion.refs_1_, bf16[80,704]{1,0:T(8,128)(2,1)S(1)} %collective-permute-done.refs_2_, ...), custom_call_target="tpu_custom_call" | custom-call | flops 6039797760 | bytes 5242880 | tf_op jit(solution)/shard_map/scores/pallas_call | solution.py:158
  50.7 8.8 %scores.3 = (bf16[16,1280,256]{2,1,0:T(8,128)(2,1)S(1)}, f32[16,256]{1,0:T(8,128)S(1)}, f32[16,256]{1,0:T(8,128)S(1)}, bf16[320,128]{1,0:T(8,128)(2,1)S(1)}) custom-call(s32[5]{0:T(128)S(1)} %stack.23.refs_0_.meta, bf16[320,704]{1,0:T(8,128)(2,1)S(1)} %collective-permute-done.4.refs_1_, ...), custom_call_target="tpu_custom_call", output_to_operand_aliasing={{0}: (3, {})} | custom-call | flops 6039797760 | bytes 5242880 | tf_op jit(solution)/shard_map/scores/pallas_call | solution.py:158
  59.6 3.8 %index_forward.1 = (f32[320,256]{1,0:T(8,128)S(1)}, f32[2,24,256]{2,1,0:T(8,128)S(1)}, f32[2,24,256]{2,1,0:T(8,128)S(1)}) custom-call(s32[5]{0:T(128)S(1)} %stack.23.refs_0_.meta, bf16[320,128]{1,0:T(8,128)(2,1)S(1)} %get-tuple-element.56.keys, f32[16,256]{1,0:T(8,128)S(1)} %get-tuple-element.57.m0, f32[16,256]{1,0:T(8,128)S(1)} %get-tuple-element.58.l0, ...), custom_call_target="tpu_custom_call" | custom-call | flops 1342177280 | bytes 5242880 | tf_op jit(solution)/shard_map/index_forward/pallas_call | solution.py:334
  66.9 3.5 %collective-permute-done.18.up = f32[2,8,256]{2,1,0:T(8,128)S(1)} collective-permute-done((f32[2,8,256]{2,1,0:T(8,128)S(1)}, f32[2,8,256]{2,1,0:T(8,128)S(1)}, u32[]{:S(2)}, u32[]{:S(2)}) %collective-permute-start.18) | collective-permute-done | bytes 16416 | tf_op jit(solution)/shard_map/ppermute | solution.py:40
  70.3 3.3 %head_sum.1 = (bf16[336,256]{1,0:T(8,128)(2,1)S(1)}, bf16[336,256]{1,0:T(8,128)(2,1)S(1)}, bf16[336,256]{1,0:T(8,128)(2,1)S(1)}, bf16[336,256]{1,0:T(8,128)(2,1)S(1)}) custom-call(s32[5]{0:T(128)S(1)} %stack.23.refs_0_.meta, bf16[16,1280,256]{2,1,0:T(8,128)(2,1)S(1)} %get-tuple-element.65.e_ref, f32[16,256]{1,0:T(8,128)S(1)} %get-tuple-element.57.m0, ...), custom_call_target="tpu_custom_call" | custom-call | bytes 11534336 | tf_op jit(solution)/shard_map/head_sum/pallas_call | solution.py:234
  75.5 2.9 %collective-permute-start.21 = (bf16[336,256]{1,0:T(8,128)(2,1)S(1)}, bf16[336,256]{1,0:T(8,128)(2,1)S(1)}, u32[]{:S(2)}, u32[]{:S(2)}) collective-permute-start(bf16[336,256]{1,0:T(8,128)(2,1)S(1)} %get-tuple-element.73), channel_id=1, source_target_pairs={{0,128},{1,129},{4,132},{5,133},{8,136},{9,137},{12,140},{13,141},... | collective-permute-start | bytes 516104 | tf_op jit(solution)/shard_map/ppermute | solution.py:40
  80.6 4.4 %collective-permute-done.21.t2 = bf16[336,256]{1,0:T(8,128)(2,1)S(1)} collective-permute-done((bf16[336,256]{1,0:T(8,128)(2,1)S(1)}, bf16[336,256]{1,0:T(8,128)(2,1)S(1)}, u32[]{:S(2)}, u32[]{:S(2)}) %collective-permute-start.21) | collective-permute-done | bytes 172064 | tf_op jit(solution)/shard_map/ppermute | solution.py:40
  85.0 2.7 %collective-permute-done.22.t3 = bf16[336,256]{1,0:T(8,128)(2,1)S(1)} collective-permute-done((bf16[336,256]{1,0:T(8,128)(2,1)S(1)}, bf16[336,256]{1,0:T(8,128)(2,1)S(1)}, u32[]{:S(2)}, u32[]{:S(2)}) %collective-permute-start.22) | collective-permute-done | bytes 172064 | tf_op jit(solution)/shard_map/ppermute | solution.py:40
  87.7 7.9 %index_backward.1 = (f32[80,128]{1,0:T(8,128)S(1)}, f32[80,128]{1,0:T(8,128)S(1)}, bf16[16,32,128]{2,1,0:T(8,128)(2,1)}) custom-call(s32[5]{0:T(128)S(1)} %stack.23.refs_0_.meta, bf16[320,128]{1,0:T(8,128)(2,1)S(1)} %get-tuple-element.56.keys, f32[320,256]{1,0:T(8,128)S(1)} %get-tuple-element.64.logits, bf16[336,256]{1,0:T(8,128)(2,1)S(1)} %get-tuple-element.71.t0, ...), custom_call_target="tpu_custom_call" | custom-call | flops 2684354560 | bytes 6291456 | tf_op jit(solution)/shard_map/index_backward/pallas_call | solution.py:416
  95.6 5.0 %all-to-all-start = ((bf16[16,32,128]{2,1,0:T(8,128)(2,1)}), bf16[16,32,128]{2,1,0:T(8,128)(2,1)S(1)}, u32[]{:S(2)}, u32[]{:S(2)}) async-start(bf16[16,32,128]{2,1,0:T(8,128)(2,1)} %get-tuple-element.75), calls=%async_computation | async-start | bytes 262144 | tf_op jit(solution)/shard_map/all_to_all | solution.py:534
  100.7 10.2 %all-to-all-done = bf16[16,32,128]{2,1,0:T(8,128)(2,1)S(1)} async-done(((bf16[16,32,128]{2,1,0:T(8,128)(2,1)}), bf16[16,32,128]{2,1,0:T(8,128)(2,1)S(1)}, u32[]{:S(2)}, u32[]{:S(2)}) %all-to-all-start) | async-done | bytes 131104 | tf_op jit(solution)/shard_map/all_to_all | solution.py:534
  110.9 2.0 %collective-permute-start.24 = (bf16[112,128]{1,0:T(8,128)(2,1)S(1)}, bf16[112,128]{1,0:T(8,128)(2,1)S(1)}, u32[]{:S(2)}, u32[]{:S(2)}) collective-permute-start(bf16[112,128]{1,0:T(8,128)(2,1)S(1)} %pad_maximum_fusion.3), channel_id=1, source_target_pairs={{0,128},{1,129},{4,132},{5,133},{8,136},{9,137},{12,140},{13,141},... | collective-permute-start | bytes 86024 | tf_op jit(solution)/shard_map/ppermute | solution.py:40
  112.9 3.5 %collective-permute-done.24 = bf16[112,128]{1,0:T(8,128)(2,1)S(1)} collective-permute-done((bf16[112,128]{1,0:T(8,128)(2,1)S(1)}, bf16[112,128]{1,0:T(8,128)(2,1)S(1)}, u32[]{:S(2)}, u32[]{:S(2)}) %collective-permute-start.24) | collective-permute-done | bytes 28704 | tf_op jit(solution)/shard_map/ppermute | solution.py:40
  116.4 2.5 %collective-permute-start.25 = (bf16[224,128]{1,0:T(8,128)(2,1)S(1)}, bf16[224,128]{1,0:T(8,128)(2,1)S(1)}, u32[]{:S(2)}, u32[]{:S(2)}) collective-permute-start(bf16[224,128]{1,0:T(8,128)(2,1)S(1)} %pad_maximum_fusion.2.p0), channel_id=1, source_target_pairs={{0,32},{1,33},{4,36},{5,37},{8,40},{9,41},{12,44},{13,45},{16,48},... | collective-permute-start | bytes 172040 | tf_op jit(solution)/shard_map/ppermute | solution.py:40
  121.0 3.6 %collective-permute-done.26.p2 = bf16[224,128]{1,0:T(8,128)(2,1)S(1)} collective-permute-done((bf16[224,128]{1,0:T(8,128)(2,1)S(1)}, bf16[224,128]{1,0:T(8,128)(2,1)S(1)}, u32[]{:S(2)}, u32[]{:S(2)}) %collective-permute-start.26) | collective-permute-done | bytes 57376 | tf_op jit(solution)/shard_map/ppermute | solution.py:40
  (62 shorter events, 23.9 us)
Async XLA Ops:
  3.0 24.8 %collective-permute-start.7 = (bf16[4,576,128]{2,1,0:T(8,128)(2,1)S(1)}, bf16[4,576,128]{2,1,0:T(8,128)(2,1)S(1)}, u32[]{:S(2)}, u32[]{:S(2)}) collective-permute-start(bf16[4,576,128]{2,1,0:T(8,128)(2,1)S(1)} %get-tuple-element.84), channel_id=1, source_target_pairs={{0,32},{1,33},{4,36},{5,37},{8,40},{9,41},{12,44},{13,45},{16,48},... | collective-permute-start | bytes 1769480 | tf_op jit(solution)/shard_map/ppermute | solution.py:40
  4.6 23.3 %collective-permute-start.8 = (bf16[4,576,128]{2,1,0:T(8,128)(2,1)S(1)}, bf16[4,576,128]{2,1,0:T(8,128)(2,1)S(1)}, u32[]{:S(2)}, u32[]{:S(2)}) collective-permute-start(bf16[4,576,128]{2,1,0:T(8,128)(2,1)S(1)} %get-tuple-element.83), channel_id=1, source_target_pairs={{0,96},{1,97},{4,100},{5,101},{8,104},{9,105},{12,108},{13,109},{1... | collective-permute-start | bytes 1769480 | tf_op jit(solution)/shard_map/ppermute | solution.py:40
  5.4 8.4 %collective-permute-start = (bf16[80,704]{1,0:T(8,128)(2,1)S(1)}, bf16[80,704]{1,0:T(8,128)(2,1)S(1)}, u32[]{:S(2)}, u32[]{:S(2)}) collective-permute-start(bf16[80,704]{1,0:T(8,128)(2,1)S(1)} %fusion.refs_1_), channel_id=1, source_target_pairs={{0,4},{1,5},{4,8},{5,9},{8,12},{9,13},{12,16},{13,17},{16,20},{17,... | collective-permute-start | bytes 337928 | tf_op jit(solution)/shard_map/ppermute | solution.py:40
  7.0 6.8 %collective-permute-start.1 = (bf16[80,704]{1,0:T(8,128)(2,1)S(1)}, bf16[80,704]{1,0:T(8,128)(2,1)S(1)}, u32[]{:S(2)}, u32[]{:S(2)}) collective-permute-start(bf16[80,704]{1,0:T(8,128)(2,1)S(1)} %fusion.refs_1_), channel_id=1, source_target_pairs={{0,28},{1,29},{4,0},{5,1},{8,4},{9,5},{12,8},{13,9},{16,12},{17,13... | collective-permute-start | bytes 337928 | tf_op jit(solution)/shard_map/ppermute | solution.py:40
  13.8 6.1 %collective-permute-start.2 = (bf16[80,704]{1,0:T(8,128)(2,1)S(1)}, bf16[80,704]{1,0:T(8,128)(2,1)S(1)}, u32[]{:S(2)}, u32[]{:S(2)}) collective-permute-start(bf16[80,704]{1,0:T(8,128)(2,1)S(1)} %collective-permute-done.refs_2_), channel_id=1, source_target_pairs={{0,4},{1,5},{4,8},{5,9},{8,12},{9,13},{12,16},{13,17},{16,20},{17,... | collective-permute-start | bytes 337928 | tf_op jit(solution)/shard_map/ppermute | solution.py:40
  13.8 6.1 %collective-permute-start.3 = (bf16[80,704]{1,0:T(8,128)(2,1)S(1)}, bf16[80,704]{1,0:T(8,128)(2,1)S(1)}, u32[]{:S(2)}, u32[]{:S(2)}) collective-permute-start(bf16[80,704]{1,0:T(8,128)(2,1)S(1)} %collective-permute-done.1.refs_3_), channel_id=1, source_target_pairs={{0,28},{1,29},{4,0},{5,1},{8,4},{9,5},{12,8},{13,9},{16,12},{17,13... | collective-permute-start | bytes 337928 | tf_op jit(solution)/shard_map/ppermute | solution.py:40
  19.9 6.5 %collective-permute-start.5 = (bf16[80,704]{1,0:T(8,128)(2,1)S(1)}, bf16[80,704]{1,0:T(8,128)(2,1)S(1)}, u32[]{:S(2)}, u32[]{:S(2)}) collective-permute-start(bf16[80,704]{1,0:T(8,128)(2,1)S(1)} %collective-permute-done.2.refs_4_), channel_id=1, source_target_pairs={{0,4},{1,5},{4,8},{5,9},{8,12},{9,13},{12,16},{13,17},{16,20},{17,... | collective-permute-start | bytes 337928 | tf_op jit(solution)/shard_map/ppermute | solution.py:40
  22.9 4.9 %collective-permute-start.6 = (bf16[80,704]{1,0:T(8,128)(2,1)S(1)}, bf16[80,704]{1,0:T(8,128)(2,1)S(1)}, u32[]{:S(2)}, u32[]{:S(2)}) collective-permute-start(bf16[80,704]{1,0:T(8,128)(2,1)S(1)} %collective-permute-done.3.refs_5_), channel_id=1, source_target_pairs={{0,28},{1,29},{4,0},{5,1},{8,4},{9,5},{12,8},{13,9},{16,12},{17,13... | collective-permute-start | bytes 337928 | tf_op jit(solution)/shard_map/ppermute | solution.py:40
  27.8 7.5 %collective-permute-start.13 = (bf16[4,576,128]{2,1,0:T(8,128)(2,1)S(1)}, bf16[4,576,128]{2,1,0:T(8,128)(2,1)S(1)}, u32[]{:S(2)}, u32[]{:S(2)}) collective-permute-start(bf16[4,576,128]{2,1,0:T(8,128)(2,1)S(1)} %collective-permute-done.7.refs_11_.refs_7_), channel_id=1, source_target_pairs={{0,1},{1,0},{4,5},{5,4},{8,9},{9,8},{12,13},{13,12},{16,17},{17,16... | collective-permute-start | bytes 1769480 | tf_op jit(solution)/shard_map/ppermute | solution.py:40
  27.8 7.5 %collective-permute-start.14 = (bf16[4,576,128]{2,1,0:T(8,128)(2,1)S(1)}, bf16[4,576,128]{2,1,0:T(8,128)(2,1)S(1)}, u32[]{:S(2)}, u32[]{:S(2)}) collective-permute-start(bf16[4,576,128]{2,1,0:T(8,128)(2,1)S(1)} %collective-permute-done.8.refs_13_.refs_9_), channel_id=1, source_target_pairs={{0,1},{1,0},{4,5},{5,4},{8,9},{9,8},{12,13},{13,12},{16,17},{17,16... | collective-permute-start | bytes 1769480 | tf_op jit(solution)/shard_map/ppermute | solution.py:40
  28.3 10.7 %collective-permute-start.12 = (bf16[8,576,128]{2,1,0:T(8,128)(2,1)S(1)}, bf16[8,576,128]{2,1,0:T(8,128)(2,1)S(1)}, u32[]{:S(2)}, u32[]{:S(2)}) collective-permute-start(bf16[8,576,128]{2,1,0:T(8,128)(2,1)S(1)} %bitcast.18), channel_id=1, source_target_pairs={{0,1},{1,0},{4,5},{5,4},{8,9},{9,8},{12,13},{13,12},{16,17},{17,16... | collective-permute-start | bytes 3538952 | tf_op jit(solution)/shard_map/ppermute | solution.py:40
  28.4 6.9 %collective-permute-start.10 = (bf16[80,704]{1,0:T(8,128)(2,1)S(1)}, bf16[80,704]{1,0:T(8,128)(2,1)S(1)}, u32[]{:S(2)}, u32[]{:S(2)}) collective-permute-start(bf16[80,704]{1,0:T(8,128)(2,1)S(1)} %collective-permute-done.5.refs_6_), channel_id=1, source_target_pairs={{0,4},{1,5},{4,8},{5,9},{8,12},{9,13},{12,16},{13,17},{16,20},{17,... | collective-permute-start | bytes 337928 | tf_op jit(solution)/shard_map/ppermute | solution.py:40
  35.3 24.2 %collective-permute-start.15 = (bf16[64,128,128]{2,1,0:T(8,128)(2,1)S(1)}, bf16[64,128,128]{2,1,0:T(8,128)(2,1)S(1)}, u32[]{:S(2)}, u32[]{:S(2)}) collective-permute-start(bf16[64,128,128]{2,1,0:T(8,128)(2,1)S(1)} %bitcast.14), channel_id=1, source_target_pairs={{0,1},{1,0},{4,5},{5,4},{8,9},{9,8},{12,13},{13,12},{16,17},{17,16... | collective-permute-start | bytes 6291464 | tf_op jit(solution)/shard_map/ppermute | solution.py:40
  35.4 15.0 %collective-permute-start.4 = (bf16[320,704]{1,0:T(8,128)(2,1)S(1)}, bf16[320,704]{1,0:T(8,128)(2,1)S(1)}, u32[]{:S(2)}, u32[]{:S(2)}) collective-permute-start(bf16[320,704]{1,0:T(8,128)(2,1)S(1)} %pad_maximum_fusion), channel_id=1, source_target_pairs={{0,2},{1,3},{4,6},{5,7},{8,10},{9,11},{12,14},{13,15},{16,18},{17,... | collective-permute-start | bytes 1351688 | tf_op jit(solution)/shard_map/ppermute | solution.py:40
  37.1 13.6 %collective-permute-start.11 = (bf16[320,704]{1,0:T(8,128)(2,1)S(1)}, bf16[320,704]{1,0:T(8,128)(2,1)S(1)}, u32[]{:S(2)}, u32[]{:S(2)}) collective-permute-start(bf16[320,704]{1,0:T(8,128)(2,1)S(1)} %pad_maximum_fusion.1), channel_id=1, source_target_pairs={{0,130},{1,131},{4,134},{5,135},{8,138},{9,139},{12,142},{13,143},... | collective-permute-start | bytes 1351688 | tf_op jit(solution)/shard_map/ppermute | solution.py:40
  39.0 20.5 %collective-permute-start.16 = (f32[64,128]{1,0:T(8,128)S(1)}, f32[64,128]{1,0:T(8,128)S(1)}, u32[]{:S(2)}, u32[]{:S(2)}) collective-permute-start(f32[64,128]{1,0:T(8,128)S(1)} %bitcast.21), channel_id=1, source_target_pairs={{0,1},{1,0},{4,5},{5,4},{8,9},{9,8},{12,13},{13,12},{16,17},{17,16... | collective-permute-start | bytes 98312 | tf_op jit(solution)/shard_map/ppermute | solution.py:40
  64.8 5.6 %collective-permute-start.19 = (f32[2,16,256]{2,1,0:T(8,128)S(1)}, f32[2,16,256]{2,1,0:T(8,128)S(1)}, u32[]{:S(2)}, u32[]{:S(2)}) collective-permute-start(f32[2,16,256]{2,1,0:T(8,128)S(1)} %get-tuple-element.70), channel_id=1, source_target_pairs={{0,96},{1,97},{4,100},{5,101},{8,104},{9,105},{12,108},{13,109},{1... | collective-permute-start | bytes 98312 | tf_op jit(solution)/shard_map/ppermute | solution.py:40
  73.6 7.0 %collective-permute-start.20 = (bf16[336,256]{1,0:T(8,128)(2,1)S(1)}, bf16[336,256]{1,0:T(8,128)(2,1)S(1)}, u32[]{:S(2)}, u32[]{:S(2)}) collective-permute-start(bf16[336,256]{1,0:T(8,128)(2,1)S(1)} %get-tuple-element.72), channel_id=1, source_target_pairs={{0,64},{1,65},{4,68},{5,69},{8,72},{9,73},{12,76},{13,77},{16,80},... | collective-permute-start | bytes 516104 | tf_op jit(solution)/shard_map/ppermute | solution.py:40
  75.5 9.5 %collective-permute-start.21 = (bf16[336,256]{1,0:T(8,128)(2,1)S(1)}, bf16[336,256]{1,0:T(8,128)(2,1)S(1)}, u32[]{:S(2)}, u32[]{:S(2)}) collective-permute-start(bf16[336,256]{1,0:T(8,128)(2,1)S(1)} %get-tuple-element.73), channel_id=1, source_target_pairs={{0,128},{1,129},{4,132},{5,133},{8,136},{9,137},{12,140},{13,141},... | collective-permute-start | bytes 516104 | tf_op jit(solution)/shard_map/ppermute | solution.py:40
  78.4 9.3 %collective-permute-start.22 = (bf16[336,256]{1,0:T(8,128)(2,1)S(1)}, bf16[336,256]{1,0:T(8,128)(2,1)S(1)}, u32[]{:S(2)}, u32[]{:S(2)}) collective-permute-start(bf16[336,256]{1,0:T(8,128)(2,1)S(1)} %get-tuple-element.74), channel_id=1, source_target_pairs={{0,192},{1,193},{4,196},{5,197},{8,200},{9,201},{12,204},{13,205},... | collective-permute-start | bytes 516104 | tf_op jit(solution)/shard_map/ppermute | solution.py:40
  95.6 5.0 %collective-permute-start.23 = (f32[80,128]{1,0:T(8,128)S(1)}, f32[80,128]{1,0:T(8,128)S(1)}, u32[]{:S(2)}, u32[]{:S(2)}) collective-permute-start(f32[80,128]{1,0:T(8,128)S(1)} %get-tuple-element.77), channel_id=1, source_target_pairs={{0,1},{1,0},{4,5},{5,4},{8,9},{9,8},{12,13},{13,12},{16,17},{17,16... | collective-permute-start | bytes 122888 | tf_op jit(solution)/shard_map/ppermute | solution.py:40
  95.6 15.2 %all-to-all-start = ((bf16[16,32,128]{2,1,0:T(8,128)(2,1)}), bf16[16,32,128]{2,1,0:T(8,128)(2,1)S(1)}, u32[]{:S(2)}, u32[]{:S(2)}) async-start(bf16[16,32,128]{2,1,0:T(8,128)(2,1)} %get-tuple-element.75), calls=%async_computation | async-start | bytes 262144 | tf_op jit(solution)/shard_map/all_to_all | solution.py:534
  110.9 5.5 %collective-permute-start.24 = (bf16[112,128]{1,0:T(8,128)(2,1)S(1)}, bf16[112,128]{1,0:T(8,128)(2,1)S(1)}, u32[]{:S(2)}, u32[]{:S(2)}) collective-permute-start(bf16[112,128]{1,0:T(8,128)(2,1)S(1)} %pad_maximum_fusion.3), channel_id=1, source_target_pairs={{0,128},{1,129},{4,132},{5,133},{8,136},{9,137},{12,140},{13,141},... | collective-permute-start | bytes 86024 | tf_op jit(solution)/shard_map/ppermute | solution.py:40
  118.8 5.8 %collective-permute-start.26 = (bf16[224,128]{1,0:T(8,128)(2,1)S(1)}, bf16[224,128]{1,0:T(8,128)(2,1)S(1)}, u32[]{:S(2)}, u32[]{:S(2)}) collective-permute-start(bf16[224,128]{1,0:T(8,128)(2,1)S(1)} %pad_maximum_fusion.2.p0), channel_id=1, source_target_pairs={{0,64},{1,65},{4,68},{5,69},{8,72},{9,73},{12,76},{13,77},{16,80},... | collective-permute-start | bytes 172040 | tf_op jit(solution)/shard_map/ppermute | solution.py:40
  (8 other events, 54.7 us)

commit v12 on v11

--- a/solution.py
+++ b/solution.py
@@ -499,9 +499,8 @@
     queries = main_queries.transpose(0, 2, 1)
     f1, b1 = shift(own, dz=1), shift(own, dz=7)
     queries_far = swap_core(queries)
-    halves = after(queries, own)
-    left, right = shift(halves[:4], dx=1), shift(halves[4:], dx=3)
-    f1, b1 = lax.optimization_barrier((f1, b1))
+    f1, b1, left, right = lax.optimization_barrier((f1, b1, queries[:4], queries[4:]))
+    left, right = shift(left, dx=1), shift(right, dx=3)
     f2, b2 = shift(f1, dz=1), shift(b1, dz=7)
     f2, b2 = lax.optimization_barrier((f2, b2))
     f3, b3 = shift(f2, dz=1), shift(b2, dz=7)

time: 127 us -> 127 us (level)
  transfers between devices with their start and end apart: 29 -> 29, of which waited for: 15 -> 15; matrix products, arithmetic and copies ran while one was open for 3% -> 4% of each run, Pallas kernels for 15% -> 15%
where the time goes in v12:
time: 127 us; the launch traced here: 126 us
  waiting for transfers between devices  42.3 us (33%)
  starting transfers between devices  41.5 us (33%)
  Pallas kernels  34.8 us (27%)
  local copies, waits for them, and re-layouts  4.54 us (4%)
  between operations  1.51 us (1%)
    ppermute x28, starting transfers between devices, shift(): return lax.ppermute(value, ALL, pairs)  36.2 us
    ppermute x28, waiting for transfers between devices, shift(): return lax.ppermute(value, ALL, pairs)  32.1 us
    pallas_call x2, Pallas kernels, score_call(): pl.pallas_call(lambda *refs: score_kernel(chunk, spans, *refs), grid_spec...  18.5 us
    all_to_all x1, waiting for transfers between devices, body(): kg = lax.all_to_all(kg, ('z', 'ylo'), 0, 0, tiled=True)  10.2 us
    pallas_call x1, Pallas kernels, backward_call(): pl.pallas_call(backward_kernel, grid_spec=pltpu.PrefetchScalarGridSpec(nu...  7.89 us
    all_to_all x1, starting transfers between devices, body(): kg = lax.all_to_all(kg, ('z', 'ylo'), 0, 0, tiled=True)  5.3 us
    pallas_call x1, Pallas kernels, forward_call(): pl.pallas_call(forward_kernel, grid_spec=pltpu.PrefetchScalarGridSpec(num...  3.86 us
    pallas_call x1, Pallas kernels, head_sum_call(): pl.pallas_call(head_sum_kernel, grid_spec=pltpu.PrefetchScalarGridSpec(nu...  3.29 us
  transfers between devices with their start and end apart: 29, of which 15 were waited for; matrix products, arithmetic and copies ran while one was open for 4% of the time, Pallas kernels for 15%

profile of v12, /device:TPU:2, one launch (start us, length us, event | category | flops | bytes accessed | tf_op | source)
XLA Modules:
  0.0 125.8 jit_solution(5620810536051174603)
XLA Ops:
  1.7 1.9 %collective-permute-start = (bf16[80,704]{1,0:T(8,128)(2,1)S(1)}, bf16[80,704]{1,0:T(8,128)(2,1)S(1)}, u32[]{:S(2)}, u32[]{:S(2)}) collective-permute-start(bf16[80,704]{1,0:T(8,128)(2,1)S(1)} %fusion.refs_1_), channel_id=1, source_target_pairs={{0,4},{1,5},{4,8},{5,9},{8,12},{9,13},{12,16},{13,17},{16,20},{17,... | collective-permute-start | bytes 337928 | tf_op jit(solution)/shard_map/ppermute | solution.py:40
  3.6 4.0 %collective-permute-start.1 = (bf16[80,704]{1,0:T(8,128)(2,1)S(1)}, bf16[80,704]{1,0:T(8,128)(2,1)S(1)}, u32[]{:S(2)}, u32[]{:S(2)}) collective-permute-start(bf16[80,704]{1,0:T(8,128)(2,1)S(1)} %fusion.refs_1_), channel_id=1, source_target_pairs={{0,28},{1,29},{4,0},{5,1},{8,4},{9,5},{12,8},{13,9},{16,12},{17,13... | collective-permute-start | bytes 337928 | tf_op jit(solution)/shard_map/ppermute | solution.py:40
  13.6 3.2 %collective-permute-start.3 = (bf16[80,704]{1,0:T(8,128)(2,1)S(1)}, bf16[80,704]{1,0:T(8,128)(2,1)S(1)}, u32[]{:S(2)}, u32[]{:S(2)}) collective-permute-start(bf16[80,704]{1,0:T(8,128)(2,1)S(1)} %collective-permute-done.1.refs_3_), channel_id=1, source_target_pairs={{0,28},{1,29},{4,0},{5,1},{8,4},{9,5},{12,8},{13,9},{16,12},{17,13... | collective-permute-start | bytes 337928 | tf_op jit(solution)/shard_map/ppermute | solution.py:40
  16.9 2.8 %collective-permute-done.2.refs_4_ = bf16[80,704]{1,0:T(8,128)(2,1)S(1)} collective-permute-done((bf16[80,704]{1,0:T(8,128)(2,1)S(1)}, bf16[80,704]{1,0:T(8,128)(2,1)S(1)}, u32[]{:S(2)}, u32[]{:S(2)}) %collective-permute-start.2) | collective-permute-done | bytes 112672 | tf_op jit(solution)/shard_map/ppermute | solution.py:40
  19.7 2.6 %collective-permute-start.5 = (bf16[80,704]{1,0:T(8,128)(2,1)S(1)}, bf16[80,704]{1,0:T(8,128)(2,1)S(1)}, u32[]{:S(2)}, u32[]{:S(2)}) collective-permute-start(bf16[80,704]{1,0:T(8,128)(2,1)S(1)} %collective-permute-done.2.refs_4_), channel_id=1, source_target_pairs={{0,4},{1,5},{4,8},{5,9},{8,12},{9,13},{12,16},{13,17},{16,20},{17,... | collective-permute-start | bytes 337928 | tf_op jit(solution)/shard_map/ppermute | solution.py:40
  23.2 3.0 %copy.13 = bf16[128,64,128]{2,0,1:T(8,128)(2,1)S(1)} copy(bf16[128,64,128]{2,1,0:T(8,128)(2,1)} %param.9) | data formatting | bytes 4194304 | tf_op args[2]
  27.8 2.0 %collective-permute-start.10 = (bf16[80,704]{1,0:T(8,128)(2,1)S(1)}, bf16[80,704]{1,0:T(8,128)(2,1)S(1)}, u32[]{:S(2)}, u32[]{:S(2)}) collective-permute-start(bf16[80,704]{1,0:T(8,128)(2,1)S(1)} %collective-permute-done.5.refs_6_), channel_id=1, source_target_pairs={{0,4},{1,5},{4,8},{5,9},{8,12},{9,13},{12,16},{13,17},{16,20},{17,... | collective-permute-start | bytes 337928 | tf_op jit(solution)/shard_map/ppermute | solution.py:40
  29.8 4.8 %collective-permute-done.10.refs_8_ = bf16[80,704]{1,0:T(8,128)(2,1)S(1)} collective-permute-done((bf16[80,704]{1,0:T(8,128)(2,1)S(1)}, bf16[80,704]{1,0:T(8,128)(2,1)S(1)}, u32[]{:S(2)}, u32[]{:S(2)}) %collective-permute-start.10) | collective-permute-done | bytes 112672 | tf_op jit(solution)/shard_map/ppermute | solution.py:40
  36.4 1.9 %collective-permute-start.11 = (bf16[320,704]{1,0:T(8,128)(2,1)S(1)}, bf16[320,704]{1,0:T(8,128)(2,1)S(1)}, u32[]{:S(2)}, u32[]{:S(2)}) collective-permute-start(bf16[320,704]{1,0:T(8,128)(2,1)S(1)} %pad_maximum_fusion.1), channel_id=1, source_target_pairs={{0,130},{1,131},{4,134},{5,135},{8,138},{9,139},{12,142},{13,143},... | collective-permute-start | bytes 1351688 | tf_op jit(solution)/shard_map/ppermute | solution.py:40
  38.4 9.7 %scores.2 = (bf16[16,1280,256]{2,1,0:T(8,128)(2,1)S(1)}, f32[16,256]{1,0:T(8,128)S(1)}, f32[16,256]{1,0:T(8,128)S(1)}, bf16[320,128]{1,0:T(8,128)(2,1)S(1)}) custom-call(s32[5]{0:T(128)S(1)} %stack.23.refs_0_.meta, bf16[80,704]{1,0:T(8,128)(2,1)S(1)} %fusion.refs_1_, bf16[80,704]{1,0:T(8,128)(2,1)S(1)} %collective-permute-done.refs_2_, ...), custom_call_target="tpu_custom_call" | custom-call | flops 6039797760 | bytes 5242880 | tf_op jit(solution)/shard_map/scores/pallas_call | solution.py:158
  50.0 8.8 %scores.3 = (bf16[16,1280,256]{2,1,0:T(8,128)(2,1)S(1)}, f32[16,256]{1,0:T(8,128)S(1)}, f32[16,256]{1,0:T(8,128)S(1)}, bf16[320,128]{1,0:T(8,128)(2,1)S(1)}) custom-call(s32[5]{0:T(128)S(1)} %stack.23.refs_0_.meta, bf16[320,704]{1,0:T(8,128)(2,1)S(1)} %collective-permute-done.4.refs_1_, ...), custom_call_target="tpu_custom_call", output_to_operand_aliasing={{0}: (3, {})} | custom-call | flops 6039797760 | bytes 5242880 | tf_op jit(solution)/shard_map/scores/pallas_call | solution.py:158
  58.9 3.9 %index_forward.1 = (f32[320,256]{1,0:T(8,128)S(1)}, f32[2,24,256]{2,1,0:T(8,128)S(1)}, f32[2,24,256]{2,1,0:T(8,128)S(1)}) custom-call(s32[5]{0:T(128)S(1)} %stack.23.refs_0_.meta, bf16[320,128]{1,0:T(8,128)(2,1)S(1)} %get-tuple-element.58.keys, f32[16,256]{1,0:T(8,128)S(1)} %get-tuple-element.59.m0, f32[16,256]{1,0:T(8,128)S(1)} %get-tuple-element.60.l0, ...), custom_call_target="tpu_custom_call" | custom-call | flops 1342177280 | bytes 5242880 | tf_op jit(solution)/shard_map/index_forward/pallas_call | solution.py:334
  66.2 3.5 %collective-permute-done.18.up = f32[2,8,256]{2,1,0:T(8,128)S(1)} collective-permute-done((f32[2,8,256]{2,1,0:T(8,128)S(1)}, f32[2,8,256]{2,1,0:T(8,128)S(1)}, u32[]{:S(2)}, u32[]{:S(2)}) %collective-permute-start.18) | collective-permute-done | bytes 16416 | tf_op jit(solution)/shard_map/ppermute | solution.py:40
  69.7 3.3 %head_sum.1 = (bf16[336,256]{1,0:T(8,128)(2,1)S(1)}, bf16[336,256]{1,0:T(8,128)(2,1)S(1)}, bf16[336,256]{1,0:T(8,128)(2,1)S(1)}, bf16[336,256]{1,0:T(8,128)(2,1)S(1)}) custom-call(s32[5]{0:T(128)S(1)} %stack.23.refs_0_.meta, bf16[16,1280,256]{2,1,0:T(8,128)(2,1)S(1)} %get-tuple-element.67.e_ref, f32[16,256]{1,0:T(8,128)S(1)} %get-tuple-element.59.m0, ...), custom_call_target="tpu_custom_call" | custom-call | bytes 11534336 | tf_op jit(solution)/shard_map/head_sum/pallas_call | solution.py:234
  74.8 2.9 %collective-permute-start.21 = (bf16[336,256]{1,0:T(8,128)(2,1)S(1)}, bf16[336,256]{1,0:T(8,128)(2,1)S(1)}, u32[]{:S(2)}, u32[]{:S(2)}) collective-permute-start(bf16[336,256]{1,0:T(8,128)(2,1)S(1)} %get-tuple-element.75), channel_id=1, source_target_pairs={{0,128},{1,129},{4,132},{5,133},{8,136},{9,137},{12,140},{13,141},... | collective-permute-start | bytes 516104 | tf_op jit(solution)/shard_map/ppermute | solution.py:40
  80.0 4.4 %collective-permute-done.21.t2 = bf16[336,256]{1,0:T(8,128)(2,1)S(1)} collective-permute-done((bf16[336,256]{1,0:T(8,128)(2,1)S(1)}, bf16[336,256]{1,0:T(8,128)(2,1)S(1)}, u32[]{:S(2)}, u32[]{:S(2)}) %collective-permute-start.21) | collective-permute-done | bytes 172064 | tf_op jit(solution)/shard_map/ppermute | solution.py:40
  84.4 2.7 %collective-permute-done.22.t3 = bf16[336,256]{1,0:T(8,128)(2,1)S(1)} collective-permute-done((bf16[336,256]{1,0:T(8,128)(2,1)S(1)}, bf16[336,256]{1,0:T(8,128)(2,1)S(1)}, u32[]{:S(2)}, u32[]{:S(2)}) %collective-permute-start.22) | collective-permute-done | bytes 172064 | tf_op jit(solution)/shard_map/ppermute | solution.py:40
  87.0 7.9 %index_backward.1 = (f32[80,128]{1,0:T(8,128)S(1)}, f32[80,128]{1,0:T(8,128)S(1)}, bf16[16,32,128]{2,1,0:T(8,128)(2,1)}) custom-call(s32[5]{0:T(128)S(1)} %stack.23.refs_0_.meta, bf16[320,128]{1,0:T(8,128)(2,1)S(1)} %get-tuple-element.58.keys, f32[320,256]{1,0:T(8,128)S(1)} %get-tuple-element.66.logits, bf16[336,256]{1,0:T(8,128)(2,1)S(1)} %get-tuple-element.73.t0, ...), custom_call_target="tpu_custom_call" | custom-call | flops 2684354560 | bytes 6291456 | tf_op jit(solution)/shard_map/index_backward/pallas_call | solution.py:416
  94.9 5.3 %all-to-all-start = ((bf16[16,32,128]{2,1,0:T(8,128)(2,1)}), bf16[16,32,128]{2,1,0:T(8,128)(2,1)S(1)}, u32[]{:S(2)}, u32[]{:S(2)}) async-start(bf16[16,32,128]{2,1,0:T(8,128)(2,1)} %get-tuple-element.77), calls=%async_computation | async-start | bytes 262144 | tf_op jit(solution)/shard_map/all_to_all | solution.py:533
  100.3 10.2 %all-to-all-done = bf16[16,32,128]{2,1,0:T(8,128)(2,1)S(1)} async-done(((bf16[16,32,128]{2,1,0:T(8,128)(2,1)}), bf16[16,32,128]{2,1,0:T(8,128)(2,1)S(1)}, u32[]{:S(2)}, u32[]{:S(2)}) %all-to-all-start) | async-done | bytes 131104 | tf_op jit(solution)/shard_map/all_to_all | solution.py:533
  110.5 2.0 %collective-permute-start.24 = (bf16[112,128]{1,0:T(8,128)(2,1)S(1)}, bf16[112,128]{1,0:T(8,128)(2,1)S(1)}, u32[]{:S(2)}, u32[]{:S(2)}) collective-permute-start(bf16[112,128]{1,0:T(8,128)(2,1)S(1)} %pad_maximum_fusion.3), channel_id=1, source_target_pairs={{0,128},{1,129},{4,132},{5,133},{8,136},{9,137},{12,140},{13,141},... | collective-permute-start | bytes 86024 | tf_op jit(solution)/shard_map/ppermute | solution.py:40
  112.5 3.5 %collective-permute-done.24 = bf16[112,128]{1,0:T(8,128)(2,1)S(1)} collective-permute-done((bf16[112,128]{1,0:T(8,128)(2,1)S(1)}, bf16[112,128]{1,0:T(8,128)(2,1)S(1)}, u32[]{:S(2)}, u32[]{:S(2)}) %collective-permute-start.24) | collective-permute-done | bytes 28704 | tf_op jit(solution)/shard_map/ppermute | solution.py:40
  116.0 2.5 %collective-permute-start.25 = (bf16[224,128]{1,0:T(8,128)(2,1)S(1)}, bf16[224,128]{1,0:T(8,128)(2,1)S(1)}, u32[]{:S(2)}, u32[]{:S(2)}) collective-permute-start(bf16[224,128]{1,0:T(8,128)(2,1)S(1)} %pad_maximum_fusion.2.p0), channel_id=1, source_target_pairs={{0,32},{1,33},{4,36},{5,37},{8,40},{9,41},{12,44},{13,45},{16,48},... | collective-permute-start | bytes 172040 | tf_op jit(solution)/shard_map/ppermute | solution.py:40
  120.6 3.6 %collective-permute-done.26.p2 = bf16[224,128]{1,0:T(8,128)(2,1)S(1)} collective-permute-done((bf16[224,128]{1,0:T(8,128)(2,1)S(1)}, bf16[224,128]{1,0:T(8,128)(2,1)S(1)}, u32[]{:S(2)}, u32[]{:S(2)}) %collective-permute-start.26) | collective-permute-done | bytes 57376 | tf_op jit(solution)/shard_map/ppermute | solution.py:40
  (62 shorter events, 23.8 us)
Async XLA Ops:
  1.7 9.2 %collective-permute-start = (bf16[80,704]{1,0:T(8,128)(2,1)S(1)}, bf16[80,704]{1,0:T(8,128)(2,1)S(1)}, u32[]{:S(2)}, u32[]{:S(2)}) collective-permute-start(bf16[80,704]{1,0:T(8,128)(2,1)S(1)} %fusion.refs_1_), channel_id=1, source_target_pairs={{0,4},{1,5},{4,8},{5,9},{8,12},{9,13},{12,16},{13,17},{16,20},{17,... | collective-permute-start | bytes 337928 | tf_op jit(solution)/shard_map/ppermute | solution.py:40
  3.6 7.3 %collective-permute-start.1 = (bf16[80,704]{1,0:T(8,128)(2,1)S(1)}, bf16[80,704]{1,0:T(8,128)(2,1)S(1)}, u32[]{:S(2)}, u32[]{:S(2)}) collective-permute-start(bf16[80,704]{1,0:T(8,128)(2,1)S(1)} %fusion.refs_1_), channel_id=1, source_target_pairs={{0,28},{1,29},{4,0},{5,1},{8,4},{9,5},{12,8},{13,9},{16,12},{17,13... | collective-permute-start | bytes 337928 | tf_op jit(solution)/shard_map/ppermute | solution.py:40
  10.9 16.3 %collective-permute-start.7 = (bf16[4,576,128]{2,1,0:T(8,128)(2,1)S(1)}, bf16[4,576,128]{2,1,0:T(8,128)(2,1)S(1)}, u32[]{:S(2)}, u32[]{:S(2)}) collective-permute-start(bf16[4,576,128]{2,1,0:T(8,128)(2,1)S(1)} %get-tuple-element.49), channel_id=1, source_target_pairs={{0,32},{1,33},{4,36},{5,37},{8,40},{9,41},{12,44},{13,45},{16,48},... | collective-permute-start | bytes 1769480 | tf_op jit(solution)/shard_map/ppermute | solution.py:40
  12.4 14.8 %collective-permute-start.8 = (bf16[4,576,128]{2,1,0:T(8,128)(2,1)S(1)}, bf16[4,576,128]{2,1,0:T(8,128)(2,1)S(1)}, u32[]{:S(2)}, u32[]{:S(2)}) collective-permute-start(bf16[4,576,128]{2,1,0:T(8,128)(2,1)S(1)} %get-tuple-element.50), channel_id=1, source_target_pairs={{0,96},{1,97},{4,100},{5,101},{8,104},{9,105},{12,108},{13,109},{1... | collective-permute-start | bytes 1769480 | tf_op jit(solution)/shard_map/ppermute | solution.py:40
  13.5 6.2 %collective-permute-start.2 = (bf16[80,704]{1,0:T(8,128)(2,1)S(1)}, bf16[80,704]{1,0:T(8,128)(2,1)S(1)}, u32[]{:S(2)}, u32[]{:S(2)}) collective-permute-start(bf16[80,704]{1,0:T(8,128)(2,1)S(1)} %collective-permute-done.refs_2_), channel_id=1, source_target_pairs={{0,4},{1,5},{4,8},{5,9},{8,12},{9,13},{12,16},{13,17},{16,20},{17,... | collective-permute-start | bytes 337928 | tf_op jit(solution)/shard_map/ppermute | solution.py:40
  13.6 6.1 %collective-permute-start.3 = (bf16[80,704]{1,0:T(8,128)(2,1)S(1)}, bf16[80,704]{1,0:T(8,128)(2,1)S(1)}, u32[]{:S(2)}, u32[]{:S(2)}) collective-permute-start(bf16[80,704]{1,0:T(8,128)(2,1)S(1)} %collective-permute-done.1.refs_3_), channel_id=1, source_target_pairs={{0,28},{1,29},{4,0},{5,1},{8,4},{9,5},{12,8},{13,9},{16,12},{17,13... | collective-permute-start | bytes 337928 | tf_op jit(solution)/shard_map/ppermute | solution.py:40
  19.7 6.5 %collective-permute-start.5 = (bf16[80,704]{1,0:T(8,128)(2,1)S(1)}, bf16[80,704]{1,0:T(8,128)(2,1)S(1)}, u32[]{:S(2)}, u32[]{:S(2)}) collective-permute-start(bf16[80,704]{1,0:T(8,128)(2,1)S(1)} %collective-permute-done.2.refs_4_), channel_id=1, source_target_pairs={{0,4},{1,5},{4,8},{5,9},{8,12},{9,13},{12,16},{13,17},{16,20},{17,... | collective-permute-start | bytes 337928 | tf_op jit(solution)/shard_map/ppermute | solution.py:40
  22.3 4.9 %collective-permute-start.6 = (bf16[80,704]{1,0:T(8,128)(2,1)S(1)}, bf16[80,704]{1,0:T(8,128)(2,1)S(1)}, u32[]{:S(2)}, u32[]{:S(2)}) collective-permute-start(bf16[80,704]{1,0:T(8,128)(2,1)S(1)} %collective-permute-done.3.refs_5_), channel_id=1, source_target_pairs={{0,28},{1,29},{4,0},{5,1},{8,4},{9,5},{12,8},{13,9},{16,12},{17,13... | collective-permute-start | bytes 337928 | tf_op jit(solution)/shard_map/ppermute | solution.py:40
  27.2 7.5 %collective-permute-start.13 = (bf16[4,576,128]{2,1,0:T(8,128)(2,1)S(1)}, bf16[4,576,128]{2,1,0:T(8,128)(2,1)S(1)}, u32[]{:S(2)}, u32[]{:S(2)}) collective-permute-start(bf16[4,576,128]{2,1,0:T(8,128)(2,1)S(1)} %collective-permute-done.7.refs_11_.refs_7_), channel_id=1, source_target_pairs={{0,1},{1,0},{4,5},{5,4},{8,9},{9,8},{12,13},{13,12},{16,17},{17,16... | collective-permute-start | bytes 1769480 | tf_op jit(solution)/shard_map/ppermute | solution.py:40
  27.2 7.5 %collective-permute-start.14 = (bf16[4,576,128]{2,1,0:T(8,128)(2,1)S(1)}, bf16[4,576,128]{2,1,0:T(8,128)(2,1)S(1)}, u32[]{:S(2)}, u32[]{:S(2)}) collective-permute-start(bf16[4,576,128]{2,1,0:T(8,128)(2,1)S(1)} %collective-permute-done.8.refs_13_.refs_9_), channel_id=1, source_target_pairs={{0,1},{1,0},{4,5},{5,4},{8,9},{9,8},{12,13},{13,12},{16,17},{17,16... | collective-permute-start | bytes 1769480 | tf_op jit(solution)/shard_map/ppermute | solution.py:40
  27.7 10.7 %collective-permute-start.12 = (bf16[8,576,128]{2,1,0:T(8,128)(2,1)S(1)}, bf16[8,576,128]{2,1,0:T(8,128)(2,1)S(1)}, u32[]{:S(2)}, u32[]{:S(2)}) collective-permute-start(bf16[8,576,128]{2,1,0:T(8,128)(2,1)S(1)} %bitcast.18), channel_id=1, source_target_pairs={{0,1},{1,0},{4,5},{5,4},{8,9},{9,8},{12,13},{13,12},{16,17},{17,16... | collective-permute-start | bytes 3538952 | tf_op jit(solution)/shard_map/ppermute | solution.py:40
  27.8 6.9 %collective-permute-start.10 = (bf16[80,704]{1,0:T(8,128)(2,1)S(1)}, bf16[80,704]{1,0:T(8,128)(2,1)S(1)}, u32[]{:S(2)}, u32[]{:S(2)}) collective-permute-start(bf16[80,704]{1,0:T(8,128)(2,1)S(1)} %collective-permute-done.5.refs_6_), channel_id=1, source_target_pairs={{0,4},{1,5},{4,8},{5,9},{8,12},{9,13},{12,16},{13,17},{16,20},{17,... | collective-permute-start | bytes 337928 | tf_op jit(solution)/shard_map/ppermute | solution.py:40
  34.6 24.2 %collective-permute-start.15 = (bf16[64,128,128]{2,1,0:T(8,128)(2,1)S(1)}, bf16[64,128,128]{2,1,0:T(8,128)(2,1)S(1)}, u32[]{:S(2)}, u32[]{:S(2)}) collective-permute-start(bf16[64,128,128]{2,1,0:T(8,128)(2,1)S(1)} %bitcast.14), channel_id=1, source_target_pairs={{0,1},{1,0},{4,5},{5,4},{8,9},{9,8},{12,13},{13,12},{16,17},{17,16... | collective-permute-start | bytes 6291464 | tf_op jit(solution)/shard_map/ppermute | solution.py:40
  34.7 15.0 %collective-permute-start.4 = (bf16[320,704]{1,0:T(8,128)(2,1)S(1)}, bf16[320,704]{1,0:T(8,128)(2,1)S(1)}, u32[]{:S(2)}, u32[]{:S(2)}) collective-permute-start(bf16[320,704]{1,0:T(8,128)(2,1)S(1)} %pad_maximum_fusion), channel_id=1, source_target_pairs={{0,2},{1,3},{4,6},{5,7},{8,10},{9,11},{12,14},{13,15},{16,18},{17,... | collective-permute-start | bytes 1351688 | tf_op jit(solution)/shard_map/ppermute | solution.py:40
  36.4 13.6 %collective-permute-start.11 = (bf16[320,704]{1,0:T(8,128)(2,1)S(1)}, bf16[320,704]{1,0:T(8,128)(2,1)S(1)}, u32[]{:S(2)}, u32[]{:S(2)}) collective-permute-start(bf16[320,704]{1,0:T(8,128)(2,1)S(1)} %pad_maximum_fusion.1), channel_id=1, source_target_pairs={{0,130},{1,131},{4,134},{5,135},{8,138},{9,139},{12,142},{13,143},... | collective-permute-start | bytes 1351688 | tf_op jit(solution)/shard_map/ppermute | solution.py:40
  38.3 20.5 %collective-permute-start.16 = (f32[64,128]{1,0:T(8,128)S(1)}, f32[64,128]{1,0:T(8,128)S(1)}, u32[]{:S(2)}, u32[]{:S(2)}) collective-permute-start(f32[64,128]{1,0:T(8,128)S(1)} %bitcast.21), channel_id=1, source_target_pairs={{0,1},{1,0},{4,5},{5,4},{8,9},{9,8},{12,13},{13,12},{16,17},{17,16... | collective-permute-start | bytes 98312 | tf_op jit(solution)/shard_map/ppermute | solution.py:40
  64.1 5.6 %collective-permute-start.19 = (f32[2,16,256]{2,1,0:T(8,128)S(1)}, f32[2,16,256]{2,1,0:T(8,128)S(1)}, u32[]{:S(2)}, u32[]{:S(2)}) collective-permute-start(f32[2,16,256]{2,1,0:T(8,128)S(1)} %get-tuple-element.72), channel_id=1, source_target_pairs={{0,96},{1,97},{4,100},{5,101},{8,104},{9,105},{12,108},{13,109},{1... | collective-permute-start | bytes 98312 | tf_op jit(solution)/shard_map/ppermute | solution.py:40
  73.0 7.0 %collective-permute-start.20 = (bf16[336,256]{1,0:T(8,128)(2,1)S(1)}, bf16[336,256]{1,0:T(8,128)(2,1)S(1)}, u32[]{:S(2)}, u32[]{:S(2)}) collective-permute-start(bf16[336,256]{1,0:T(8,128)(2,1)S(1)} %get-tuple-element.74), channel_id=1, source_target_pairs={{0,64},{1,65},{4,68},{5,69},{8,72},{9,73},{12,76},{13,77},{16,80},... | collective-permute-start | bytes 516104 | tf_op jit(solution)/shard_map/ppermute | solution.py:40
  74.8 9.5 %collective-permute-start.21 = (bf16[336,256]{1,0:T(8,128)(2,1)S(1)}, bf16[336,256]{1,0:T(8,128)(2,1)S(1)}, u32[]{:S(2)}, u32[]{:S(2)}) collective-permute-start(bf16[336,256]{1,0:T(8,128)(2,1)S(1)} %get-tuple-element.75), channel_id=1, source_target_pairs={{0,128},{1,129},{4,132},{5,133},{8,136},{9,137},{12,140},{13,141},... | collective-permute-start | bytes 516104 | tf_op jit(solution)/shard_map/ppermute | solution.py:40
  77.7 9.3 %collective-permute-start.22 = (bf16[336,256]{1,0:T(8,128)(2,1)S(1)}, bf16[336,256]{1,0:T(8,128)(2,1)S(1)}, u32[]{:S(2)}, u32[]{:S(2)}) collective-permute-start(bf16[336,256]{1,0:T(8,128)(2,1)S(1)} %get-tuple-element.76), channel_id=1, source_target_pairs={{0,192},{1,193},{4,196},{5,197},{8,200},{9,201},{12,204},{13,205},... | collective-permute-start | bytes 516104 | tf_op jit(solution)/shard_map/ppermute | solution.py:40
  94.9 5.3 %collective-permute-start.23 = (f32[80,128]{1,0:T(8,128)S(1)}, f32[80,128]{1,0:T(8,128)S(1)}, u32[]{:S(2)}, u32[]{:S(2)}) collective-permute-start(f32[80,128]{1,0:T(8,128)S(1)} %get-tuple-element.79), channel_id=1, source_target_pairs={{0,1},{1,0},{4,5},{5,4},{8,9},{9,8},{12,13},{13,12},{16,17},{17,16... | collective-permute-start | bytes 122888 | tf_op jit(solution)/shard_map/ppermute | solution.py:40
  94.9 15.5 %all-to-all-start = ((bf16[16,32,128]{2,1,0:T(8,128)(2,1)}), bf16[16,32,128]{2,1,0:T(8,128)(2,1)S(1)}, u32[]{:S(2)}, u32[]{:S(2)}) async-start(bf16[16,32,128]{2,1,0:T(8,128)(2,1)} %get-tuple-element.77), calls=%async_computation | async-start | bytes 262144 | tf_op jit(solution)/shard_map/all_to_all | solution.py:533
  110.5 5.5 %collective-permute-start.24 = (bf16[112,128]{1,0:T(8,128)(2,1)S(1)}, bf16[112,128]{1,0:T(8,128)(2,1)S(1)}, u32[]{:S(2)}, u32[]{:S(2)}) collective-permute-start(bf16[112,128]{1,0:T(8,128)(2,1)S(1)} %pad_maximum_fusion.3), channel_id=1, source_target_pairs={{0,128},{1,129},{4,132},{5,133},{8,136},{9,137},{12,140},{13,141},... | collective-permute-start | bytes 86024 | tf_op jit(solution)/shard_map/ppermute | solution.py:40
  118.4 5.8 %collective-permute-start.26 = (bf16[224,128]{1,0:T(8,128)(2,1)S(1)}, bf16[224,128]{1,0:T(8,128)(2,1)S(1)}, u32[]{:S(2)}, u32[]{:S(2)}) collective-permute-start(bf16[224,128]{1,0:T(8,128)(2,1)S(1)} %pad_maximum_fusion.2.p0), channel_id=1, source_target_pairs={{0,64},{1,65},{4,68},{5,69},{8,72},{9,73},{12,76},{13,77},{16,80},... | collective-permute-start | bytes 172040 | tf_op jit(solution)/shard_map/ppermute | solution.py:40
  (8 other events, 53.6 us)

commit v13 on v12

--- a/solution.py
+++ b/solution.py
@@ -505,9 +505,9 @@
     f2, b2 = lax.optimization_barrier((f2, b2))
     f3, b3 = shift(f2, dz=1), shift(b2, dz=7)
     pb = swap_core(pa)
-    ia = index_queries.transpose(1, 0, 2)
-    f3, b3, left, right, ia, pb = lax.optimization_barrier((f3, b3, left, right, ia, pb))
+    f3, b3, left, right, pb = lax.optimization_barrier((f3, b3, left, right, pb))
     f4 = shift(f3, dz=1)
+    f4, ia = lax.optimization_barrier((f4, index_queries.transpose(1, 0, 2)))
     left_far, right_far = swap_core(left), swap_core(right)
     y0, y1 = jnp.concatenate([own, f1, b1, f2]), jnp.concatenate([b2, f3, b3, f4])
     y0, y1 = shift(y0, dy=1), shift(y1, dy=3)
@@ -522,8 +522,8 @@
     here, up, down = pair_call(ours, swap_core(sent))
     up, down = shift(up, dx=1), shift(down, dx=3)
     sums = head_sum_call(meta, exps, m0, m1, here, up, down)
-    group = (dict(dx=2), dict(dy=2), dict(dx=2, dy=2))
-    target = [sums[0]] + [shift(part, **move) for part, move in zip(sums[1:], group)]
+    far = shift(sums[3], dx=2, dy=2)
+    target = [sums[0], far, shift(sums[1], dx=2), shift(sums[2], dy=2)]
 
     mine, other, kg = backward_call(meta, keys, logits, target, ia, ib, wa, wb)
     rows_out = mine + swap_core(other)

time: 127 us -> 126 us (level); the launches traced: 126 us -> 126 us
  waiting for transfers between devices: 42.3 us -> 40.4 us
  starting transfers between devices: 41.5 us -> 42.9 us
    ppermute x28, waiting for transfers between devices: 32.1 us -> 30.2 us  [shift(): return lax.ppermute(value, ALL, pairs)]
  transfers between devices with their start and end apart: 29 -> 29, of which waited for: 15 -> 18; matrix products, arithmetic and copies ran while one was open for 4% -> 4% of each run, Pallas kernels for 15% -> 15%
where the time goes in v13:
time: 126 us
  starting transfers between devices  42.9 us (34%)
  waiting for transfers between devices  40.4 us (32%)
  Pallas kernels  34.6 us (27%)
  local copies, waits for them, and re-layouts  5.5 us (4%)
  between operations  1.49 us (1%)
    ppermute x28, starting transfers between devices, shift(): return lax.ppermute(value, ALL, pairs)  37.4 us
    ppermute x28, waiting for transfers between devices, shift(): return lax.ppermute(value, ALL, pairs)  30.2 us
    pallas_call x2, Pallas kernels, score_call(): pl.pallas_call(lambda *refs: score_kernel(chunk, spans, *refs), grid_spec...  18.3 us
    all_to_all x1, waiting for transfers between devices, body(): kg = lax.all_to_all(kg, ('z', 'ylo'), 0, 0, tiled=True)  10.2 us
    pallas_call x1, Pallas kernels, backward_call(): pl.pallas_call(backward_kernel, grid_spec=pltpu.PrefetchScalarGridSpec(nu...  7.89 us
    all_to_all x1, starting transfers between devices, body(): kg = lax.all_to_all(kg, ('z', 'ylo'), 0, 0, tiled=True)  5.49 us
    pallas_call x1, Pallas kernels, forward_call(): pl.pallas_call(forward_kernel, grid_spec=pltpu.PrefetchScalarGridSpec(num...  3.85 us
    pallas_call x1, Pallas kernels, head_sum_call(): pl.pallas_call(head_sum_kernel, grid_spec=pltpu.PrefetchScalarGridSpec(nu...  3.29 us
  transfers between devices with their start and end apart: 29, of which 18 were waited for; matrix products, arithmetic and copies ran while one was open for 4% of the time, Pallas kernels for 15%

profile of v13, /device:TPU:2, one launch (start us, length us, event | category | flops | bytes accessed | tf_op | source)
XLA Modules:
  0.0 126.1 jit_solution(4551191254308369741)
XLA Ops:
  1.8 1.9 %collective-permute-start = (bf16[80,704]{1,0:T(8,128)(2,1)S(1)}, bf16[80,704]{1,0:T(8,128)(2,1)S(1)}, u32[]{:S(2)}, u32[]{:S(2)}) collective-permute-start(bf16[80,704]{1,0:T(8,128)(2,1)S(1)} %fusion.refs_1_), channel_id=1, source_target_pairs={{0,4},{1,5},{4,8},{5,9},{8,12},{9,13},{12,16},{13,17},{16,20},{17,... | collective-permute-start | bytes 337928 | tf_op jit(solution)/shard_map/ppermute | solution.py:40
  3.7 4.0 %collective-permute-start.1 = (bf16[80,704]{1,0:T(8,128)(2,1)S(1)}, bf16[80,704]{1,0:T(8,128)(2,1)S(1)}, u32[]{:S(2)}, u32[]{:S(2)}) collective-permute-start(bf16[80,704]{1,0:T(8,128)(2,1)S(1)} %fusion.refs_1_), channel_id=1, source_target_pairs={{0,28},{1,29},{4,0},{5,1},{8,4},{9,5},{12,8},{13,9},{16,12},{17,13... | collective-permute-start | bytes 337928 | tf_op jit(solution)/shard_map/ppermute | solution.py:40
  7.7 2.4 %fusion.2 = (bf16[4,576,128]{2,1,0:T(8,128)(2,1)}, bf16[4,576,128]{2,1,0:T(8,128)(2,1)}) fusion(bf16[8,576,128]{2,1,0:T(8,128)(2,1)} %bitcast.17), kind=kLoop, calls=%fused_computation.13 | loop fusion | bytes 2359296 | tf_op jit(solution)/shard_map/slice | solution.py:502
  13.7 3.2 %collective-permute-start.3 = (bf16[80,704]{1,0:T(8,128)(2,1)S(1)}, bf16[80,704]{1,0:T(8,128)(2,1)S(1)}, u32[]{:S(2)}, u32[]{:S(2)}) collective-permute-start(bf16[80,704]{1,0:T(8,128)(2,1)S(1)} %collective-permute-done.1.refs_3_), channel_id=1, source_target_pairs={{0,28},{1,29},{4,0},{5,1},{8,4},{9,5},{12,8},{13,9},{16,12},{17,13... | collective-permute-start | bytes 337928 | tf_op jit(solution)/shard_map/ppermute | solution.py:40
  17.0 2.8 %collective-permute-done.2.refs_4_ = bf16[80,704]{1,0:T(8,128)(2,1)S(1)} collective-permute-done((bf16[80,704]{1,0:T(8,128)(2,1)S(1)}, bf16[80,704]{1,0:T(8,128)(2,1)S(1)}, u32[]{:S(2)}, u32[]{:S(2)}) %collective-permute-start.2) | collective-permute-done | bytes 112672 | tf_op jit(solution)/shard_map/ppermute | solution.py:40
  19.8 2.6 %collective-permute-start.5 = (bf16[80,704]{1,0:T(8,128)(2,1)S(1)}, bf16[80,704]{1,0:T(8,128)(2,1)S(1)}, u32[]{:S(2)}, u32[]{:S(2)}) collective-permute-start(bf16[80,704]{1,0:T(8,128)(2,1)S(1)} %collective-permute-done.2.refs_4_), channel_id=1, source_target_pairs={{0,4},{1,5},{4,8},{5,9},{8,12},{9,13},{12,16},{13,17},{16,20},{17,... | collective-permute-start | bytes 337928 | tf_op jit(solution)/shard_map/ppermute | solution.py:40
  27.9 2.0 %collective-permute-start.10 = (bf16[80,704]{1,0:T(8,128)(2,1)S(1)}, bf16[80,704]{1,0:T(8,128)(2,1)S(1)}, u32[]{:S(2)}, u32[]{:S(2)}) collective-permute-start(bf16[80,704]{1,0:T(8,128)(2,1)S(1)} %collective-permute-done.5.refs_6_), channel_id=1, source_target_pairs={{0,4},{1,5},{4,8},{5,9},{8,12},{9,13},{12,16},{13,17},{16,20},{17,... | collective-permute-start | bytes 337928 | tf_op jit(solution)/shard_map/ppermute | solution.py:40
  29.9 2.9 %copy.13 = bf16[128,64,128]{2,0,1:T(8,128)(2,1)S(1)} copy(bf16[128,64,128]{2,1,0:T(8,128)(2,1)} %param.9) | data formatting | bytes 4194304 | tf_op args[2]
  36.5 1.9 %collective-permute-start.11 = (bf16[320,704]{1,0:T(8,128)(2,1)S(1)}, bf16[320,704]{1,0:T(8,128)(2,1)S(1)}, u32[]{:S(2)}, u32[]{:S(2)}) collective-permute-start(bf16[320,704]{1,0:T(8,128)(2,1)S(1)} %pad_maximum_fusion.1), channel_id=1, source_target_pairs={{0,130},{1,131},{4,134},{5,135},{8,138},{9,139},{12,142},{13,143},... | collective-permute-start | bytes 1351688 | tf_op jit(solution)/shard_map/ppermute | solution.py:40
  38.5 9.6 %scores.2 = (bf16[16,1280,256]{2,1,0:T(8,128)(2,1)S(1)}, f32[16,256]{1,0:T(8,128)S(1)}, f32[16,256]{1,0:T(8,128)S(1)}, bf16[320,128]{1,0:T(8,128)(2,1)S(1)}) custom-call(s32[5]{0:T(128)S(1)} %stack.23.refs_0_.meta, bf16[80,704]{1,0:T(8,128)(2,1)S(1)} %fusion.refs_1_, bf16[80,704]{1,0:T(8,128)(2,1)S(1)} %collective-permute-done.refs_2_, ...), custom_call_target="tpu_custom_call" | custom-call | flops 6039797760 | bytes 5242880 | tf_op jit(solution)/shard_map/scores/pallas_call | solution.py:158
  50.1 8.7 %scores.3 = (bf16[16,1280,256]{2,1,0:T(8,128)(2,1)S(1)}, f32[16,256]{1,0:T(8,128)S(1)}, f32[16,256]{1,0:T(8,128)S(1)}, bf16[320,128]{1,0:T(8,128)(2,1)S(1)}) custom-call(s32[5]{0:T(128)S(1)} %stack.23.refs_0_.meta, bf16[320,704]{1,0:T(8,128)(2,1)S(1)} %collective-permute-done.4.refs_1_, ...), custom_call_target="tpu_custom_call", output_to_operand_aliasing={{0}: (3, {})} | custom-call | flops 6039797760 | bytes 5242880 | tf_op jit(solution)/shard_map/scores/pallas_call | solution.py:158
  58.9 3.9 %index_forward.1 = (f32[320,256]{1,0:T(8,128)S(1)}, f32[2,24,256]{2,1,0:T(8,128)S(1)}, f32[2,24,256]{2,1,0:T(8,128)S(1)}) custom-call(s32[5]{0:T(128)S(1)} %stack.23.refs_0_.meta, bf16[320,128]{1,0:T(8,128)(2,1)S(1)} %get-tuple-element.60.keys, f32[16,256]{1,0:T(8,128)S(1)} %get-tuple-element.61.m0, f32[16,256]{1,0:T(8,128)S(1)} %get-tuple-element.62.l0, ...), custom_call_target="tpu_custom_call" | custom-call | flops 1342177280 | bytes 5242880 | tf_op jit(solution)/shard_map/index_forward/pallas_call | solution.py:334
  66.2 3.4 %collective-permute-done.18.up = f32[2,8,256]{2,1,0:T(8,128)S(1)} collective-permute-done((f32[2,8,256]{2,1,0:T(8,128)S(1)}, f32[2,8,256]{2,1,0:T(8,128)S(1)}, u32[]{:S(2)}, u32[]{:S(2)}) %collective-permute-start.18) | collective-permute-done | bytes 16416 | tf_op jit(solution)/shard_map/ppermute | solution.py:40
  69.7 3.3 %head_sum.1 = (bf16[336,256]{1,0:T(8,128)(2,1)S(1)}, bf16[336,256]{1,0:T(8,128)(2,1)S(1)}, bf16[336,256]{1,0:T(8,128)(2,1)S(1)}, bf16[336,256]{1,0:T(8,128)(2,1)S(1)}) custom-call(s32[5]{0:T(128)S(1)} %stack.23.refs_0_.meta, bf16[16,1280,256]{2,1,0:T(8,128)(2,1)S(1)} %get-tuple-element.69.e_ref, f32[16,256]{1,0:T(8,128)S(1)} %get-tuple-element.61.m0, ...), custom_call_target="tpu_custom_call" | custom-call | bytes 11534336 | tf_op jit(solution)/shard_map/head_sum/pallas_call | solution.py:234
  73.0 4.2 %collective-permute-start.20 = (bf16[336,256]{1,0:T(8,128)(2,1)S(1)}, bf16[336,256]{1,0:T(8,128)(2,1)S(1)}, u32[]{:S(2)}, u32[]{:S(2)}) collective-permute-start(bf16[336,256]{1,0:T(8,128)(2,1)S(1)} %get-tuple-element.76), channel_id=1, source_target_pairs={{0,192},{1,193},{4,196},{5,197},{8,200},{9,201},{12,204},{13,205},... | collective-permute-start | bytes 516104 | tf_op jit(solution)/shard_map/ppermute | solution.py:40
  79.5 4.4 %collective-permute-done.20.t1 = bf16[336,256]{1,0:T(8,128)(2,1)S(1)} collective-permute-done((bf16[336,256]{1,0:T(8,128)(2,1)S(1)}, bf16[336,256]{1,0:T(8,128)(2,1)S(1)}, u32[]{:S(2)}, u32[]{:S(2)}) %collective-permute-start.20) | collective-permute-done | bytes 172064 | tf_op jit(solution)/shard_map/ppermute | solution.py:40
  86.4 7.9 %index_backward.1 = (f32[80,128]{1,0:T(8,128)S(1)}, f32[80,128]{1,0:T(8,128)S(1)}, bf16[16,32,128]{2,1,0:T(8,128)(2,1)}) custom-call(s32[5]{0:T(128)S(1)} %stack.23.refs_0_.meta, bf16[320,128]{1,0:T(8,128)(2,1)S(1)} %get-tuple-element.60.keys, f32[320,256]{1,0:T(8,128)S(1)} %get-tuple-element.68.logits, bf16[336,256]{1,0:T(8,128)(2,1)S(1)} %get-tuple-element.75.t0, ...), custom_call_target="tpu_custom_call" | custom-call | flops 2684354560 | bytes 6291456 | tf_op jit(solution)/shard_map/index_backward/pallas_call | solution.py:416
  94.3 5.5 %all-to-all-start = ((bf16[16,32,128]{2,1,0:T(8,128)(2,1)}), bf16[16,32,128]{2,1,0:T(8,128)(2,1)S(1)}, u32[]{:S(2)}, u32[]{:S(2)}) async-start(bf16[16,32,128]{2,1,0:T(8,128)(2,1)} %get-tuple-element.79), calls=%async_computation | async-start | bytes 262144 | tf_op jit(solution)/shard_map/all_to_all | solution.py:533
  99.9 10.2 %all-to-all-done = bf16[16,32,128]{2,1,0:T(8,128)(2,1)S(1)} async-done(((bf16[16,32,128]{2,1,0:T(8,128)(2,1)}), bf16[16,32,128]{2,1,0:T(8,128)(2,1)S(1)}, u32[]{:S(2)}, u32[]{:S(2)}) %all-to-all-start) | async-done | bytes 131104 | tf_op jit(solution)/shard_map/all_to_all | solution.py:533
  110.1 2.7 %collective-permute-start.24 = (bf16[112,128]{1,0:T(8,128)(2,1)S(1)}, bf16[112,128]{1,0:T(8,128)(2,1)S(1)}, u32[]{:S(2)}, u32[]{:S(2)}) collective-permute-start(bf16[112,128]{1,0:T(8,128)(2,1)S(1)} %pad_maximum_fusion.3), channel_id=1, source_target_pairs={{0,128},{1,129},{4,132},{5,133},{8,136},{9,137},{12,140},{13,141},... | collective-permute-start | bytes 86024 | tf_op jit(solution)/shard_map/ppermute | solution.py:40
  112.7 2.8 %collective-permute-done.24 = bf16[112,128]{1,0:T(8,128)(2,1)S(1)} collective-permute-done((bf16[112,128]{1,0:T(8,128)(2,1)S(1)}, bf16[112,128]{1,0:T(8,128)(2,1)S(1)}, u32[]{:S(2)}, u32[]{:S(2)}) %collective-permute-start.24) | collective-permute-done | bytes 28704 | tf_op jit(solution)/shard_map/ppermute | solution.py:40
  116.0 4.8 %collective-permute-start.26 = (bf16[224,128]{1,0:T(8,128)(2,1)S(1)}, bf16[224,128]{1,0:T(8,128)(2,1)S(1)}, u32[]{:S(2)}, u32[]{:S(2)}) collective-permute-start(bf16[224,128]{1,0:T(8,128)(2,1)S(1)} %pad_maximum_fusion.2.p0), channel_id=1, source_target_pairs={{0,64},{1,65},{4,68},{5,69},{8,72},{9,73},{12,76},{13,77},{16,80},... | collective-permute-start | bytes 172040 | tf_op jit(solution)/shard_map/ppermute | solution.py:40
  120.8 2.1 %collective-permute-done.26.p2 = bf16[224,128]{1,0:T(8,128)(2,1)S(1)} collective-permute-done((bf16[224,128]{1,0:T(8,128)(2,1)S(1)}, bf16[224,128]{1,0:T(8,128)(2,1)S(1)}, u32[]{:S(2)}, u32[]{:S(2)}) %collective-permute-start.26) | collective-permute-done | bytes 57376 | tf_op jit(solution)/shard_map/ppermute | solution.py:40
  122.9 2.0 %collective-permute-done.27.p3 = bf16[224,128]{1,0:T(8,128)(2,1)S(1)} collective-permute-done((bf16[224,128]{1,0:T(8,128)(2,1)S(1)}, bf16[224,128]{1,0:T(8,128)(2,1)S(1)}, u32[]{:S(2)}, u32[]{:S(2)}) %collective-permute-start.27) | collective-permute-done | bytes 57376 | tf_op jit(solution)/shard_map/ppermute | solution.py:40
  (62 shorter events, 25.4 us)
Async XLA Ops:
  1.8 9.2 %collective-permute-start = (bf16[80,704]{1,0:T(8,128)(2,1)S(1)}, bf16[80,704]{1,0:T(8,128)(2,1)S(1)}, u32[]{:S(2)}, u32[]{:S(2)}) collective-permute-start(bf16[80,704]{1,0:T(8,128)(2,1)S(1)} %fusion.refs_1_), channel_id=1, source_target_pairs={{0,4},{1,5},{4,8},{5,9},{8,12},{9,13},{12,16},{13,17},{16,20},{17,... | collective-permute-start | bytes 337928 | tf_op jit(solution)/shard_map/ppermute | solution.py:40
  3.7 7.3 %collective-permute-start.1 = (bf16[80,704]{1,0:T(8,128)(2,1)S(1)}, bf16[80,704]{1,0:T(8,128)(2,1)S(1)}, u32[]{:S(2)}, u32[]{:S(2)}) collective-permute-start(bf16[80,704]{1,0:T(8,128)(2,1)S(1)} %fusion.refs_1_), channel_id=1, source_target_pairs={{0,28},{1,29},{4,0},{5,1},{8,4},{9,5},{12,8},{13,9},{16,12},{17,13... | collective-permute-start | bytes 337928 | tf_op jit(solution)/shard_map/ppermute | solution.py:40
  11.0 16.3 %collective-permute-start.7 = (bf16[4,576,128]{2,1,0:T(8,128)(2,1)}, bf16[4,576,128]{2,1,0:T(8,128)(2,1)S(1)}, u32[]{:S(2)}, u32[]{:S(2)}) collective-permute-start(bf16[4,576,128]{2,1,0:T(8,128)(2,1)} %get-tuple-element.50), channel_id=1, source_target_pairs={{0,32},{1,33},{4,36},{5,37},{8,40},{9,41},{12,44},{13,45},{16,48},... | collective-permute-start | bytes 1769480 | tf_op jit(solution)/shard_map/ppermute | solution.py:40
  12.5 14.8 %collective-permute-start.8 = (bf16[4,576,128]{2,1,0:T(8,128)(2,1)}, bf16[4,576,128]{2,1,0:T(8,128)(2,1)S(1)}, u32[]{:S(2)}, u32[]{:S(2)}) collective-permute-start(bf16[4,576,128]{2,1,0:T(8,128)(2,1)} %get-tuple-element.51), channel_id=1, source_target_pairs={{0,96},{1,97},{4,100},{5,101},{8,104},{9,105},{12,108},{13,109},{1... | collective-permute-start | bytes 1769480 | tf_op jit(solution)/shard_map/ppermute | solution.py:40
  13.6 6.2 %collective-permute-start.2 = (bf16[80,704]{1,0:T(8,128)(2,1)S(1)}, bf16[80,704]{1,0:T(8,128)(2,1)S(1)}, u32[]{:S(2)}, u32[]{:S(2)}) collective-permute-start(bf16[80,704]{1,0:T(8,128)(2,1)S(1)} %collective-permute-done.refs_2_), channel_id=1, source_target_pairs={{0,4},{1,5},{4,8},{5,9},{8,12},{9,13},{12,16},{13,17},{16,20},{17,... | collective-permute-start | bytes 337928 | tf_op jit(solution)/shard_map/ppermute | solution.py:40
  13.7 6.1 %collective-permute-start.3 = (bf16[80,704]{1,0:T(8,128)(2,1)S(1)}, bf16[80,704]{1,0:T(8,128)(2,1)S(1)}, u32[]{:S(2)}, u32[]{:S(2)}) collective-permute-start(bf16[80,704]{1,0:T(8,128)(2,1)S(1)} %collective-permute-done.1.refs_3_), channel_id=1, source_target_pairs={{0,28},{1,29},{4,0},{5,1},{8,4},{9,5},{12,8},{13,9},{16,12},{17,13... | collective-permute-start | bytes 337928 | tf_op jit(solution)/shard_map/ppermute | solution.py:40
  19.8 6.1 %collective-permute-start.5 = (bf16[80,704]{1,0:T(8,128)(2,1)S(1)}, bf16[80,704]{1,0:T(8,128)(2,1)S(1)}, u32[]{:S(2)}, u32[]{:S(2)}) collective-permute-start(bf16[80,704]{1,0:T(8,128)(2,1)S(1)} %collective-permute-done.2.refs_4_), channel_id=1, source_target_pairs={{0,4},{1,5},{4,8},{5,9},{8,12},{9,13},{12,16},{13,17},{16,20},{17,... | collective-permute-start | bytes 337928 | tf_op jit(solution)/shard_map/ppermute | solution.py:40
  27.3 7.5 %collective-permute-start.13 = (bf16[4,576,128]{2,1,0:T(8,128)(2,1)S(1)}, bf16[4,576,128]{2,1,0:T(8,128)(2,1)S(1)}, u32[]{:S(2)}, u32[]{:S(2)}) collective-permute-start(bf16[4,576,128]{2,1,0:T(8,128)(2,1)S(1)} %collective-permute-done.7.refs_11_.refs_7_), channel_id=1, source_target_pairs={{0,1},{1,0},{4,5},{5,4},{8,9},{9,8},{12,13},{13,12},{16,17},{17,16... | collective-permute-start | bytes 1769480 | tf_op jit(solution)/shard_map/ppermute | solution.py:40
  27.3 7.5 %collective-permute-start.14 = (bf16[4,576,128]{2,1,0:T(8,128)(2,1)S(1)}, bf16[4,576,128]{2,1,0:T(8,128)(2,1)S(1)}, u32[]{:S(2)}, u32[]{:S(2)}) collective-permute-start(bf16[4,576,128]{2,1,0:T(8,128)(2,1)S(1)} %collective-permute-done.8.refs_13_.refs_9_), channel_id=1, source_target_pairs={{0,1},{1,0},{4,5},{5,4},{8,9},{9,8},{12,13},{13,12},{16,17},{17,16... | collective-permute-start | bytes 1769480 | tf_op jit(solution)/shard_map/ppermute | solution.py:40
  27.8 10.7 %collective-permute-start.12 = (bf16[8,576,128]{2,1,0:T(8,128)(2,1)S(1)}, bf16[8,576,128]{2,1,0:T(8,128)(2,1)S(1)}, u32[]{:S(2)}, u32[]{:S(2)}) collective-permute-start(bf16[8,576,128]{2,1,0:T(8,128)(2,1)S(1)} %bitcast.18), channel_id=1, source_target_pairs={{0,1},{1,0},{4,5},{5,4},{8,9},{9,8},{12,13},{13,12},{16,17},{17,16... | collective-permute-start | bytes 3538952 | tf_op jit(solution)/shard_map/ppermute | solution.py:40
  27.9 6.9 %collective-permute-start.10 = (bf16[80,704]{1,0:T(8,128)(2,1)S(1)}, bf16[80,704]{1,0:T(8,128)(2,1)S(1)}, u32[]{:S(2)}, u32[]{:S(2)}) collective-permute-start(bf16[80,704]{1,0:T(8,128)(2,1)S(1)} %collective-permute-done.5.refs_6_), channel_id=1, source_target_pairs={{0,4},{1,5},{4,8},{5,9},{8,12},{9,13},{12,16},{13,17},{16,20},{17,... | collective-permute-start | bytes 337928 | tf_op jit(solution)/shard_map/ppermute | solution.py:40
  34.7 24.1 %collective-permute-start.15 = (bf16[64,128,128]{2,1,0:T(8,128)(2,1)S(1)}, bf16[64,128,128]{2,1,0:T(8,128)(2,1)S(1)}, u32[]{:S(2)}, u32[]{:S(2)}) collective-permute-start(bf16[64,128,128]{2,1,0:T(8,128)(2,1)S(1)} %bitcast.14), channel_id=1, source_target_pairs={{0,1},{1,0},{4,5},{5,4},{8,9},{9,8},{12,13},{13,12},{16,17},{17,16... | collective-permute-start | bytes 6291464 | tf_op jit(solution)/shard_map/ppermute | solution.py:40
  34.8 15.0 %collective-permute-start.4 = (bf16[320,704]{1,0:T(8,128)(2,1)S(1)}, bf16[320,704]{1,0:T(8,128)(2,1)S(1)}, u32[]{:S(2)}, u32[]{:S(2)}) collective-permute-start(bf16[320,704]{1,0:T(8,128)(2,1)S(1)} %pad_maximum_fusion), channel_id=1, source_target_pairs={{0,2},{1,3},{4,6},{5,7},{8,10},{9,11},{12,14},{13,15},{16,18},{17,... | collective-permute-start | bytes 1351688 | tf_op jit(solution)/shard_map/ppermute | solution.py:40
  36.5 13.6 %collective-permute-start.11 = (bf16[320,704]{1,0:T(8,128)(2,1)S(1)}, bf16[320,704]{1,0:T(8,128)(2,1)S(1)}, u32[]{:S(2)}, u32[]{:S(2)}) collective-permute-start(bf16[320,704]{1,0:T(8,128)(2,1)S(1)} %pad_maximum_fusion.1), channel_id=1, source_target_pairs={{0,130},{1,131},{4,134},{5,135},{8,138},{9,139},{12,142},{13,143},... | collective-permute-start | bytes 1351688 | tf_op jit(solution)/shard_map/ppermute | solution.py:40
  38.4 20.4 %collective-permute-start.16 = (f32[64,128]{1,0:T(8,128)S(1)}, f32[64,128]{1,0:T(8,128)S(1)}, u32[]{:S(2)}, u32[]{:S(2)}) collective-permute-start(f32[64,128]{1,0:T(8,128)S(1)} %bitcast.21), channel_id=1, source_target_pairs={{0,1},{1,0},{4,5},{5,4},{8,9},{9,8},{12,13},{13,12},{16,17},{17,16... | collective-permute-start | bytes 98312 | tf_op jit(solution)/shard_map/ppermute | solution.py:40
  64.1 5.6 %collective-permute-start.19 = (f32[2,16,256]{2,1,0:T(8,128)S(1)}, f32[2,16,256]{2,1,0:T(8,128)S(1)}, u32[]{:S(2)}, u32[]{:S(2)}) collective-permute-start(f32[2,16,256]{2,1,0:T(8,128)S(1)} %get-tuple-element.74), channel_id=1, source_target_pairs={{0,96},{1,97},{4,100},{5,101},{8,104},{9,105},{12,108},{13,109},{1... | collective-permute-start | bytes 98312 | tf_op jit(solution)/shard_map/ppermute | solution.py:40
  73.0 10.9 %collective-permute-start.20 = (bf16[336,256]{1,0:T(8,128)(2,1)S(1)}, bf16[336,256]{1,0:T(8,128)(2,1)S(1)}, u32[]{:S(2)}, u32[]{:S(2)}) collective-permute-start(bf16[336,256]{1,0:T(8,128)(2,1)S(1)} %get-tuple-element.76), channel_id=1, source_target_pairs={{0,192},{1,193},{4,196},{5,197},{8,200},{9,201},{12,204},{13,205},... | collective-permute-start | bytes 516104 | tf_op jit(solution)/shard_map/ppermute | solution.py:40
  77.2 8.4 %collective-permute-start.21 = (bf16[336,256]{1,0:T(8,128)(2,1)S(1)}, bf16[336,256]{1,0:T(8,128)(2,1)S(1)}, u32[]{:S(2)}, u32[]{:S(2)}) collective-permute-start(bf16[336,256]{1,0:T(8,128)(2,1)S(1)} %get-tuple-element.77), channel_id=1, source_target_pairs={{0,64},{1,65},{4,68},{5,69},{8,72},{9,73},{12,76},{13,77},{16,80},... | collective-permute-start | bytes 516104 | tf_op jit(solution)/shard_map/ppermute | solution.py:40
  78.9 7.5 %collective-permute-start.22 = (bf16[336,256]{1,0:T(8,128)(2,1)S(1)}, bf16[336,256]{1,0:T(8,128)(2,1)S(1)}, u32[]{:S(2)}, u32[]{:S(2)}) collective-permute-start(bf16[336,256]{1,0:T(8,128)(2,1)S(1)} %get-tuple-element.78), channel_id=1, source_target_pairs={{0,128},{1,129},{4,132},{5,133},{8,136},{9,137},{12,140},{13,141},... | collective-permute-start | bytes 516104 | tf_op jit(solution)/shard_map/ppermute | solution.py:40
  94.3 5.5 %collective-permute-start.23 = (f32[80,128]{1,0:T(8,128)S(1)}, f32[80,128]{1,0:T(8,128)S(1)}, u32[]{:S(2)}, u32[]{:S(2)}) collective-permute-start(f32[80,128]{1,0:T(8,128)S(1)} %get-tuple-element.81), channel_id=1, source_target_pairs={{0,1},{1,0},{4,5},{5,4},{8,9},{9,8},{12,13},{13,12},{16,17},{17,16... | collective-permute-start | bytes 122888 | tf_op jit(solution)/shard_map/ppermute | solution.py:40
  94.3 15.7 %all-to-all-start = ((bf16[16,32,128]{2,1,0:T(8,128)(2,1)}), bf16[16,32,128]{2,1,0:T(8,128)(2,1)S(1)}, u32[]{:S(2)}, u32[]{:S(2)}) async-start(bf16[16,32,128]{2,1,0:T(8,128)(2,1)} %get-tuple-element.79), calls=%async_computation | async-start | bytes 262144 | tf_op jit(solution)/shard_map/all_to_all | solution.py:533
  110.1 5.5 %collective-permute-start.24 = (bf16[112,128]{1,0:T(8,128)(2,1)S(1)}, bf16[112,128]{1,0:T(8,128)(2,1)S(1)}, u32[]{:S(2)}, u32[]{:S(2)}) collective-permute-start(bf16[112,128]{1,0:T(8,128)(2,1)S(1)} %pad_maximum_fusion.3), channel_id=1, source_target_pairs={{0,128},{1,129},{4,132},{5,133},{8,136},{9,137},{12,140},{13,141},... | collective-permute-start | bytes 86024 | tf_op jit(solution)/shard_map/ppermute | solution.py:40
  115.5 5.2 %collective-permute-start.25 = (bf16[224,128]{1,0:T(8,128)(2,1)S(1)}, bf16[224,128]{1,0:T(8,128)(2,1)S(1)}, u32[]{:S(2)}, u32[]{:S(2)}) collective-permute-start(bf16[224,128]{1,0:T(8,128)(2,1)S(1)} %pad_maximum_fusion.2.p0), channel_id=1, source_target_pairs={{0,32},{1,33},{4,36},{5,37},{8,40},{9,41},{12,44},{13,45},{16,48},... | collective-permute-start | bytes 172040 | tf_op jit(solution)/shard_map/ppermute | solution.py:40
  116.0 6.9 %collective-permute-start.26 = (bf16[224,128]{1,0:T(8,128)(2,1)S(1)}, bf16[224,128]{1,0:T(8,128)(2,1)S(1)}, u32[]{:S(2)}, u32[]{:S(2)}) collective-permute-start(bf16[224,128]{1,0:T(8,128)(2,1)S(1)} %pad_maximum_fusion.2.p0), channel_id=1, source_target_pairs={{0,64},{1,65},{4,68},{5,69},{8,72},{9,73},{12,76},{13,77},{16,80},... | collective-permute-start | bytes 172040 | tf_op jit(solution)/shard_map/ppermute | solution.py:40
  (8 other events, 73.9 us)

commit v14 on v13

--- a/solution.py
+++ b/solution.py
@@ -441,17 +441,17 @@
 PART = 7 * UNIT
 
 
-def finish_kernel(meta, p0, p1, p2, p3, div, weight, key, held):
+def finish_kernel(meta, *refs):
+    parts, (div, weight, key, held) = refs[:8], refs[8:]
     quarter = meta[4]
-    for r, pair in enumerate((p0, p1, p2, p3)):
-        held[r] = pair[...]
+    for r, part in enumerate(parts):
+        held[r] = part[...]
     x, yhi = (quarter & 1) * 2 + meta[3], quarter >> 1
     rows = jnp.zeros((PART - 2 * UNIT, 128), jnp.float32)
     rest = [jnp.zeros((UNIT, DI), jnp.float32)] * 2
     for y in range(2):
         for k in range(4):
-            at = pl.ds(pl.multiple_of((yhi ^ y) * PART, UNIT), PART)
-            part = held[(x - k) & 3, at, :].astype(jnp.float32)
+            part = held[(yhi ^ y) * 4 + ((x - k) & 3)].astype(jnp.float32)
             rows = rows + part[2 * UNIT :]
             half = k & 1
             first = half * HALF + (y * 2 + (k >> 1)) * UNIT
@@ -463,20 +463,20 @@
     div[...] = rows[NI : NI + 1] + rows[NI + 8 : NI + 9]
 
 
-def finish_call(meta, *pairs):
+def finish_call(meta, *parts):
     return pl.pallas_call(
         finish_kernel,
         grid_spec=pltpu.PrefetchScalarGridSpec(
             num_scalar_prefetch=1,
             grid=(1,),
-            in_specs=[HERE] * 4,
+            in_specs=[HERE] * 8,
             out_specs=[HERE] * 3,
-            scratch_shapes=[pltpu.VMEM((4, 2 * PART, 128), jnp.bfloat16)],
+            scratch_shapes=[pltpu.VMEM((8, PART, 128), jnp.bfloat16)],
         ),
         out_shape=[jax.ShapeDtypeStruct((rows, 128), jnp.float32) for rows in (1, NI, 2 * HALF)],
         compiler_params=pltpu.CompilerParams(vmem_limit_bytes=2 << 20),
         name="finish",
-    )(meta, *in_vmem(*pairs))
+    )(meta, *in_vmem(*parts))
 
 
 def after(value, *others):
@@ -533,8 +533,8 @@
     kg = lax.all_to_all(kg, ("z", "ylo"), 0, 0, tiled=True)
     kg = jnp.sum(kg.astype(jnp.float32), axis=0)
     part = jnp.concatenate([kg, tail]).astype(jnp.bfloat16)
-    pair = jnp.concatenate([part, shift(part, dy=2)])
-    div, weight, key_grad = finish_call(meta, pair, *(shift(pair, dx=dx) for dx in (1, 2, 3)))
+    moves = [(dx, dy) for dy in (0, 2) for dx in range(4)][1:]
+    div, weight, key_grad = finish_call(meta, part, *(shift(part, dx=dx, dy=dy) for dx, dy in moves))
     return div.reshape(128), weight.T, key_grad
 
 

time: 126 us -> 132 us (1.048); the launches traced: 126 us -> 131 us
  starting transfers between devices: 42.9 us -> 49.2 us
  waiting for transfers between devices: 40.4 us -> 38.9 us
    ppermute x28 -> x31, starting transfers between devices: 37.4 us -> 43.7 us  [shift(): return lax.ppermute(value, ALL, pairs)]
    ppermute x28 -> x31, waiting for transfers between devices: 30.2 us -> 28.7 us  [shift(): return lax.ppermute(value, ALL, pairs)]
  transfers between devices with their start and end apart: 29 -> 32, of which waited for: 18 -> 16; matrix products, arithmetic and copies ran while one was open for 4% -> 4% of each run, Pallas kernels for 15% -> 14%
where the time goes in v14:
time: 132 us; the launch traced here: 131 us
  starting transfers between devices  49.2 us (37%)
  waiting for transfers between devices  38.9 us (29%)
  Pallas kernels  34.3 us (26%)
  local copies, waits for them, and re-layouts  5.5 us (4%)
  between operations  1.5 us (1%)
    ppermute x31, starting transfers between devices, shift(): return lax.ppermute(value, ALL, pairs)  43.7 us
    ppermute x31, waiting for transfers between devices, shift(): return lax.ppermute(value, ALL, pairs)  28.7 us
    pallas_call x2, Pallas kernels, score_call(): pl.pallas_call(lambda *refs: score_kernel(chunk, spans, *refs), grid_spec...  18.1 us
    all_to_all x1, waiting for transfers between devices, body(): kg = lax.all_to_all(kg, ('z', 'ylo'), 0, 0, tiled=True)  10.2 us
    pallas_call x1, Pallas kernels, backward_call(): pl.pallas_call(backward_kernel, grid_spec=pltpu.PrefetchScalarGridSpec(nu...  7.81 us
    all_to_all x1, starting transfers between devices, body(): kg = lax.all_to_all(kg, ('z', 'ylo'), 0, 0, tiled=True)  5.47 us
    pallas_call x1, Pallas kernels, forward_call(): pl.pallas_call(forward_kernel, grid_spec=pltpu.PrefetchScalarGridSpec(num...  3.86 us
    pallas_call x1, Pallas kernels, head_sum_call(): pl.pallas_call(head_sum_kernel, grid_spec=pltpu.PrefetchScalarGridSpec(nu...  3.29 us
  transfers between devices with their start and end apart: 32, of which 16 were waited for; matrix products, arithmetic and copies ran while one was open for 4% of the time, Pallas kernels for 14%

profile of v14, /device:TPU:2, one launch (start us, length us, event | category | flops | bytes accessed | tf_op | source)
XLA Modules:
  0.0 130.7 jit_solution(1672361152994865146)
XLA Ops:
  1.8 1.9 %collective-permute-start = (bf16[80,704]{1,0:T(8,128)(2,1)S(1)}, bf16[80,704]{1,0:T(8,128)(2,1)S(1)}, u32[]{:S(2)}, u32[]{:S(2)}) collective-permute-start(bf16[80,704]{1,0:T(8,128)(2,1)S(1)} %fusion.refs_1_), channel_id=1, source_target_pairs={{0,4},{1,5},{4,8},{5,9},{8,12},{9,13},{12,16},{13,17},{16,20},{17,... | collective-permute-start | bytes 337928 | tf_op jit(solution)/shard_map/ppermute | solution.py:40
  3.7 4.0 %collective-permute-start.1 = (bf16[80,704]{1,0:T(8,128)(2,1)S(1)}, bf16[80,704]{1,0:T(8,128)(2,1)S(1)}, u32[]{:S(2)}, u32[]{:S(2)}) collective-permute-start(bf16[80,704]{1,0:T(8,128)(2,1)S(1)} %fusion.refs_1_), channel_id=1, source_target_pairs={{0,28},{1,29},{4,0},{5,1},{8,4},{9,5},{12,8},{13,9},{16,12},{17,13... | collective-permute-start | bytes 337928 | tf_op jit(solution)/shard_map/ppermute | solution.py:40
  7.7 2.4 %fusion.2 = (bf16[4,576,128]{2,1,0:T(8,128)(2,1)}, bf16[4,576,128]{2,1,0:T(8,128)(2,1)}) fusion(bf16[8,576,128]{2,1,0:T(8,128)(2,1)} %bitcast.17), kind=kLoop, calls=%fused_computation.12 | loop fusion | bytes 2359296 | tf_op jit(solution)/shard_map/slice | solution.py:502
  13.7 3.2 %collective-permute-start.3 = (bf16[80,704]{1,0:T(8,128)(2,1)S(1)}, bf16[80,704]{1,0:T(8,128)(2,1)S(1)}, u32[]{:S(2)}, u32[]{:S(2)}) collective-permute-start(bf16[80,704]{1,0:T(8,128)(2,1)S(1)} %collective-permute-done.1.refs_3_), channel_id=1, source_target_pairs={{0,28},{1,29},{4,0},{5,1},{8,4},{9,5},{12,8},{13,9},{16,12},{17,13... | collective-permute-start | bytes 337928 | tf_op jit(solution)/shard_map/ppermute | solution.py:40
  17.0 2.8 %collective-permute-done.2.refs_4_ = bf16[80,704]{1,0:T(8,128)(2,1)S(1)} collective-permute-done((bf16[80,704]{1,0:T(8,128)(2,1)S(1)}, bf16[80,704]{1,0:T(8,128)(2,1)S(1)}, u32[]{:S(2)}, u32[]{:S(2)}) %collective-permute-start.2) | collective-permute-done | bytes 112672 | tf_op jit(solution)/shard_map/ppermute | solution.py:40
  19.8 2.6 %collective-permute-start.5 = (bf16[80,704]{1,0:T(8,128)(2,1)S(1)}, bf16[80,704]{1,0:T(8,128)(2,1)S(1)}, u32[]{:S(2)}, u32[]{:S(2)}) collective-permute-start(bf16[80,704]{1,0:T(8,128)(2,1)S(1)} %collective-permute-done.2.refs_4_), channel_id=1, source_target_pairs={{0,4},{1,5},{4,8},{5,9},{8,12},{9,13},{12,16},{13,17},{16,20},{17,... | collective-permute-start | bytes 337928 | tf_op jit(solution)/shard_map/ppermute | solution.py:40
  27.9 2.0 %collective-permute-start.10 = (bf16[80,704]{1,0:T(8,128)(2,1)S(1)}, bf16[80,704]{1,0:T(8,128)(2,1)S(1)}, u32[]{:S(2)}, u32[]{:S(2)}) collective-permute-start(bf16[80,704]{1,0:T(8,128)(2,1)S(1)} %collective-permute-done.5.refs_6_), channel_id=1, source_target_pairs={{0,4},{1,5},{4,8},{5,9},{8,12},{9,13},{12,16},{13,17},{16,20},{17,... | collective-permute-start | bytes 337928 | tf_op jit(solution)/shard_map/ppermute | solution.py:40
  29.9 2.9 %copy.13 = bf16[128,64,128]{2,0,1:T(8,128)(2,1)S(1)} copy(bf16[128,64,128]{2,1,0:T(8,128)(2,1)} %param.9) | data formatting | bytes 4194304 | tf_op args[2]
  36.5 1.9 %collective-permute-start.11 = (bf16[320,704]{1,0:T(8,128)(2,1)S(1)}, bf16[320,704]{1,0:T(8,128)(2,1)S(1)}, u32[]{:S(2)}, u32[]{:S(2)}) collective-permute-start(bf16[320,704]{1,0:T(8,128)(2,1)S(1)} %pad_maximum_fusion.1), channel_id=1, source_target_pairs={{0,130},{1,131},{4,134},{5,135},{8,138},{9,139},{12,142},{13,143},... | collective-permute-start | bytes 1351688 | tf_op jit(solution)/shard_map/ppermute | solution.py:40
  38.5 9.5 %scores.2 = (bf16[16,1280,256]{2,1,0:T(8,128)(2,1)S(1)}, f32[16,256]{1,0:T(8,128)S(1)}, f32[16,256]{1,0:T(8,128)S(1)}, bf16[320,128]{1,0:T(8,128)(2,1)S(1)}) custom-call(s32[5]{0:T(128)S(1)} %stack.23.refs_0_.meta, bf16[80,704]{1,0:T(8,128)(2,1)S(1)} %fusion.refs_1_, bf16[80,704]{1,0:T(8,128)(2,1)S(1)} %collective-permute-done.refs_2_, ...), custom_call_target="tpu_custom_call" | custom-call | flops 6039797760 | bytes 5242880 | tf_op jit(solution)/shard_map/scores/pallas_call | solution.py:158
  50.1 8.7 %scores.3 = (bf16[16,1280,256]{2,1,0:T(8,128)(2,1)S(1)}, f32[16,256]{1,0:T(8,128)S(1)}, f32[16,256]{1,0:T(8,128)S(1)}, bf16[320,128]{1,0:T(8,128)(2,1)S(1)}) custom-call(s32[5]{0:T(128)S(1)} %stack.23.refs_0_.meta, bf16[320,704]{1,0:T(8,128)(2,1)S(1)} %collective-permute-done.4.refs_1_, ...), custom_call_target="tpu_custom_call", output_to_operand_aliasing={{0}: (3, {})} | custom-call | flops 6039797760 | bytes 5242880 | tf_op jit(solution)/shard_map/scores/pallas_call | solution.py:158
  58.8 3.9 %index_forward.1 = (f32[320,256]{1,0:T(8,128)S(1)}, f32[2,24,256]{2,1,0:T(8,128)S(1)}, f32[2,24,256]{2,1,0:T(8,128)S(1)}) custom-call(s32[5]{0:T(128)S(1)} %stack.23.refs_0_.meta, bf16[320,128]{1,0:T(8,128)(2,1)S(1)} %get-tuple-element.60.keys, f32[16,256]{1,0:T(8,128)S(1)} %get-tuple-element.61.m0, f32[16,256]{1,0:T(8,128)S(1)} %get-tuple-element.62.l0, ...), custom_call_target="tpu_custom_call" | custom-call | flops 1342177280 | bytes 5242880 | tf_op jit(solution)/shard_map/index_forward/pallas_call | solution.py:334
  66.1 3.4 %collective-permute-done.18.up = f32[2,8,256]{2,1,0:T(8,128)S(1)} collective-permute-done((f32[2,8,256]{2,1,0:T(8,128)S(1)}, f32[2,8,256]{2,1,0:T(8,128)S(1)}, u32[]{:S(2)}, u32[]{:S(2)}) %collective-permute-start.18) | collective-permute-done | bytes 16416 | tf_op jit(solution)/shard_map/ppermute | solution.py:40
  69.5 3.3 %head_sum.1 = (bf16[336,256]{1,0:T(8,128)(2,1)S(1)}, bf16[336,256]{1,0:T(8,128)(2,1)S(1)}, bf16[336,256]{1,0:T(8,128)(2,1)S(1)}, bf16[336,256]{1,0:T(8,128)(2,1)S(1)}) custom-call(s32[5]{0:T(128)S(1)} %stack.23.refs_0_.meta, bf16[16,1280,256]{2,1,0:T(8,128)(2,1)S(1)} %get-tuple-element.69.e_ref, f32[16,256]{1,0:T(8,128)S(1)} %get-tuple-element.61.m0, ...), custom_call_target="tpu_custom_call" | custom-call | bytes 11534336 | tf_op jit(solution)/shard_map/head_sum/pallas_call | solution.py:234
  72.8 4.2 %collective-permute-start.20 = (bf16[336,256]{1,0:T(8,128)(2,1)S(1)}, bf16[336,256]{1,0:T(8,128)(2,1)S(1)}, u32[]{:S(2)}, u32[]{:S(2)}) collective-permute-start(bf16[336,256]{1,0:T(8,128)(2,1)S(1)} %get-tuple-element.76), channel_id=1, source_target_pairs={{0,192},{1,193},{4,196},{5,197},{8,200},{9,201},{12,204},{13,205},... | collective-permute-start | bytes 516104 | tf_op jit(solution)/shard_map/ppermute | solution.py:40
  79.4 4.4 %collective-permute-done.20.t1 = bf16[336,256]{1,0:T(8,128)(2,1)S(1)} collective-permute-done((bf16[336,256]{1,0:T(8,128)(2,1)S(1)}, bf16[336,256]{1,0:T(8,128)(2,1)S(1)}, u32[]{:S(2)}, u32[]{:S(2)}) %collective-permute-start.20) | collective-permute-done | bytes 172064 | tf_op jit(solution)/shard_map/ppermute | solution.py:40
  86.3 7.8 %index_backward.1 = (f32[80,128]{1,0:T(8,128)S(1)}, f32[80,128]{1,0:T(8,128)S(1)}, bf16[16,32,128]{2,1,0:T(8,128)(2,1)}) custom-call(s32[5]{0:T(128)S(1)} %stack.23.refs_0_.meta, bf16[320,128]{1,0:T(8,128)(2,1)S(1)} %get-tuple-element.60.keys, f32[320,256]{1,0:T(8,128)S(1)} %get-tuple-element.68.logits, bf16[336,256]{1,0:T(8,128)(2,1)S(1)} %get-tuple-element.75.t0, ...), custom_call_target="tpu_custom_call" | custom-call | flops 2684354560 | bytes 6291456 | tf_op jit(solution)/shard_map/index_backward/pallas_call | solution.py:416
  94.1 5.5 %all-to-all-start = ((bf16[16,32,128]{2,1,0:T(8,128)(2,1)}), bf16[16,32,128]{2,1,0:T(8,128)(2,1)S(1)}, u32[]{:S(2)}, u32[]{:S(2)}) async-start(bf16[16,32,128]{2,1,0:T(8,128)(2,1)} %get-tuple-element.79), calls=%async_computation | async-start | bytes 262144 | tf_op jit(solution)/shard_map/all_to_all | solution.py:533
  99.7 10.2 %all-to-all-done = bf16[16,32,128]{2,1,0:T(8,128)(2,1)S(1)} async-done(((bf16[16,32,128]{2,1,0:T(8,128)(2,1)}), bf16[16,32,128]{2,1,0:T(8,128)(2,1)S(1)}, u32[]{:S(2)}, u32[]{:S(2)}) %all-to-all-start) | async-done | bytes 131104 | tf_op jit(solution)/shard_map/all_to_all | solution.py:533
  110.4 4.7 %collective-permute-start.25 = (bf16[112,128]{1,0:T(8,128)(2,1)S(1)}, bf16[112,128]{1,0:T(8,128)(2,1)S(1)}, u32[]{:S(2)}, u32[]{:S(2)}) collective-permute-start(bf16[112,128]{1,0:T(8,128)(2,1)S(1)} %pad_maximum_fusion.2.refs_0_), channel_id=1, source_target_pairs={{0,64},{1,65},{4,68},{5,69},{8,72},{9,73},{12,76},{13,77},{16,80},... | collective-permute-start | bytes 86024 | tf_op jit(solution)/shard_map/ppermute | solution.py:40
  115.1 2.4 %collective-permute-start.27 = (bf16[112,128]{1,0:T(8,128)(2,1)S(1)}, bf16[112,128]{1,0:T(8,128)(2,1)S(1)}, u32[]{:S(2)}, u32[]{:S(2)}) collective-permute-start(bf16[112,128]{1,0:T(8,128)(2,1)S(1)} %pad_maximum_fusion.2.refs_0_), channel_id=1, source_target_pairs={{0,128},{1,129},{4,132},{5,133},{8,136},{9,137},{12,140},{13,141},... | collective-permute-start | bytes 86024 | tf_op jit(solution)/shard_map/ppermute | solution.py:40
  117.6 2.5 %collective-permute-start.28 = (bf16[112,128]{1,0:T(8,128)(2,1)S(1)}, bf16[112,128]{1,0:T(8,128)(2,1)S(1)}, u32[]{:S(2)}, u32[]{:S(2)}) collective-permute-start(bf16[112,128]{1,0:T(8,128)(2,1)S(1)} %pad_maximum_fusion.2.refs_0_), channel_id=1, source_target_pairs={{0,160},{1,161},{4,164},{5,165},{8,168},{9,169},{12,172},{13,173},... | collective-permute-start | bytes 86024 | tf_op jit(solution)/shard_map/ppermute | solution.py:40
  120.1 3.1 %collective-permute-start.29 = (bf16[112,128]{1,0:T(8,128)(2,1)S(1)}, bf16[112,128]{1,0:T(8,128)(2,1)S(1)}, u32[]{:S(2)}, u32[]{:S(2)}) collective-permute-start(bf16[112,128]{1,0:T(8,128)(2,1)S(1)} %pad_maximum_fusion.2.refs_0_), channel_id=1, source_target_pairs={{0,192},{1,193},{4,196},{5,197},{8,200},{9,201},{12,204},{13,205},... | collective-permute-start | bytes 86024 | tf_op jit(solution)/shard_map/ppermute | solution.py:40
  124.1 3.8 %collective-permute-done.29.refs_6_ = bf16[112,128]{1,0:T(8,128)(2,1)S(1)} collective-permute-done((bf16[112,128]{1,0:T(8,128)(2,1)S(1)}, bf16[112,128]{1,0:T(8,128)(2,1)S(1)}, u32[]{:S(2)}, u32[]{:S(2)}) %collective-permute-start.29) | collective-permute-done | bytes 28704 | tf_op jit(solution)/shard_map/ppermute | solution.py:40
  (67 shorter events, 28.0 us)
Async XLA Ops:
  1.8 9.2 %collective-permute-start = (bf16[80,704]{1,0:T(8,128)(2,1)S(1)}, bf16[80,704]{1,0:T(8,128)(2,1)S(1)}, u32[]{:S(2)}, u32[]{:S(2)}) collective-permute-start(bf16[80,704]{1,0:T(8,128)(2,1)S(1)} %fusion.refs_1_), channel_id=1, source_target_pairs={{0,4},{1,5},{4,8},{5,9},{8,12},{9,13},{12,16},{13,17},{16,20},{17,... | collective-permute-start | bytes 337928 | tf_op jit(solution)/shard_map/ppermute | solution.py:40
  3.7 7.3 %collective-permute-start.1 = (bf16[80,704]{1,0:T(8,128)(2,1)S(1)}, bf16[80,704]{1,0:T(8,128)(2,1)S(1)}, u32[]{:S(2)}, u32[]{:S(2)}) collective-permute-start(bf16[80,704]{1,0:T(8,128)(2,1)S(1)} %fusion.refs_1_), channel_id=1, source_target_pairs={{0,28},{1,29},{4,0},{5,1},{8,4},{9,5},{12,8},{13,9},{16,12},{17,13... | collective-permute-start | bytes 337928 | tf_op jit(solution)/shard_map/ppermute | solution.py:40
  11.0 16.3 %collective-permute-start.7 = (bf16[4,576,128]{2,1,0:T(8,128)(2,1)}, bf16[4,576,128]{2,1,0:T(8,128)(2,1)S(1)}, u32[]{:S(2)}, u32[]{:S(2)}) collective-permute-start(bf16[4,576,128]{2,1,0:T(8,128)(2,1)} %get-tuple-element.50), channel_id=1, source_target_pairs={{0,32},{1,33},{4,36},{5,37},{8,40},{9,41},{12,44},{13,45},{16,48},... | collective-permute-start | bytes 1769480 | tf_op jit(solution)/shard_map/ppermute | solution.py:40
  12.5 14.8 %collective-permute-start.8 = (bf16[4,576,128]{2,1,0:T(8,128)(2,1)}, bf16[4,576,128]{2,1,0:T(8,128)(2,1)S(1)}, u32[]{:S(2)}, u32[]{:S(2)}) collective-permute-start(bf16[4,576,128]{2,1,0:T(8,128)(2,1)} %get-tuple-element.51), channel_id=1, source_target_pairs={{0,96},{1,97},{4,100},{5,101},{8,104},{9,105},{12,108},{13,109},{1... | collective-permute-start | bytes 1769480 | tf_op jit(solution)/shard_map/ppermute | solution.py:40
  13.6 6.2 %collective-permute-start.2 = (bf16[80,704]{1,0:T(8,128)(2,1)S(1)}, bf16[80,704]{1,0:T(8,128)(2,1)S(1)}, u32[]{:S(2)}, u32[]{:S(2)}) collective-permute-start(bf16[80,704]{1,0:T(8,128)(2,1)S(1)} %collective-permute-done.refs_2_), channel_id=1, source_target_pairs={{0,4},{1,5},{4,8},{5,9},{8,12},{9,13},{12,16},{13,17},{16,20},{17,... | collective-permute-start | bytes 337928 | tf_op jit(solution)/shard_map/ppermute | solution.py:40
  27.3 7.5 %collective-permute-start.13 = (bf16[4,576,128]{2,1,0:T(8,128)(2,1)S(1)}, bf16[4,576,128]{2,1,0:T(8,128)(2,1)S(1)}, u32[]{:S(2)}, u32[]{:S(2)}) collective-permute-start(bf16[4,576,128]{2,1,0:T(8,128)(2,1)S(1)} %collective-permute-done.7.refs_11_.refs_7_), channel_id=1, source_target_pairs={{0,1},{1,0},{4,5},{5,4},{8,9},{9,8},{12,13},{13,12},{16,17},{17,16... | collective-permute-start | bytes 1769480 | tf_op jit(solution)/shard_map/ppermute | solution.py:40
  27.3 7.5 %collective-permute-start.14 = (bf16[4,576,128]{2,1,0:T(8,128)(2,1)S(1)}, bf16[4,576,128]{2,1,0:T(8,128)(2,1)S(1)}, u32[]{:S(2)}, u32[]{:S(2)}) collective-permute-start(bf16[4,576,128]{2,1,0:T(8,128)(2,1)S(1)} %collective-permute-done.8.refs_13_.refs_9_), channel_id=1, source_target_pairs={{0,1},{1,0},{4,5},{5,4},{8,9},{9,8},{12,13},{13,12},{16,17},{17,16... | collective-permute-start | bytes 1769480 | tf_op jit(solution)/shard_map/ppermute | solution.py:40
  27.8 10.7 %collective-permute-start.12 = (bf16[8,576,128]{2,1,0:T(8,128)(2,1)S(1)}, bf16[8,576,128]{2,1,0:T(8,128)(2,1)S(1)}, u32[]{:S(2)}, u32[]{:S(2)}) collective-permute-start(bf16[8,576,128]{2,1,0:T(8,128)(2,1)S(1)} %bitcast.18), channel_id=1, source_target_pairs={{0,1},{1,0},{4,5},{5,4},{8,9},{9,8},{12,13},{13,12},{16,17},{17,16... | collective-permute-start | bytes 3538952 | tf_op jit(solution)/shard_map/ppermute | solution.py:40
  27.9 6.9 %collective-permute-start.10 = (bf16[80,704]{1,0:T(8,128)(2,1)S(1)}, bf16[80,704]{1,0:T(8,128)(2,1)S(1)}, u32[]{:S(2)}, u32[]{:S(2)}) collective-permute-start(bf16[80,704]{1,0:T(8,128)(2,1)S(1)} %collective-permute-done.5.refs_6_), channel_id=1, source_target_pairs={{0,4},{1,5},{4,8},{5,9},{8,12},{9,13},{12,16},{13,17},{16,20},{17,... | collective-permute-start | bytes 337928 | tf_op jit(solution)/shard_map/ppermute | solution.py:40
  34.7 24.0 %collective-permute-start.15 = (bf16[64,128,128]{2,1,0:T(8,128)(2,1)S(1)}, bf16[64,128,128]{2,1,0:T(8,128)(2,1)S(1)}, u32[]{:S(2)}, u32[]{:S(2)}) collective-permute-start(bf16[64,128,128]{2,1,0:T(8,128)(2,1)S(1)} %bitcast.14), channel_id=1, source_target_pairs={{0,1},{1,0},{4,5},{5,4},{8,9},{9,8},{12,13},{13,12},{16,17},{17,16... | collective-permute-start | bytes 6291464 | tf_op jit(solution)/shard_map/ppermute | solution.py:40
  34.8 15.0 %collective-permute-start.4 = (bf16[320,704]{1,0:T(8,128)(2,1)S(1)}, bf16[320,704]{1,0:T(8,128)(2,1)S(1)}, u32[]{:S(2)}, u32[]{:S(2)}) collective-permute-start(bf16[320,704]{1,0:T(8,128)(2,1)S(1)} %pad_maximum_fusion), channel_id=1, source_target_pairs={{0,2},{1,3},{4,6},{5,7},{8,10},{9,11},{12,14},{13,15},{16,18},{17,... | collective-permute-start | bytes 1351688 | tf_op jit(solution)/shard_map/ppermute | solution.py:40
  36.5 13.6 %collective-permute-start.11 = (bf16[320,704]{1,0:T(8,128)(2,1)S(1)}, bf16[320,704]{1,0:T(8,128)(2,1)S(1)}, u32[]{:S(2)}, u32[]{:S(2)}) collective-permute-start(bf16[320,704]{1,0:T(8,128)(2,1)S(1)} %pad_maximum_fusion.1), channel_id=1, source_target_pairs={{0,130},{1,131},{4,134},{5,135},{8,138},{9,139},{12,142},{13,143},... | collective-permute-start | bytes 1351688 | tf_op jit(solution)/shard_map/ppermute | solution.py:40
  38.4 20.3 %collective-permute-start.16 = (f32[64,128]{1,0:T(8,128)S(1)}, f32[64,128]{1,0:T(8,128)S(1)}, u32[]{:S(2)}, u32[]{:S(2)}) collective-permute-start(f32[64,128]{1,0:T(8,128)S(1)} %bitcast.21), channel_id=1, source_target_pairs={{0,1},{1,0},{4,5},{5,4},{8,9},{9,8},{12,13},{13,12},{16,17},{17,16... | collective-permute-start | bytes 98312 | tf_op jit(solution)/shard_map/ppermute | solution.py:40
  72.8 11.0 %collective-permute-start.20 = (bf16[336,256]{1,0:T(8,128)(2,1)S(1)}, bf16[336,256]{1,0:T(8,128)(2,1)S(1)}, u32[]{:S(2)}, u32[]{:S(2)}) collective-permute-start(bf16[336,256]{1,0:T(8,128)(2,1)S(1)} %get-tuple-element.76), channel_id=1, source_target_pairs={{0,192},{1,193},{4,196},{5,197},{8,200},{9,201},{12,204},{13,205},... | collective-permute-start | bytes 516104 | tf_op jit(solution)/shard_map/ppermute | solution.py:40
  77.0 8.4 %collective-permute-start.21 = (bf16[336,256]{1,0:T(8,128)(2,1)S(1)}, bf16[336,256]{1,0:T(8,128)(2,1)S(1)}, u32[]{:S(2)}, u32[]{:S(2)}) collective-permute-start(bf16[336,256]{1,0:T(8,128)(2,1)S(1)} %get-tuple-element.77), channel_id=1, source_target_pairs={{0,64},{1,65},{4,68},{5,69},{8,72},{9,73},{12,76},{13,77},{16,80},... | collective-permute-start | bytes 516104 | tf_op jit(solution)/shard_map/ppermute | solution.py:40
  78.8 7.5 %collective-permute-start.22 = (bf16[336,256]{1,0:T(8,128)(2,1)S(1)}, bf16[336,256]{1,0:T(8,128)(2,1)S(1)}, u32[]{:S(2)}, u32[]{:S(2)}) collective-permute-start(bf16[336,256]{1,0:T(8,128)(2,1)S(1)} %get-tuple-element.78), channel_id=1, source_target_pairs={{0,128},{1,129},{4,132},{5,133},{8,136},{9,137},{12,140},{13,141},... | collective-permute-start | bytes 516104 | tf_op jit(solution)/shard_map/ppermute | solution.py:40
  94.1 15.7 %all-to-all-start = ((bf16[16,32,128]{2,1,0:T(8,128)(2,1)}), bf16[16,32,128]{2,1,0:T(8,128)(2,1)S(1)}, u32[]{:S(2)}, u32[]{:S(2)}) async-start(bf16[16,32,128]{2,1,0:T(8,128)(2,1)} %get-tuple-element.79), calls=%async_computation | async-start | bytes 262144 | tf_op jit(solution)/shard_map/all_to_all | solution.py:533
  109.9 10.2 %collective-permute-start.24 = (bf16[112,128]{1,0:T(8,128)(2,1)S(1)}, bf16[112,128]{1,0:T(8,128)(2,1)S(1)}, u32[]{:S(2)}, u32[]{:S(2)}) collective-permute-start(bf16[112,128]{1,0:T(8,128)(2,1)S(1)} %pad_maximum_fusion.2.refs_0_), channel_id=1, source_target_pairs={{0,32},{1,33},{4,36},{5,37},{8,40},{9,41},{12,44},{13,45},{16,48},... | collective-permute-start | bytes 86024 | tf_op jit(solution)/shard_map/ppermute | solution.py:40
  110.4 12.8 %collective-permute-start.25 = (bf16[112,128]{1,0:T(8,128)(2,1)S(1)}, bf16[112,128]{1,0:T(8,128)(2,1)S(1)}, u32[]{:S(2)}, u32[]{:S(2)}) collective-permute-start(bf16[112,128]{1,0:T(8,128)(2,1)S(1)} %pad_maximum_fusion.2.refs_0_), channel_id=1, source_target_pairs={{0,64},{1,65},{4,68},{5,69},{8,72},{9,73},{12,76},{13,77},{16,80},... | collective-permute-start | bytes 86024 | tf_op jit(solution)/shard_map/ppermute | solution.py:40
  115.1 9.0 %collective-permute-start.26 = (bf16[112,128]{1,0:T(8,128)(2,1)S(1)}, bf16[112,128]{1,0:T(8,128)(2,1)S(1)}, u32[]{:S(2)}, u32[]{:S(2)}) collective-permute-start(bf16[112,128]{1,0:T(8,128)(2,1)S(1)} %pad_maximum_fusion.2.refs_0_), channel_id=1, source_target_pairs={{0,96},{1,97},{4,100},{5,101},{8,104},{9,105},{12,108},{13,109},{1... | collective-permute-start | bytes 86024 | tf_op jit(solution)/shard_map/ppermute | solution.py:40
  115.1 9.0 %collective-permute-start.27 = (bf16[112,128]{1,0:T(8,128)(2,1)S(1)}, bf16[112,128]{1,0:T(8,128)(2,1)S(1)}, u32[]{:S(2)}, u32[]{:S(2)}) collective-permute-start(bf16[112,128]{1,0:T(8,128)(2,1)S(1)} %pad_maximum_fusion.2.refs_0_), channel_id=1, source_target_pairs={{0,128},{1,129},{4,132},{5,133},{8,136},{9,137},{12,140},{13,141},... | collective-permute-start | bytes 86024 | tf_op jit(solution)/shard_map/ppermute | solution.py:40
  117.6 6.5 %collective-permute-start.28 = (bf16[112,128]{1,0:T(8,128)(2,1)S(1)}, bf16[112,128]{1,0:T(8,128)(2,1)S(1)}, u32[]{:S(2)}, u32[]{:S(2)}) collective-permute-start(bf16[112,128]{1,0:T(8,128)(2,1)S(1)} %pad_maximum_fusion.2.refs_0_), channel_id=1, source_target_pairs={{0,160},{1,161},{4,164},{5,165},{8,168},{9,169},{12,172},{13,173},... | collective-permute-start | bytes 86024 | tf_op jit(solution)/shard_map/ppermute | solution.py:40
  120.1 7.8 %collective-permute-start.29 = (bf16[112,128]{1,0:T(8,128)(2,1)S(1)}, bf16[112,128]{1,0:T(8,128)(2,1)S(1)}, u32[]{:S(2)}, u32[]{:S(2)}) collective-permute-start(bf16[112,128]{1,0:T(8,128)(2,1)S(1)} %pad_maximum_fusion.2.refs_0_), channel_id=1, source_target_pairs={{0,192},{1,193},{4,196},{5,197},{8,200},{9,201},{12,204},{13,205},... | collective-permute-start | bytes 86024 | tf_op jit(solution)/shard_map/ppermute | solution.py:40
  123.2 6.3 %collective-permute-start.30 = (bf16[112,128]{1,0:T(8,128)(2,1)S(1)}, bf16[112,128]{1,0:T(8,128)(2,1)S(1)}, u32[]{:S(2)}, u32[]{:S(2)}) collective-permute-start(bf16[112,128]{1,0:T(8,128)(2,1)S(1)} %pad_maximum_fusion.2.refs_0_), channel_id=1, source_target_pairs={{0,224},{1,225},{4,228},{5,229},{8,232},{9,233},{12,236},{13,237},... | collective-permute-start | bytes 86024 | tf_op jit(solution)/shard_map/ppermute | solution.py:40
  (11 other events, 93.0 us)

commit v15 on v13

--- a/solution.py
+++ b/solution.py
@@ -502,21 +502,21 @@
     f1, b1, left, right = lax.optimization_barrier((f1, b1, queries[:4], queries[4:]))
     left, right = shift(left, dx=1), shift(right, dx=3)
     f2, b2 = shift(f1, dz=1), shift(b1, dz=7)
+    y0 = shift(jnp.concatenate([own, f1, b1]), dy=1)
+    pb = swap_core(pa)
     f2, b2 = lax.optimization_barrier((f2, b2))
     f3, b3 = shift(f2, dz=1), shift(b2, dz=7)
-    pb = swap_core(pa)
-    f3, b3, left, right, pb = lax.optimization_barrier((f3, b3, left, right, pb))
+    f3, b3, left, right, pb, y0 = lax.optimization_barrier((f3, b3, left, right, pb, y0))
     f4 = shift(f3, dz=1)
+    left_far, right_far = swap_core(left), swap_core(right)
     f4, ia = lax.optimization_barrier((f4, index_queries.transpose(1, 0, 2)))
-    left_far, right_far = swap_core(left), swap_core(right)
-    y0, y1 = jnp.concatenate([own, f1, b1, f2]), jnp.concatenate([b2, f3, b3, f4])
-    y0, y1 = shift(y0, dy=1), shift(y1, dy=3)
+    y1, y2 = shift(jnp.concatenate([f2, b2]), dy=1), shift(jnp.concatenate([f3, b3, f4]), dy=3)
     ia, wa = lax.optimization_barrier((ia, wa, f4, left_far, right_far))[:2]
     ib, wb = swap_core(ia), swap_core(wa)
 
     sides = (queries, queries_far, left, left_far, right, right_far, pa, pb)
     exps, m0, l0, keys = score_call(meta, 0, [own, f1, b1, f2, b2, f3, b3, f4], [], *sides)
-    exps, m1, l1, keys = score_call(meta, 1, [y0, y1], in_vmem(exps, keys), *sides)
+    exps, m1, l1, keys = score_call(meta, 1, [y0, y1, y2], in_vmem(exps, keys), *sides)
 
     logits, ours, sent = forward_call(meta, keys, (m0, l0, m1, l1), ia, ib, pa, pb, wa, wb)
     here, up, down = pair_call(ours, swap_core(sent))

time: 126 us -> 126 us (level)
  waiting for transfers between devices: 40.4 us -> 37.5 us
  starting transfers between devices: 42.9 us -> 44.6 us
    ppermute x28 -> x29, waiting for transfers between devices: 30.2 us -> 27.3 us  [shift(): return lax.ppermute(value, ALL, pairs)]
    ppermute x28 -> x29, starting transfers between devices: 37.4 us -> 39.1 us  [shift(): return lax.ppermute(value, ALL, pairs)]
  transfers between devices with their start and end apart: 29 -> 30, of which waited for: 18 -> 15; matrix products, arithmetic and copies ran while one was open for 4% -> 5% of each run, Pallas kernels for 15% -> 15%
where the time goes in v15:
time: 126 us
  starting transfers between devices  44.6 us (35%)
  waiting for transfers between devices  37.5 us (30%)
  Pallas kernels  34.7 us (28%)
  local copies, waits for them, and re-layouts  5.5 us (4%)
  other arithmetic  1.99 us (2%)
  between operations  1.5 us (1%)
    ppermute x29, starting transfers between devices, shift(): return lax.ppermute(value, ALL, pairs)  39.1 us
    ppermute x29, waiting for transfers between devices, shift(): return lax.ppermute(value, ALL, pairs)  27.3 us
    pallas_call x2, Pallas kernels, score_call(): pl.pallas_call(lambda *refs: score_kernel(chunk, spans, *refs), grid_spec...  18.3 us
    all_to_all x1, waiting for transfers between devices, body(): kg = lax.all_to_all(kg, ('z', 'ylo'), 0, 0, tiled=True)  10.2 us
    pallas_call x1, Pallas kernels, backward_call(): pl.pallas_call(backward_kernel, grid_spec=pltpu.PrefetchScalarGridSpec(nu...  7.89 us
    all_to_all x1, starting transfers between devices, body(): kg = lax.all_to_all(kg, ('z', 'ylo'), 0, 0, tiled=True)  5.52 us
    pallas_call x1, Pallas kernels, forward_call(): pl.pallas_call(forward_kernel, grid_spec=pltpu.PrefetchScalarGridSpec(num...  3.94 us
    pallas_call x1, Pallas kernels, head_sum_call(): pl.pallas_call(head_sum_kernel, grid_spec=pltpu.PrefetchScalarGridSpec(nu...  3.29 us
  transfers between devices with their start and end apart: 30, of which 15 were waited for; matrix products, arithmetic and copies ran while one was open for 5% of the time, Pallas kernels for 15%

profile of v15, /device:TPU:2, one launch (start us, length us, event | category | flops | bytes accessed | tf_op | source)
XLA Modules:
  0.0 125.9 jit_solution(13028555912671552960)
XLA Ops:
  1.8 1.9 %collective-permute-start = (bf16[80,704]{1,0:T(8,128)(2,1)S(1)}, bf16[80,704]{1,0:T(8,128)(2,1)S(1)}, u32[]{:S(2)}, u32[]{:S(2)}) collective-permute-start(bf16[80,704]{1,0:T(8,128)(2,1)S(1)} %fusion.refs_1_), channel_id=1, source_target_pairs={{0,4},{1,5},{4,8},{5,9},{8,12},{9,13},{12,16},{13,17},{16,20},{17,... | collective-permute-start | bytes 337928 | tf_op jit(solution)/shard_map/ppermute | solution.py:40
  3.7 4.0 %collective-permute-start.1 = (bf16[80,704]{1,0:T(8,128)(2,1)S(1)}, bf16[80,704]{1,0:T(8,128)(2,1)S(1)}, u32[]{:S(2)}, u32[]{:S(2)}) collective-permute-start(bf16[80,704]{1,0:T(8,128)(2,1)S(1)} %fusion.refs_1_), channel_id=1, source_target_pairs={{0,28},{1,29},{4,0},{5,1},{8,4},{9,5},{12,8},{13,9},{16,12},{17,13... | collective-permute-start | bytes 337928 | tf_op jit(solution)/shard_map/ppermute | solution.py:40
  7.7 2.4 %fusion.2 = (bf16[4,576,128]{2,1,0:T(8,128)(2,1)}, bf16[4,576,128]{2,1,0:T(8,128)(2,1)}) fusion(bf16[8,576,128]{2,1,0:T(8,128)(2,1)} %bitcast.17), kind=kLoop, calls=%fused_computation.14 | loop fusion | bytes 2359296 | tf_op jit(solution)/shard_map/slice | solution.py:502
  16.1 3.2 %collective-permute-start.3 = (bf16[80,704]{1,0:T(8,128)(2,1)S(1)}, bf16[80,704]{1,0:T(8,128)(2,1)S(1)}, u32[]{:S(2)}, u32[]{:S(2)}) collective-permute-start(bf16[80,704]{1,0:T(8,128)(2,1)S(1)} %collective-permute-done.1.refs_3_), channel_id=1, source_target_pairs={{0,28},{1,29},{4,0},{5,1},{8,4},{9,5},{12,8},{13,9},{16,12},{17,13... | collective-permute-start | bytes 337928 | tf_op jit(solution)/shard_map/ppermute | solution.py:40
  19.5 2.7 %collective-permute-done.2.refs_4_ = bf16[80,704]{1,0:T(8,128)(2,1)S(1)} collective-permute-done((bf16[80,704]{1,0:T(8,128)(2,1)S(1)}, bf16[80,704]{1,0:T(8,128)(2,1)S(1)}, u32[]{:S(2)}, u32[]{:S(2)}) %collective-permute-start.2) | collective-permute-done | bytes 112672 | tf_op jit(solution)/shard_map/ppermute | solution.py:40
  22.2 2.5 %collective-permute-start.4 = (bf16[80,704]{1,0:T(8,128)(2,1)S(1)}, bf16[80,704]{1,0:T(8,128)(2,1)S(1)}, u32[]{:S(2)}, u32[]{:S(2)}) collective-permute-start(bf16[80,704]{1,0:T(8,128)(2,1)S(1)} %collective-permute-done.2.refs_4_), channel_id=1, source_target_pairs={{0,4},{1,5},{4,8},{5,9},{8,12},{9,13},{12,16},{13,17},{16,20},{17,... | collective-permute-start | bytes 337928 | tf_op jit(solution)/shard_map/ppermute | solution.py:40
  25.4 3.7 %collective-permute-done.4.refs_6_ = bf16[80,704]{1,0:T(8,128)(2,1)S(1)} collective-permute-done((bf16[80,704]{1,0:T(8,128)(2,1)S(1)}, bf16[80,704]{1,0:T(8,128)(2,1)S(1)}, u32[]{:S(2)}, u32[]{:S(2)}) %collective-permute-start.4) | collective-permute-done | bytes 112672 | tf_op jit(solution)/shard_map/ppermute | solution.py:40
  30.3 2.0 %collective-permute-start.11 = (bf16[80,704]{1,0:T(8,128)(2,1)S(1)}, bf16[80,704]{1,0:T(8,128)(2,1)S(1)}, u32[]{:S(2)}, u32[]{:S(2)}) collective-permute-start(bf16[80,704]{1,0:T(8,128)(2,1)S(1)} %collective-permute-done.4.refs_6_), channel_id=1, source_target_pairs={{0,4},{1,5},{4,8},{5,9},{8,12},{9,13},{12,16},{13,17},{16,20},{17,... | collective-permute-start | bytes 337928 | tf_op jit(solution)/shard_map/ppermute | solution.py:40
  32.4 2.9 %copy.13 = bf16[128,64,128]{2,0,1:T(8,128)(2,1)S(1)} copy(bf16[128,64,128]{2,1,0:T(8,128)(2,1)} %param.9) | data formatting | bytes 4194304 | tf_op args[2]
  40.9 9.6 %scores.2 = (bf16[16,1280,256]{2,1,0:T(8,128)(2,1)S(1)}, f32[16,256]{1,0:T(8,128)S(1)}, f32[16,256]{1,0:T(8,128)S(1)}, bf16[320,128]{1,0:T(8,128)(2,1)S(1)}) custom-call(s32[5]{0:T(128)S(1)} %stack.23.refs_0_.meta, bf16[80,704]{1,0:T(8,128)(2,1)S(1)} %fusion.refs_1_, bf16[80,704]{1,0:T(8,128)(2,1)S(1)} %collective-permute-done.refs_2_, ...), custom_call_target="tpu_custom_call" | custom-call | flops 6039797760 | bytes 5242880 | tf_op jit(solution)/shard_map/scores/pallas_call | solution.py:158
  50.5 8.8 %scores.3 = (bf16[16,1280,256]{2,1,0:T(8,128)(2,1)S(1)}, f32[16,256]{1,0:T(8,128)S(1)}, f32[16,256]{1,0:T(8,128)S(1)}, bf16[320,128]{1,0:T(8,128)(2,1)S(1)}) custom-call(s32[5]{0:T(128)S(1)} %stack.23.refs_0_.meta, bf16[240,704]{1,0:T(8,128)(2,1)S(1)} %collective-permute-done.9.refs_1_, ...), custom_call_target="tpu_custom_call", output_to_operand_aliasing={{0}: (4, {})} | custom-call | flops 6039797760 | bytes 5242880 | tf_op jit(solution)/shard_map/scores/pallas_call | solution.py:158
  59.3 3.9 %index_forward.1 = (f32[320,256]{1,0:T(8,128)S(1)}, f32[2,24,256]{2,1,0:T(8,128)S(1)}, f32[2,24,256]{2,1,0:T(8,128)S(1)}) custom-call(s32[5]{0:T(128)S(1)} %stack.23.refs_0_.meta, bf16[320,128]{1,0:T(8,128)(2,1)S(1)} %get-tuple-element.62.keys, f32[16,256]{1,0:T(8,128)S(1)} %get-tuple-element.63.m0, f32[16,256]{1,0:T(8,128)S(1)} %get-tuple-element.64.l0, ...), custom_call_target="tpu_custom_call" | custom-call | flops 1342177280 | bytes 5242880 | tf_op jit(solution)/shard_map/index_forward/pallas_call | solution.py:334
  66.8 3.4 %collective-permute-done.19.up = f32[2,8,256]{2,1,0:T(8,128)S(1)} collective-permute-done((f32[2,8,256]{2,1,0:T(8,128)S(1)}, f32[2,8,256]{2,1,0:T(8,128)S(1)}, u32[]{:S(2)}, u32[]{:S(2)}) %collective-permute-start.19) | collective-permute-done | bytes 16416 | tf_op jit(solution)/shard_map/ppermute | solution.py:40
  70.3 3.3 %head_sum.1 = (bf16[336,256]{1,0:T(8,128)(2,1)S(1)}, bf16[336,256]{1,0:T(8,128)(2,1)S(1)}, bf16[336,256]{1,0:T(8,128)(2,1)S(1)}, bf16[336,256]{1,0:T(8,128)(2,1)S(1)}) custom-call(s32[5]{0:T(128)S(1)} %stack.23.refs_0_.meta, bf16[16,1280,256]{2,1,0:T(8,128)(2,1)S(1)} %get-tuple-element.71.e_ref, f32[16,256]{1,0:T(8,128)S(1)} %get-tuple-element.63.m0, ...), custom_call_target="tpu_custom_call" | custom-call | bytes 11534336 | tf_op jit(solution)/shard_map/head_sum/pallas_call | solution.py:234
  73.6 3.0 %collective-permute-start.21 = (bf16[336,256]{1,0:T(8,128)(2,1)S(1)}, bf16[336,256]{1,0:T(8,128)(2,1)S(1)}, u32[]{:S(2)}, u32[]{:S(2)}) collective-permute-start(bf16[336,256]{1,0:T(8,128)(2,1)S(1)} %get-tuple-element.78), channel_id=1, source_target_pairs={{0,192},{1,193},{4,196},{5,197},{8,200},{9,201},{12,204},{13,205},... | collective-permute-start | bytes 516104 | tf_op jit(solution)/shard_map/ppermute | solution.py:40
  80.2 4.5 %collective-permute-done.21.t1 = bf16[336,256]{1,0:T(8,128)(2,1)S(1)} collective-permute-done((bf16[336,256]{1,0:T(8,128)(2,1)S(1)}, bf16[336,256]{1,0:T(8,128)(2,1)S(1)}, u32[]{:S(2)}, u32[]{:S(2)}) %collective-permute-start.21) | collective-permute-done | bytes 172064 | tf_op jit(solution)/shard_map/ppermute | solution.py:40
  86.5 7.9 %index_backward.1 = (f32[80,128]{1,0:T(8,128)S(1)}, f32[80,128]{1,0:T(8,128)S(1)}, bf16[16,32,128]{2,1,0:T(8,128)(2,1)}) custom-call(s32[5]{0:T(128)S(1)} %stack.23.refs_0_.meta, bf16[320,128]{1,0:T(8,128)(2,1)S(1)} %get-tuple-element.62.keys, f32[320,256]{1,0:T(8,128)S(1)} %get-tuple-element.70.logits, bf16[336,256]{1,0:T(8,128)(2,1)S(1)} %get-tuple-element.77.t0, ...), custom_call_target="tpu_custom_call" | custom-call | flops 2684354560 | bytes 6291456 | tf_op jit(solution)/shard_map/index_backward/pallas_call | solution.py:416
  94.4 5.5 %all-to-all-start = ((bf16[16,32,128]{2,1,0:T(8,128)(2,1)}), bf16[16,32,128]{2,1,0:T(8,128)(2,1)S(1)}, u32[]{:S(2)}, u32[]{:S(2)}) async-start(bf16[16,32,128]{2,1,0:T(8,128)(2,1)} %get-tuple-element.81), calls=%async_computation | async-start | bytes 262144 | tf_op jit(solution)/shard_map/all_to_all | solution.py:533
  99.9 10.2 %all-to-all-done = bf16[16,32,128]{2,1,0:T(8,128)(2,1)S(1)} async-done(((bf16[16,32,128]{2,1,0:T(8,128)(2,1)}), bf16[16,32,128]{2,1,0:T(8,128)(2,1)S(1)}, u32[]{:S(2)}, u32[]{:S(2)}) %all-to-all-start) | async-done | bytes 131104 | tf_op jit(solution)/shard_map/all_to_all | solution.py:533
  110.1 2.6 %collective-permute-start.25 = (bf16[112,128]{1,0:T(8,128)(2,1)S(1)}, bf16[112,128]{1,0:T(8,128)(2,1)S(1)}, u32[]{:S(2)}, u32[]{:S(2)}) collective-permute-start(bf16[112,128]{1,0:T(8,128)(2,1)S(1)} %pad_maximum_fusion.4), channel_id=1, source_target_pairs={{0,128},{1,129},{4,132},{5,133},{8,136},{9,137},{12,140},{13,141},... | collective-permute-start | bytes 86024 | tf_op jit(solution)/shard_map/ppermute | solution.py:40
  112.8 2.9 %collective-permute-done.25 = bf16[112,128]{1,0:T(8,128)(2,1)S(1)} collective-permute-done((bf16[112,128]{1,0:T(8,128)(2,1)S(1)}, bf16[112,128]{1,0:T(8,128)(2,1)S(1)}, u32[]{:S(2)}, u32[]{:S(2)}) %collective-permute-start.25) | collective-permute-done | bytes 28704 | tf_op jit(solution)/shard_map/ppermute | solution.py:40
  115.8 4.7 %collective-permute-start.27 = (bf16[224,128]{1,0:T(8,128)(2,1)S(1)}, bf16[224,128]{1,0:T(8,128)(2,1)S(1)}, u32[]{:S(2)}, u32[]{:S(2)}) collective-permute-start(bf16[224,128]{1,0:T(8,128)(2,1)S(1)} %pad_maximum_fusion.3.p0), channel_id=1, source_target_pairs={{0,64},{1,65},{4,68},{5,69},{8,72},{9,73},{12,76},{13,77},{16,80},... | collective-permute-start | bytes 172040 | tf_op jit(solution)/shard_map/ppermute | solution.py:40
  120.5 2.1 %collective-permute-done.27.p2 = bf16[224,128]{1,0:T(8,128)(2,1)S(1)} collective-permute-done((bf16[224,128]{1,0:T(8,128)(2,1)S(1)}, bf16[224,128]{1,0:T(8,128)(2,1)S(1)}, u32[]{:S(2)}, u32[]{:S(2)}) %collective-permute-start.27) | collective-permute-done | bytes 57376 | tf_op jit(solution)/shard_map/ppermute | solution.py:40
  122.6 2.0 %collective-permute-done.28.p3 = bf16[224,128]{1,0:T(8,128)(2,1)S(1)} collective-permute-done((bf16[224,128]{1,0:T(8,128)(2,1)S(1)}, bf16[224,128]{1,0:T(8,128)(2,1)S(1)}, u32[]{:S(2)}, u32[]{:S(2)}) %collective-permute-start.28) | collective-permute-done | bytes 57376 | tf_op jit(solution)/shard_map/ppermute | solution.py:40
  (65 shorter events, 24.6 us)
Async XLA Ops:
  1.8 9.2 %collective-permute-start = (bf16[80,704]{1,0:T(8,128)(2,1)S(1)}, bf16[80,704]{1,0:T(8,128)(2,1)S(1)}, u32[]{:S(2)}, u32[]{:S(2)}) collective-permute-start(bf16[80,704]{1,0:T(8,128)(2,1)S(1)} %fusion.refs_1_), channel_id=1, source_target_pairs={{0,4},{1,5},{4,8},{5,9},{8,12},{9,13},{12,16},{13,17},{16,20},{17,... | collective-permute-start | bytes 337928 | tf_op jit(solution)/shard_map/ppermute | solution.py:40
  3.7 7.3 %collective-permute-start.1 = (bf16[80,704]{1,0:T(8,128)(2,1)S(1)}, bf16[80,704]{1,0:T(8,128)(2,1)S(1)}, u32[]{:S(2)}, u32[]{:S(2)}) collective-permute-start(bf16[80,704]{1,0:T(8,128)(2,1)S(1)} %fusion.refs_1_), channel_id=1, source_target_pairs={{0,28},{1,29},{4,0},{5,1},{8,4},{9,5},{12,8},{13,9},{16,12},{17,13... | collective-permute-start | bytes 337928 | tf_op jit(solution)/shard_map/ppermute | solution.py:40
  11.0 18.7 %collective-permute-start.6 = (bf16[4,576,128]{2,1,0:T(8,128)(2,1)}, bf16[4,576,128]{2,1,0:T(8,128)(2,1)S(1)}, u32[]{:S(2)}, u32[]{:S(2)}) collective-permute-start(bf16[4,576,128]{2,1,0:T(8,128)(2,1)} %get-tuple-element.51), channel_id=1, source_target_pairs={{0,32},{1,33},{4,36},{5,37},{8,40},{9,41},{12,44},{13,45},{16,48},... | collective-permute-start | bytes 1769480 | tf_op jit(solution)/shard_map/ppermute | solution.py:40
  12.5 17.2 %collective-permute-start.7 = (bf16[4,576,128]{2,1,0:T(8,128)(2,1)}, bf16[4,576,128]{2,1,0:T(8,128)(2,1)S(1)}, u32[]{:S(2)}, u32[]{:S(2)}) collective-permute-start(bf16[4,576,128]{2,1,0:T(8,128)(2,1)} %get-tuple-element.52), channel_id=1, source_target_pairs={{0,96},{1,97},{4,100},{5,101},{8,104},{9,105},{12,108},{13,109},{1... | collective-permute-start | bytes 1769480 | tf_op jit(solution)/shard_map/ppermute | solution.py:40
  13.8 15.8 %collective-permute-start.9 = (bf16[240,704]{1,0:T(8,128)(2,1)}, bf16[240,704]{1,0:T(8,128)(2,1)S(1)}, u32[]{:S(2)}, u32[]{:S(2)}) collective-permute-start(bf16[240,704]{1,0:T(8,128)(2,1)} %pad_maximum_fusion), channel_id=1, source_target_pairs={{0,2},{1,3},{4,6},{5,7},{8,10},{9,11},{12,14},{13,15},{16,18},{17,... | collective-permute-start | bytes 1013768 | tf_op jit(solution)/shard_map/ppermute | solution.py:40
  16.0 6.2 %collective-permute-start.2 = (bf16[80,704]{1,0:T(8,128)(2,1)S(1)}, bf16[80,704]{1,0:T(8,128)(2,1)S(1)}, u32[]{:S(2)}, u32[]{:S(2)}) collective-permute-start(bf16[80,704]{1,0:T(8,128)(2,1)S(1)} %collective-permute-done.refs_2_), channel_id=1, source_target_pairs={{0,4},{1,5},{4,8},{5,9},{8,12},{9,13},{12,16},{13,17},{16,20},{17,... | collective-permute-start | bytes 337928 | tf_op jit(solution)/shard_map/ppermute | solution.py:40
  16.1 6.1 %collective-permute-start.3 = (bf16[80,704]{1,0:T(8,128)(2,1)S(1)}, bf16[80,704]{1,0:T(8,128)(2,1)S(1)}, u32[]{:S(2)}, u32[]{:S(2)}) collective-permute-start(bf16[80,704]{1,0:T(8,128)(2,1)S(1)} %collective-permute-done.1.refs_3_), channel_id=1, source_target_pairs={{0,28},{1,29},{4,0},{5,1},{8,4},{9,5},{12,8},{13,9},{16,12},{17,13... | collective-permute-start | bytes 337928 | tf_op jit(solution)/shard_map/ppermute | solution.py:40
  22.2 6.9 %collective-permute-start.4 = (bf16[80,704]{1,0:T(8,128)(2,1)S(1)}, bf16[80,704]{1,0:T(8,128)(2,1)S(1)}, u32[]{:S(2)}, u32[]{:S(2)}) collective-permute-start(bf16[80,704]{1,0:T(8,128)(2,1)S(1)} %collective-permute-done.2.refs_4_), channel_id=1, source_target_pairs={{0,4},{1,5},{4,8},{5,9},{8,12},{9,13},{12,16},{13,17},{16,20},{17,... | collective-permute-start | bytes 337928 | tf_op jit(solution)/shard_map/ppermute | solution.py:40
  29.6 7.6 %collective-permute-start.14 = (bf16[4,576,128]{2,1,0:T(8,128)(2,1)S(1)}, bf16[4,576,128]{2,1,0:T(8,128)(2,1)S(1)}, u32[]{:S(2)}, u32[]{:S(2)}) collective-permute-start(bf16[4,576,128]{2,1,0:T(8,128)(2,1)S(1)} %collective-permute-done.6.refs_11_.refs_8_), channel_id=1, source_target_pairs={{0,1},{1,0},{4,5},{5,4},{8,9},{9,8},{12,13},{13,12},{16,17},{17,16... | collective-permute-start | bytes 1769480 | tf_op jit(solution)/shard_map/ppermute | solution.py:40
  29.7 7.5 %collective-permute-start.15 = (bf16[4,576,128]{2,1,0:T(8,128)(2,1)S(1)}, bf16[4,576,128]{2,1,0:T(8,128)(2,1)S(1)}, u32[]{:S(2)}, u32[]{:S(2)}) collective-permute-start(bf16[4,576,128]{2,1,0:T(8,128)(2,1)S(1)} %collective-permute-done.7.refs_13_.refs_10_), channel_id=1, source_target_pairs={{0,1},{1,0},{4,5},{5,4},{8,9},{9,8},{12,13},{13,12},{16,17},{17,16... | collective-permute-start | bytes 1769480 | tf_op jit(solution)/shard_map/ppermute | solution.py:40
  30.2 10.6 %collective-permute-start.13 = (bf16[8,576,128]{2,1,0:T(8,128)(2,1)S(1)}, bf16[8,576,128]{2,1,0:T(8,128)(2,1)S(1)}, u32[]{:S(2)}, u32[]{:S(2)}) collective-permute-start(bf16[8,576,128]{2,1,0:T(8,128)(2,1)S(1)} %bitcast.18), channel_id=1, source_target_pairs={{0,1},{1,0},{4,5},{5,4},{8,9},{9,8},{12,13},{13,12},{16,17},{17,16... | collective-permute-start | bytes 3538952 | tf_op jit(solution)/shard_map/ppermute | solution.py:40
  30.3 6.9 %collective-permute-start.11 = (bf16[80,704]{1,0:T(8,128)(2,1)S(1)}, bf16[80,704]{1,0:T(8,128)(2,1)S(1)}, u32[]{:S(2)}, u32[]{:S(2)}) collective-permute-start(bf16[80,704]{1,0:T(8,128)(2,1)S(1)} %collective-permute-done.4.refs_6_), channel_id=1, source_target_pairs={{0,4},{1,5},{4,8},{5,9},{8,12},{9,13},{12,16},{13,17},{16,20},{17,... | collective-permute-start | bytes 337928 | tf_op jit(solution)/shard_map/ppermute | solution.py:40
  37.2 22.1 %collective-permute-start.16 = (bf16[64,128,128]{2,1,0:T(8,128)(2,1)S(1)}, bf16[64,128,128]{2,1,0:T(8,128)(2,1)S(1)}, u32[]{:S(2)}, u32[]{:S(2)}) collective-permute-start(bf16[64,128,128]{2,1,0:T(8,128)(2,1)S(1)} %bitcast.14), channel_id=1, source_target_pairs={{0,1},{1,0},{4,5},{5,4},{8,9},{9,8},{12,13},{13,12},{16,17},{17,16... | collective-permute-start | bytes 6291464 | tf_op jit(solution)/shard_map/ppermute | solution.py:40
  37.2 13.2 %collective-permute-start.10 = (bf16[160,704]{1,0:T(8,128)(2,1)S(1)}, bf16[160,704]{1,0:T(8,128)(2,1)S(1)}, u32[]{:S(2)}, u32[]{:S(2)}) collective-permute-start(bf16[160,704]{1,0:T(8,128)(2,1)S(1)} %pad_maximum_fusion.2), channel_id=1, source_target_pairs={{0,2},{1,3},{4,6},{5,7},{8,10},{9,11},{12,14},{13,15},{16,18},{17,... | collective-permute-start | bytes 675848 | tf_op jit(solution)/shard_map/ppermute | solution.py:40
  39.1 11.4 %collective-permute-start.12 = (bf16[240,704]{1,0:T(8,128)(2,1)S(1)}, bf16[240,704]{1,0:T(8,128)(2,1)S(1)}, u32[]{:S(2)}, u32[]{:S(2)}) collective-permute-start(bf16[240,704]{1,0:T(8,128)(2,1)S(1)} %pad_maximum_fusion.1), channel_id=1, source_target_pairs={{0,130},{1,131},{4,134},{5,135},{8,138},{9,139},{12,142},{13,143},... | collective-permute-start | bytes 1013768 | tf_op jit(solution)/shard_map/ppermute | solution.py:40
  40.9 18.4 %collective-permute-start.17 = (f32[64,128]{1,0:T(8,128)S(1)}, f32[64,128]{1,0:T(8,128)S(1)}, u32[]{:S(2)}, u32[]{:S(2)}) collective-permute-start(f32[64,128]{1,0:T(8,128)S(1)} %bitcast.21), channel_id=1, source_target_pairs={{0,1},{1,0},{4,5},{5,4},{8,9},{9,8},{12,13},{13,12},{16,17},{17,16... | collective-permute-start | bytes 98312 | tf_op jit(solution)/shard_map/ppermute | solution.py:40
  64.7 5.6 %collective-permute-start.20 = (f32[2,16,256]{2,1,0:T(8,128)S(1)}, f32[2,16,256]{2,1,0:T(8,128)S(1)}, u32[]{:S(2)}, u32[]{:S(2)}) collective-permute-start(f32[2,16,256]{2,1,0:T(8,128)S(1)} %get-tuple-element.76), channel_id=1, source_target_pairs={{0,96},{1,97},{4,100},{5,101},{8,104},{9,105},{12,108},{13,109},{1... | collective-permute-start | bytes 98312 | tf_op jit(solution)/shard_map/ppermute | solution.py:40
  73.6 11.0 %collective-permute-start.21 = (bf16[336,256]{1,0:T(8,128)(2,1)S(1)}, bf16[336,256]{1,0:T(8,128)(2,1)S(1)}, u32[]{:S(2)}, u32[]{:S(2)}) collective-permute-start(bf16[336,256]{1,0:T(8,128)(2,1)S(1)} %get-tuple-element.78), channel_id=1, source_target_pairs={{0,192},{1,193},{4,196},{5,197},{8,200},{9,201},{12,204},{13,205},... | collective-permute-start | bytes 516104 | tf_op jit(solution)/shard_map/ppermute | solution.py:40
  76.6 8.6 %collective-permute-start.22 = (bf16[336,256]{1,0:T(8,128)(2,1)S(1)}, bf16[336,256]{1,0:T(8,128)(2,1)S(1)}, u32[]{:S(2)}, u32[]{:S(2)}) collective-permute-start(bf16[336,256]{1,0:T(8,128)(2,1)S(1)} %get-tuple-element.79), channel_id=1, source_target_pairs={{0,64},{1,65},{4,68},{5,69},{8,72},{9,73},{12,76},{13,77},{16,80},... | collective-permute-start | bytes 516104 | tf_op jit(solution)/shard_map/ppermute | solution.py:40
  78.3 8.1 %collective-permute-start.23 = (bf16[336,256]{1,0:T(8,128)(2,1)S(1)}, bf16[336,256]{1,0:T(8,128)(2,1)S(1)}, u32[]{:S(2)}, u32[]{:S(2)}) collective-permute-start(bf16[336,256]{1,0:T(8,128)(2,1)S(1)} %get-tuple-element.80), channel_id=1, source_target_pairs={{0,128},{1,129},{4,132},{5,133},{8,136},{9,137},{12,140},{13,141},... | collective-permute-start | bytes 516104 | tf_op jit(solution)/shard_map/ppermute | solution.py:40
  94.3 5.5 %collective-permute-start.24 = (f32[80,128]{1,0:T(8,128)S(1)}, f32[80,128]{1,0:T(8,128)S(1)}, u32[]{:S(2)}, u32[]{:S(2)}) collective-permute-start(f32[80,128]{1,0:T(8,128)S(1)} %get-tuple-element.83), channel_id=1, source_target_pairs={{0,1},{1,0},{4,5},{5,4},{8,9},{9,8},{12,13},{13,12},{16,17},{17,16... | collective-permute-start | bytes 122888 | tf_op jit(solution)/shard_map/ppermute | solution.py:40
  94.4 15.8 %all-to-all-start = ((bf16[16,32,128]{2,1,0:T(8,128)(2,1)}), bf16[16,32,128]{2,1,0:T(8,128)(2,1)S(1)}, u32[]{:S(2)}, u32[]{:S(2)}) async-start(bf16[16,32,128]{2,1,0:T(8,128)(2,1)} %get-tuple-element.81), calls=%async_computation | async-start | bytes 262144 | tf_op jit(solution)/shard_map/all_to_all | solution.py:533
  110.1 5.5 %collective-permute-start.25 = (bf16[112,128]{1,0:T(8,128)(2,1)S(1)}, bf16[112,128]{1,0:T(8,128)(2,1)S(1)}, u32[]{:S(2)}, u32[]{:S(2)}) collective-permute-start(bf16[112,128]{1,0:T(8,128)(2,1)S(1)} %pad_maximum_fusion.4), channel_id=1, source_target_pairs={{0,128},{1,129},{4,132},{5,133},{8,136},{9,137},{12,140},{13,141},... | collective-permute-start | bytes 86024 | tf_op jit(solution)/shard_map/ppermute | solution.py:40
  115.8 6.8 %collective-permute-start.27 = (bf16[224,128]{1,0:T(8,128)(2,1)S(1)}, bf16[224,128]{1,0:T(8,128)(2,1)S(1)}, u32[]{:S(2)}, u32[]{:S(2)}) collective-permute-start(bf16[224,128]{1,0:T(8,128)(2,1)S(1)} %pad_maximum_fusion.3.p0), channel_id=1, source_target_pairs={{0,64},{1,65},{4,68},{5,69},{8,72},{9,73},{12,76},{13,77},{16,80},... | collective-permute-start | bytes 172040 | tf_op jit(solution)/shard_map/ppermute | solution.py:40
  (9 other events, 87.4 us)
